TPU v7x, 32 devices: a whole 2x2x4 slice. The times are simulated.
32 devices in a mesh: groups: 2 (over y), section: 4 (over z), head: 4 (over x, core).
Axes of the slice: x: 2, y: 2, z: 4, core: 2. Of those that a mesh axis runs over, the one named last changes fastest.
Arguments:
- rising: bfloat16 [8, 128, 1024], P(('groups', 'section')), parts along dimension 0, may hold values from -24 to 24
- falling: bfloat16 [8, 128, 1024], P(('groups', 'section')), parts along dimension 0, may hold values from -6 to 6
- stash: bfloat16 [8, 3, 128, 1024], P(('groups', 'section')), parts along dimension 0, may hold values from -24 to 24
- queue: bfloat16 [12, 128, 1024], P('groups'), parts along dimension 0, may hold values from -24 to 24
- order: int32 [12], P('groups'), parts along dimension 0, may hold values from 0 to 5, each once
- buckets: int32 [128, 128], replicated, may hold values from 0 to 31, as said below
- bias_table: float32 [4, 32, 64], P('section', None, 'head'), may hold values from -3 to 260
- gain: float32 [4, 1024], P('section'), may hold values from 0.1 to 1.9
- w_qkv: bfloat16 [4, 1024, 64, 3, 128], P('section', None, 'head'), may hold values from -0.1875 to 0.1875
- w_out: bfloat16 [4, 64, 128, 1024], P('section', 'head'), may hold values from -0.0625 to 0.0625
Outputs:
- rising_out: bfloat16 [8, 128, 1024], P(('groups', 'section')), parts along dimension 0
- falling_out: bfloat16 [8, 128, 1024], P(('groups', 'section')), parts along dimension 0
- table_grad: float32 [8, 32, 64], P(('groups', 'section'), None, 'head'), parts along dimension 0
There are 2 independent parts, one for each index of `groups`. A program takes and returns all parts, laid end to end along the dimension named above; an argument that names none is the same for every part. Nothing has to cross between parts.
Inputs may be any that keep to these rules, and one draw needn't show every extreme that they name: `order`: a permutation of 0 to 5. T5's bidirectional bucket of the key's position minus the query's, 32 buckets, distances of 128 or more in the outermost; positions rise by 1 to 4 from token to token, with one jump of 128 or more.
All inputs are finite; a program needn't handle non-finite values.
Results may differ from a plain program's by a relative error of at most 0.019.
Values may be sent and summed in bfloat16 or wider, within the bound.
No kernel may reach another device: no remote copies, remote signals or barrier semaphores. Data moves between devices by JAX's collectives and lax.ppermute only.
A program may use at most 128 MiB of HBM per device.

v0:
```python
import functools

import jax
import jax.numpy as jnp
from jax import lax
from jax.experimental import pallas as pl
from jax.experimental.pallas import tpu as pltpu
from jax.sharding import PartitionSpec as P

TICKS = 3
EPSILON = 1e-06
LANES = 128
ROWS16 = 16
LAST = (((1,), (1,)), ((), ()))
FIRST = (((0,), (0,)), ((), ()))
F32 = jnp.float32
BF16 = jnp.bfloat16
WHOLE = pl.BlockSpec(memory_space=pltpu.VMEM)
SCALARS = pl.BlockSpec(memory_space=pltpu.SMEM)
MIB = 1 << 20


def dot(a, b, dims=None):
    if dims is None:
        return jnp.dot(a, b, preferred_element_type=F32)
    return lax.dot_general(a, b, dims, preferred_element_type=F32)


def rms_normed(rows, gain_row):
    x = rows.astype(F32)
    inverse = lax.rsqrt(jnp.mean(x * x, axis=-1, keepdims=True) + EPSILON)
    return (x * inverse * gain_row).astype(BF16)


def relayout_kernel(heads, x_ref, gain_ref, w_ref, w_out_ref, qkv_ref, normed):
    @pl.when(pl.program_id(0) == 0)
    def _():
        normed[...] = rms_normed(x_ref[0], gain_ref[...])

    depth = w_ref.shape[0]
    size = ROWS16 * ROWS16
    row = lax.broadcasted_iota(jnp.int32, (size, size), 0)
    col = lax.broadcasted_iota(jnp.int32, (size, size), 1)
    wanted = (row & (ROWS16 - 1)) * ROWS16 + (row >> 4)
    permute = (col == wanted).astype(F32).astype(BF16)

    def step(i, carry):
        d0 = pl.multiple_of(i * 2 * ROWS16, 2 * ROWS16)
        first = w_ref[pl.ds(d0, ROWS16)].reshape(size, LANES)
        second = w_ref[pl.ds(d0 + ROWS16, ROWS16)].reshape(size, LANES)
        moved = dot(permute, jnp.concatenate([first, second], axis=1)).astype(BF16)
        for h in range(ROWS16):
            piece = moved[h * ROWS16 : (h + 1) * ROWS16]
            lanes = slice(h * LANES, (h + 1) * LANES)
            w_out_ref[0, pl.ds(d0, ROWS16), lanes] = piece[:, :LANES]
            w_out_ref[0, pl.ds(d0 + ROWS16, ROWS16), lanes] = piece[:, LANES:]
        return carry

    lax.fori_loop(0, depth // (2 * ROWS16), step, 0, unroll=2)
    qkv_ref[0] = dot(normed[...], w_out_ref[0]).astype(BF16)


def probs_of(query, key, table_row, bucket_ids, scale):
    bias = jnp.take_along_axis(
        jnp.broadcast_to(table_row, bucket_ids.shape), bucket_ids, axis=1
    )
    scores = dot(query, key, LAST) * scale + bias
    raised = jnp.exp(scores - jnp.max(scores, axis=-1, keepdims=True))
    return raised * (1.0 / jnp.sum(raised, axis=-1, keepdims=True))


def head_group(heads):
    return 4 if heads % 4 == 0 else 1


def forward_kernel(
    heads, projected, place_ref, *refs
):
    if projected:
        qkv_ref, table_ref, bucket_ref, wo_ref, send_ref, keep_ref, attended = refs
    else:
        (mine_ref, other_ref, arrival_ref, gain_ref, w_ref, table_ref, bucket_ref, wo_ref,
         send_ref, keep_ref, x_ref, attended) = refs
    head_dim = LANES
    scale = head_dim ** (-0.5)
    core = place_ref[0]
    half = send_ref.shape[0]
    group = head_group(heads)
    width = group * head_dim
    normed = None
    if not projected:
        x_ref[pl.ds(pl.multiple_of(core * half, half), half)] = mine_ref[...]
        x_ref[pl.ds(pl.multiple_of((1 - core) * half, half), half)] = other_ref[...]

        @pl.when(place_ref[1] == 0)
        def _():
            x_ref[...] = arrival_ref[...]

        normed = rms_normed(x_ref[...], gain_ref[...])

    def step(g, carry):
        at = pl.ds(pl.multiple_of(g * width, width), width)
        if projected:
            query, key, value = (qkv_ref[c, :, at] for c in range(3))
        else:
            query, key, value = (dot(normed, w_ref[c, :, at]).astype(BF16) for c in range(3))
        outs = []
        for h in range(group):
            sl = slice(h * head_dim, (h + 1) * head_dim)
            probs = probs_of(
                query[:, sl], key[:, sl], table_ref[pl.ds(g * group + h, 1)], bucket_ref[...], scale
            )
            outs.append(dot(probs.astype(BF16), value[:, sl]).astype(BF16))
        attended[:, at] = jnp.concatenate(outs, axis=1)
        return carry

    lax.fori_loop(0, heads // group, step, 0)
    send_at = pl.ds(pl.multiple_of((1 - core) * half, half), half)
    keep_at = pl.ds(pl.multiple_of(core * half, half), half)
    send_ref[...] = dot(attended[send_at], wo_ref[...]).astype(BF16)
    keep_ref[...] = dot(attended[keep_at], wo_ref[...])


def stash_kernel(x_ref, gain_ref, w_ref, qkv_ref, normed):
    ticks, tokens, _ = x_ref.shape
    for t in range(ticks):
        normed[t * tokens : (t + 1) * tokens] = rms_normed(x_ref[t], gain_ref[...])
    width = min(512, w_ref.shape[2])

    def step(i, carry):
        at = pl.ds(pl.multiple_of(i * width, width), width)
        for c in range(3):
            out = dot(normed[...], w_ref[c, :, at]).astype(BF16)
            for t in range(ticks):
                qkv_ref[t, c, :, at] = out[t * tokens : (t + 1) * tokens]
        return carry

    lax.fori_loop(0, w_ref.shape[2] // width, step, 0)


def backward_kernel(heads, first, place_ref, *refs):
    if first:
        (g_in_ref, qkv_ref, table_ref, bucket_ref, w_ref, wo_ref,
         send_ref, keep_ref, acc_ref, stacked) = refs
        g_ref = g_in_ref
    else:
        (mine_ref, other_ref, qkv_ref, table_ref, bucket_ref, w_ref, wo_ref, acc_in_ref,
         send_ref, keep_ref, acc_ref, stacked, g_ref) = refs
    head_dim = LANES
    scale = head_dim ** (-0.5)
    core = place_ref[0]
    half = send_ref.shape[0]
    group = head_group(heads)
    width = group * head_dim
    if not first:
        g_ref[pl.ds(pl.multiple_of(core * half, half), half)] = mine_ref[...]
        g_ref[pl.ds(pl.multiple_of((1 - core) * half, half), half)] = other_ref[...]

    def step(g, carry):
        at = pl.ds(pl.multiple_of(g * width, width), width)
        query, key, value = (qkv_ref[c, :, at] for c in range(3))
        grad_attn = dot(g_ref[...], wo_ref[at], LAST).astype(BF16)
        grads = ([], [], [])
        for h in range(group):
            sl = slice(h * head_dim, (h + 1) * head_dim)
            q, k, v, ga = query[:, sl], key[:, sl], value[:, sl], grad_attn[:, sl]
            probs = probs_of(q, k, table_ref[pl.ds(g * group + h, 1)], bucket_ref[...], scale)
            probs16 = probs.astype(BF16)
            grad_probs = dot(ga, v, LAST)
            row = jnp.sum(probs * grad_probs, axis=-1, keepdims=True)
            grad_scores = probs * (grad_probs - row)
            grad16 = grad_scores.astype(BF16)
            if first:
                acc_ref[g * group + h] = grad_scores
            else:
                acc_ref[g * group + h] = acc_in_ref[g * group + h] + grad_scores
            grads[0].append((dot(grad16, k) * scale).astype(BF16))
            grads[1].append((dot(grad16, q, FIRST) * scale).astype(BF16))
            grads[2].append(dot(probs16, ga, FIRST).astype(BF16))
        for c in range(3):
            stacked[c, :, at] = jnp.concatenate(grads[c], axis=1)
        return carry

    lax.fori_loop(0, heads // group, step, 0)
    total = dot(stacked[0], w_ref[0], LAST)
    total += dot(stacked[1], w_ref[1], LAST)
    total += dot(stacked[2], w_ref[2], LAST)

    @pl.when(core == 0)
    def _():
        send_ref[...] = total[half:].astype(BF16)
        keep_ref[...] = total[:half]

    @pl.when(core != 0)
    def _():
        send_ref[...] = total[:half].astype(BF16)
        keep_ref[...] = total[half:]


def finish_back_kernel(x_ref, g_ref, gain_ref, first_ref, second_ref, out_ref):
    x = x_ref[...].astype(F32)
    inverse = lax.rsqrt(jnp.mean(x * x, axis=-1, keepdims=True) + EPSILON)
    weighted = gain_ref[...] * (first_ref[...].astype(F32) + second_ref[...].astype(F32))
    mean = jnp.mean(x * weighted, axis=-1, keepdims=True)
    cubed = inverse * inverse * inverse
    out_ref[...] = (g_ref[...].astype(F32) + inverse * weighted - x * cubed * mean).astype(BF16)


def table_kernel(buckets_here, acc_ref, bucket_ref, out_ref):
    heads, tokens, _ = acc_ref.shape
    rows = 8
    cells = heads * rows
    columns = buckets_here * rows
    total = jnp.zeros((cells, columns), F32)
    for i in range(tokens // rows):
        at = slice(i * rows, (i + 1) * rows)
        ids = bucket_ref[at]
        hits = jnp.concatenate(
            [(ids == b).astype(F32) for b in range(buckets_here)], axis=0
        ).astype(BF16)
        part = acc_ref[:, at, :].reshape(cells, tokens)
        high = part.astype(BF16)
        low = (part - high.astype(F32)).astype(BF16)
        total += dot(high, hits, LAST) + dot(low, hits, LAST)
    row = lax.broadcasted_iota(jnp.int32, (cells, columns), 0)
    col = lax.broadcasted_iota(jnp.int32, (cells, columns), 1)
    total = jnp.where((row & (rows - 1)) == (col & (rows - 1)), total, 0.0)
    out_ref[...] = jnp.sum(total.reshape(heads, rows, columns), axis=1)


def call(kernel, out_shape, args, scratch=(), specs=None, flops=0, limit=40, **more):
    return pl.pallas_call(
        kernel,
        out_shape=out_shape,
        in_specs=specs or [WHOLE] * len(args),
        out_specs=jax.tree.map(lambda _: WHOLE, out_shape),
        scratch_shapes=list(scratch),
        compiler_params=pltpu.CompilerParams(vmem_limit_bytes=limit * MIB),
        cost_estimate=pl.CostEstimate(flops=flops, bytes_accessed=1 << 20, transcendentals=0),
        **more,
    )(*args)


def shape(dims, dtype=BF16):
    return jax.ShapeDtypeStruct(dims, dtype)


def vmem(x):
    return pltpu.with_memory_space_constraint(x, pltpu.VMEM)


def shifted(block, axis, distance):
    devices = range(lax.axis_size(axis))
    route = [(i - distance, i) for i in devices if i - distance in devices]
    return lax.ppermute(block, axis, route)


def swapped(block, bit):
    return lax.ppermute(block, "head", [(i, i ^ bit) for i in range(lax.axis_size("head"))])


def per_device(rising, falling, stash, queue, order, buckets, bias_table, gain, w_qkv, w_out):
    section_index = lax.axis_index("section")
    section_count = lax.axis_size("section")
    head_index = lax.axis_index("head")
    head_count = lax.axis_size("head")
    _, model_width, heads, _, head_dim = w_qkv.shape
    tokens = buckets.shape[0]
    bucket_count = bias_table.shape[1]
    half = tokens // 2
    inner = heads * head_dim
    core = head_index % 2
    place = jnp.stack([core, section_index]).astype(jnp.int32)
    table = jnp.pad(bias_table[0].T, ((0, 0), (0, LANES - bucket_count)))
    wo = w_out[0].reshape(inner, model_width)
    is_last = section_index == section_count - 1
    per_mac = 2 * tokens * model_width * inner

    def own_half(full):
        return lax.dynamic_slice_in_dim(full, core * half, half, 0)

    if heads % ROWS16 == 0:
        rows_first = jnp.transpose(w_qkv[0], (0, 2, 1, 3)).reshape(model_width, 3 * heads, head_dim)
        weights, qkv = pl.pallas_call(
            functools.partial(relayout_kernel, heads),
            grid=(3,),
            out_shape=(shape((3, model_width, inner)), shape((3, tokens, inner))),
            in_specs=[
                pl.BlockSpec((1, tokens, model_width), lambda c: (0, 0, 0)),
                pl.BlockSpec((1, model_width), lambda c: (0, 0)),
                pl.BlockSpec((model_width, heads, head_dim), lambda c: (0, c, 0)),
            ],
            out_specs=(
                pl.BlockSpec((1, model_width, inner), lambda c: (c, 0, 0)),
                pl.BlockSpec((1, tokens, inner), lambda c: (c, 0, 0)),
            ),
            scratch_shapes=[pltpu.VMEM((tokens, model_width), BF16)],
            compiler_params=pltpu.CompilerParams(vmem_limit_bytes=40 * MIB),
            cost_estimate=pl.CostEstimate(
                flops=9 * per_mac, bytes_accessed=8 * w_qkv.size, transcendentals=0
            ),
        )(rising, gain, rows_first)
    else:
        weights = jnp.transpose(w_qkv[0], (2, 0, 1, 3)).reshape(3, model_width, inner)
        qkv = call(
            stash_kernel,
            shape((1, 3, tokens, inner)),
            (rising, gain, weights),
            scratch=[pltpu.VMEM((tokens, model_width), BF16)],
            flops=3 * per_mac,
        )[0]

    def forward(x_parts, projections):
        scratch = [pltpu.VMEM((tokens, inner), BF16)]
        common = (table, buckets, wo)
        if x_parts is None:
            args = (place, projections) + common
        else:
            args = (place,) + x_parts + (gain, weights) + common
            scratch = [pltpu.VMEM((tokens, model_width), BF16)] + scratch
        return call(
            functools.partial(forward_kernel, heads, x_parts is None),
            (shape((half, model_width)), shape((half, model_width), F32)),
            args,
            scratch=scratch,
            specs=[SCALARS] + [WHOLE] * (len(args) - 1),
            flops=per_mac * (2 if x_parts is None else 5),
        )

    def backward(g_parts, projections, acc):
        scratch = [pltpu.VMEM((3, tokens, inner), BF16)]
        first = acc is None
        args = (place,) + g_parts + (projections, table, buckets, weights, wo)
        if not first:
            args += (acc,)
            scratch += [pltpu.VMEM((tokens, model_width), BF16)]
        return call(
            functools.partial(backward_kernel, heads, first),
            (
                shape((half, model_width)),
                shape((half, model_width), F32),
                shape((heads, tokens, tokens), F32),
            ),
            args,
            scratch=scratch,
            specs=[SCALARS] + [WHOLE] * (len(args) - 1),
            flops=per_mac * 6,
        )

    def reduced(send, keep):
        pair = (keep + swapped(send, 1).astype(F32)).astype(BF16)
        bit = 2
        while 2 * bit < head_count:
            pair = (pair.astype(F32) + swapped(pair, bit).astype(F32)).astype(BF16)
            bit *= 2
        return pair, swapped(pair, bit)

    x_half = own_half(rising[0])
    g_half = own_half(falling[0])
    x_parts = None
    g_parts = (falling[0],)
    acc = None
    stashed = None
    for t in range(TICKS):
        send, keep = forward(x_parts, qkv)
        first, second = reduced(send, keep)
        lifted = (x_half.astype(F32) + (first.astype(F32) + second.astype(F32))).astype(BF16)
        if stashed is None:
            stashed = call(
                stash_kernel,
                shape((TICKS, 3, tokens, inner)),
                (stash[0], gain, weights),
                scratch=[pltpu.VMEM((TICKS * tokens, model_width), BF16)],
                flops=3 * TICKS * per_mac,
            )
        send, keep, acc = backward(g_parts, stashed[t], acc)
        first, second = reduced(send, keep)
        lowered = call(
            finish_back_kernel,
            shape((half, model_width)),
            (own_half(stash[0, t]), g_half, gain, first, second),
        )
        if t + 1 < TICKS:
            arrival = lax.dynamic_index_in_dim(queue, order[t], 0, keepdims=False)
            climbed = shifted(lifted, "section", 1)
            x_parts = (climbed, swapped(climbed, 1), arrival)
            x_half = jnp.where(section_index == 0, own_half(arrival), climbed)
            g_half = jnp.where(is_last, lifted, shifted(lowered, "section", -1))
            g_parts = (g_half, swapped(g_half, 1))

    def whole(mine):
        other = swapped(mine, 1)
        low = jnp.where(core == 0, mine, other)
        high = jnp.where(core == 0, other, mine)
        return jnp.concatenate([low, high], axis=0)[None]

    cells = call(
        functools.partial(table_kernel, bucket_count), shape((heads, bucket_count * 8), F32), (acc, buckets)
    )
    table_grad = cells.reshape(heads, bucket_count, 8).sum(-1).T[None]
    return (whole(lifted), whole(lowered), table_grad)


def solution(mesh):
    return jax.shard_map(
        per_device,
        mesh=mesh,
        in_specs=(
            P(("groups", "section"), None, None),
            P(("groups", "section"), None, None),
            P(("groups", "section"), None, None, None),
            P("groups", None, None),
            P("groups"),
            P(),
            P("section", None, "head"),
            P("section", None),
            P("section", None, "head", None, None),
            P("section", "head", None, None),
        ),
        out_specs=(
            P(("groups", "section"), None, None),
            P(("groups", "section"), None, None),
            P(("groups", "section"), None, "head"),
        ),
        check_vma=False,
    )
```

profile of v0, /device:TPU:0, one launch (start us, length us, event | category | flops | bytes accessed | tf_op | source)
XLA Modules:
  0.0 197.8 jit_solution(13977475716930055552)
XLA Ops:
  3.1 17.0 %shard_map.121 = (bf16[3,1024,2048]{2,1,0:T(8,128)(2,1)S(1)}, bf16[3,128,2048]{2,1,0:T(8,128)(2,1)S(1)}) custom-call(bf16[1,128,1024]{2,1,0:T(8,128)(2,1)S(1)} %copy-done.19, f32[1,1024]{1,0:T(1,128)S(1)} %copy-done.17, bf16[1024,48,128]{2,1,0:T(8,128)(2,1)} %bitcast.65), custom_call_target="tpu_custom_call" | custom-call | flops 4831838208 | bytes 50331648 | tf_op jit(solution)/shard_map/pallas_call | solution.py:284
  20.1 4.6 %copy-done = bf16[3,1024,2048]{2,1,0:T(8,128)(2,1)} copy-done((bf16[3,1024,2048]{2,1,0:T(8,128)(2,1)}, bf16[3,1024,2048]{2,1,0:T(8,128)(2,1)S(1)}, u32[]{:S(2)}) %copy-start) | copy-done | bytes 12582936
  24.7 8.3 %shard_map.122 = (bf16[64,1024]{1,0:T(8,128)(2,1)}, f32[64,1024]{1,0:T(8,128)S(1)}) custom-call(s32[2]{0:T(128)S(1)} %pad_add_fusion.place_ref, bf16[3,128,2048]{2,1,0:T(8,128)(2,1)S(1)} %get-tuple-element.20.refs_0_, f32[16,128]{1,0:T(8,128)S(1)} %pad.4.refs_1_.refs_5_.refs_2_.refs_3_, s32[128,128]{1,0:T(8,128)S(1)} %copy-done.6, ...), custom_call_target="tpu_custom_call" | custom-call | flops 1073741824 | bytes 1048576 | tf_op jit(solution)/shard_map/pallas_call | solution.py:232
  34.1 10.5 %shard_map.125 = bf16[3,3,128,2048]{3,2,1,0:T(8,128)(2,1)S(1)} custom-call(bf16[3,128,1024]{2,1,0:T(8,128)(2,1)S(1)} %bitcast.61, f32[1,1024]{1,0:T(1,128)S(1)} %copy-done.18, bf16[3,1024,2048]{2,1,0:T(8,128)(2,1)} %copy-done), custom_call_target="tpu_custom_call" | custom-call | flops 4831838208 | bytes 1048576 | tf_op jit(solution)/shard_map/pallas_call | solution.py:232
  45.5 18.8 %shard_map.126 = (bf16[64,1024]{1,0:T(8,128)(2,1)}, f32[64,1024]{1,0:T(8,128)S(1)}, f32[16,128,128]{2,1,0:T(8,128)S(1)}) custom-call(s32[2]{0:T(128)S(1)} %pad_add_fusion.place_ref, bf16[128,1024]{1,0:T(8,128)(2,1)S(1)} %bitcast.62, bf16[3,128,2048]{2,1,0:T(8,128)(2,1)S(1)} %get-tuple-element.46.refs_1_, f32[16,128]{1,0:T(8,128)S(1)} %pad.4.refs_1_.refs_5_.refs_2_.refs_3_, ...), custom_call_target="tpu_custom_call" | custom-call | flops 3221225472 | bytes 1048576 | tf_op jit(solution)/shard_map/pallas_call | solution.py:232
  68.9 3.0 %collective-permute-start.12 = (bf16[64,1024]{1,0:T(8,128)(2,1)S(1)}, bf16[64,1024]{1,0:T(8,128)(2,1)S(1)}, u32[]{:S(2)}, u32[]{:S(2)}) collective-permute-start(bf16[64,1024]{1,0:T(8,128)(2,1)S(1)} %add_convert_fusion.2.first_ref), channel_id=1, source_target_pairs={{0,2},{1,3},{2,0},{3,1},{4,6},{5,7},{6,4},{7,5},{8,10},{9,11},{10,... | collective-permute-start | bytes 393224 | tf_op jit(solution)/shard_map/ppermute | solution.py:259
  73.0 2.8 %collective-permute-done.12.second_ref = bf16[64,1024]{1,0:T(8,128)(2,1)S(1)} collective-permute-done((bf16[64,1024]{1,0:T(8,128)(2,1)S(1)}, bf16[64,1024]{1,0:T(8,128)(2,1)S(1)}, u32[]{:S(2)}, u32[]{:S(2)}) %collective-permute-start.12) | collective-permute-done | bytes 131104 | tf_op jit(solution)/shard_map/ppermute | solution.py:259
  76.0 1.3 collective-permute-start.13
  77.3 1.6 dynamic-slice_bitcast_fusion.4.x_ref
  78.8 4.2 %collective-permute-done.13 = bf16[64,1024]{1,0:T(8,128)(2,1)} collective-permute-done((bf16[64,1024]{1,0:T(8,128)(2,1)S(1)}, bf16[64,1024]{1,0:T(8,128)(2,1)}, u32[]{:S(2)}, u32[]{:S(2)}) %collective-permute-start.13) | collective-permute-done | bytes 131104 | tf_op jit(solution)/shard_map/ppermute | solution.py:255
  83.0 1.8 broadcast_select_fusion.1
  84.8 4.1 %collective-permute-start.2 = (bf16[64,1024]{1,0:T(8,128)(2,1)}, bf16[64,1024]{1,0:T(8,128)(2,1)S(1)}, u32[]{:S(2)}, u32[]{:S(2)}) collective-permute-start(bf16[64,1024]{1,0:T(8,128)(2,1)} %get-tuple-element.43), channel_id=1, source_target_pairs={{0,4},{4,8},{8,12},{1,5},{5,9},{9,13},{2,6},{6,10},{10,14},{3,7},{... | collective-permute-start | bytes 393224 | tf_op jit(solution)/shard_map/ppermute | solution.py:255
  93.4 1.9 dynamic-slice_bitcast_fusion
  95.8 2.2 %copy-done.2 = bf16[1,16,128,1024]{3,2,1,0:T(8,128)(2,1)S(1)} copy-done((bf16[1,16,128,1024]{3,2,1,0:T(8,128)(2,1)S(1)}, bf16[1,16,128,1024]{3,2,1,0:T(8,128)(2,1)}, u32[]{:S(2)}) %copy-start.2) | copy-done | bytes 4194328
  98.0 18.3 %shard_map.128 = (bf16[64,1024]{1,0:T(8,128)(2,1)S(1)}, f32[64,1024]{1,0:T(8,128)S(1)}, f32[16,128,128]{2,1,0:T(8,128)S(1)}) custom-call(s32[2]{0:T(128)S(1)} %pad_add_fusion.place_ref, bf16[64,1024]{1,0:T(8,128)(2,1)S(1)} %get-tuple-element.42.refs_0_.g_ref, bf16[64,1024]{1,0:T(8,128)(2,1)} %collective-permute-done.14.refs_1_, ...), custom_call_target="tpu_custom_call" | custom-call | flops 3221225472 | bytes 1048576 | tf_op jit(solution)/shard_map/pallas_call | solution.py:232
  116.4 13.0 %shard_map.123 = (bf16[64,1024]{1,0:T(8,128)(2,1)S(1)}, f32[64,1024]{1,0:T(8,128)S(1)}) custom-call(s32[2]{0:T(128)S(1)} %pad_add_fusion.place_ref, bf16[64,1024]{1,0:T(8,128)(2,1)S(1)} %collective-permute-done.2.refs_0_, bf16[64,1024]{1,0:T(8,128)(2,1)S(1)} %collective-permute-done.3.refs_1_, bf16[128,1024]{1,0:T(8,128)(2,1)S(1)} %get-tuple-element.48.refs_2_, ...), custom_call_target="tpu_custom_call" | custom-call | flops 2684354560 | bytes 1048576 | tf_op jit(solution)/shard_map/pallas_call | solution.py:232
  129.8 2.1 %collective-permute-start.16 = (bf16[64,1024]{1,0:T(8,128)(2,1)S(1)}, bf16[64,1024]{1,0:T(8,128)(2,1)S(1)}, u32[]{:S(2)}, u32[]{:S(2)}) collective-permute-start(bf16[64,1024]{1,0:T(8,128)(2,1)S(1)} %add_convert_fusion.1.first_ref), channel_id=1, source_target_pairs={{0,2},{1,3},{2,0},{3,1},{4,6},{5,7},{6,4},{7,5},{8,10},{9,11},{10,... | collective-permute-start | bytes 393224 | tf_op jit(solution)/shard_map/ppermute | solution.py:259
  131.9 1.1 collective-permute-start.5
  133.0 3.2 %collective-permute-done.16.second_ref = bf16[64,1024]{1,0:T(8,128)(2,1)S(1)} collective-permute-done((bf16[64,1024]{1,0:T(8,128)(2,1)S(1)}, bf16[64,1024]{1,0:T(8,128)(2,1)S(1)}, u32[]{:S(2)}, u32[]{:S(2)}) %collective-permute-start.16) | collective-permute-done | bytes 131104 | tf_op jit(solution)/shard_map/ppermute | solution.py:259
  136.3 1.3 collective-permute-start.17
  138.6 4.6 %collective-permute-done.17 = bf16[64,1024]{1,0:T(8,128)(2,1)S(1)} collective-permute-done((bf16[64,1024]{1,0:T(8,128)(2,1)S(1)}, bf16[64,1024]{1,0:T(8,128)(2,1)S(1)}, u32[]{:S(2)}, u32[]{:S(2)}) %collective-permute-start.17) | collective-permute-done | bytes 131104 | tf_op jit(solution)/shard_map/ppermute | solution.py:255
  143.2 1.0 broadcast_select_fusion
  144.2 3.5 %collective-permute-start.6 = (bf16[64,1024]{1,0:T(8,128)(2,1)S(1)}, bf16[64,1024]{1,0:T(8,128)(2,1)S(1)}, u32[]{:S(2)}, u32[]{:S(2)}) collective-permute-start(bf16[64,1024]{1,0:T(8,128)(2,1)S(1)} %get-tuple-element.41), channel_id=1, source_target_pairs={{0,4},{4,8},{8,12},{1,5},{5,9},{9,13},{2,6},{6,10},{10,14},{3,7},{... | collective-permute-start | bytes 393224 | tf_op jit(solution)/shard_map/ppermute | solution.py:255
  147.7 2.4 %collective-permute-done.6.refs_0_ = bf16[64,1024]{1,0:T(8,128)(2,1)S(1)} collective-permute-done((bf16[64,1024]{1,0:T(8,128)(2,1)S(1)}, bf16[64,1024]{1,0:T(8,128)(2,1)S(1)}, u32[]{:S(2)}, u32[]{:S(2)}) %collective-permute-start.6) | collective-permute-done | bytes 131104 | tf_op jit(solution)/shard_map/ppermute | solution.py:255
  150.2 2.2 %copy-done.4 = bf16[1,16,128,1024]{3,2,1,0:T(8,128)(2,1)S(1)} copy-done((bf16[1,16,128,1024]{3,2,1,0:T(8,128)(2,1)S(1)}, bf16[1,16,128,1024]{3,2,1,0:T(8,128)(2,1)}, u32[]{:S(2)}) %copy-start.4) | copy-done | bytes 4194328
  152.4 1.2 copy-done.12
  153.6 18.3 %shard_map.130 = (bf16[64,1024]{1,0:T(8,128)(2,1)S(1)}, f32[64,1024]{1,0:T(8,128)S(1)}, f32[16,128,128]{2,1,0:T(8,128)S(1)}) custom-call(s32[2]{0:T(128)S(1)} %pad_add_fusion.place_ref, bf16[64,1024]{1,0:T(8,128)(2,1)S(1)} %get-tuple-element.40.refs_0_.g_ref, bf16[64,1024]{1,0:T(8,128)(2,1)S(1)} %collective-permute-done.18.refs_1_, ...), custom_call_target="tpu_custom_call" | custom-call | flops 3221225472 | bytes 1048576 | tf_op jit(solution)/shard_map/pallas_call | solution.py:232
  172.5 13.0 %shard_map.124 = (bf16[64,1024]{1,0:T(8,128)(2,1)S(1)}, f32[64,1024]{1,0:T(8,128)S(1)}) custom-call(s32[2]{0:T(128)S(1)} %pad_add_fusion.place_ref, bf16[64,1024]{1,0:T(8,128)(2,1)S(1)} %collective-permute-done.6.refs_0_, bf16[64,1024]{1,0:T(8,128)(2,1)S(1)} %collective-permute-done.7.refs_1_, bf16[128,1024]{1,0:T(8,128)(2,1)S(1)} %copy-done.8, ...), custom_call_target="tpu_custom_call" | custom-call | flops 2684354560 | bytes 1048576 | tf_op jit(solution)/shard_map/pallas_call | solution.py:232
  185.6 2.1 %collective-permute-start.20 = (bf16[64,1024]{1,0:T(8,128)(2,1)S(1)}, bf16[64,1024]{1,0:T(8,128)(2,1)S(1)}, u32[]{:S(2)}, u32[]{:S(2)}) collective-permute-start(bf16[64,1024]{1,0:T(8,128)(2,1)S(1)} %add_convert_fusion.first_ref), channel_id=1, source_target_pairs={{0,2},{1,3},{2,0},{3,1},{4,6},{5,7},{6,4},{7,5},{8,10},{9,11},{10,... | collective-permute-start | bytes 393224 | tf_op jit(solution)/shard_map/ppermute | solution.py:259
  187.7 1.3 collective-permute-start.9
  190.6 1.5 collective-permute-done.20.second_ref
  192.3 2.3 %collective-permute-done.9 = bf16[64,1024]{1,0:T(8,128)(2,1)S(1)} collective-permute-done((bf16[64,1024]{1,0:T(8,128)(2,1)S(1)}, bf16[64,1024]{1,0:T(8,128)(2,1)S(1)}, u32[]{:S(2)}, u32[]{:S(2)}) %collective-permute-start.9) | collective-permute-done | bytes 131104 | tf_op jit(solution)/shard_map/ppermute | solution.py:259
  (96 shorter events, 18.8 us)
Async XLA Ops:
  3.1 21.6 %copy-start.1 = (bf16[1,16,128,1024]{3,2,1,0:T(8,128)(2,1)S(1)}, bf16[1,16,128,1024]{3,2,1,0:T(8,128)(2,1)}, u32[]{:S(2)}) copy-start(bf16[1,16,128,1024]{3,2,1,0:T(8,128)(2,1)} %param.19) | copy-start | bytes 12582916
  3.1 21.6 %copy-start.6 = (s32[128,128]{1,0:T(8,128)S(1)}, s32[128,128]{1,0:T(8,128)}, u32[]{:S(2)}) copy-start(s32[128,128]{1,0:T(8,128)} %bucket_ref.1) | copy-start | bytes 196612
  24.7 9.4 %copy-start.18 = (f32[1,1024]{1,0:T(1,128)S(1)}, f32[1,1024]{1,0:T(1,128)}, u32[]{:S(2)}) copy-start(f32[1,1024]{1,0:T(1,128)} %gain_ref.9) | copy-start | bytes 12292
  33.6 38.3 %collective-permute-start = (bf16[64,1024]{1,0:T(8,128)(2,1)}, bf16[64,1024]{1,0:T(8,128)(2,1)}, u32[]{:S(2)}, u32[]{:S(2)}) collective-permute-start(bf16[64,1024]{1,0:T(8,128)(2,1)} %get-tuple-element.22), channel_id=1, source_target_pairs={{0,1},{1,0},{2,3},{3,2},{4,5},{5,4},{6,7},{7,6},{8,9},{9,8},{10,11... | collective-permute-start | bytes 393224 | tf_op jit(solution)/shard_map/ppermute | solution.py:259
  66.0 1.9 collective-permute-start.11
  66.9 22.0 %copy-start.22 = (s32[6]{0:T(128)S(1)}, s32[6]{0:T(128)}, u32[]{:S(2)}) copy-start(s32[6]{0:T(128)} %param.14) | copy-start | bytes 76
  68.9 6.9 %collective-permute-start.12 = (bf16[64,1024]{1,0:T(8,128)(2,1)S(1)}, bf16[64,1024]{1,0:T(8,128)(2,1)S(1)}, u32[]{:S(2)}, u32[]{:S(2)}) collective-permute-start(bf16[64,1024]{1,0:T(8,128)(2,1)S(1)} %add_convert_fusion.2.first_ref), channel_id=1, source_target_pairs={{0,2},{1,3},{2,0},{3,1},{4,6},{5,7},{6,4},{7,5},{8,10},{9,11},{10,... | collective-permute-start | bytes 393224 | tf_op jit(solution)/shard_map/ppermute | solution.py:259
  72.9 5.9 %collective-permute-start.1 = (bf16[64,1024]{1,0:T(8,128)(2,1)S(1)}, bf16[64,1024]{1,0:T(8,128)(2,1)}, u32[]{:S(2)}, u32[]{:S(2)}) collective-permute-start(bf16[64,1024]{1,0:T(8,128)(2,1)S(1)} %add_convert_fusion.7), channel_id=1, source_target_pairs={{0,2},{1,3},{2,0},{3,1},{4,6},{5,7},{6,4},{7,5},{8,10},{9,11},{10,... | collective-permute-start | bytes 393224 | tf_op jit(solution)/shard_map/ppermute | solution.py:259
  76.0 7.0 %collective-permute-start.13 = (bf16[64,1024]{1,0:T(8,128)(2,1)S(1)}, bf16[64,1024]{1,0:T(8,128)(2,1)}, u32[]{:S(2)}, u32[]{:S(2)}) collective-permute-start(bf16[64,1024]{1,0:T(8,128)(2,1)S(1)} %shard_map.127), channel_id=1, source_target_pairs={{4,0},{8,4},{12,8},{5,1},{9,5},{13,9},{6,2},{10,6},{14,10},{7,3},{... | collective-permute-start | bytes 393224 | tf_op jit(solution)/shard_map/ppermute | solution.py:255
  84.8 10.5 %collective-permute-start.2 = (bf16[64,1024]{1,0:T(8,128)(2,1)}, bf16[64,1024]{1,0:T(8,128)(2,1)S(1)}, u32[]{:S(2)}, u32[]{:S(2)}) collective-permute-start(bf16[64,1024]{1,0:T(8,128)(2,1)} %get-tuple-element.43), channel_id=1, source_target_pairs={{0,4},{4,8},{8,12},{1,5},{5,9},{9,13},{2,6},{6,10},{10,14},{3,7},{... | collective-permute-start | bytes 393224 | tf_op jit(solution)/shard_map/ppermute | solution.py:255
  88.9 6.9 %collective-permute-start.14 = (bf16[64,1024]{1,0:T(8,128)(2,1)S(1)}, bf16[64,1024]{1,0:T(8,128)(2,1)}, u32[]{:S(2)}, u32[]{:S(2)}) collective-permute-start(bf16[64,1024]{1,0:T(8,128)(2,1)S(1)} %get-tuple-element.42.refs_0_.g_ref), channel_id=1, source_target_pairs={{0,1},{1,0},{2,3},{3,2},{4,5},{5,4},{6,7},{7,6},{8,9},{9,8},{10,11... | collective-permute-start | bytes 393224 | tf_op jit(solution)/shard_map/ppermute | solution.py:259
  95.3 21.1 %collective-permute-start.3 = (bf16[64,1024]{1,0:T(8,128)(2,1)S(1)}, bf16[64,1024]{1,0:T(8,128)(2,1)S(1)}, u32[]{:S(2)}, u32[]{:S(2)}) collective-permute-start(bf16[64,1024]{1,0:T(8,128)(2,1)S(1)} %collective-permute-done.2.refs_0_), channel_id=1, source_target_pairs={{0,1},{1,0},{2,3},{3,2},{4,5},{5,4},{6,7},{7,6},{8,9},{9,8},{10,11... | collective-permute-start | bytes 393224 | tf_op jit(solution)/shard_map/ppermute | solution.py:259
  98.0 18.5 %copy-start.3 = (bf16[1,16,128,1024]{3,2,1,0:T(8,128)(2,1)S(1)}, bf16[1,16,128,1024]{3,2,1,0:T(8,128)(2,1)}, u32[]{:S(2)}) copy-start(bf16[1,16,128,1024]{3,2,1,0:T(8,128)(2,1)} %param.19) | copy-start | bytes 12582916
  116.3 13.2 %copy-start.11 = (f32[16,128,128]{2,1,0:T(8,128)}, f32[16,128,128]{2,1,0:T(8,128)S(1)}, u32[]{:S(2)}) copy-start(f32[16,128,128]{2,1,0:T(8,128)S(1)} %get-tuple-element.33.refs_7_) | copy-start | bytes 3145732
  116.3 13.4 %collective-permute-start.15 = (bf16[64,1024]{1,0:T(8,128)(2,1)S(1)}, bf16[64,1024]{1,0:T(8,128)(2,1)S(1)}, u32[]{:S(2)}, u32[]{:S(2)}) collective-permute-start(bf16[64,1024]{1,0:T(8,128)(2,1)S(1)} %get-tuple-element.32), channel_id=1, source_target_pairs={{0,1},{1,0},{2,3},{3,2},{4,5},{5,4},{6,7},{7,6},{8,9},{9,8},{10,11... | collective-permute-start | bytes 393224 | tf_op jit(solution)/shard_map/ppermute | solution.py:259
  116.4 19.7 %copy-start.14 = (bf16[64,1024]{1,0:T(8,128)(2,1)S(1)}, bf16[64,1024]{1,0:T(8,128)(2,1)}, u32[]{:S(2)}) copy-start(bf16[64,1024]{1,0:T(8,128)(2,1)} %dynamic-slice_bitcast_fusion.4.x_ref) | copy-start | bytes 393220
  129.5 2.4 %collective-permute-start.4 = (bf16[64,1024]{1,0:T(8,128)(2,1)S(1)}, bf16[64,1024]{1,0:T(8,128)(2,1)S(1)}, u32[]{:S(2)}, u32[]{:S(2)}) collective-permute-start(bf16[64,1024]{1,0:T(8,128)(2,1)S(1)} %get-tuple-element.25), channel_id=1, source_target_pairs={{0,1},{1,0},{2,3},{3,2},{4,5},{5,4},{6,7},{7,6},{8,9},{9,8},{10,11... | collective-permute-start | bytes 393224 | tf_op jit(solution)/shard_map/ppermute | solution.py:259
  129.8 6.4 %collective-permute-start.16 = (bf16[64,1024]{1,0:T(8,128)(2,1)S(1)}, bf16[64,1024]{1,0:T(8,128)(2,1)S(1)}, u32[]{:S(2)}, u32[]{:S(2)}) collective-permute-start(bf16[64,1024]{1,0:T(8,128)(2,1)S(1)} %add_convert_fusion.1.first_ref), channel_id=1, source_target_pairs={{0,2},{1,3},{2,0},{3,1},{4,6},{5,7},{6,4},{7,5},{8,10},{9,11},{10,... | collective-permute-start | bytes 393224 | tf_op jit(solution)/shard_map/ppermute | solution.py:259
  131.9 6.7 %collective-permute-start.5 = (bf16[64,1024]{1,0:T(8,128)(2,1)S(1)}, bf16[64,1024]{1,0:T(8,128)(2,1)S(1)}, u32[]{:S(2)}, u32[]{:S(2)}) collective-permute-start(bf16[64,1024]{1,0:T(8,128)(2,1)S(1)} %add_convert_fusion.6), channel_id=1, source_target_pairs={{0,2},{1,3},{2,0},{3,1},{4,6},{5,7},{6,4},{7,5},{8,10},{9,11},{10,... | collective-permute-start | bytes 393224 | tf_op jit(solution)/shard_map/ppermute | solution.py:259
  136.3 6.9 %collective-permute-start.17 = (bf16[64,1024]{1,0:T(8,128)(2,1)S(1)}, bf16[64,1024]{1,0:T(8,128)(2,1)S(1)}, u32[]{:S(2)}, u32[]{:S(2)}) collective-permute-start(bf16[64,1024]{1,0:T(8,128)(2,1)S(1)} %shard_map.129), channel_id=1, source_target_pairs={{4,0},{8,4},{12,8},{5,1},{9,5},{13,9},{6,2},{10,6},{14,10},{7,3},{... | collective-permute-start | bytes 393224 | tf_op jit(solution)/shard_map/ppermute | solution.py:255
  144.2 6.0 %collective-permute-start.6 = (bf16[64,1024]{1,0:T(8,128)(2,1)S(1)}, bf16[64,1024]{1,0:T(8,128)(2,1)S(1)}, u32[]{:S(2)}, u32[]{:S(2)}) collective-permute-start(bf16[64,1024]{1,0:T(8,128)(2,1)S(1)} %get-tuple-element.41), channel_id=1, source_target_pairs={{0,4},{4,8},{8,12},{1,5},{5,9},{9,13},{2,6},{6,10},{10,14},{3,7},{... | collective-permute-start | bytes 393224 | tf_op jit(solution)/shard_map/ppermute | solution.py:255
  147.7 2.5 %collective-permute-start.18 = (bf16[64,1024]{1,0:T(8,128)(2,1)S(1)}, bf16[64,1024]{1,0:T(8,128)(2,1)S(1)}, u32[]{:S(2)}, u32[]{:S(2)}) collective-permute-start(bf16[64,1024]{1,0:T(8,128)(2,1)S(1)} %get-tuple-element.40.refs_0_.g_ref), channel_id=1, source_target_pairs={{0,1},{1,0},{2,3},{3,2},{4,5},{5,4},{6,7},{7,6},{8,9},{9,8},{10,11... | collective-permute-start | bytes 393224 | tf_op jit(solution)/shard_map/ppermute | solution.py:259
  150.2 22.3 %collective-permute-start.7 = (bf16[64,1024]{1,0:T(8,128)(2,1)S(1)}, bf16[64,1024]{1,0:T(8,128)(2,1)S(1)}, u32[]{:S(2)}, u32[]{:S(2)}) collective-permute-start(bf16[64,1024]{1,0:T(8,128)(2,1)S(1)} %collective-permute-done.6.refs_0_), channel_id=1, source_target_pairs={{0,1},{1,0},{2,3},{3,2},{4,5},{5,4},{6,7},{7,6},{8,9},{9,8},{10,11... | collective-permute-start | bytes 393224 | tf_op jit(solution)/shard_map/ppermute | solution.py:259
  153.6 18.9 %copy-start.5 = (bf16[1,16,128,1024]{3,2,1,0:T(8,128)(2,1)S(1)}, bf16[1,16,128,1024]{3,2,1,0:T(8,128)(2,1)}, u32[]{:S(2)}) copy-start(bf16[1,16,128,1024]{3,2,1,0:T(8,128)(2,1)} %param.19) | copy-start | bytes 12582916
  153.6 18.9 %copy-start.8 = (bf16[128,1024]{1,0:T(8,128)(2,1)S(1)}, bf16[128,1024]{1,0:T(8,128)(2,1)}, u32[]{:S(2)}) copy-start(bf16[128,1024]{1,0:T(8,128)(2,1)} %get-tuple-element.47.refs_2_) | copy-start | bytes 786436
  171.9 13.7 %collective-permute-start.19 = (bf16[64,1024]{1,0:T(8,128)(2,1)S(1)}, bf16[64,1024]{1,0:T(8,128)(2,1)S(1)}, u32[]{:S(2)}, u32[]{:S(2)}) collective-permute-start(bf16[64,1024]{1,0:T(8,128)(2,1)S(1)} %get-tuple-element.35), channel_id=1, source_target_pairs={{0,1},{1,0},{2,3},{3,2},{4,5},{5,4},{6,7},{7,6},{8,9},{9,8},{10,11... | collective-permute-start | bytes 393224 | tf_op jit(solution)/shard_map/ppermute | solution.py:259
  172.5 16.6 %copy-start.20 = (bf16[1,1,128,1024]{3,2,1,0:T(8,128)(2,1)S(1)}, bf16[1,1,128,1024]{3,2,1,0:T(8,128)(2,1)}, u32[]{:S(2)}) copy-start(bf16[1,1,128,1024]{3,2,1,0:T(8,128)(2,1)} %get-tuple-element.49) | copy-start | bytes 786436
  185.5 2.2 %collective-permute-start.8 = (bf16[64,1024]{1,0:T(8,128)(2,1)S(1)}, bf16[64,1024]{1,0:T(8,128)(2,1)S(1)}, u32[]{:S(2)}, u32[]{:S(2)}) collective-permute-start(bf16[64,1024]{1,0:T(8,128)(2,1)S(1)} %get-tuple-element.27), channel_id=1, source_target_pairs={{0,1},{1,0},{2,3},{3,2},{4,5},{5,4},{6,7},{7,6},{8,9},{9,8},{10,11... | collective-permute-start | bytes 393224 | tf_op jit(solution)/shard_map/ppermute | solution.py:259
  185.6 6.5 %collective-permute-start.20 = (bf16[64,1024]{1,0:T(8,128)(2,1)S(1)}, bf16[64,1024]{1,0:T(8,128)(2,1)S(1)}, u32[]{:S(2)}, u32[]{:S(2)}) collective-permute-start(bf16[64,1024]{1,0:T(8,128)(2,1)S(1)} %add_convert_fusion.first_ref), channel_id=1, source_target_pairs={{0,2},{1,3},{2,0},{3,1},{4,6},{5,7},{6,4},{7,5},{8,10},{9,11},{10,... | collective-permute-start | bytes 393224 | tf_op jit(solution)/shard_map/ppermute | solution.py:259
  187.7 6.9 %collective-permute-start.9 = (bf16[64,1024]{1,0:T(8,128)(2,1)S(1)}, bf16[64,1024]{1,0:T(8,128)(2,1)S(1)}, u32[]{:S(2)}, u32[]{:S(2)}) collective-permute-start(bf16[64,1024]{1,0:T(8,128)(2,1)S(1)} %add_convert_fusion.4), channel_id=1, source_target_pairs={{0,2},{1,3},{2,0},{3,1},{4,6},{5,7},{6,4},{7,5},{8,10},{9,11},{10,... | collective-permute-start | bytes 393224 | tf_op jit(solution)/shard_map/ppermute | solution.py:259
  192.2 3.5 %collective-permute-start.21 = (bf16[64,1024]{1,0:T(8,128)(2,1)S(1)}, bf16[64,1024]{1,0:T(8,128)(2,1)S(1)}, u32[]{:S(2)}, u32[]{:S(2)}) collective-permute-start(bf16[64,1024]{1,0:T(8,128)(2,1)S(1)} %shard_map.131), channel_id=1, source_target_pairs={{0,1},{1,0},{2,3},{3,2},{4,5},{5,4},{6,7},{7,6},{8,9},{9,8},{10,11... | collective-permute-start | bytes 393224 | tf_op jit(solution)/shard_map/ppermute | solution.py:259
  195.7 1.4 collective-permute-start.10
  (13 other events, 32.8 us)
where the time goes:
time: 199 us; the launch traced here: 198 us
  Pallas kernels  118 us (59%)
  local copies, waits for them, and re-layouts  22.5 us (11%)
  waiting for transfers between devices  22.5 us (11%)
  starting transfers between devices  22.1 us (11%)
  other arithmetic  7.58 us (4%)
  between operations  4.85 us (2%)
    pallas_call x11, Pallas kernels, call(): pl.pallas_call(kernel, out_shape=out_shape, in_specs=specs or [WHOLE] * l...  101 us
    pallas_call x1, Pallas kernels, per_device(): pl.pallas_call(functools.partial(relayout_kernel, heads), grid=(3,), out_...  17 us
    unnamed x47, local copies, waits for them, and re-layouts  15.3 us
    ppermute x18, starting transfers between devices, swapped(): lax.ppermute(block, 'head', [(i, i ^ bit) for i in range(lax.axis_size('h...  12 us
    ppermute x18, waiting for transfers between devices, swapped(): lax.ppermute(block, 'head', [(i, i ^ bit) for i in range(lax.axis_size('h...  11.3 us
    ppermute x4, waiting for transfers between devices, shifted(): return lax.ppermute(block, axis, route)  11.1 us
    ppermute x4, starting transfers between devices, shifted(): return lax.ppermute(block, axis, route)  10.1 us
  transfers between devices with their start and end apart: 22, of which 9 were waited for; matrix products, arithmetic and copies ran while one was open for 6% of the time, Pallas kernels for 47%

commit v1 on v0

v1 whole, which is shorter than its diff:
```python
import functools

import jax
import jax.numpy as jnp
from jax import lax
from jax.experimental import pallas as pl
from jax.experimental.pallas import tpu as pltpu
from jax.sharding import PartitionSpec as P

TICKS = 3
EPSILON = 1e-06
LANES = 128
ROWS16 = 16
LAST = (((1,), (1,)), ((), ()))
FIRST = (((0,), (0,)), ((), ()))
F32 = jnp.float32
BF16 = jnp.bfloat16
WHOLE = pl.BlockSpec(memory_space=pltpu.VMEM)
SCALARS = pl.BlockSpec(memory_space=pltpu.SMEM)
UNREAD = pl.BlockSpec(memory_space=pl.ANY)
MIB = 1 << 20


def dot(a, b, dims=None):
    if dims is None:
        return jnp.dot(a, b, preferred_element_type=F32)
    return lax.dot_general(a, b, dims, preferred_element_type=F32)


def rms_normed(rows, gain_row):
    x = rows.astype(F32)
    inverse = lax.rsqrt(jnp.mean(x * x, axis=-1, keepdims=True) + EPSILON)
    return (x * inverse * gain_row).astype(BF16)


def rows_at(index, size):
    return pl.ds(pl.multiple_of(index * size, size), size)


def fill_bias(table_ref, bucket_ref, bias_ref):
    ids = bucket_ref[...].T
    for h in range(bias_ref.shape[0]):
        row = jnp.broadcast_to(table_ref[h : h + 1], ids.shape)
        bias_ref[h] = jnp.take_along_axis(row, ids, axis=1)


def bias_kernel(table_ref, bucket_ref, bias_ref):
    fill_bias(table_ref, bucket_ref, bias_ref)


def relayout_kernel(x_ref, gain_ref, table_ref, bucket_ref, w_ref, w_out_ref, qkv_ref, bias_ref, normed):
    which = pl.program_id(0)
    block = pl.program_id(1)

    @pl.when((which == 0) & (block == 0))
    def _():
        normed[...] = rms_normed(x_ref[0], gain_ref[...])
        fill_bias(table_ref, bucket_ref, bias_ref)

    depth = w_ref.shape[0]
    size = ROWS16 * ROWS16
    row = lax.broadcasted_iota(jnp.int32, (size, size), 0)
    col = lax.broadcasted_iota(jnp.int32, (size, size), 1)
    wanted = (row & (ROWS16 - 1)) * ROWS16 + (row >> 4)
    permute = (col == wanted).astype(F32).astype(BF16)

    def step(i, carry):
        d0 = pl.multiple_of(i * 2 * ROWS16, 2 * ROWS16)
        first = w_ref[pl.ds(d0, ROWS16)].reshape(size, LANES)
        second = w_ref[pl.ds(d0 + ROWS16, ROWS16)].reshape(size, LANES)
        moved = dot(permute, jnp.concatenate([first, second], axis=1)).astype(BF16)
        to = pl.multiple_of(block * depth + d0, 2 * ROWS16)
        for h in range(ROWS16):
            piece = moved[h * ROWS16 : (h + 1) * ROWS16]
            lanes = slice(h * LANES, (h + 1) * LANES)
            w_out_ref[which, pl.ds(to, ROWS16), lanes] = piece[:, :LANES]
            w_out_ref[which, pl.ds(to + ROWS16, ROWS16), lanes] = piece[:, LANES:]
        return carry

    lax.fori_loop(0, depth // (2 * ROWS16), step, 0, unroll=4)

    @pl.when(block == pl.num_programs(1) - 1)
    def _():
        qkv_ref[which] = dot(normed[...], w_out_ref[which]).astype(BF16)


def probs_of(query, key, bias, scale):
    scores = dot(key, query, LAST) * scale + bias
    raised = jnp.exp(scores - jnp.max(scores, axis=0, keepdims=True))
    return raised * (1.0 / jnp.sum(raised, axis=0, keepdims=True))


def attend(query, key, value, bias_ref, heads, first_head):
    scale = LANES ** (-0.5)
    lanes = [slice(h * LANES, (h + 1) * LANES) for h in range(heads)]
    probs = [
        probs_of(query[:, sl], key[:, sl], bias_ref[first_head + h], scale).astype(BF16)
        for h, sl in enumerate(lanes)
    ]
    return [dot(p, value[:, sl], FIRST).astype(BF16) for p, sl in zip(probs, lanes)]


def first_attend_kernel(qkv_ref, bias_ref, out_ref):
    heads = bias_ref.shape[0]
    group = heads // 2

    def step(g, carry):
        at = rows_at(g, group * LANES)
        query, key, value = (qkv_ref[c, :, at] for c in range(3))
        outs = attend(query, key, value, bias_ref, group, g * group)
        out_ref[:, at] = jnp.concatenate(outs, axis=1)
        return carry

    lax.fori_loop(0, 2, step, 0)


def project_attend(normed, w_ref, bias_ref, out_ref, part):
    heads = bias_ref.shape[0] // 2
    at = slice(part * heads * LANES, (part + 1) * heads * LANES)
    query, key, value = (dot(normed, w_ref[c, :, at]).astype(BF16) for c in range(3))
    outs = attend(query, key, value, bias_ref, heads, part * heads)
    for h, out in enumerate(outs):
        out_ref[:, h * LANES : (h + 1) * LANES] = out


def forward_a_kernel(
    tick, place_ref, order_ref, mine_ref, other_ref, queue_ref, gain_ref, w_ref, bias_ref,
    out_ref, normed_ref, x_half_ref, x_ref,
):
    core = place_ref[0]
    half = mine_ref.shape[0]
    x_ref[rows_at(core, half)] = mine_ref[...]
    x_ref[rows_at(1 - core, half)] = other_ref[...]

    @pl.when(place_ref[1] == 0)
    def _():
        x_ref[...] = queue_ref[order_ref[tick - 1]]

    x_half_ref[...] = x_ref[rows_at(core, half)]
    normed = rms_normed(x_ref[...], gain_ref[...])
    normed_ref[...] = normed
    project_attend(normed, w_ref, bias_ref, out_ref, 0)


def forward_b_kernel(normed_ref, w_ref, bias_ref, out_ref):
    project_attend(normed_ref[...], w_ref, bias_ref, out_ref, 1)


def forward_c_kernel(place_ref, *refs):
    *attended, wo_ref, send_ref, keep_ref, joined = refs
    core = place_ref[0]
    half = send_ref.shape[0]
    width = 0
    for a in attended:
        joined[:, width : width + a.shape[1]] = a[...]
        width += a.shape[1]
    total = dot(joined[...], wo_ref[...])
    split_halves(core, total, send_ref, keep_ref)


def split_halves(core, total, send_ref, keep_ref):
    half = send_ref.shape[0]

    @pl.when(core == 0)
    def _():
        send_ref[...] = total[half:].astype(BF16)
        keep_ref[...] = total[:half]

    @pl.when(core != 0)
    def _():
        send_ref[...] = total[:half].astype(BF16)
        keep_ref[...] = total[half:]


def stash_kernel(x_ref, gain_ref, w_ref, *refs):
    *outs, normed = refs
    ticks, tokens, _ = x_ref.shape
    for t in range(ticks):
        normed[t * tokens : (t + 1) * tokens] = rms_normed(x_ref[t], gain_ref[...])
    width = min(512, w_ref.shape[2])

    def step(i, carry):
        at = rows_at(i, width)
        for c in range(3):
            out = dot(normed[...], w_ref[c, :, at]).astype(BF16)
            for t in range(ticks):
                outs[t][c, :, at] = out[t * tokens : (t + 1) * tokens]
        return carry

    lax.fori_loop(0, w_ref.shape[2] // width, step, 0)


def grad_attend(g, qkv_ref, bias_ref, wo_ref, acc_in_ref, stacked_ref, acc_ref, part):
    heads = bias_ref.shape[0] // 2
    scale = LANES ** (-0.5)
    at = slice(part * heads * LANES, (part + 1) * heads * LANES)
    grad_attn = dot(wo_ref[at], g, LAST).astype(BF16)
    for h in range(heads):
        here = slice((part * heads + h) * LANES, (part * heads + h + 1) * LANES)
        own = slice(h * LANES, (h + 1) * LANES)
        q, k, v = (qkv_ref[c, :, here] for c in range(3))
        ga = grad_attn[own]
        probs = probs_of(q, k, bias_ref[part * heads + h], scale)
        grad_probs = dot(v, ga)
        total = jnp.sum(probs * grad_probs, axis=0, keepdims=True)
        grad_scores = probs * (grad_probs - total)
        grad16 = grad_scores.astype(BF16)
        if acc_in_ref is None:
            acc_ref[h] = grad_scores
        else:
            acc_ref[h] = acc_in_ref[h] + grad_scores
        stacked_ref[0, :, own] = (dot(grad16, k, FIRST) * scale).astype(BF16)
        stacked_ref[1, :, own] = (dot(grad16, q) * scale).astype(BF16)
        stacked_ref[2, :, own] = dot(probs.astype(BF16), ga, LAST).astype(BF16)


def backward_a_kernel(first, place_ref, *refs):
    core = place_ref[0]
    if first:
        full_ref, qkv_ref, bias_ref, wo_ref, stacked_ref, acc_ref, g_ref, g_half_ref = refs
        acc_in_ref = None
        half = g_half_ref.shape[0]
        g_ref[...] = full_ref[...]
    else:
        (mine_ref, other_ref, qkv_ref, bias_ref, wo_ref, acc_in_ref,
         stacked_ref, acc_ref, g_ref, g_half_ref) = refs
        half = g_half_ref.shape[0]
        g_ref[rows_at(core, half)] = mine_ref[...]
        g_ref[rows_at(1 - core, half)] = other_ref[...]
    g_half_ref[...] = g_ref[rows_at(core, half)]
    grad_attend(g_ref[...], qkv_ref, bias_ref, wo_ref, acc_in_ref, stacked_ref, acc_ref, 0)


def backward_b_kernel(first, g_ref, qkv_ref, bias_ref, wo_ref, *refs):
    acc_in_ref = None if first else refs[0]
    stacked_ref, acc_ref = refs[-2:]
    grad_attend(g_ref[...], qkv_ref, bias_ref, wo_ref, acc_in_ref, stacked_ref, acc_ref, 1)


def backward_c_kernel(place_ref, low_ref, high_ref, w_ref, send_ref, keep_ref):
    width = low_ref.shape[2]
    total = None
    for c in range(3):
        for part, ref in enumerate((low_ref, high_ref)):
            term = dot(w_ref[c, :, part * width : (part + 1) * width], ref[c], LAST)
            total = term if total is None else total + term
    split_halves(place_ref[0], total.T, send_ref, keep_ref)


def pair_kernel(keep_ref, received_ref, out_ref):
    out_ref[...] = (keep_ref[...].astype(F32) + received_ref[...].astype(F32)).astype(BF16)


def finish_up_kernel(x_ref, first_ref, second_ref, out_ref):
    total = first_ref[...].astype(F32) + second_ref[...].astype(F32)
    out_ref[...] = (x_ref[...].astype(F32) + total).astype(BF16)


def finish_down_kernel(tick, place_ref, stash_ref, g_ref, gain_ref, first_ref, second_ref, out_ref):
    half = out_ref.shape[0]
    x = stash_ref[tick, rows_at(place_ref[0], half)].astype(F32)
    inverse = lax.rsqrt(jnp.mean(x * x, axis=-1, keepdims=True) + EPSILON)
    weighted = gain_ref[...] * (first_ref[...].astype(F32) + second_ref[...].astype(F32))
    mean = jnp.mean(x * weighted, axis=-1, keepdims=True)
    cubed = inverse * inverse * inverse
    out_ref[...] = (g_ref[...].astype(F32) + inverse * weighted - x * cubed * mean).astype(BF16)


def choose_kernel(place_ref, own_ref, arrived_ref, out_ref):
    @pl.when(place_ref[2] == 1)
    def _():
        out_ref[...] = own_ref[...]

    @pl.when(place_ref[2] == 0)
    def _():
        out_ref[...] = arrived_ref[...]


def join_kernel(place_ref, mine_ref, other_ref, out_ref):
    core = place_ref[0]
    half = mine_ref.shape[0]
    out_ref[0, rows_at(core, half)] = mine_ref[...]
    out_ref[0, rows_at(1 - core, half)] = other_ref[...]


def table_kernel(buckets_here, low_ref, high_ref, bucket_ref, out_ref):
    heads, tokens, _ = low_ref.shape
    rows = 8
    cells = 2 * heads * rows
    columns = buckets_here * rows
    total = jnp.zeros((cells, columns), F32)
    turned = bucket_ref[...].T
    for i in range(tokens // rows):
        at = slice(i * rows, (i + 1) * rows)
        ids = turned[at]
        hits = jnp.concatenate(
            [(ids == b).astype(F32) for b in range(buckets_here)], axis=0
        ).astype(BF16)
        part = jnp.concatenate(
            [r[:, at, :].reshape(heads * rows, tokens) for r in (low_ref, high_ref)], axis=0
        )
        high = part.astype(BF16)
        low = (part - high.astype(F32)).astype(BF16)
        total += dot(high, hits, LAST) + dot(low, hits, LAST)
    row = lax.broadcasted_iota(jnp.int32, (cells, columns), 0)
    col = lax.broadcasted_iota(jnp.int32, (cells, columns), 1)
    total = jnp.where((row & (rows - 1)) == (col & (rows - 1)), total, 0.0)
    summed = jnp.sum(total.reshape(2 * heads, rows, columns), axis=1)
    spread = lax.broadcasted_iota(jnp.int32, (columns, buckets_here), 0) >> 3
    bucket = lax.broadcasted_iota(jnp.int32, (columns, buckets_here), 1)
    fold = (spread == bucket).astype(F32)
    out_ref[...] = jnp.dot(
        summed, fold, preferred_element_type=F32, precision=lax.Precision.HIGHEST
    )


def shape(dims, dtype=BF16):
    return jax.ShapeDtypeStruct(dims, dtype)


class Chain:
    def __init__(self):
        self.before = None

    def __call__(self, kernel, out_shape, args, scratch=(), scalars=0, after=(), flops=0, limit=16):
        outs = out_shape if isinstance(out_shape, tuple) else (out_shape,)
        extra = tuple(after) + (() if self.before is None else (self.before,))
        count = len(args)

        def body(*refs):
            kernel(*refs[:count], *refs[count + len(extra) :])

        results = pl.pallas_call(
            body,
            out_shape=outs,
            in_specs=[SCALARS] * scalars + [WHOLE] * (count - scalars) + [UNREAD] * len(extra),
            out_specs=tuple(WHOLE for _ in outs),
            scratch_shapes=list(scratch),
            compiler_params=pltpu.CompilerParams(vmem_limit_bytes=limit * MIB),
            cost_estimate=pl.CostEstimate(flops=flops, bytes_accessed=MIB, transcendentals=0),
        )(*args, *extra)
        self.before = results[0]
        return results if isinstance(out_shape, tuple) else results[0]


def vmem(x):
    return pltpu.with_memory_space_constraint(x, pltpu.VMEM)


def shifted(block, axis, distance):
    devices = range(lax.axis_size(axis))
    route = [(i - distance, i) for i in devices if i - distance in devices]
    return lax.ppermute(block, axis, route)


def swapped(block, bit):
    return lax.ppermute(block, "head", [(i, i ^ bit) for i in range(lax.axis_size("head"))])


def per_device(rising, falling, stash, queue, order, buckets, bias_table, gain, w_qkv, w_out):
    section_index = lax.axis_index("section")
    section_count = lax.axis_size("section")
    head_index = lax.axis_index("head")
    head_count = lax.axis_size("head")
    _, model_width, heads, _, head_dim = w_qkv.shape
    tokens = buckets.shape[0]
    bucket_count = bias_table.shape[1]
    half = tokens // 2
    inner = heads * head_dim
    core = head_index % 2
    is_last = section_index == section_count - 1
    place = jnp.stack([core, section_index, is_last]).astype(jnp.int32)
    table = jnp.pad(bias_table[0].T, ((0, 0), (0, LANES - bucket_count)))
    wo = vmem(w_out[0].reshape(inner, model_width))
    per_mac = 2 * tokens * model_width * inner
    run = Chain()
    pairs = [1 << b for b in range(1, head_count.bit_length() - 1)]

    if heads % ROWS16 == 0:
        rows_first = jnp.transpose(w_qkv[0], (0, 2, 1, 3)).reshape(model_width, 3 * heads, head_dim)
        blocks = 4
        depth = model_width // blocks
        fixed = lambda rank: lambda c, b: (0,) * rank
        weights, qkv, bias = pl.pallas_call(
            relayout_kernel,
            grid=(3, blocks),
            out_shape=(
                pltpu.VMEM((3, model_width, inner), BF16),
                shape((3, tokens, inner)),
                shape((heads, tokens, tokens), F32),
            ),
            in_specs=[
                pl.BlockSpec((1, tokens, model_width), fixed(3)),
                pl.BlockSpec((1, model_width), fixed(2)),
                pl.BlockSpec((heads, LANES), fixed(2)),
                pl.BlockSpec((tokens, tokens), fixed(2)),
                pl.BlockSpec((depth, heads, head_dim), lambda c, b: (b, c, 0)),
            ],
            out_specs=(
                WHOLE,
                pl.BlockSpec((3, tokens, inner), fixed(3)),
                pl.BlockSpec((heads, tokens, tokens), fixed(3)),
            ),
            scratch_shapes=[pltpu.VMEM((tokens, model_width), BF16)],
            compiler_params=pltpu.CompilerParams(vmem_limit_bytes=24 * MIB),
            cost_estimate=pl.CostEstimate(
                flops=9 * per_mac, bytes_accessed=2 * w_qkv.size, transcendentals=0
            ),
        )(rising, gain, table, buckets, rows_first)
        run.before = qkv
    else:
        weights = jnp.transpose(w_qkv[0], (2, 0, 1, 3)).reshape(3, model_width, inner)
        bias = run(bias_kernel, shape((heads, tokens, tokens), F32), (table, buckets))
        qkv = run(
            stash_kernel,
            shape((3, tokens, inner)),
            (rising, gain, weights),
            scratch=[pltpu.VMEM((tokens, model_width), BF16)],
            flops=3 * per_mac,
        )
    weights = vmem(weights)
    halves = (shape((half, model_width)), shape((half, model_width), F32))
    half_rows = shape((half, model_width))
    acc_shape = shape((heads // 2, tokens, tokens), F32)
    part_shape = shape((tokens, inner // 2))
    stacked_shape = shape((3, tokens, inner // 2))
    row_scratch = pltpu.VMEM((tokens, model_width), BF16)

    def out_projection(attended):
        return run(
            forward_c_kernel,
            halves,
            (place,) + attended + (wo,),
            scratch=[pltpu.VMEM((tokens, inner), BF16)],
            scalars=1,
            flops=per_mac,
        )

    def across(pair):
        for bit in pairs[:-1]:
            pair = run(pair_kernel, half_rows, (pair, swapped(pair, bit)))
        return pair, swapped(pair, pairs[-1])

    x_half = lax.dynamic_slice_in_dim(rising[0], core * half, half, 0)
    stashed = None
    pending = None
    acc = (None, None)
    x_mine = x_other = g_mine = g_other = None

    def finish_down(state):
        tick, g_half, first, second = state
        return run(
            functools.partial(finish_down_kernel, tick),
            half_rows,
            (place, stash[0], g_half, gain, first, second),
            scalars=1,
        )

    for t in range(TICKS):
        final = t + 1 == TICKS
        if t == 0:
            attended = (run(first_attend_kernel, shape((tokens, inner)), (qkv, bias)),)
        else:
            low, normed, x_half = run(
                functools.partial(forward_a_kernel, t),
                (part_shape, shape((tokens, model_width)), half_rows),
                (place, order, x_mine, x_other, queue, gain, weights, bias),
                scratch=[row_scratch],
                scalars=2,
                flops=3 * per_mac,
            )
            send, keep, g_half = pending
            pair = run(pair_kernel, half_rows, (keep, swapped(send, 1)))
            first, second = across(pair)
            high = run(forward_b_kernel, part_shape, (normed, weights, bias), flops=3 * per_mac)
            lowered = finish_down((t - 1, g_half, first, second))
            descended = shifted(lowered, "section", -1)
            attended = (low, high)
        send, keep = out_projection(attended)
        swap_up = swapped(send, 1)
        if t == 0:
            stashed = run(
                stash_kernel,
                (shape((3, tokens, inner)),) * TICKS,
                (stash[0], gain, weights),
                scratch=[pltpu.VMEM((TICKS * tokens, model_width), BF16)],
                flops=3 * TICKS * per_mac,
            )
            g_parts = (falling[0],)
        else:
            g_mine = run(choose_kernel, half_rows, (place, lifted, descended), scalars=1)
            g_other = swapped(g_mine, 1)
            g_parts = (g_mine, g_other)

        def add_up():
            return across(run(pair_kernel, half_rows, (keep, swap_up)))

        if t == 0:
            first, second = add_up()
        acc_args = () if t == 0 else (acc[0],)
        stacked_low, acc_low, g_full, g_half = run(
            functools.partial(backward_a_kernel, t == 0),
            (stacked_shape, acc_shape, shape((tokens, model_width)), half_rows),
            (place,) + g_parts + (stashed[t], bias, wo) + acc_args,
            scalars=1,
            flops=3 * per_mac,
        )
        if t > 0:
            first, second = add_up()
            after = ()
        else:
            lifted = run(finish_up_kernel, half_rows, (x_half, first, second))
            climbed = shifted(lifted, "section", 1)
            after = ()
        acc_args = () if t == 0 else (acc[1],)
        stacked_high, acc_high = run(
            functools.partial(backward_b_kernel, t == 0),
            (stacked_shape, acc_shape),
            (g_full, stashed[t], bias, wo) + acc_args,
            flops=3 * per_mac,
        )
        acc = (acc_low, acc_high)
        if t > 0:
            lifted = run(finish_up_kernel, half_rows, (x_half, first, second))
            if not final:
                climbed = shifted(lifted, "section", 1)
        if not final:
            x_mine = climbed
            x_other = swapped(climbed, 1)
            after = (climbed,) if t == 0 else ()
        else:
            x_other = swapped(lifted, 1)
        send, keep = run(
            backward_c_kernel,
            halves,
            (place, stacked_low, stacked_high, weights),
            scalars=1,
            after=after,
            flops=3 * per_mac,
        )
        pending = (send, keep, g_half)

    send, keep, g_half = pending
    received = swapped(send, 1)
    rows = shape((1, tokens, model_width))
    rising_out = run(join_kernel, rows, (place, lifted, x_other), scalars=1)
    pair = run(pair_kernel, half_rows, (keep, received))
    first, second = across(pair)
    table_grad = run(
        functools.partial(table_kernel, bucket_count),
        shape((heads, bucket_count), F32),
        acc + (buckets,),
    )
    lowered = finish_down((TICKS - 1, g_half, first, second))
    falling_out = run(join_kernel, rows, (place, lowered, swapped(lowered, 1)), scalars=1)
    return (rising_out, falling_out, table_grad.T[None])


def solution(mesh):
    return jax.shard_map(
        per_device,
        mesh=mesh,
        in_specs=(
            P(("groups", "section"), None, None),
            P(("groups", "section"), None, None),
            P(("groups", "section"), None, None, None),
            P("groups", None, None),
            P("groups"),
            P(),
            P("section", None, "head"),
            P("section", None),
            P("section", None, "head", None, None),
            P("section", "head", None, None),
        ),
        out_specs=(
            P(("groups", "section"), None, None),
            P(("groups", "section"), None, None),
            P(("groups", "section"), None, "head"),
        ),
        check_vma=False,
    )
```

time: 199 us -> 149 us (0.75)
  Pallas kernels: 118 us -> 75.8 us
  other arithmetic: 7.58 us -> 0.08 us
  waiting for transfers between devices: 22.5 us -> 27.9 us
  between operations: 4.85 us -> 1.11 us
  starting transfers between devices: 22.1 us -> 18.9 us
    pallas_call x12 -> x36, Pallas kernels: 118 us -> 75.8 us  [the longest x35 63.4 us: __call__(): pl.pallas_call(body, out_shape=outs, in_specs=[SCALARS] * scalars + [WHOL...]
    unnamed x47 -> x48, local copies, waits for them, and re-layouts: 15.3 us -> 22.6 us
    ppermute x18, waiting for transfers between devices: 11.3 us -> 16.5 us  [swapped(): lax.ppermute(block, 'head', [(i, i ^ bit) for i in range(lax.axis_size('h...]
    convert_element_type x7 -> x0, other arithmetic: 3.13 us -> none  [the longest x6 2.13 us: reduced(): pair = (keep + swapped(send, 1).astype(F32)).astype(BF16)]
    select_n x4 -> x0, other arithmetic: 2.89 us -> none  [the longest x2 2.84 us: per_device(): g_half = jnp.where(is_last, lifted, shifted(lowered, 'section', -1))]
    ppermute x18, starting transfers between devices: 12 us -> 9.08 us  [swapped(): lax.ppermute(block, 'head', [(i, i ^ bit) for i in range(lax.axis_size('h...]
    squeeze x2 -> x0, local copies, waits for them, and re-layouts: 2.35 us -> none  [the longest x1 1.86 us: per_device(): arrival = lax.dynamic_index_in_dim(queue, order[t], 0, keepdims=False)]
  transfers between devices with their start and end apart: 22 -> 22, of which waited for: 9 -> 12; matrix products, arithmetic and copies ran while one was open for 6% -> 1% of each run, Pallas kernels for 47% -> 35%
where the time goes in v1:
time: 149 us; the launch traced here: 148 us
  Pallas kernels  75.8 us (51%)
  waiting for transfers between devices  27.9 us (19%)
  local copies, waits for them, and re-layouts  24.2 us (16%)
  starting transfers between devices  18.9 us (13%)
    pallas_call x35, Pallas kernels, __call__(): pl.pallas_call(body, out_shape=outs, in_specs=[SCALARS] * scalars + [WHOL...  63.4 us
    unnamed x48, local copies, waits for them, and re-layouts  22.6 us
    ppermute x18, waiting for transfers between devices, swapped(): lax.ppermute(block, 'head', [(i, i ^ bit) for i in range(lax.axis_size('h...  16.5 us
    pallas_call x1, Pallas kernels, per_device(): pl.pallas_call(relayout_kernel, grid=(3, blocks), out_shape=(pltpu.VMEM((...  12.4 us
    ppermute x4, waiting for transfers between devices, shifted(): return lax.ppermute(block, axis, route)  11.4 us
    ppermute x4, starting transfers between devices, shifted(): return lax.ppermute(block, axis, route)  9.81 us
    ppermute x18, starting transfers between devices, swapped(): lax.ppermute(block, 'head', [(i, i ^ bit) for i in range(lax.axis_size('h...  9.08 us
  transfers between devices with their start and end apart: 22, of which 12 were waited for; matrix products, arithmetic and copies ran while one was open for 1% of the time, Pallas kernels for 35%

profile of v1, /device:TPU:0, one launch (start us, length us, event | category | flops | bytes accessed | tf_op | source)
XLA Modules:
  0.0 147.9 jit_solution(1917201320840305682)
XLA Ops:
  3.8 4.6 %copy-done.23 = bf16[1,1024,16,3,128]{4,2,3,1,0:T(8,128)(2,1)S(1)} copy-done((bf16[1,1024,16,3,128]{4,2,3,1,0:T(8,128)(2,1)S(1)}, bf16[1,1024,16,3,128]{4,2,3,1,0:T(8,128)(2,1)}, u32[]{:S(2)}) %copy-start.23) | copy-done | bytes 12582936
  8.4 12.4 %shard_map.121 = (bf16[3,1024,2048]{2,1,0:T(8,128)(2,1)S(1)}, bf16[3,128,2048]{2,1,0:T(8,128)(2,1)S(1)}, f32[16,128,128]{2,1,0:T(8,128)S(1)}) custom-call(bf16[1,128,1024]{2,1,0:T(8,128)(2,1)S(1)} %copy-done.20, f32[1,1024]{1,0:T(1,128)S(1)} %copy-done.16, f32[16,128]{1,0:T(8,128)S(1)} %pad.4.table_ref, s32[128,128]{1,0:T(8,128)S(1)} %copy-done.18, ...), custom_call_target="tpu_custom_call" | custom-call | flops 4831838208 | bytes 12582912 | tf_op jit(solution)/shard_map/pallas_call | solution.py:384
  23.0 2.0 %shard_map.123 = (bf16[64,1024]{1,0:T(8,128)(2,1)}, f32[64,1024]{1,0:T(8,128)S(1)}) custom-call(s32[3]{0:T(128)S(1)} %pad_add_fusion.refs_0_, bf16[128,2048]{1,0:T(8,128)(2,1)S(1)} %shard_map.122.refs_1_.refs_3_, bf16[2048,1024]{1,0:T(8,128)(2,1)S(1)} %bitcast.19, bf16[128,2048]{1,0:T(8,128)(2,1)S(1)} %shard_map.122.refs_1_.refs_3_), custom_call_target="tpu_custom_call" | custom-call | flops 536870912 | bytes 1048576 | tf_op jit(solution)/shard_map/pallas_call | solution.py:333
  26.1 5.9 %shard_map.124 = (bf16[3,128,2048]{2,1,0:T(8,128)(2,1)S(1)}, bf16[3,128,2048]{2,1,0:T(8,128)(2,1)S(1)}, bf16[3,128,2048]{2,1,0:T(8,128)(2,1)S(1)}) custom-call(bf16[3,128,1024]{2,1,0:T(8,128)(2,1)S(1)} %bitcast.28, f32[1,1024]{1,0:T(1,128)S(1)} %copy-done.17, bf16[3,1024,2048]{2,1,0:T(8,128)(2,1)S(1)} %get-tuple-element.49.refs_2_.refs_3_.refs_6_.refs_1_, ...), custom_call_target="tpu_custom_call" | custom-call | flops 4831838208 | bytes 1048576 | tf_op jit(solution)/shard_map/pallas_call | solution.py:333
  32.1 4.6 %copy-done = bf16[3,1024,2048]{2,1,0:T(8,128)(2,1)} copy-done((bf16[3,1024,2048]{2,1,0:T(8,128)(2,1)}, bf16[3,1024,2048]{2,1,0:T(8,128)(2,1)S(1)}, u32[]{:S(2)}) %copy-start) | copy-done | bytes 12582936
  40.9 2.5 %collective-permute-start.1 = (bf16[64,1024]{1,0:T(8,128)(2,1)S(1)}, bf16[64,1024]{1,0:T(8,128)(2,1)S(1)}, u32[]{:S(2)}, u32[]{:S(2)}) collective-permute-start(bf16[64,1024]{1,0:T(8,128)(2,1)S(1)} %shard_map.125.refs_5_.refs_1_), channel_id=1, source_target_pairs={{0,2},{1,3},{2,0},{3,1},{4,6},{5,7},{6,4},{7,5},{8,10},{9,11},{10,... | collective-permute-start | bytes 393224 | tf_op jit(solution)/shard_map/ppermute | solution.py:357
  43.5 2.2 %copy-done.3 = bf16[1,16,128,1024]{3,2,1,0:T(8,128)(2,1)S(1)} copy-done((bf16[1,16,128,1024]{3,2,1,0:T(8,128)(2,1)S(1)}, bf16[1,16,128,1024]{3,2,1,0:T(8,128)(2,1)}, u32[]{:S(2)}) %copy-start.3) | copy-done | bytes 4194328
  45.7 4.3 %shard_map.126 = (bf16[3,128,1024]{2,1,0:T(8,128)(2,1)S(1)}, f32[8,128,128]{2,1,0:T(8,128)S(1)}, bf16[128,1024]{1,0:T(8,128)(2,1)S(1)}, bf16[64,1024]{1,0:T(8,128)(2,1)S(1)}) custom-call(s32[3]{0:T(128)S(1)} %pad_add_fusion.refs_0_, bf16[128,1024]{1,0:T(8,128)(2,1)S(1)} %bitcast.32, bf16[3,128,2048]{2,1,0:T(8,128)(2,1)S(1)} %get-tuple-element.50.refs_2_.refs_1_, ...), custom_call_target="tpu_custom_call" | custom-call | flops 1610612736 | bytes 1048576 | tf_op jit(solution)/shard_map/pallas_call | solution.py:333
  50.1 3.5 %collective-permute-start.2 = (bf16[64,1024]{1,0:T(8,128)(2,1)S(1)}, bf16[64,1024]{1,0:T(8,128)(2,1)S(1)}, u32[]{:S(2)}, u32[]{:S(2)}) collective-permute-start(bf16[64,1024]{1,0:T(8,128)(2,1)S(1)} %shard_map.127.refs_4_.refs_1_), channel_id=1, source_target_pairs={{0,4},{4,8},{8,12},{1,5},{5,9},{9,13},{2,6},{6,10},{10,14},{3,7},{... | collective-permute-start | bytes 393224 | tf_op jit(solution)/shard_map/ppermute | solution.py:353
  53.6 2.2 %copy-done.4 = bf16[1,16,128,1024]{3,2,1,0:T(8,128)(2,1)S(1)} copy-done((bf16[1,16,128,1024]{3,2,1,0:T(8,128)(2,1)S(1)}, bf16[1,16,128,1024]{3,2,1,0:T(8,128)(2,1)}, u32[]{:S(2)}) %copy-start.4) | copy-done | bytes 4194328
  55.8 3.8 %shard_map.128 = (bf16[3,128,1024]{2,1,0:T(8,128)(2,1)S(1)}, f32[8,128,128]{2,1,0:T(8,128)S(1)}) custom-call(bf16[128,1024]{1,0:T(8,128)(2,1)S(1)} %get-tuple-element.52.refs_0_, bf16[3,128,2048]{2,1,0:T(8,128)(2,1)S(1)} %get-tuple-element.50.refs_2_.refs_1_, f32[16,128,128]{2,1,0:T(8,128)S(1)} %get-tuple-element.46.refs_1_.refs_3_.refs_2_.refs_7_.refs_4_, ...), custom_call_target="tpu_custom_call" | custom-call | flops 1610612736 | bytes 1048576 | tf_op jit(solution)/shard_map/pallas_call | solution.py:333
  59.7 4.0 %shard_map.129 = (bf16[64,1024]{1,0:T(8,128)(2,1)S(1)}, f32[64,1024]{1,0:T(8,128)S(1)}) custom-call(s32[3]{0:T(128)S(1)} %pad_add_fusion.refs_0_, bf16[3,128,1024]{2,1,0:T(8,128)(2,1)S(1)} %get-tuple-element.51.refs_3_.refs_1_, bf16[3,128,1024]{2,1,0:T(8,128)(2,1)S(1)} %get-tuple-element.53.refs_2_.refs_5_, bf16[3,1024,2048]{2,1,0:T(8,128)(2,1)S(1)} %copy-done.1, ...), custom_call_target="tpu_custom_call" | custom-call | flops 1610612736 | bytes 1048576 | tf_op jit(solution)/shard_map/pallas_call | solution.py:333
  64.2 2.3 %shard_map.130 = (bf16[128,1024]{1,0:T(8,128)(2,1)S(1)}, bf16[128,1024]{1,0:T(8,128)(2,1)S(1)}, bf16[64,1024]{1,0:T(8,128)(2,1)S(1)}) custom-call(s32[3]{0:T(128)S(1)} %pad_add_fusion.refs_0_, s32[6]{0:T(128)S(1)} %copy-done.22, bf16[64,1024]{1,0:T(8,128)(2,1)S(1)} %collective-permute-done.2.refs_4_.refs_2_, ...), custom_call_target="tpu_custom_call" | custom-call | flops 1610612736 | bytes 1048576 | tf_op jit(solution)/shard_map/pallas_call | solution.py:333
  67.2 1.4 shard_map.132.refs_6_.refs_2_
  68.6 3.4 %collective-permute-done.5.refs_5_ = bf16[64,1024]{1,0:T(8,128)(2,1)S(1)} collective-permute-done((bf16[64,1024]{1,0:T(8,128)(2,1)S(1)}, bf16[64,1024]{1,0:T(8,128)(2,1)S(1)}, u32[]{:S(2)}, u32[]{:S(2)}) %collective-permute-start.5) | collective-permute-done | bytes 131104 | tf_op jit(solution)/shard_map/ppermute | solution.py:357
  72.8 1.4 collective-permute-start.7
  75.6 4.2 %collective-permute-done.7.refs_2_ = bf16[64,1024]{1,0:T(8,128)(2,1)S(1)} collective-permute-done((bf16[64,1024]{1,0:T(8,128)(2,1)S(1)}, bf16[64,1024]{1,0:T(8,128)(2,1)S(1)}, u32[]{:S(2)}, u32[]{:S(2)}) %collective-permute-start.7) | collective-permute-done | bytes 131104 | tf_op jit(solution)/shard_map/ppermute | solution.py:353
  81.8 4.4 %shard_map.136 = (bf16[3,128,1024]{2,1,0:T(8,128)(2,1)S(1)}, f32[8,128,128]{2,1,0:T(8,128)S(1)}, bf16[128,1024]{1,0:T(8,128)(2,1)S(1)}, bf16[64,1024]{1,0:T(8,128)(2,1)S(1)}) custom-call(s32[3]{0:T(128)S(1)} %pad_add_fusion.refs_0_, bf16[64,1024]{1,0:T(8,128)(2,1)S(1)} %shard_map.135.refs_1_.refs_7_, bf16[64,1024]{1,0:T(8,128)(2,1)S(1)} %collective-permute-done.8.refs_2_, ...), custom_call_target="tpu_custom_call" | custom-call | flops 1610612736 | bytes 1048576 | tf_op jit(solution)/shard_map/pallas_call | solution.py:333
  86.8 3.8 %shard_map.138 = (bf16[3,128,1024]{2,1,0:T(8,128)(2,1)S(1)}, f32[8,128,128]{2,1,0:T(8,128)S(1)}) custom-call(bf16[128,1024]{1,0:T(8,128)(2,1)S(1)} %get-tuple-element.65.refs_0_, bf16[3,128,2048]{2,1,0:T(8,128)(2,1)S(1)} %copy-done.11, f32[16,128,128]{2,1,0:T(8,128)S(1)} %get-tuple-element.46.refs_1_.refs_3_.refs_2_.refs_7_.refs_4_, ...), custom_call_target="tpu_custom_call" | custom-call | flops 1610612736 | bytes 1048576 | tf_op jit(solution)/shard_map/pallas_call | solution.py:333
  91.8 3.5 %collective-permute-start.10 = (bf16[64,1024]{1,0:T(8,128)(2,1)S(1)}, bf16[64,1024]{1,0:T(8,128)(2,1)S(1)}, u32[]{:S(2)}, u32[]{:S(2)}) collective-permute-start(bf16[64,1024]{1,0:T(8,128)(2,1)S(1)} %shard_map.139.refs_4_.refs_1_), channel_id=1, source_target_pairs={{0,4},{4,8},{8,12},{1,5},{5,9},{9,13},{2,6},{6,10},{10,14},{3,7},{... | collective-permute-start | bytes 393224 | tf_op jit(solution)/shard_map/ppermute | solution.py:353
  95.3 2.5 %collective-permute-done.10.refs_2_ = bf16[64,1024]{1,0:T(8,128)(2,1)S(1)} collective-permute-done((bf16[64,1024]{1,0:T(8,128)(2,1)S(1)}, bf16[64,1024]{1,0:T(8,128)(2,1)S(1)}, u32[]{:S(2)}, u32[]{:S(2)}) %collective-permute-start.10) | collective-permute-done | bytes 131104 | tf_op jit(solution)/shard_map/ppermute | solution.py:353
  97.8 4.0 %shard_map.140 = (bf16[64,1024]{1,0:T(8,128)(2,1)S(1)}, f32[64,1024]{1,0:T(8,128)S(1)}) custom-call(s32[3]{0:T(128)S(1)} %pad_add_fusion.refs_0_, bf16[3,128,1024]{2,1,0:T(8,128)(2,1)S(1)} %get-tuple-element.64.refs_2_.refs_1_, bf16[3,128,1024]{2,1,0:T(8,128)(2,1)S(1)} %get-tuple-element.67.refs_3_.refs_2_, bf16[3,1024,2048]{2,1,0:T(8,128)(2,1)S(1)} %copy-done.1, ...), custom_call_target="tpu_custom_call" | custom-call | flops 1610612736 | bytes 1048576 | tf_op jit(solution)/shard_map/pallas_call | solution.py:333
  102.4 2.3 %shard_map.141 = (bf16[128,1024]{1,0:T(8,128)(2,1)S(1)}, bf16[128,1024]{1,0:T(8,128)(2,1)S(1)}, bf16[64,1024]{1,0:T(8,128)(2,1)S(1)}) custom-call(s32[3]{0:T(128)S(1)} %pad_add_fusion.refs_0_, s32[6]{0:T(128)S(1)} %copy-done.22, bf16[64,1024]{1,0:T(8,128)(2,1)S(1)} %collective-permute-done.10.refs_2_, bf16[64,1024]{1,0:T(8,128)(2,1)S(1)} %collective-permute-done.11.refs_3_, ...), custom_call_target="tpu_custom_call" | custom-call | flops 1610612736 | bytes 1048576 | tf_op jit(solution)/shard_map/pallas_call | solution.py:333
  105.4 1.4 shard_map.143.refs_6_.refs_2_
  106.9 3.4 %collective-permute-done.13.refs_5_ = bf16[64,1024]{1,0:T(8,128)(2,1)S(1)} collective-permute-done((bf16[64,1024]{1,0:T(8,128)(2,1)S(1)}, bf16[64,1024]{1,0:T(8,128)(2,1)S(1)}, u32[]{:S(2)}, u32[]{:S(2)}) %collective-permute-start.13) | collective-permute-done | bytes 131104 | tf_op jit(solution)/shard_map/ppermute | solution.py:357
  111.0 1.4 collective-permute-start.15
  113.8 4.7 %collective-permute-done.15.refs_2_ = bf16[64,1024]{1,0:T(8,128)(2,1)S(1)} collective-permute-done((bf16[64,1024]{1,0:T(8,128)(2,1)S(1)}, bf16[64,1024]{1,0:T(8,128)(2,1)S(1)}, u32[]{:S(2)}, u32[]{:S(2)}) %collective-permute-start.15) | collective-permute-done | bytes 131104 | tf_op jit(solution)/shard_map/ppermute | solution.py:353
  120.4 4.4 %shard_map.147 = (bf16[3,128,1024]{2,1,0:T(8,128)(2,1)S(1)}, f32[8,128,128]{2,1,0:T(8,128)S(1)}, bf16[128,1024]{1,0:T(8,128)(2,1)S(1)}, bf16[64,1024]{1,0:T(8,128)(2,1)S(1)}) custom-call(s32[3]{0:T(128)S(1)} %pad_add_fusion.refs_0_, bf16[64,1024]{1,0:T(8,128)(2,1)S(1)} %shard_map.146.refs_1_.refs_7_, bf16[64,1024]{1,0:T(8,128)(2,1)S(1)} %collective-permute-done.16.refs_2_, ...), custom_call_target="tpu_custom_call" | custom-call | flops 1610612736 | bytes 1048576 | tf_op jit(solution)/shard_map/pallas_call | solution.py:333
  125.5 3.8 %shard_map.149 = (bf16[3,128,1024]{2,1,0:T(8,128)(2,1)S(1)}, f32[8,128,128]{2,1,0:T(8,128)S(1)}) custom-call(bf16[128,1024]{1,0:T(8,128)(2,1)S(1)} %get-tuple-element.79.refs_0_, bf16[3,128,2048]{2,1,0:T(8,128)(2,1)S(1)} %copy-done.9, f32[16,128,128]{2,1,0:T(8,128)S(1)} %get-tuple-element.46.refs_1_.refs_3_.refs_2_.refs_7_.refs_4_, ...), custom_call_target="tpu_custom_call" | custom-call | flops 1610612736 | bytes 1048576 | tf_op jit(solution)/shard_map/pallas_call | solution.py:333
  130.5 4.0 %shard_map.151 = (bf16[64,1024]{1,0:T(8,128)(2,1)S(1)}, f32[64,1024]{1,0:T(8,128)S(1)}) custom-call(s32[3]{0:T(128)S(1)} %pad_add_fusion.refs_0_, bf16[3,128,1024]{2,1,0:T(8,128)(2,1)S(1)} %get-tuple-element.78.refs_2_.refs_1_, bf16[3,128,1024]{2,1,0:T(8,128)(2,1)S(1)} %get-tuple-element.81.refs_3_.refs_2_, bf16[3,1024,2048]{2,1,0:T(8,128)(2,1)S(1)} %copy-done.1, ...), custom_call_target="tpu_custom_call" | custom-call | flops 1610612736 | bytes 1048576 | tf_op jit(solution)/shard_map/pallas_call | solution.py:333
  138.9 1.7 %shard_map.154.refs_6_ = f32[16,32]{1,0:T(8,128)} custom-call(f32[8,128,128]{2,1,0:T(8,128)S(1)} %get-tuple-element.85.refs_0_, f32[8,128,128]{2,1,0:T(8,128)S(1)} %get-tuple-element.86.refs_1_, s32[128,128]{1,0:T(8,128)S(1)} %copy-done.19, bf16[64,1024]{1,0:T(8,128)(2,1)S(1)} %shard_map.153.refs_3_.refs_4_), custom_call_target="tpu_custom_call" | custom-call | bytes 1048576 | tf_op jit(solution)/shard_map/pallas_call | solution.py:333
  140.5 3.3 %collective-permute-done.20.refs_5_ = bf16[64,1024]{1,0:T(8,128)(2,1)S(1)} collective-permute-done((bf16[64,1024]{1,0:T(8,128)(2,1)S(1)}, bf16[64,1024]{1,0:T(8,128)(2,1)S(1)}, u32[]{:S(2)}, u32[]{:S(2)}) %collective-permute-start.20) | collective-permute-done | bytes 131104 | tf_op jit(solution)/shard_map/ppermute | solution.py:357
  (99 shorter events, 33.6 us)
Async XLA Ops:
  3.8 4.6 %copy-start.23 = (bf16[1,1024,16,3,128]{4,2,3,1,0:T(8,128)(2,1)S(1)}, bf16[1,1024,16,3,128]{4,2,3,1,0:T(8,128)(2,1)}, u32[]{:S(2)}) copy-start(bf16[1,1024,16,3,128]{4,2,3,1,0:T(8,128)(2,1)} %param.18) | copy-start | bytes 37748740
  25.7 14.3 %collective-permute-start = (bf16[64,1024]{1,0:T(8,128)(2,1)}, bf16[64,1024]{1,0:T(8,128)(2,1)S(1)}, u32[]{:S(2)}, u32[]{:S(2)}) collective-permute-start(bf16[64,1024]{1,0:T(8,128)(2,1)} %get-tuple-element.48.refs_3_), channel_id=1, source_target_pairs={{0,1},{1,0},{2,3},{3,2},{4,5},{5,4},{6,7},{7,6},{8,9},{9,8},{10,11... | collective-permute-start | bytes 393224 | tf_op jit(solution)/shard_map/ppermute | solution.py:357
  32.1 4.6 %copy-start = (bf16[3,1024,2048]{2,1,0:T(8,128)(2,1)}, bf16[3,1024,2048]{2,1,0:T(8,128)(2,1)S(1)}, u32[]{:S(2)}) copy-start(bf16[3,1024,2048]{2,1,0:T(8,128)(2,1)S(1)} %get-tuple-element.49.refs_2_.refs_3_.refs_6_.refs_1_) | copy-start | bytes 37748740
  39.0 4.5 %copy-start.13 = (bf16[1,128,1024]{2,1,0:T(8,128)(2,1)S(1)}, bf16[1,128,1024]{2,1,0:T(8,128)(2,1)}, u32[]{:S(2)}) copy-start(bf16[1,128,1024]{2,1,0:T(8,128)(2,1)} %param.11) | copy-start | bytes 786436
  40.9 9.1 %collective-permute-start.1 = (bf16[64,1024]{1,0:T(8,128)(2,1)S(1)}, bf16[64,1024]{1,0:T(8,128)(2,1)S(1)}, u32[]{:S(2)}, u32[]{:S(2)}) collective-permute-start(bf16[64,1024]{1,0:T(8,128)(2,1)S(1)} %shard_map.125.refs_5_.refs_1_), channel_id=1, source_target_pairs={{0,2},{1,3},{2,0},{3,1},{4,6},{5,7},{6,4},{7,5},{8,10},{9,11},{10,... | collective-permute-start | bytes 393224 | tf_op jit(solution)/shard_map/ppermute | solution.py:357
  45.7 14.0 %copy-start.1 = (bf16[3,1024,2048]{2,1,0:T(8,128)(2,1)S(1)}, bf16[3,1024,2048]{2,1,0:T(8,128)(2,1)}, u32[]{:S(2)}) copy-start(bf16[3,1024,2048]{2,1,0:T(8,128)(2,1)} %copy-done) | copy-start | bytes 37748740
  50.1 9.5 %collective-permute-start.2 = (bf16[64,1024]{1,0:T(8,128)(2,1)S(1)}, bf16[64,1024]{1,0:T(8,128)(2,1)S(1)}, u32[]{:S(2)}, u32[]{:S(2)}) collective-permute-start(bf16[64,1024]{1,0:T(8,128)(2,1)S(1)} %shard_map.127.refs_4_.refs_1_), channel_id=1, source_target_pairs={{0,4},{4,8},{8,12},{1,5},{5,9},{9,13},{2,6},{6,10},{10,14},{3,7},{... | collective-permute-start | bytes 393224 | tf_op jit(solution)/shard_map/ppermute | solution.py:353
  59.5 4.7 %collective-permute-start.3 = (bf16[64,1024]{1,0:T(8,128)(2,1)S(1)}, bf16[64,1024]{1,0:T(8,128)(2,1)S(1)}, u32[]{:S(2)}, u32[]{:S(2)}) collective-permute-start(bf16[64,1024]{1,0:T(8,128)(2,1)S(1)} %collective-permute-done.2.refs_4_.refs_2_), channel_id=1, source_target_pairs={{0,1},{1,0},{2,3},{3,2},{4,5},{5,4},{6,7},{7,6},{8,9},{9,8},{10,11... | collective-permute-start | bytes 393224 | tf_op jit(solution)/shard_map/ppermute | solution.py:357
  59.6 4.6 %copy-start.7 = (bf16[6,128,1024]{2,1,0:T(8,128)(2,1)S(1)}, bf16[6,128,1024]{2,1,0:T(8,128)(2,1)}, u32[]{:S(2)}) copy-start(bf16[6,128,1024]{2,1,0:T(8,128)(2,1)} %refs_4_.3) | copy-start | bytes 4718596
  59.6 4.6 %copy-start.22 = (s32[6]{0:T(128)S(1)}, s32[6]{0:T(128)}, u32[]{:S(2)}) copy-start(s32[6]{0:T(128)} %refs_1_.5) | copy-start | bytes 76
  63.7 2.8 %collective-permute-start.4 = (bf16[64,1024]{1,0:T(8,128)(2,1)S(1)}, bf16[64,1024]{1,0:T(8,128)(2,1)S(1)}, u32[]{:S(2)}, u32[]{:S(2)}) collective-permute-start(bf16[64,1024]{1,0:T(8,128)(2,1)S(1)} %get-tuple-element.54.refs_8_), channel_id=1, source_target_pairs={{0,1},{1,0},{2,3},{3,2},{4,5},{5,4},{6,7},{7,6},{8,9},{9,8},{10,11... | collective-permute-start | bytes 393224 | tf_op jit(solution)/shard_map/ppermute | solution.py:357
  66.6 5.5 %collective-permute-start.5 = (bf16[64,1024]{1,0:T(8,128)(2,1)S(1)}, bf16[64,1024]{1,0:T(8,128)(2,1)S(1)}, u32[]{:S(2)}, u32[]{:S(2)}) collective-permute-start(bf16[64,1024]{1,0:T(8,128)(2,1)S(1)} %shard_map.131.refs_3_.refs_4_), channel_id=1, source_target_pairs={{0,2},{1,3},{2,0},{3,1},{4,6},{5,7},{6,4},{7,5},{8,10},{9,11},{10,... | collective-permute-start | bytes 393224 | tf_op jit(solution)/shard_map/ppermute | solution.py:357
  67.2 7.1 %copy-start.5 = (bf16[1,16,128,1024]{3,2,1,0:T(8,128)(2,1)S(1)}, bf16[1,16,128,1024]{3,2,1,0:T(8,128)(2,1)}, u32[]{:S(2)}) copy-start(bf16[1,16,128,1024]{3,2,1,0:T(8,128)(2,1)} %param.19) | copy-start | bytes 12582916
  72.8 9.0 %copy-start.11 = (bf16[3,128,2048]{2,1,0:T(8,128)(2,1)S(1)}, bf16[3,128,2048]{2,1,0:T(8,128)(2,1)}, u32[]{:S(2)}) copy-start(bf16[3,128,2048]{2,1,0:T(8,128)(2,1)} %copy-done.10) | copy-start | bytes 4718596
  72.8 7.0 %collective-permute-start.7 = (bf16[64,1024]{1,0:T(8,128)(2,1)S(1)}, bf16[64,1024]{1,0:T(8,128)(2,1)S(1)}, u32[]{:S(2)}, u32[]{:S(2)}) collective-permute-start(bf16[64,1024]{1,0:T(8,128)(2,1)S(1)} %shard_map.133.refs_4_), channel_id=1, source_target_pairs={{4,0},{8,4},{12,8},{5,1},{9,5},{13,9},{6,2},{10,6},{14,10},{7,3},{... | collective-permute-start | bytes 393224 | tf_op jit(solution)/shard_map/ppermute | solution.py:353
  80.4 1.4 collective-permute-start.8
  80.4 5.7 %collective-permute-start.6 = (bf16[64,1024]{1,0:T(8,128)(2,1)S(1)}, bf16[64,1024]{1,0:T(8,128)(2,1)S(1)}, u32[]{:S(2)}, u32[]{:S(2)}) collective-permute-start(bf16[64,1024]{1,0:T(8,128)(2,1)S(1)} %get-tuple-element.61.refs_3_), channel_id=1, source_target_pairs={{0,1},{1,0},{2,3},{3,2},{4,5},{5,4},{6,7},{7,6},{8,9},{9,8},{10,11... | collective-permute-start | bytes 393224 | tf_op jit(solution)/shard_map/ppermute | solution.py:357
  86.2 5.6 %collective-permute-start.9 = (bf16[64,1024]{1,0:T(8,128)(2,1)S(1)}, bf16[64,1024]{1,0:T(8,128)(2,1)S(1)}, u32[]{:S(2)}, u32[]{:S(2)}) collective-permute-start(bf16[64,1024]{1,0:T(8,128)(2,1)S(1)} %shard_map.137.refs_5_.refs_1_), channel_id=1, source_target_pairs={{0,2},{1,3},{2,0},{3,1},{4,6},{5,7},{6,4},{7,5},{8,10},{9,11},{10,... | collective-permute-start | bytes 393224 | tf_op jit(solution)/shard_map/ppermute | solution.py:357
  91.8 6.0 %collective-permute-start.10 = (bf16[64,1024]{1,0:T(8,128)(2,1)S(1)}, bf16[64,1024]{1,0:T(8,128)(2,1)S(1)}, u32[]{:S(2)}, u32[]{:S(2)}) collective-permute-start(bf16[64,1024]{1,0:T(8,128)(2,1)S(1)} %shard_map.139.refs_4_.refs_1_), channel_id=1, source_target_pairs={{0,4},{4,8},{8,12},{1,5},{5,9},{9,13},{2,6},{6,10},{10,14},{3,7},{... | collective-permute-start | bytes 393224 | tf_op jit(solution)/shard_map/ppermute | solution.py:353
  97.8 4.6 %collective-permute-start.11 = (bf16[64,1024]{1,0:T(8,128)(2,1)S(1)}, bf16[64,1024]{1,0:T(8,128)(2,1)S(1)}, u32[]{:S(2)}, u32[]{:S(2)}) collective-permute-start(bf16[64,1024]{1,0:T(8,128)(2,1)S(1)} %collective-permute-done.10.refs_2_), channel_id=1, source_target_pairs={{0,1},{1,0},{2,3},{3,2},{4,5},{5,4},{6,7},{7,6},{8,9},{9,8},{10,11... | collective-permute-start | bytes 393224 | tf_op jit(solution)/shard_map/ppermute | solution.py:357
  101.9 2.9 %collective-permute-start.12 = (bf16[64,1024]{1,0:T(8,128)(2,1)S(1)}, bf16[64,1024]{1,0:T(8,128)(2,1)S(1)}, u32[]{:S(2)}, u32[]{:S(2)}) collective-permute-start(bf16[64,1024]{1,0:T(8,128)(2,1)S(1)} %get-tuple-element.68.refs_8_), channel_id=1, source_target_pairs={{0,1},{1,0},{2,3},{3,2},{4,5},{5,4},{6,7},{7,6},{8,9},{9,8},{10,11... | collective-permute-start | bytes 393224 | tf_op jit(solution)/shard_map/ppermute | solution.py:357
  104.8 5.5 %collective-permute-start.13 = (bf16[64,1024]{1,0:T(8,128)(2,1)S(1)}, bf16[64,1024]{1,0:T(8,128)(2,1)S(1)}, u32[]{:S(2)}, u32[]{:S(2)}) collective-permute-start(bf16[64,1024]{1,0:T(8,128)(2,1)S(1)} %shard_map.142.refs_3_.refs_4_), channel_id=1, source_target_pairs={{0,2},{1,3},{2,0},{3,1},{4,6},{5,7},{6,4},{7,5},{8,10},{9,11},{10,... | collective-permute-start | bytes 393224 | tf_op jit(solution)/shard_map/ppermute | solution.py:357
  111.0 9.4 %copy-start.9 = (bf16[3,128,2048]{2,1,0:T(8,128)(2,1)S(1)}, bf16[3,128,2048]{2,1,0:T(8,128)(2,1)}, u32[]{:S(2)}) copy-start(bf16[3,128,2048]{2,1,0:T(8,128)(2,1)} %copy-done.8) | copy-start | bytes 4718596
  111.0 7.4 %collective-permute-start.15 = (bf16[64,1024]{1,0:T(8,128)(2,1)S(1)}, bf16[64,1024]{1,0:T(8,128)(2,1)S(1)}, u32[]{:S(2)}, u32[]{:S(2)}) collective-permute-start(bf16[64,1024]{1,0:T(8,128)(2,1)S(1)} %shard_map.144.refs_4_), channel_id=1, source_target_pairs={{4,0},{8,4},{12,8},{5,1},{9,5},{13,9},{6,2},{10,6},{14,10},{7,3},{... | collective-permute-start | bytes 393224 | tf_op jit(solution)/shard_map/ppermute | solution.py:353
  119.0 1.4 collective-permute-start.16
  119.1 5.7 %collective-permute-start.14 = (bf16[64,1024]{1,0:T(8,128)(2,1)S(1)}, bf16[64,1024]{1,0:T(8,128)(2,1)S(1)}, u32[]{:S(2)}, u32[]{:S(2)}) collective-permute-start(bf16[64,1024]{1,0:T(8,128)(2,1)S(1)} %get-tuple-element.75.refs_3_), channel_id=1, source_target_pairs={{0,1},{1,0},{2,3},{3,2},{4,5},{5,4},{6,7},{7,6},{8,9},{9,8},{10,11... | collective-permute-start | bytes 393224 | tf_op jit(solution)/shard_map/ppermute | solution.py:357
  124.8 5.6 %collective-permute-start.17 = (bf16[64,1024]{1,0:T(8,128)(2,1)S(1)}, bf16[64,1024]{1,0:T(8,128)(2,1)S(1)}, u32[]{:S(2)}, u32[]{:S(2)}) collective-permute-start(bf16[64,1024]{1,0:T(8,128)(2,1)S(1)} %shard_map.148.refs_5_.refs_1_), channel_id=1, source_target_pairs={{0,2},{1,3},{2,0},{3,1},{4,6},{5,7},{6,4},{7,5},{8,10},{9,11},{10,... | collective-permute-start | bytes 393224 | tf_op jit(solution)/shard_map/ppermute | solution.py:357
  130.5 8.4 %copy-start.19 = (s32[128,128]{1,0:T(8,128)S(1)}, s32[128,128]{1,0:T(8,128)}, u32[]{:S(2)}) copy-start(s32[128,128]{1,0:T(8,128)} %refs_2_.1) | copy-start | bytes 196612
  134.5 1.4 collective-permute-start.18
  134.6 2.6 %collective-permute-start.19 = (bf16[64,1024]{1,0:T(8,128)(2,1)S(1)}, bf16[64,1024]{1,0:T(8,128)(2,1)S(1)}, u32[]{:S(2)}, u32[]{:S(2)}) collective-permute-start(bf16[64,1024]{1,0:T(8,128)(2,1)S(1)} %get-tuple-element.82.refs_3_), channel_id=1, source_target_pairs={{0,1},{1,0},{2,3},{3,2},{4,5},{5,4},{6,7},{7,6},{8,9},{9,8},{10,11... | collective-permute-start | bytes 393224 | tf_op jit(solution)/shard_map/ppermute | solution.py:357
  138.2 5.6 %collective-permute-start.20 = (bf16[64,1024]{1,0:T(8,128)(2,1)S(1)}, bf16[64,1024]{1,0:T(8,128)(2,1)S(1)}, u32[]{:S(2)}, u32[]{:S(2)}) collective-permute-start(bf16[64,1024]{1,0:T(8,128)(2,1)S(1)} %shard_map.153.refs_3_.refs_4_), channel_id=1, source_target_pairs={{0,2},{1,3},{2,0},{3,1},{4,6},{5,7},{6,4},{7,5},{8,10},{9,11},{10,... | collective-permute-start | bytes 393224 | tf_op jit(solution)/shard_map/ppermute | solution.py:357
  145.2 1.4 collective-permute-start.21
  (14 other events, 21.0 us)

commit v2 on v1

--- a/solution.py
+++ b/solution.py
@@ -39,8 +39,10 @@
 
 def fill_bias(table_ref, bucket_ref, bias_ref):
     ids = bucket_ref[...].T
-    for h in range(bias_ref.shape[0]):
-        row = jnp.broadcast_to(table_ref[h : h + 1], ids.shape)
+    rows, count = table_ref.shape
+    table = jnp.concatenate([table_ref[...], jnp.zeros((rows, LANES - count), F32)], axis=1)
+    for h in range(rows):
+        row = jnp.broadcast_to(table[h : h + 1], ids.shape)
         bias_ref[h] = jnp.take_along_axis(row, ids, axis=1)
 
 
@@ -48,12 +50,17 @@
     fill_bias(table_ref, bucket_ref, bias_ref)
 
 
-def relayout_kernel(x_ref, gain_ref, table_ref, bucket_ref, w_ref, w_out_ref, qkv_ref, bias_ref, normed):
+def relayout_kernel(
+    place_ref, x_ref, gain_ref, table_ref, bucket_ref, w_ref, back_ref,
+    w_out_ref, qkv_ref, bias_ref, back_out_ref, normed, arrived,
+):
     which = pl.program_id(0)
     block = pl.program_id(1)
+    back_copy = pltpu.make_async_copy(back_ref, back_out_ref, arrived)
 
     @pl.when((which == 0) & (block == 0))
     def _():
+        back_copy.start()
         normed[...] = rms_normed(x_ref[0], gain_ref[...])
         fill_bias(table_ref, bucket_ref, bias_ref)
 
@@ -83,6 +90,10 @@
     def _():
         qkv_ref[which] = dot(normed[...], w_out_ref[which]).astype(BF16)
 
+    @pl.when((which == pl.num_programs(0) - 1) & (block == pl.num_programs(1) - 1))
+    def _():
+        back_copy.wait()
+
 
 def probs_of(query, key, bias, scale):
     scores = dot(key, query, LAST) * scale + bias
@@ -100,9 +111,10 @@
     return [dot(p, value[:, sl], FIRST).astype(BF16) for p, sl in zip(probs, lanes)]
 
 
-def first_attend_kernel(qkv_ref, bias_ref, out_ref):
+def first_attend_kernel(place_ref, x_ref, qkv_ref, bias_ref, out_ref, x_half_ref):
     heads = bias_ref.shape[0]
     group = heads // 2
+    x_half_ref[...] = x_ref[0, rows_at(place_ref[0], x_half_ref.shape[0])]
 
     def step(g, carry):
         at = rows_at(g, group * LANES)
@@ -190,18 +202,36 @@
     lax.fori_loop(0, w_ref.shape[2] // width, step, 0)
 
 
-def grad_attend(g, qkv_ref, bias_ref, wo_ref, acc_in_ref, stacked_ref, acc_ref, part):
-    heads = bias_ref.shape[0] // 2
+def probs_kernel(qkv_ref, bias_ref, out_ref):
+    heads = bias_ref.shape[0]
+    group = heads // 2
+    scale = LANES ** (-0.5)
+
+    def step(g, carry):
+        at = rows_at(g, group * LANES)
+        query, key = (qkv_ref[c, :, at] for c in range(2))
+        for h in range(group):
+            sl = slice(h * LANES, (h + 1) * LANES)
+            out_ref[g * group + h] = probs_of(
+                query[:, sl], key[:, sl], bias_ref[g * group + h], scale
+            )
+        return carry
+
+    lax.fori_loop(0, 2, step, 0)
+
+
+def grad_attend(g, qkv_ref, probs_ref, wo_ref, acc_in_ref, stacked_ref, acc_ref, part):
+    heads = probs_ref.shape[0] // 2
     scale = LANES ** (-0.5)
     at = slice(part * heads * LANES, (part + 1) * heads * LANES)
-    grad_attn = dot(wo_ref[at], g, LAST).astype(BF16)
+    grad_attn = dot(g, wo_ref[at], LAST).astype(BF16)
     for h in range(heads):
         here = slice((part * heads + h) * LANES, (part * heads + h + 1) * LANES)
         own = slice(h * LANES, (h + 1) * LANES)
         q, k, v = (qkv_ref[c, :, here] for c in range(3))
-        ga = grad_attn[own]
-        probs = probs_of(q, k, bias_ref[part * heads + h], scale)
-        grad_probs = dot(v, ga)
+        ga = grad_attn[:, own]
+        probs = probs_ref[part * heads + h]
+        grad_probs = dot(v, ga, LAST)
         total = jnp.sum(probs * grad_probs, axis=0, keepdims=True)
         grad_scores = probs * (grad_probs - total)
         grad16 = grad_scores.astype(BF16)
@@ -211,30 +241,30 @@
             acc_ref[h] = acc_in_ref[h] + grad_scores
         stacked_ref[0, :, own] = (dot(grad16, k, FIRST) * scale).astype(BF16)
         stacked_ref[1, :, own] = (dot(grad16, q) * scale).astype(BF16)
-        stacked_ref[2, :, own] = dot(probs.astype(BF16), ga, LAST).astype(BF16)
+        stacked_ref[2, :, own] = dot(probs.astype(BF16), ga).astype(BF16)
 
 
 def backward_a_kernel(first, place_ref, *refs):
     core = place_ref[0]
     if first:
-        full_ref, qkv_ref, bias_ref, wo_ref, stacked_ref, acc_ref, g_ref, g_half_ref = refs
+        full_ref, qkv_ref, probs_ref, wo_ref, stacked_ref, acc_ref, g_ref, g_half_ref = refs
         acc_in_ref = None
         half = g_half_ref.shape[0]
         g_ref[...] = full_ref[...]
     else:
-        (mine_ref, other_ref, qkv_ref, bias_ref, wo_ref, acc_in_ref,
+        (mine_ref, other_ref, qkv_ref, probs_ref, wo_ref, acc_in_ref,
          stacked_ref, acc_ref, g_ref, g_half_ref) = refs
         half = g_half_ref.shape[0]
         g_ref[rows_at(core, half)] = mine_ref[...]
         g_ref[rows_at(1 - core, half)] = other_ref[...]
     g_half_ref[...] = g_ref[rows_at(core, half)]
-    grad_attend(g_ref[...], qkv_ref, bias_ref, wo_ref, acc_in_ref, stacked_ref, acc_ref, 0)
-
-
-def backward_b_kernel(first, g_ref, qkv_ref, bias_ref, wo_ref, *refs):
+    grad_attend(g_ref[...], qkv_ref, probs_ref, wo_ref, acc_in_ref, stacked_ref, acc_ref, 0)
+
+
+def backward_b_kernel(first, g_ref, qkv_ref, probs_ref, wo_ref, *refs):
     acc_in_ref = None if first else refs[0]
     stacked_ref, acc_ref = refs[-2:]
-    grad_attend(g_ref[...], qkv_ref, bias_ref, wo_ref, acc_in_ref, stacked_ref, acc_ref, 1)
+    grad_attend(g_ref[...], qkv_ref, probs_ref, wo_ref, acc_in_ref, stacked_ref, acc_ref, 1)
 
 
 def backward_c_kernel(place_ref, low_ref, high_ref, w_ref, send_ref, keep_ref):
@@ -242,38 +272,41 @@
     total = None
     for c in range(3):
         for part, ref in enumerate((low_ref, high_ref)):
-            term = dot(w_ref[c, :, part * width : (part + 1) * width], ref[c], LAST)
+            term = dot(ref[c], w_ref[c, :, part * width : (part + 1) * width], LAST)
             total = term if total is None else total + term
-    split_halves(place_ref[0], total.T, send_ref, keep_ref)
-
-
-def pair_kernel(keep_ref, received_ref, out_ref):
-    out_ref[...] = (keep_ref[...].astype(F32) + received_ref[...].astype(F32)).astype(BF16)
-
-
-def finish_up_kernel(x_ref, first_ref, second_ref, out_ref):
-    total = first_ref[...].astype(F32) + second_ref[...].astype(F32)
-    out_ref[...] = (x_ref[...].astype(F32) + total).astype(BF16)
-
-
-def finish_down_kernel(tick, place_ref, stash_ref, g_ref, gain_ref, first_ref, second_ref, out_ref):
+    split_halves(place_ref[0], total, send_ref, keep_ref)
+
+
+def pair_kernel(first_ref, second_ref, out_ref):
+    out_ref[...] = (first_ref[...].astype(F32) + second_ref[...].astype(F32)).astype(BF16)
+
+
+def up_term_kernel(place_ref, keep_ref, received_ref, x_ref, out_ref):
+    residual = place_ref[3].astype(F32)
+    total = keep_ref[...] + received_ref[...].astype(F32)
+    out_ref[...] = (total + residual * x_ref[...].astype(F32)).astype(BF16)
+
+
+def down_term_kernel(tick, place_ref, stash_ref, gain_ref, keep_ref, received_ref, g_ref, out_ref):
     half = out_ref.shape[0]
+    residual = place_ref[3].astype(F32)
     x = stash_ref[tick, rows_at(place_ref[0], half)].astype(F32)
     inverse = lax.rsqrt(jnp.mean(x * x, axis=-1, keepdims=True) + EPSILON)
-    weighted = gain_ref[...] * (first_ref[...].astype(F32) + second_ref[...].astype(F32))
+    weighted = gain_ref[...] * (keep_ref[...] + received_ref[...].astype(F32))
     mean = jnp.mean(x * weighted, axis=-1, keepdims=True)
     cubed = inverse * inverse * inverse
-    out_ref[...] = (g_ref[...].astype(F32) + inverse * weighted - x * cubed * mean).astype(BF16)
-
-
-def choose_kernel(place_ref, own_ref, arrived_ref, out_ref):
+    back = inverse * weighted - x * cubed * mean
+    out_ref[...] = (residual * g_ref[...].astype(F32) + back).astype(BF16)
+
+
+def choose_kernel(place_ref, own_ref, own_second_ref, first_ref, second_ref, out_ref):
     @pl.when(place_ref[2] == 1)
     def _():
-        out_ref[...] = own_ref[...]
+        pair_kernel(own_ref, own_second_ref, out_ref)
 
     @pl.when(place_ref[2] == 0)
     def _():
-        out_ref[...] = arrived_ref[...]
+        pair_kernel(first_ref, second_ref, out_ref)
 
 
 def join_kernel(place_ref, mine_ref, other_ref, out_ref):
@@ -343,18 +376,31 @@
         return results if isinstance(out_shape, tuple) else results[0]
 
 
-def vmem(x):
-    return pltpu.with_memory_space_constraint(x, pltpu.VMEM)
-
-
-def shifted(block, axis, distance):
-    devices = range(lax.axis_size(axis))
-    route = [(i - distance, i) for i in devices if i - distance in devices]
-    return lax.ppermute(block, axis, route)
+def in_hbm(x):
+    return pltpu.with_memory_space_constraint(x, pltpu.HBM)
+
+
+def moved(block, step, bit):
+    sections, heads = lax.axis_size("section"), lax.axis_size("head")
+    route = [
+        (s * heads + h, (s + step) * heads + (h ^ bit))
+        for s in range(sections)
+        if s + step in range(sections)
+        for h in range(heads)
+    ]
+    return lax.ppermute(block, ("section", "head"), route)
 
 
 def swapped(block, bit):
     return lax.ppermute(block, "head", [(i, i ^ bit) for i in range(lax.axis_size("head"))])
+
+
+def swapped_in_last(block, bit):
+    sections, heads = lax.axis_size("section"), lax.axis_size("head")
+    base = (sections - 1) * heads
+    return lax.ppermute(
+        block, ("section", "head"), [(base + h, base + (h ^ bit)) for h in range(heads)]
+    )
 
 
 def per_device(rising, falling, stash, queue, order, buckets, bias_table, gain, w_qkv, w_out):
@@ -364,61 +410,70 @@
     head_count = lax.axis_size("head")
     _, model_width, heads, _, head_dim = w_qkv.shape
     tokens = buckets.shape[0]
-    bucket_count = bias_table.shape[1]
     half = tokens // 2
     inner = heads * head_dim
     core = head_index % 2
     is_last = section_index == section_count - 1
-    place = jnp.stack([core, section_index, is_last]).astype(jnp.int32)
-    table = jnp.pad(bias_table[0].T, ((0, 0), (0, LANES - bucket_count)))
-    wo = vmem(w_out[0].reshape(inner, model_width))
+    place = jnp.stack([core, section_index, is_last, head_index < 2]).astype(jnp.int32)
+    table = bias_table[0].T
+    back = w_out[0].reshape(inner, model_width)
     per_mac = 2 * tokens * model_width * inner
     run = Chain()
-    pairs = [1 << b for b in range(1, head_count.bit_length() - 1)]
+    bits = [1 << b for b in range(1, head_count.bit_length() - 1)]
+    cross = bits[-1]
+    qkv_shape = shape((3, tokens, inner))
+    scores_shape = shape((heads, tokens, tokens), F32)
 
     if heads % ROWS16 == 0:
         rows_first = jnp.transpose(w_qkv[0], (0, 2, 1, 3)).reshape(model_width, 3 * heads, head_dim)
         blocks = 4
         depth = model_width // blocks
         fixed = lambda rank: lambda c, b: (0,) * rank
-        weights, qkv, bias = pl.pallas_call(
+        weights, qkv, bias, wo = pl.pallas_call(
             relayout_kernel,
             grid=(3, blocks),
             out_shape=(
                 pltpu.VMEM((3, model_width, inner), BF16),
-                shape((3, tokens, inner)),
-                shape((heads, tokens, tokens), F32),
+                qkv_shape,
+                scores_shape,
+                pltpu.VMEM((inner, model_width), BF16),
             ),
             in_specs=[
+                SCALARS,
                 pl.BlockSpec((1, tokens, model_width), fixed(3)),
                 pl.BlockSpec((1, model_width), fixed(2)),
-                pl.BlockSpec((heads, LANES), fixed(2)),
+                pl.BlockSpec(table.shape, fixed(2)),
                 pl.BlockSpec((tokens, tokens), fixed(2)),
                 pl.BlockSpec((depth, heads, head_dim), lambda c, b: (b, c, 0)),
+                UNREAD,
             ],
             out_specs=(
                 WHOLE,
                 pl.BlockSpec((3, tokens, inner), fixed(3)),
                 pl.BlockSpec((heads, tokens, tokens), fixed(3)),
+                WHOLE,
             ),
-            scratch_shapes=[pltpu.VMEM((tokens, model_width), BF16)],
+            scratch_shapes=[pltpu.VMEM((tokens, model_width), BF16), pltpu.SemaphoreType.DMA],
             compiler_params=pltpu.CompilerParams(vmem_limit_bytes=24 * MIB),
             cost_estimate=pl.CostEstimate(
                 flops=9 * per_mac, bytes_accessed=2 * w_qkv.size, transcendentals=0
             ),
-        )(rising, gain, table, buckets, rows_first)
+        )(
+            place, in_hbm(rising), in_hbm(gain), in_hbm(table), in_hbm(buckets),
+            in_hbm(rows_first), in_hbm(back),
+        )
         run.before = qkv
     else:
+        wo = back
         weights = jnp.transpose(w_qkv[0], (2, 0, 1, 3)).reshape(3, model_width, inner)
-        bias = run(bias_kernel, shape((heads, tokens, tokens), F32), (table, buckets))
+        bias = run(bias_kernel, scores_shape, (table, buckets))
         qkv = run(
             stash_kernel,
-            shape((3, tokens, inner)),
+            qkv_shape,
             (rising, gain, weights),
             scratch=[pltpu.VMEM((tokens, model_width), BF16)],
             flops=3 * per_mac,
         )
-    weights = vmem(weights)
     halves = (shape((half, model_width)), shape((half, model_width), F32))
     half_rows = shape((half, model_width))
     acc_shape = shape((heads // 2, tokens, tokens), F32)
@@ -426,40 +481,32 @@
     stacked_shape = shape((3, tokens, inner // 2))
     row_scratch = pltpu.VMEM((tokens, model_width), BF16)
 
-    def out_projection(attended):
-        return run(
-            forward_c_kernel,
-            halves,
-            (place,) + attended + (wo,),
-            scratch=[pltpu.VMEM((tokens, inner), BF16)],
+    def but_last_bit(term):
+        for bit in bits[:-1]:
+            term = run(pair_kernel, half_rows, (term, swapped(term, bit)))
+        return term
+
+    def down_term(tick, keep, received, g_half):
+        term = run(
+            functools.partial(down_term_kernel, tick),
+            half_rows,
+            (place, stash[0], gain, keep, received, g_half),
             scalars=1,
-            flops=per_mac,
-        )
-
-    def across(pair):
-        for bit in pairs[:-1]:
-            pair = run(pair_kernel, half_rows, (pair, swapped(pair, bit)))
-        return pair, swapped(pair, pairs[-1])
-
-    x_half = lax.dynamic_slice_in_dim(rising[0], core * half, half, 0)
-    stashed = None
-    pending = None
-    acc = (None, None)
-    x_mine = x_other = g_mine = g_other = None
-
-    def finish_down(state):
-        tick, g_half, first, second = state
-        return run(
-            functools.partial(finish_down_kernel, tick),
-            half_rows,
-            (place, stash[0], g_half, gain, first, second),
-            scalars=1,
-        )
-
+        )
+        return but_last_bit(term)
+
+    stashed = arrivals = None
+    acc = ()
     for t in range(TICKS):
         final = t + 1 == TICKS
         if t == 0:
-            attended = (run(first_attend_kernel, shape((tokens, inner)), (qkv, bias)),)
+            full, x_half = run(
+                first_attend_kernel,
+                (shape((tokens, inner)), half_rows),
+                (place, rising, qkv, bias),
+                scalars=1,
+            )
+            attended = (full,)
         else:
             low, normed, x_half = run(
                 functools.partial(forward_a_kernel, t),
@@ -469,89 +516,79 @@
                 scalars=2,
                 flops=3 * per_mac,
             )
-            send, keep, g_half = pending
-            pair = run(pair_kernel, half_rows, (keep, swapped(send, 1)))
-            first, second = across(pair)
+            fallen = down_term(t - 1, keep, received, g_half)
+            arrivals = (up, in_last, moved(fallen, -1, 0), moved(fallen, -1, cross))
             high = run(forward_b_kernel, part_shape, (normed, weights, bias), flops=3 * per_mac)
-            lowered = finish_down((t - 1, g_half, first, second))
-            descended = shifted(lowered, "section", -1)
             attended = (low, high)
-        send, keep = out_projection(attended)
-        swap_up = swapped(send, 1)
+        send, keep = run(
+            forward_c_kernel,
+            halves,
+            (place,) + attended + (wo,),
+            scratch=[pltpu.VMEM((tokens, inner), BF16)],
+            scalars=1,
+            flops=per_mac,
+        )
+        received = swapped(send, 1)
         if t == 0:
             stashed = run(
                 stash_kernel,
-                (shape((3, tokens, inner)),) * TICKS,
+                (qkv_shape,) * TICKS,
                 (stash[0], gain, weights),
                 scratch=[pltpu.VMEM((TICKS * tokens, model_width), BF16)],
                 flops=3 * TICKS * per_mac,
             )
+        else:
+            probs = run(probs_kernel, scores_shape, (stashed[t], bias), flops=per_mac)
+        up = but_last_bit(
+            run(up_term_kernel, half_rows, (place, keep, received, x_half), scalars=1)
+        )
+        if final:
+            climbed = (up, swapped(up, cross))
+        else:
+            climbed = (moved(up, 1, 0), moved(up, 1, cross))
+            in_last = swapped_in_last(up, cross)
+        if t == 0:
+            probs = run(probs_kernel, scores_shape, (stashed[t], bias), flops=per_mac)
             g_parts = (falling[0],)
         else:
-            g_mine = run(choose_kernel, half_rows, (place, lifted, descended), scalars=1)
-            g_other = swapped(g_mine, 1)
-            g_parts = (g_mine, g_other)
-
-        def add_up():
-            return across(run(pair_kernel, half_rows, (keep, swap_up)))
-
-        if t == 0:
-            first, second = add_up()
-        acc_args = () if t == 0 else (acc[0],)
+            g_mine = run(choose_kernel, half_rows, (place,) + arrivals, scalars=1)
+            g_parts = (g_mine, swapped(g_mine, 1))
+
         stacked_low, acc_low, g_full, g_half = run(
             functools.partial(backward_a_kernel, t == 0),
             (stacked_shape, acc_shape, shape((tokens, model_width)), half_rows),
-            (place,) + g_parts + (stashed[t], bias, wo) + acc_args,
+            (place,) + g_parts + (stashed[t], probs, wo) + acc[:1],
             scalars=1,
-            flops=3 * per_mac,
-        )
-        if t > 0:
-            first, second = add_up()
-            after = ()
-        else:
-            lifted = run(finish_up_kernel, half_rows, (x_half, first, second))
-            climbed = shifted(lifted, "section", 1)
-            after = ()
-        acc_args = () if t == 0 else (acc[1],)
+            flops=2 * per_mac,
+        )
         stacked_high, acc_high = run(
             functools.partial(backward_b_kernel, t == 0),
             (stacked_shape, acc_shape),
-            (g_full, stashed[t], bias, wo) + acc_args,
-            flops=3 * per_mac,
+            (g_full, stashed[t], probs, wo) + acc[1:],
+            flops=2 * per_mac,
         )
         acc = (acc_low, acc_high)
-        if t > 0:
-            lifted = run(finish_up_kernel, half_rows, (x_half, first, second))
-            if not final:
-                climbed = shifted(lifted, "section", 1)
-        if not final:
-            x_mine = climbed
-            x_other = swapped(climbed, 1)
-            after = (climbed,) if t == 0 else ()
-        else:
-            x_other = swapped(lifted, 1)
+        x_mine = run(pair_kernel, half_rows, climbed)
+        x_other = swapped(x_mine, 1)
         send, keep = run(
             backward_c_kernel,
             halves,
             (place, stacked_low, stacked_high, weights),
             scalars=1,
-            after=after,
             flops=3 * per_mac,
         )
-        pending = (send, keep, g_half)
-
-    send, keep, g_half = pending
-    received = swapped(send, 1)
+        received = swapped(send, 1)
+
     rows = shape((1, tokens, model_width))
-    rising_out = run(join_kernel, rows, (place, lifted, x_other), scalars=1)
-    pair = run(pair_kernel, half_rows, (keep, received))
-    first, second = across(pair)
+    rising_out = run(join_kernel, rows, (place, x_mine, x_other), scalars=1)
+    fallen = down_term(TICKS - 1, keep, received, g_half)
+    fallen_other = swapped(fallen, cross)
     table_grad = run(
-        functools.partial(table_kernel, bucket_count),
-        shape((heads, bucket_count), F32),
+        functools.partial(table_kernel, bias_table.shape[1]),
+        shape((heads, bias_table.shape[1]), F32),
         acc + (buckets,),
     )
-    lowered = finish_down((TICKS - 1, g_half, first, second))
+    lowered = run(pair_kernel, half_rows, (fallen, fallen_other))
     falling_out = run(join_kernel, rows, (place, lowered, swapped(lowered, 1)), scalars=1)
     return (rising_out, falling_out, table_grad.T[None])
 

time: 149 us -> 129 us (0.87)
  local copies, waits for them, and re-layouts: 24.2 us -> 1.69 us
  waiting for transfers between devices: 27.9 us -> 17.9 us
  starting transfers between devices: 18.9 us -> 28.2 us
  Pallas kernels: 75.8 us -> 79.6 us
    unnamed x48 -> x18, local copies, waits for them, and re-layouts: 22.6 us -> 1.69 us
    ppermute x4 -> x10, starting transfers between devices: 9.81 us -> 22.6 us  [the longest x8 21.2 us: moved(): return lax.ppermute(block, ('section', 'head'), route)]
    ppermute x18 -> x14, waiting for transfers between devices: 16.5 us -> 4.85 us  [swapped(): lax.ppermute(block, 'head', [(i, i ^ bit) for i in range(lax.axis_size('h...]
    pallas_call x1, Pallas kernels: 12.4 us -> 16.1 us  [per_device(): pl.pallas_call(relayout_kernel, grid=(3, blocks), out_shape=(pltpu.VMEM((...]
    ppermute x18 -> x14, starting transfers between devices: 9.08 us -> 5.65 us  [swapped(): lax.ppermute(block, 'head', [(i, i ^ bit) for i in range(lax.axis_size('h...]
    ppermute x4 -> x10, waiting for transfers between devices: 11.4 us -> 13.1 us  [the longest x8 13 us: moved(): return lax.ppermute(block, ('section', 'head'), route)]
    pallas_call x35 -> x36, Pallas kernels: 63.4 us -> 63.5 us  [__call__(): pl.pallas_call(body, out_shape=outs, in_specs=[SCALARS] * scalars + [WHOL...]
  transfers between devices with their start and end apart: 22 -> 24, of which waited for: 12 -> 7; matrix products, arithmetic and copies ran while one was open for 1% -> 0% of each run, Pallas kernels for 35% -> 34%
where the time goes in v2:
time: 129 us
  Pallas kernels  79.6 us (62%)
  starting transfers between devices  28.2 us (22%)
  waiting for transfers between devices  17.9 us (14%)
  local copies, waits for them, and re-layouts  1.69 us (1%)
    pallas_call x36, Pallas kernels, __call__(): pl.pallas_call(body, out_shape=outs, in_specs=[SCALARS] * scalars + [WHOL...  63.5 us
    ppermute x8, starting transfers between devices, moved(): return lax.ppermute(block, ('section', 'head'), route)  21.2 us
    pallas_call x1, Pallas kernels, per_device(): pl.pallas_call(relayout_kernel, grid=(3, blocks), out_shape=(pltpu.VMEM((...  16.1 us
    ppermute x8, waiting for transfers between devices, moved(): return lax.ppermute(block, ('section', 'head'), route)  13 us
    ppermute x14, starting transfers between devices, swapped(): lax.ppermute(block, 'head', [(i, i ^ bit) for i in range(lax.axis_size('h...  5.65 us
    ppermute x14, waiting for transfers between devices, swapped(): lax.ppermute(block, 'head', [(i, i ^ bit) for i in range(lax.axis_size('h...  4.85 us
  transfers between devices with their start and end apart: 24, of which 7 were waited for; matrix products, arithmetic and copies ran while one was open for 0% of the time, Pallas kernels for 34%

profile of v2, /device:TPU:0, one launch (start us, length us, event | category | flops | bytes accessed | tf_op | source)
XLA Modules:
  0.0 128.7 jit_solution(7467853130887298561)
XLA Ops:
  0.7 16.1 %shard_map.121 = (bf16[3,1024,2048]{2,1,0:T(8,128)(2,1)S(1)}, bf16[3,128,2048]{2,1,0:T(8,128)(2,1)S(1)}, f32[16,128,128]{2,1,0:T(8,128)S(1)}, bf16[2048,1024]{1,0:T(8,128)(2,1)S(1)}) custom-call(s32[4]{0:T(128)S(1)} %pad_add_fusion.place_ref.refs_0_, bf16[1,128,1024]{2,1,0:T(8,128)(2,1)} %refs_1_.4, f32[1,1024]{1,0:T(1,128)} %refs_2_.6, f32[16,32]{1,0:T(8,128)} %bitcast.26, ...), custom_call_target="tpu_custom_call" | custom-call | flops 4831838208 | bytes 12582912 | tf_op jit(solution)/shard_map/pallas_call | solution.py:432
  16.9 1.7 %shard_map.122 = (bf16[128,2048]{1,0:T(8,128)(2,1)S(1)}, bf16[64,1024]{1,0:T(8,128)(2,1)S(1)}) custom-call(s32[4]{0:T(128)S(1)} %pad_add_fusion.place_ref.refs_0_, bf16[1,128,1024]{2,1,0:T(8,128)(2,1)S(1)} %copy-done.3, bf16[3,128,2048]{2,1,0:T(8,128)(2,1)S(1)} %get-tuple-element.48.refs_2_.refs_4_, ...), custom_call_target="tpu_custom_call" | custom-call | bytes 1048576 | tf_op jit(solution)/shard_map/pallas_call | solution.py:366
  20.5 5.9 %shard_map.124 = (bf16[3,128,2048]{2,1,0:T(8,128)(2,1)S(1)}, bf16[3,128,2048]{2,1,0:T(8,128)(2,1)S(1)}, bf16[3,128,2048]{2,1,0:T(8,128)(2,1)S(1)}) custom-call(bf16[3,128,1024]{2,1,0:T(8,128)(2,1)S(1)} %bitcast.18, f32[1,1024]{1,0:T(1,128)S(1)} %copy-done.5, bf16[3,1024,2048]{2,1,0:T(8,128)(2,1)S(1)} %get-tuple-element.55.refs_2_.refs_3_.refs_6_.refs_1_, ...), custom_call_target="tpu_custom_call" | custom-call | flops 4831838208 | bytes 1048576 | tf_op jit(solution)/shard_map/pallas_call | solution.py:366
  27.8 4.5 %collective-permute-start.1 = (bf16[64,1024]{1,0:T(8,128)(2,1)S(1)}, bf16[64,1024]{1,0:T(8,128)(2,1)S(1)}, u32[]{:S(2)}, u32[]{:S(2)}) collective-permute-start(bf16[64,1024]{1,0:T(8,128)(2,1)S(1)} %shard_map.125.refs_2_.refs_1_), channel_id=1, source_target_pairs={{0,4},{1,5},{2,6},{3,7},{4,8},{5,9},{6,10},{7,11},{8,12},{9,13},{1... | collective-permute-start | bytes 393224 | tf_op jit(solution)/shard_map/ppermute | solution.py:391
  32.4 4.4 %collective-permute-start.2 = (bf16[64,1024]{1,0:T(8,128)(2,1)S(1)}, bf16[64,1024]{1,0:T(8,128)(2,1)S(1)}, u32[]{:S(2)}, u32[]{:S(2)}) collective-permute-start(bf16[64,1024]{1,0:T(8,128)(2,1)S(1)} %shard_map.125.refs_2_.refs_1_), channel_id=1, source_target_pairs={{0,6},{1,7},{2,4},{3,5},{4,10},{5,11},{6,8},{7,9},{8,14},{9,15},{1... | collective-permute-start | bytes 393224 | tf_op jit(solution)/shard_map/ppermute | solution.py:391
  36.8 3.3 %shard_map.127 = (bf16[3,128,1024]{2,1,0:T(8,128)(2,1)S(1)}, f32[8,128,128]{2,1,0:T(8,128)S(1)}, bf16[128,1024]{1,0:T(8,128)(2,1)S(1)}, bf16[64,1024]{1,0:T(8,128)(2,1)S(1)}) custom-call(s32[4]{0:T(128)S(1)} %pad_add_fusion.place_ref.refs_0_, bf16[128,1024]{1,0:T(8,128)(2,1)S(1)} %bitcast.22, ...), custom_call_target="tpu_custom_call" | custom-call | flops 1073741824 | bytes 1048576 | tf_op jit(solution)/shard_map/pallas_call | solution.py:366
  40.1 2.8 %shard_map.128 = (bf16[3,128,1024]{2,1,0:T(8,128)(2,1)S(1)}, f32[8,128,128]{2,1,0:T(8,128)S(1)}) custom-call(bf16[128,1024]{1,0:T(8,128)(2,1)S(1)} %get-tuple-element.57.refs_0_, bf16[3,128,2048]{2,1,0:T(8,128)(2,1)S(1)} %get-tuple-element.56.refs_4_.refs_0_.refs_2_.refs_1_, f32[16,128,128]{2,1,0:T(8,128)S(1)} %shard_map.126.refs_3_.refs_5_.refs_2_, ...), custom_call_target="tpu_custom_call" | custom-call | flops 1073741824 | bytes 1048576 | tf_op jit(solution)/shard_map/pallas_call | solution.py:366
  43.1 4.8 %shard_map.130 = (bf16[64,1024]{1,0:T(8,128)(2,1)S(1)}, f32[64,1024]{1,0:T(8,128)S(1)}) custom-call(s32[4]{0:T(128)S(1)} %pad_add_fusion.place_ref.refs_0_, bf16[3,128,1024]{2,1,0:T(8,128)(2,1)S(1)} %get-tuple-element.58.refs_4_.refs_1_, bf16[3,128,1024]{2,1,0:T(8,128)(2,1)S(1)} %get-tuple-element.59.refs_2_, ...), custom_call_target="tpu_custom_call" | custom-call | flops 1610612736 | bytes 1048576 | tf_op jit(solution)/shard_map/pallas_call | solution.py:366
  48.4 2.3 %shard_map.131 = (bf16[128,1024]{1,0:T(8,128)(2,1)S(1)}, bf16[128,1024]{1,0:T(8,128)(2,1)S(1)}, bf16[64,1024]{1,0:T(8,128)(2,1)S(1)}) custom-call(s32[4]{0:T(128)S(1)} %pad_add_fusion.place_ref.refs_0_, s32[6]{0:T(128)S(1)} %copy-done.8, bf16[64,1024]{1,0:T(8,128)(2,1)S(1)} %shard_map.129.refs_4_.refs_2_, ...), custom_call_target="tpu_custom_call" | custom-call | flops 1610612736 | bytes 1048576 | tf_op jit(solution)/shard_map/pallas_call | solution.py:366
  51.4 1.4 %shard_map.133.refs_2_.refs_4_ = bf16[128,1024]{1,0:T(8,128)(2,1)S(1)} custom-call(bf16[128,1024]{1,0:T(8,128)(2,1)S(1)} %get-tuple-element.62.refs_0_, bf16[3,1024,2048]{2,1,0:T(8,128)(2,1)S(1)} %get-tuple-element.55.refs_2_.refs_3_.refs_6_.refs_1_, f32[16,128,128]{2,1,0:T(8,128)S(1)} %get-tuple-element.49.refs_3_.refs_1_.refs_7_.refs_2_, ...), custom_call_target="tpu_custom_call" | custom-call | flops 1610612736 | bytes 1048576 | tf_op jit(solution)/shard_map/pallas_call | solution.py:366
  52.9 1.3 %shard_map.134 = (bf16[64,1024]{1,0:T(8,128)(2,1)S(1)}, f32[64,1024]{1,0:T(8,128)S(1)}) custom-call(s32[4]{0:T(128)S(1)} %pad_add_fusion.place_ref.refs_0_, bf16[128,1024]{1,0:T(8,128)(2,1)S(1)} %get-tuple-element.61.refs_6_.refs_1_, bf16[128,1024]{1,0:T(8,128)(2,1)S(1)} %shard_map.133.refs_2_.refs_4_, ...), custom_call_target="tpu_custom_call" | custom-call | flops 536870912 | bytes 1048576 | tf_op jit(solution)/shard_map/pallas_call | solution.py:366
  55.0 1.3 %collective-permute-start.10 = (bf16[64,1024]{1,0:T(8,128)(2,1)S(1)}, bf16[64,1024]{1,0:T(8,128)(2,1)S(1)}, u32[]{:S(2)}, u32[]{:S(2)}) collective-permute-start(bf16[64,1024]{1,0:T(8,128)(2,1)S(1)} %shard_map.132.refs_3_), channel_id=1, source_target_pairs={{4,2},{5,3},{6,0},{7,1},{8,6},{9,7},{10,4},{11,5},{12,10},{13,11},... | collective-permute-start | bytes 393224 | tf_op jit(solution)/shard_map/ppermute | solution.py:391
  59.0 5.1 %collective-permute-done.10.refs_4_ = bf16[64,1024]{1,0:T(8,128)(2,1)S(1)} collective-permute-done((bf16[64,1024]{1,0:T(8,128)(2,1)S(1)}, bf16[64,1024]{1,0:T(8,128)(2,1)S(1)}, u32[]{:S(2)}, u32[]{:S(2)}) %collective-permute-start.10) | collective-permute-done | bytes 131104 | tf_op jit(solution)/shard_map/ppermute | solution.py:391
  64.1 1.5 %collective-permute-done.9.refs_3_ = bf16[64,1024]{1,0:T(8,128)(2,1)S(1)} collective-permute-done((bf16[64,1024]{1,0:T(8,128)(2,1)S(1)}, bf16[64,1024]{1,0:T(8,128)(2,1)S(1)}, u32[]{:S(2)}, u32[]{:S(2)}) %collective-permute-start.9) | collective-permute-done | bytes 131104 | tf_op jit(solution)/shard_map/ppermute | solution.py:391
  66.2 3.5 %collective-permute-start.6 = (bf16[64,1024]{1,0:T(8,128)(2,1)S(1)}, bf16[64,1024]{1,0:T(8,128)(2,1)S(1)}, u32[]{:S(2)}, u32[]{:S(2)}) collective-permute-start(bf16[64,1024]{1,0:T(8,128)(2,1)S(1)} %shard_map.136.refs_5_.refs_1_), channel_id=1, source_target_pairs={{0,4},{1,5},{2,6},{3,7},{4,8},{5,9},{6,10},{7,11},{8,12},{9,13},{1... | collective-permute-start | bytes 393224 | tf_op jit(solution)/shard_map/ppermute | solution.py:391
  69.7 3.7 %collective-permute-start.7 = (bf16[64,1024]{1,0:T(8,128)(2,1)S(1)}, bf16[64,1024]{1,0:T(8,128)(2,1)S(1)}, u32[]{:S(2)}, u32[]{:S(2)}) collective-permute-start(bf16[64,1024]{1,0:T(8,128)(2,1)S(1)} %shard_map.136.refs_5_.refs_1_), channel_id=1, source_target_pairs={{0,6},{1,7},{2,4},{3,5},{4,10},{5,11},{6,8},{7,9},{8,14},{9,15},{1... | collective-permute-start | bytes 393224 | tf_op jit(solution)/shard_map/ppermute | solution.py:391
  73.4 3.3 %shard_map.138 = (bf16[3,128,1024]{2,1,0:T(8,128)(2,1)S(1)}, f32[8,128,128]{2,1,0:T(8,128)S(1)}, bf16[128,1024]{1,0:T(8,128)(2,1)S(1)}, bf16[64,1024]{1,0:T(8,128)(2,1)S(1)}) custom-call(s32[4]{0:T(128)S(1)} %pad_add_fusion.place_ref.refs_0_, bf16[64,1024]{1,0:T(8,128)(2,1)S(1)} %shard_map.137.refs_1_.refs_7_, ...), custom_call_target="tpu_custom_call" | custom-call | flops 1073741824 | bytes 1048576 | tf_op jit(solution)/shard_map/pallas_call | solution.py:366
  76.7 2.8 %shard_map.139 = (bf16[3,128,1024]{2,1,0:T(8,128)(2,1)S(1)}, f32[8,128,128]{2,1,0:T(8,128)S(1)}) custom-call(bf16[128,1024]{1,0:T(8,128)(2,1)S(1)} %get-tuple-element.70.refs_0_, bf16[3,128,2048]{2,1,0:T(8,128)(2,1)S(1)} %get-tuple-element.68.refs_0_.refs_3_.refs_1_, f32[16,128,128]{2,1,0:T(8,128)S(1)} %shard_map.135.refs_4_.refs_2_, ...), custom_call_target="tpu_custom_call" | custom-call | flops 1073741824 | bytes 1048576 | tf_op jit(solution)/shard_map/pallas_call | solution.py:366
  79.6 4.8 %shard_map.141 = (bf16[64,1024]{1,0:T(8,128)(2,1)S(1)}, f32[64,1024]{1,0:T(8,128)S(1)}) custom-call(s32[4]{0:T(128)S(1)} %pad_add_fusion.place_ref.refs_0_, bf16[3,128,1024]{2,1,0:T(8,128)(2,1)S(1)} %get-tuple-element.72.refs_5_.refs_1_, bf16[3,128,1024]{2,1,0:T(8,128)(2,1)S(1)} %get-tuple-element.73.refs_2_, ...), custom_call_target="tpu_custom_call" | custom-call | flops 1610612736 | bytes 1048576 | tf_op jit(solution)/shard_map/pallas_call | solution.py:366
  85.0 2.3 %shard_map.142 = (bf16[128,1024]{1,0:T(8,128)(2,1)S(1)}, bf16[128,1024]{1,0:T(8,128)(2,1)S(1)}, bf16[64,1024]{1,0:T(8,128)(2,1)S(1)}) custom-call(s32[4]{0:T(128)S(1)} %pad_add_fusion.place_ref.refs_0_, s32[6]{0:T(128)S(1)} %copy-done.8, bf16[64,1024]{1,0:T(8,128)(2,1)S(1)} %shard_map.140.refs_4_.refs_2_, ...), custom_call_target="tpu_custom_call" | custom-call | flops 1610612736 | bytes 1048576 | tf_op jit(solution)/shard_map/pallas_call | solution.py:366
  88.0 1.4 %shard_map.144.refs_2_.refs_4_ = bf16[128,1024]{1,0:T(8,128)(2,1)S(1)} custom-call(bf16[128,1024]{1,0:T(8,128)(2,1)S(1)} %get-tuple-element.76.refs_0_, bf16[3,1024,2048]{2,1,0:T(8,128)(2,1)S(1)} %get-tuple-element.55.refs_2_.refs_3_.refs_6_.refs_1_, f32[16,128,128]{2,1,0:T(8,128)S(1)} %get-tuple-element.49.refs_3_.refs_1_.refs_7_.refs_2_, ...), custom_call_target="tpu_custom_call" | custom-call | flops 1610612736 | bytes 1048576 | tf_op jit(solution)/shard_map/pallas_call | solution.py:366
  89.5 1.3 %shard_map.145 = (bf16[64,1024]{1,0:T(8,128)(2,1)S(1)}, f32[64,1024]{1,0:T(8,128)S(1)}) custom-call(s32[4]{0:T(128)S(1)} %pad_add_fusion.place_ref.refs_0_, bf16[128,1024]{1,0:T(8,128)(2,1)S(1)} %get-tuple-element.75.refs_6_.refs_1_, bf16[128,1024]{1,0:T(8,128)(2,1)S(1)} %shard_map.144.refs_2_.refs_4_, ...), custom_call_target="tpu_custom_call" | custom-call | flops 536870912 | bytes 1048576 | tf_op jit(solution)/shard_map/pallas_call | solution.py:366
  95.6 4.2 %collective-permute-done.17.refs_3_ = bf16[64,1024]{1,0:T(8,128)(2,1)S(1)} collective-permute-done((bf16[64,1024]{1,0:T(8,128)(2,1)S(1)}, bf16[64,1024]{1,0:T(8,128)(2,1)S(1)}, u32[]{:S(2)}, u32[]{:S(2)}) %collective-permute-start.17) | collective-permute-done | bytes 131104 | tf_op jit(solution)/shard_map/ppermute | solution.py:391
  99.7 2.4 %collective-permute-done.18.refs_4_ = bf16[64,1024]{1,0:T(8,128)(2,1)S(1)} collective-permute-done((bf16[64,1024]{1,0:T(8,128)(2,1)S(1)}, bf16[64,1024]{1,0:T(8,128)(2,1)S(1)}, u32[]{:S(2)}, u32[]{:S(2)}) %collective-permute-start.18) | collective-permute-done | bytes 131104 | tf_op jit(solution)/shard_map/ppermute | solution.py:391
  102.7 1.6 %collective-permute-start.15 = (bf16[64,1024]{1,0:T(8,128)(2,1)S(1)}, bf16[64,1024]{1,0:T(8,128)(2,1)S(1)}, u32[]{:S(2)}, u32[]{:S(2)}) collective-permute-start(bf16[64,1024]{1,0:T(8,128)(2,1)S(1)} %shard_map.147.refs_5_.refs_0_), channel_id=1, source_target_pairs={{0,2},{1,3},{2,0},{3,1},{4,6},{5,7},{6,4},{7,5},{8,10},{9,11},{10,... | collective-permute-start | bytes 393224 | tf_op jit(solution)/shard_map/ppermute | solution.py:395
  104.3 3.3 %shard_map.149 = (bf16[3,128,1024]{2,1,0:T(8,128)(2,1)S(1)}, f32[8,128,128]{2,1,0:T(8,128)S(1)}, bf16[128,1024]{1,0:T(8,128)(2,1)S(1)}, bf16[64,1024]{1,0:T(8,128)(2,1)S(1)}) custom-call(s32[4]{0:T(128)S(1)} %pad_add_fusion.place_ref.refs_0_, bf16[64,1024]{1,0:T(8,128)(2,1)S(1)} %shard_map.148.refs_1_.refs_7_, ...), custom_call_target="tpu_custom_call" | custom-call | flops 1073741824 | bytes 1048576 | tf_op jit(solution)/shard_map/pallas_call | solution.py:366
  107.6 2.8 %shard_map.150 = (bf16[3,128,1024]{2,1,0:T(8,128)(2,1)S(1)}, f32[8,128,128]{2,1,0:T(8,128)S(1)}) custom-call(bf16[128,1024]{1,0:T(8,128)(2,1)S(1)} %get-tuple-element.84.refs_0_, bf16[3,128,2048]{2,1,0:T(8,128)(2,1)S(1)} %get-tuple-element.82.refs_0_.refs_3_.refs_1_, f32[16,128,128]{2,1,0:T(8,128)S(1)} %shard_map.146.refs_4_.refs_2_, ...), custom_call_target="tpu_custom_call" | custom-call | flops 1073741824 | bytes 1048576 | tf_op jit(solution)/shard_map/pallas_call | solution.py:366
  110.5 4.8 %shard_map.152 = (bf16[64,1024]{1,0:T(8,128)(2,1)S(1)}, f32[64,1024]{1,0:T(8,128)S(1)}) custom-call(s32[4]{0:T(128)S(1)} %pad_add_fusion.place_ref.refs_0_, bf16[3,128,1024]{2,1,0:T(8,128)(2,1)S(1)} %get-tuple-element.86.refs_5_.refs_1_, bf16[3,128,1024]{2,1,0:T(8,128)(2,1)S(1)} %get-tuple-element.87.refs_2_, ...), custom_call_target="tpu_custom_call" | custom-call | flops 1610612736 | bytes 1048576 | tf_op jit(solution)/shard_map/pallas_call | solution.py:366
  119.6 1.3 %collective-permute-start.22 = (bf16[64,1024]{1,0:T(8,128)(2,1)S(1)}, bf16[64,1024]{1,0:T(8,128)(2,1)S(1)}, u32[]{:S(2)}, u32[]{:S(2)}) collective-permute-start(bf16[64,1024]{1,0:T(8,128)(2,1)S(1)} %shard_map.154.refs_3_.refs_0_), channel_id=1, source_target_pairs={{0,2},{1,3},{2,0},{3,1},{4,6},{5,7},{6,4},{7,5},{8,10},{9,11},{10,... | collective-permute-start | bytes 393224 | tf_op jit(solution)/shard_map/ppermute | solution.py:395
  120.9 1.7 %shard_map.155.refs_2_ = f32[16,32]{1,0:T(8,128)} custom-call(f32[8,128,128]{2,1,0:T(8,128)S(1)} %get-tuple-element.91.refs_0_, f32[8,128,128]{2,1,0:T(8,128)S(1)} %get-tuple-element.92.refs_1_, s32[128,128]{1,0:T(8,128)S(1)} %copy-done.6, bf16[64,1024]{1,0:T(8,128)(2,1)S(1)} %shard_map.154.refs_3_.refs_0_), custom_call_target="tpu_custom_call" | custom-call | bytes 1048576 | tf_op jit(solution)/shard_map/pallas_call | solution.py:366
  122.6 2.7 %collective-permute-done.22.refs_1_ = bf16[64,1024]{1,0:T(8,128)(2,1)S(1)} collective-permute-done((bf16[64,1024]{1,0:T(8,128)(2,1)S(1)}, bf16[64,1024]{1,0:T(8,128)(2,1)S(1)}, u32[]{:S(2)}, u32[]{:S(2)}) %collective-permute-start.22) | collective-permute-done | bytes 131104 | tf_op jit(solution)/shard_map/ppermute | solution.py:395
  126.1 1.3 %collective-permute-done.23.refs_2_ = bf16[64,1024]{1,0:T(8,128)(2,1)S(1)} collective-permute-done((bf16[64,1024]{1,0:T(8,128)(2,1)S(1)}, bf16[64,1024]{1,0:T(8,128)(2,1)S(1)}, u32[]{:S(2)}, u32[]{:S(2)}) %collective-permute-start.23) | collective-permute-done | bytes 131104 | tf_op jit(solution)/shard_map/ppermute | solution.py:395
  (72 shorter events, 22.0 us)
Async XLA Ops:
  0.7 16.1 %copy-start.3 = (bf16[1,128,1024]{2,1,0:T(8,128)(2,1)S(1)}, bf16[1,128,1024]{2,1,0:T(8,128)(2,1)}, u32[]{:S(2)}) copy-start(bf16[1,128,1024]{2,1,0:T(8,128)(2,1)} %refs_1_.4) | copy-start | bytes 786436
  18.6 1.8 %copy-start = (bf16[1,3,128,1024]{3,2,1,0:T(8,128)(2,1)S(1)}, bf16[1,3,128,1024]{3,2,1,0:T(8,128)(2,1)}, u32[]{:S(2)}) copy-start(bf16[1,3,128,1024]{3,2,1,0:T(8,128)(2,1)} %param.12) | copy-start | bytes 2359300
  18.6 1.8 %copy-start.5 = (f32[1,1024]{1,0:T(1,128)S(1)}, f32[1,1024]{1,0:T(1,128)}, u32[]{:S(2)}) copy-start(f32[1,1024]{1,0:T(1,128)} %refs_2_.6) | copy-start | bytes 12292
  19.9 6.5 %collective-permute-start = (bf16[64,1024]{1,0:T(8,128)(2,1)S(1)}, bf16[64,1024]{1,0:T(8,128)(2,1)S(1)}, u32[]{:S(2)}, u32[]{:S(2)}) collective-permute-start(bf16[64,1024]{1,0:T(8,128)(2,1)S(1)} %get-tuple-element.53.refs_3_), channel_id=1, source_target_pairs={{0,1},{1,0},{2,3},{3,2},{4,5},{5,4},{6,7},{7,6},{8,9},{9,8},{10,11... | collective-permute-start | bytes 393224 | tf_op jit(solution)/shard_map/ppermute | solution.py:395
  27.0 9.8 %copy-start.4 = (bf16[1,128,1024]{2,1,0:T(8,128)(2,1)S(1)}, bf16[1,128,1024]{2,1,0:T(8,128)(2,1)}, u32[]{:S(2)}) copy-start(bf16[1,128,1024]{2,1,0:T(8,128)(2,1)} %param.11) | copy-start | bytes 786436
  27.8 15.1 %collective-permute-start.1 = (bf16[64,1024]{1,0:T(8,128)(2,1)S(1)}, bf16[64,1024]{1,0:T(8,128)(2,1)S(1)}, u32[]{:S(2)}, u32[]{:S(2)}) collective-permute-start(bf16[64,1024]{1,0:T(8,128)(2,1)S(1)} %shard_map.125.refs_2_.refs_1_), channel_id=1, source_target_pairs={{0,4},{1,5},{2,6},{3,7},{4,8},{5,9},{6,10},{7,11},{8,12},{9,13},{1... | collective-permute-start | bytes 393224 | tf_op jit(solution)/shard_map/ppermute | solution.py:391
  32.4 10.5 %collective-permute-start.2 = (bf16[64,1024]{1,0:T(8,128)(2,1)S(1)}, bf16[64,1024]{1,0:T(8,128)(2,1)S(1)}, u32[]{:S(2)}, u32[]{:S(2)}) collective-permute-start(bf16[64,1024]{1,0:T(8,128)(2,1)S(1)} %shard_map.125.refs_2_.refs_1_), channel_id=1, source_target_pairs={{0,6},{1,7},{2,4},{3,5},{4,10},{5,11},{6,8},{7,9},{8,14},{9,15},{1... | collective-permute-start | bytes 393224 | tf_op jit(solution)/shard_map/ppermute | solution.py:391
  43.0 5.5 %copy-start.1 = (bf16[6,128,1024]{2,1,0:T(8,128)(2,1)S(1)}, bf16[6,128,1024]{2,1,0:T(8,128)(2,1)}, u32[]{:S(2)}) copy-start(bf16[6,128,1024]{2,1,0:T(8,128)(2,1)} %refs_4_.3) | copy-start | bytes 4718596
  43.0 5.5 %copy-start.8 = (s32[6]{0:T(128)S(1)}, s32[6]{0:T(128)}, u32[]{:S(2)}) copy-start(s32[6]{0:T(128)} %refs_1_.7) | copy-start | bytes 76
  43.0 5.4 %collective-permute-start.3 = (bf16[64,1024]{1,0:T(8,128)(2,1)S(1)}, bf16[64,1024]{1,0:T(8,128)(2,1)S(1)}, u32[]{:S(2)}, u32[]{:S(2)}) collective-permute-start(bf16[64,1024]{1,0:T(8,128)(2,1)S(1)} %shard_map.129.refs_4_.refs_2_), channel_id=1, source_target_pairs={{0,1},{1,0},{2,3},{3,2},{4,5},{5,4},{6,7},{7,6},{8,9},{9,8},{10,11... | collective-permute-start | bytes 393224 | tf_op jit(solution)/shard_map/ppermute | solution.py:395
  47.9 2.9 %collective-permute-start.4 = (bf16[64,1024]{1,0:T(8,128)(2,1)S(1)}, bf16[64,1024]{1,0:T(8,128)(2,1)S(1)}, u32[]{:S(2)}, u32[]{:S(2)}) collective-permute-start(bf16[64,1024]{1,0:T(8,128)(2,1)S(1)} %get-tuple-element.60.refs_8_), channel_id=1, source_target_pairs={{0,1},{1,0},{2,3},{3,2},{4,5},{5,4},{6,7},{7,6},{8,9},{9,8},{10,11... | collective-permute-start | bytes 393224 | tf_op jit(solution)/shard_map/ppermute | solution.py:395
  54.2 4.2 %collective-permute-start.5 = (bf16[64,1024]{1,0:T(8,128)(2,1)S(1)}, bf16[64,1024]{1,0:T(8,128)(2,1)S(1)}, u32[]{:S(2)}, u32[]{:S(2)}) collective-permute-start(bf16[64,1024]{1,0:T(8,128)(2,1)S(1)} %get-tuple-element.66.refs_2_), channel_id=1, source_target_pairs={{0,1},{1,0},{2,3},{3,2},{4,5},{5,4},{6,7},{7,6},{8,9},{9,8},{10,11... | collective-permute-start | bytes 393224 | tf_op jit(solution)/shard_map/ppermute | solution.py:395
  54.3 4.7 %collective-permute-start.8 = (bf16[64,1024]{1,0:T(8,128)(2,1)S(1)}, bf16[64,1024]{1,0:T(8,128)(2,1)S(1)}, u32[]{:S(2)}, u32[]{:S(2)}) collective-permute-start(bf16[64,1024]{1,0:T(8,128)(2,1)S(1)} %shard_map.125.refs_2_.refs_1_), channel_id=1, source_target_pairs={{12,14},{13,15},{14,12},{15,13},{28,30},{29,31},{30,28},{31,29}} | collective-permute-start | bytes 393224 | tf_op jit(solution)/shard_map/ppermute | solution.py:401
  55.0 9.1 %collective-permute-start.10 = (bf16[64,1024]{1,0:T(8,128)(2,1)S(1)}, bf16[64,1024]{1,0:T(8,128)(2,1)S(1)}, u32[]{:S(2)}, u32[]{:S(2)}) collective-permute-start(bf16[64,1024]{1,0:T(8,128)(2,1)S(1)} %shard_map.132.refs_3_), channel_id=1, source_target_pairs={{4,2},{5,3},{6,0},{7,1},{8,6},{9,7},{10,4},{11,5},{12,10},{13,11},... | collective-permute-start | bytes 393224 | tf_op jit(solution)/shard_map/ppermute | solution.py:391
  56.3 9.3 %collective-permute-start.9 = (bf16[64,1024]{1,0:T(8,128)(2,1)S(1)}, bf16[64,1024]{1,0:T(8,128)(2,1)S(1)}, u32[]{:S(2)}, u32[]{:S(2)}) collective-permute-start(bf16[64,1024]{1,0:T(8,128)(2,1)S(1)} %shard_map.132.refs_3_), channel_id=1, source_target_pairs={{4,0},{5,1},{6,2},{7,3},{8,4},{9,5},{10,6},{11,7},{12,8},{13,9},{1... | collective-permute-start | bytes 393224 | tf_op jit(solution)/shard_map/ppermute | solution.py:391
  66.1 7.2 %collective-permute-start.11 = (bf16[64,1024]{1,0:T(8,128)(2,1)S(1)}, bf16[64,1024]{1,0:T(8,128)(2,1)S(1)}, u32[]{:S(2)}, u32[]{:S(2)}) collective-permute-start(bf16[64,1024]{1,0:T(8,128)(2,1)S(1)} %shard_map.137.refs_1_.refs_7_), channel_id=1, source_target_pairs={{0,1},{1,0},{2,3},{3,2},{4,5},{5,4},{6,7},{7,6},{8,9},{9,8},{10,11... | collective-permute-start | bytes 393224 | tf_op jit(solution)/shard_map/ppermute | solution.py:395
  66.2 13.3 %collective-permute-start.6 = (bf16[64,1024]{1,0:T(8,128)(2,1)S(1)}, bf16[64,1024]{1,0:T(8,128)(2,1)S(1)}, u32[]{:S(2)}, u32[]{:S(2)}) collective-permute-start(bf16[64,1024]{1,0:T(8,128)(2,1)S(1)} %shard_map.136.refs_5_.refs_1_), channel_id=1, source_target_pairs={{0,4},{1,5},{2,6},{3,7},{4,8},{5,9},{6,10},{7,11},{8,12},{9,13},{1... | collective-permute-start | bytes 393224 | tf_op jit(solution)/shard_map/ppermute | solution.py:391
  69.7 9.8 %collective-permute-start.7 = (bf16[64,1024]{1,0:T(8,128)(2,1)S(1)}, bf16[64,1024]{1,0:T(8,128)(2,1)S(1)}, u32[]{:S(2)}, u32[]{:S(2)}) collective-permute-start(bf16[64,1024]{1,0:T(8,128)(2,1)S(1)} %shard_map.136.refs_5_.refs_1_), channel_id=1, source_target_pairs={{0,6},{1,7},{2,4},{3,5},{4,10},{5,11},{6,8},{7,9},{8,14},{9,15},{1... | collective-permute-start | bytes 393224 | tf_op jit(solution)/shard_map/ppermute | solution.py:391
  79.5 5.4 %collective-permute-start.12 = (bf16[64,1024]{1,0:T(8,128)(2,1)S(1)}, bf16[64,1024]{1,0:T(8,128)(2,1)S(1)}, u32[]{:S(2)}, u32[]{:S(2)}) collective-permute-start(bf16[64,1024]{1,0:T(8,128)(2,1)S(1)} %shard_map.140.refs_4_.refs_2_), channel_id=1, source_target_pairs={{0,1},{1,0},{2,3},{3,2},{4,5},{5,4},{6,7},{7,6},{8,9},{9,8},{10,11... | collective-permute-start | bytes 393224 | tf_op jit(solution)/shard_map/ppermute | solution.py:395
  84.4 2.9 %collective-permute-start.13 = (bf16[64,1024]{1,0:T(8,128)(2,1)S(1)}, bf16[64,1024]{1,0:T(8,128)(2,1)S(1)}, u32[]{:S(2)}, u32[]{:S(2)}) collective-permute-start(bf16[64,1024]{1,0:T(8,128)(2,1)S(1)} %get-tuple-element.74.refs_8_), channel_id=1, source_target_pairs={{0,1},{1,0},{2,3},{3,2},{4,5},{5,4},{6,7},{7,6},{8,9},{9,8},{10,11... | collective-permute-start | bytes 393224 | tf_op jit(solution)/shard_map/ppermute | solution.py:395
  90.8 4.2 %collective-permute-start.14 = (bf16[64,1024]{1,0:T(8,128)(2,1)S(1)}, bf16[64,1024]{1,0:T(8,128)(2,1)S(1)}, u32[]{:S(2)}, u32[]{:S(2)}) collective-permute-start(bf16[64,1024]{1,0:T(8,128)(2,1)S(1)} %get-tuple-element.80.refs_2_), channel_id=1, source_target_pairs={{0,1},{1,0},{2,3},{3,2},{4,5},{5,4},{6,7},{7,6},{8,9},{9,8},{10,11... | collective-permute-start | bytes 393224 | tf_op jit(solution)/shard_map/ppermute | solution.py:395
  90.9 4.7 %collective-permute-start.16 = (bf16[64,1024]{1,0:T(8,128)(2,1)S(1)}, bf16[64,1024]{1,0:T(8,128)(2,1)S(1)}, u32[]{:S(2)}, u32[]{:S(2)}) collective-permute-start(bf16[64,1024]{1,0:T(8,128)(2,1)S(1)} %shard_map.136.refs_5_.refs_1_), channel_id=1, source_target_pairs={{12,14},{13,15},{14,12},{15,13},{28,30},{29,31},{30,28},{31,29}} | collective-permute-start | bytes 393224 | tf_op jit(solution)/shard_map/ppermute | solution.py:401
  91.5 8.2 %collective-permute-start.17 = (bf16[64,1024]{1,0:T(8,128)(2,1)S(1)}, bf16[64,1024]{1,0:T(8,128)(2,1)S(1)}, u32[]{:S(2)}, u32[]{:S(2)}) collective-permute-start(bf16[64,1024]{1,0:T(8,128)(2,1)S(1)} %shard_map.143.refs_3_), channel_id=1, source_target_pairs={{4,0},{5,1},{6,2},{7,3},{8,4},{9,5},{10,6},{11,7},{12,8},{13,9},{1... | collective-permute-start | bytes 393224 | tf_op jit(solution)/shard_map/ppermute | solution.py:391
  92.8 9.2 %collective-permute-start.18 = (bf16[64,1024]{1,0:T(8,128)(2,1)S(1)}, bf16[64,1024]{1,0:T(8,128)(2,1)S(1)}, u32[]{:S(2)}, u32[]{:S(2)}) collective-permute-start(bf16[64,1024]{1,0:T(8,128)(2,1)S(1)} %shard_map.143.refs_3_), channel_id=1, source_target_pairs={{4,2},{5,3},{6,0},{7,1},{8,6},{9,7},{10,4},{11,5},{12,10},{13,11},... | collective-permute-start | bytes 393224 | tf_op jit(solution)/shard_map/ppermute | solution.py:391
  102.7 1.6 %collective-permute-start.19 = (bf16[64,1024]{1,0:T(8,128)(2,1)S(1)}, bf16[64,1024]{1,0:T(8,128)(2,1)S(1)}, u32[]{:S(2)}, u32[]{:S(2)}) collective-permute-start(bf16[64,1024]{1,0:T(8,128)(2,1)S(1)} %shard_map.148.refs_1_.refs_7_), channel_id=1, source_target_pairs={{0,1},{1,0},{2,3},{3,2},{4,5},{5,4},{6,7},{7,6},{8,9},{9,8},{10,11... | collective-permute-start | bytes 393224 | tf_op jit(solution)/shard_map/ppermute | solution.py:395
  102.7 7.7 %collective-permute-start.15 = (bf16[64,1024]{1,0:T(8,128)(2,1)S(1)}, bf16[64,1024]{1,0:T(8,128)(2,1)S(1)}, u32[]{:S(2)}, u32[]{:S(2)}) collective-permute-start(bf16[64,1024]{1,0:T(8,128)(2,1)S(1)} %shard_map.147.refs_5_.refs_0_), channel_id=1, source_target_pairs={{0,2},{1,3},{2,0},{3,1},{4,6},{5,7},{6,4},{7,5},{8,10},{9,11},{10,... | collective-permute-start | bytes 393224 | tf_op jit(solution)/shard_map/ppermute | solution.py:395
  115.3 5.7 %copy-start.6 = (s32[128,128]{1,0:T(8,128)S(1)}, s32[128,128]{1,0:T(8,128)}, u32[]{:S(2)}) copy-start(s32[128,128]{1,0:T(8,128)} %refs_2_.7) | copy-start | bytes 196612
  115.3 1.4 %collective-permute-start.20 = (bf16[64,1024]{1,0:T(8,128)(2,1)S(1)}, bf16[64,1024]{1,0:T(8,128)(2,1)S(1)}, u32[]{:S(2)}, u32[]{:S(2)}) collective-permute-start(bf16[64,1024]{1,0:T(8,128)(2,1)S(1)} %shard_map.151.refs_4_.refs_1_), channel_id=1, source_target_pairs={{0,1},{1,0},{2,3},{3,2},{4,5},{5,4},{6,7},{7,6},{8,9},{9,8},{10,11... | collective-permute-start | bytes 393224 | tf_op jit(solution)/shard_map/ppermute | solution.py:395
  115.5 2.4 %collective-permute-start.21 = (bf16[64,1024]{1,0:T(8,128)(2,1)S(1)}, bf16[64,1024]{1,0:T(8,128)(2,1)S(1)}, u32[]{:S(2)}, u32[]{:S(2)}) collective-permute-start(bf16[64,1024]{1,0:T(8,128)(2,1)S(1)} %get-tuple-element.88.refs_3_), channel_id=1, source_target_pairs={{0,1},{1,0},{2,3},{3,2},{4,5},{5,4},{6,7},{7,6},{8,9},{9,8},{10,11... | collective-permute-start | bytes 393224 | tf_op jit(solution)/shard_map/ppermute | solution.py:395
  118.0 1.0 copy-start.2
  119.6 5.6 %collective-permute-start.22 = (bf16[64,1024]{1,0:T(8,128)(2,1)S(1)}, bf16[64,1024]{1,0:T(8,128)(2,1)S(1)}, u32[]{:S(2)}, u32[]{:S(2)}) collective-permute-start(bf16[64,1024]{1,0:T(8,128)(2,1)S(1)} %shard_map.154.refs_3_.refs_0_), channel_id=1, source_target_pairs={{0,2},{1,3},{2,0},{3,1},{4,6},{5,7},{6,4},{7,5},{8,10},{9,11},{10,... | collective-permute-start | bytes 393224 | tf_op jit(solution)/shard_map/ppermute | solution.py:395
  126.0 1.4 %collective-permute-start.23 = (bf16[64,1024]{1,0:T(8,128)(2,1)S(1)}, bf16[64,1024]{1,0:T(8,128)(2,1)S(1)}, u32[]{:S(2)}, u32[]{:S(2)}) collective-permute-start(bf16[64,1024]{1,0:T(8,128)(2,1)S(1)} %shard_map.156.refs_1_.refs_3_), channel_id=1, source_target_pairs={{0,1},{1,0},{2,3},{3,2},{4,5},{5,4},{6,7},{7,6},{8,9},{9,8},{10,11... | collective-permute-start | bytes 393224 | tf_op jit(solution)/shard_map/ppermute | solution.py:395
  (1 other events, 0.7 us)

commit v3 on v2

--- a/solution.py
+++ b/solution.py
@@ -84,7 +84,7 @@
             w_out_ref[which, pl.ds(to + ROWS16, ROWS16), lanes] = piece[:, LANES:]
         return carry
 
-    lax.fori_loop(0, depth // (2 * ROWS16), step, 0, unroll=4)
+    lax.fori_loop(0, depth // (2 * ROWS16), step, 0, unroll=8)
 
     @pl.when(block == pl.num_programs(1) - 1)
     def _():
@@ -272,9 +272,9 @@
     total = None
     for c in range(3):
         for part, ref in enumerate((low_ref, high_ref)):
-            term = dot(ref[c], w_ref[c, :, part * width : (part + 1) * width], LAST)
+            term = dot(w_ref[c, :, part * width : (part + 1) * width], ref[c], LAST)
             total = term if total is None else total + term
-    split_halves(place_ref[0], total, send_ref, keep_ref)
+    split_halves(place_ref[0], total.T, send_ref, keep_ref)
 
 
 def pair_kernel(first_ref, second_ref, out_ref):
@@ -355,7 +355,7 @@
     def __init__(self):
         self.before = None
 
-    def __call__(self, kernel, out_shape, args, scratch=(), scalars=0, after=(), flops=0, limit=16):
+    def __call__(self, kernel, out_shape, args, scratch=(), scalars=0, after=(), limit=16):
         outs = out_shape if isinstance(out_shape, tuple) else (out_shape,)
         extra = tuple(after) + (() if self.before is None else (self.before,))
         count = len(args)
@@ -370,7 +370,7 @@
             out_specs=tuple(WHOLE for _ in outs),
             scratch_shapes=list(scratch),
             compiler_params=pltpu.CompilerParams(vmem_limit_bytes=limit * MIB),
-            cost_estimate=pl.CostEstimate(flops=flops, bytes_accessed=MIB, transcendentals=0),
+            cost_estimate=pl.CostEstimate(flops=0, bytes_accessed=LANES, transcendentals=0),
         )(*args, *extra)
         self.before = results[0]
         return results if isinstance(out_shape, tuple) else results[0]
@@ -472,7 +472,6 @@
             qkv_shape,
             (rising, gain, weights),
             scratch=[pltpu.VMEM((tokens, model_width), BF16)],
-            flops=3 * per_mac,
         )
     halves = (shape((half, model_width)), shape((half, model_width), F32))
     half_rows = shape((half, model_width))
@@ -514,11 +513,10 @@
                 (place, order, x_mine, x_other, queue, gain, weights, bias),
                 scratch=[row_scratch],
                 scalars=2,
-                flops=3 * per_mac,
             )
             fallen = down_term(t - 1, keep, received, g_half)
             arrivals = (up, in_last, moved(fallen, -1, 0), moved(fallen, -1, cross))
-            high = run(forward_b_kernel, part_shape, (normed, weights, bias), flops=3 * per_mac)
+            high = run(forward_b_kernel, part_shape, (normed, weights, bias))
             attended = (low, high)
         send, keep = run(
             forward_c_kernel,
@@ -526,7 +524,6 @@
             (place,) + attended + (wo,),
             scratch=[pltpu.VMEM((tokens, inner), BF16)],
             scalars=1,
-            flops=per_mac,
         )
         received = swapped(send, 1)
         if t == 0:
@@ -535,10 +532,9 @@
                 (qkv_shape,) * TICKS,
                 (stash[0], gain, weights),
                 scratch=[pltpu.VMEM((TICKS * tokens, model_width), BF16)],
-                flops=3 * TICKS * per_mac,
             )
         else:
-            probs = run(probs_kernel, scores_shape, (stashed[t], bias), flops=per_mac)
+            probs = run(probs_kernel, scores_shape, (stashed[t], bias))
         up = but_last_bit(
             run(up_term_kernel, half_rows, (place, keep, received, x_half), scalars=1)
         )
@@ -548,7 +544,7 @@
             climbed = (moved(up, 1, 0), moved(up, 1, cross))
             in_last = swapped_in_last(up, cross)
         if t == 0:
-            probs = run(probs_kernel, scores_shape, (stashed[t], bias), flops=per_mac)
+            probs = run(probs_kernel, scores_shape, (stashed[t], bias))
             g_parts = (falling[0],)
         else:
             g_mine = run(choose_kernel, half_rows, (place,) + arrivals, scalars=1)
@@ -559,13 +555,11 @@
             (stacked_shape, acc_shape, shape((tokens, model_width)), half_rows),
             (place,) + g_parts + (stashed[t], probs, wo) + acc[:1],
             scalars=1,
-            flops=2 * per_mac,
         )
         stacked_high, acc_high = run(
             functools.partial(backward_b_kernel, t == 0),
             (stacked_shape, acc_shape),
             (g_full, stashed[t], probs, wo) + acc[1:],
-            flops=2 * per_mac,
         )
         acc = (acc_low, acc_high)
         x_mine = run(pair_kernel, half_rows, climbed)
@@ -575,19 +569,18 @@
             halves,
             (place, stacked_low, stacked_high, weights),
             scalars=1,
-            flops=3 * per_mac,
         )
         received = swapped(send, 1)
 
     rows = shape((1, tokens, model_width))
-    rising_out = run(join_kernel, rows, (place, x_mine, x_other), scalars=1)
-    fallen = down_term(TICKS - 1, keep, received, g_half)
-    fallen_other = swapped(fallen, cross)
     table_grad = run(
         functools.partial(table_kernel, bias_table.shape[1]),
         shape((heads, bias_table.shape[1]), F32),
         acc + (buckets,),
     )
+    fallen = down_term(TICKS - 1, keep, received, g_half)
+    fallen_other = swapped(fallen, cross)
+    rising_out = run(join_kernel, rows, (place, x_mine, x_other), scalars=1)
     lowered = run(pair_kernel, half_rows, (fallen, fallen_other))
     falling_out = run(join_kernel, rows, (place, lowered, swapped(lowered, 1)), scalars=1)
     return (rising_out, falling_out, table_grad.T[None])

time: 129 us -> 126 us (0.977)
  Pallas kernels: 79.6 us -> 75.7 us
    pallas_call x36, Pallas kernels: 63.5 us -> 61.2 us  [__call__(): pl.pallas_call(body, out_shape=outs, in_specs=[SCALARS] * scalars + [WHOL...]
    pallas_call x1, Pallas kernels: 16.1 us -> 14.5 us  [per_device(): pl.pallas_call(relayout_kernel, grid=(3, blocks), out_shape=(pltpu.VMEM((...]
  transfers between devices with their start and end apart: 24 -> 24, of which waited for: 7 -> 7; matrix products, arithmetic and copies ran while one was open for 0% -> 0% of each run, Pallas kernels for 34% -> 32%
where the time goes in v3:
time: 126 us; the launch traced here: 125 us
  Pallas kernels  75.7 us (60%)
  starting transfers between devices  28.4 us (23%)
  waiting for transfers between devices  18.2 us (14%)
  local copies, waits for them, and re-layouts  1.69 us (1%)
    pallas_call x36, Pallas kernels, __call__(): pl.pallas_call(body, out_shape=outs, in_specs=[SCALARS] * scalars + [WHOL...  61.2 us
    ppermute x8, starting transfers between devices, moved(): return lax.ppermute(block, ('section', 'head'), route)  21.4 us
    pallas_call x1, Pallas kernels, per_device(): pl.pallas_call(relayout_kernel, grid=(3, blocks), out_shape=(pltpu.VMEM((...  14.5 us
    ppermute x8, waiting for transfers between devices, moved(): return lax.ppermute(block, ('section', 'head'), route)  12.9 us
    ppermute x14, starting transfers between devices, swapped(): lax.ppermute(block, 'head', [(i, i ^ bit) for i in range(lax.axis_size('h...  5.74 us
    ppermute x14, waiting for transfers between devices, swapped(): lax.ppermute(block, 'head', [(i, i ^ bit) for i in range(lax.axis_size('h...  5.25 us
  transfers between devices with their start and end apart: 24, of which 7 were waited for; matrix products, arithmetic and copies ran while one was open for 0% of the time, Pallas kernels for 32%

profile of v3, /device:TPU:0, one launch (start us, length us, event | category | flops | bytes accessed | tf_op | source)
XLA Modules:
  0.0 125.3 jit_solution(716621991123878406)
XLA Ops:
  0.7 14.5 %shard_map.121 = (bf16[3,1024,2048]{2,1,0:T(8,128)(2,1)S(1)}, bf16[3,128,2048]{2,1,0:T(8,128)(2,1)S(1)}, f32[16,128,128]{2,1,0:T(8,128)S(1)}, bf16[2048,1024]{1,0:T(8,128)(2,1)S(1)}) custom-call(s32[4]{0:T(128)S(1)} %pad_add_fusion.place_ref.refs_0_, bf16[1,128,1024]{2,1,0:T(8,128)(2,1)} %refs_1_.4, f32[1,1024]{1,0:T(1,128)} %refs_2_.7, f32[16,32]{1,0:T(8,128)} %bitcast.26, ...), custom_call_target="tpu_custom_call" | custom-call | flops 4831838208 | bytes 12582912 | tf_op jit(solution)/shard_map/pallas_call | solution.py:432
  15.3 1.7 %shard_map.122 = (bf16[128,2048]{1,0:T(8,128)(2,1)S(1)}, bf16[64,1024]{1,0:T(8,128)(2,1)S(1)}) custom-call(s32[4]{0:T(128)S(1)} %pad_add_fusion.place_ref.refs_0_, bf16[1,128,1024]{2,1,0:T(8,128)(2,1)S(1)} %copy-done.3, bf16[3,128,2048]{2,1,0:T(8,128)(2,1)S(1)} %get-tuple-element.48.refs_2_.refs_4_, ...), custom_call_target="tpu_custom_call" | custom-call | bytes 128 | tf_op jit(solution)/shard_map/pallas_call | solution.py:366
  18.9 5.9 %shard_map.124 = (bf16[3,128,2048]{2,1,0:T(8,128)(2,1)S(1)}, bf16[3,128,2048]{2,1,0:T(8,128)(2,1)S(1)}, bf16[3,128,2048]{2,1,0:T(8,128)(2,1)S(1)}) custom-call(bf16[3,128,1024]{2,1,0:T(8,128)(2,1)S(1)} %bitcast.18, f32[1,1024]{1,0:T(1,128)S(1)} %copy-done.5, bf16[3,1024,2048]{2,1,0:T(8,128)(2,1)S(1)} %get-tuple-element.55.refs_2_.refs_3_.refs_6_.refs_1_, ...), custom_call_target="tpu_custom_call" | custom-call | bytes 128 | tf_op jit(solution)/shard_map/pallas_call | solution.py:366
  25.4 4.6 %collective-permute-start.1 = (bf16[64,1024]{1,0:T(8,128)(2,1)S(1)}, bf16[64,1024]{1,0:T(8,128)(2,1)S(1)}, u32[]{:S(2)}, u32[]{:S(2)}) collective-permute-start(bf16[64,1024]{1,0:T(8,128)(2,1)S(1)} %shard_map.125.refs_2_.refs_1_), channel_id=1, source_target_pairs={{0,4},{1,5},{2,6},{3,7},{4,8},{5,9},{6,10},{7,11},{8,12},{9,13},{1... | collective-permute-start | bytes 393224 | tf_op jit(solution)/shard_map/ppermute | solution.py:391
  30.1 4.4 %collective-permute-start.2 = (bf16[64,1024]{1,0:T(8,128)(2,1)S(1)}, bf16[64,1024]{1,0:T(8,128)(2,1)S(1)}, u32[]{:S(2)}, u32[]{:S(2)}) collective-permute-start(bf16[64,1024]{1,0:T(8,128)(2,1)S(1)} %shard_map.125.refs_2_.refs_1_), channel_id=1, source_target_pairs={{0,6},{1,7},{2,4},{3,5},{4,10},{5,11},{6,8},{7,9},{8,14},{9,15},{1... | collective-permute-start | bytes 393224 | tf_op jit(solution)/shard_map/ppermute | solution.py:391
  35.3 3.3 %shard_map.127 = (bf16[3,128,1024]{2,1,0:T(8,128)(2,1)S(1)}, f32[8,128,128]{2,1,0:T(8,128)S(1)}, bf16[128,1024]{1,0:T(8,128)(2,1)S(1)}, bf16[64,1024]{1,0:T(8,128)(2,1)S(1)}) custom-call(s32[4]{0:T(128)S(1)} %pad_add_fusion.place_ref.refs_0_, bf16[128,1024]{1,0:T(8,128)(2,1)S(1)} %bitcast.22, ...), custom_call_target="tpu_custom_call" | custom-call | bytes 128 | tf_op jit(solution)/shard_map/pallas_call | solution.py:366
  38.7 2.8 %shard_map.128 = (bf16[3,128,1024]{2,1,0:T(8,128)(2,1)S(1)}, f32[8,128,128]{2,1,0:T(8,128)S(1)}) custom-call(bf16[128,1024]{1,0:T(8,128)(2,1)S(1)} %get-tuple-element.57.refs_0_, bf16[3,128,2048]{2,1,0:T(8,128)(2,1)S(1)} %get-tuple-element.56.refs_4_.refs_0_.refs_2_.refs_1_, f32[16,128,128]{2,1,0:T(8,128)S(1)} %shard_map.126.refs_3_.refs_5_.refs_2_, ...), custom_call_target="tpu_custom_call" | custom-call | bytes 128 | tf_op jit(solution)/shard_map/pallas_call | solution.py:366
  41.6 4.0 %shard_map.130 = (bf16[64,1024]{1,0:T(8,128)(2,1)S(1)}, f32[64,1024]{1,0:T(8,128)S(1)}) custom-call(s32[4]{0:T(128)S(1)} %pad_add_fusion.place_ref.refs_0_, bf16[3,128,1024]{2,1,0:T(8,128)(2,1)S(1)} %get-tuple-element.58.refs_4_.refs_1_, bf16[3,128,1024]{2,1,0:T(8,128)(2,1)S(1)} %get-tuple-element.59.refs_2_, ...), custom_call_target="tpu_custom_call" | custom-call | bytes 128 | tf_op jit(solution)/shard_map/pallas_call | solution.py:366
  46.2 2.3 %shard_map.131 = (bf16[128,1024]{1,0:T(8,128)(2,1)S(1)}, bf16[128,1024]{1,0:T(8,128)(2,1)S(1)}, bf16[64,1024]{1,0:T(8,128)(2,1)S(1)}) custom-call(s32[4]{0:T(128)S(1)} %pad_add_fusion.place_ref.refs_0_, s32[6]{0:T(128)S(1)} %copy-done.8, bf16[64,1024]{1,0:T(8,128)(2,1)S(1)} %shard_map.129.refs_4_.refs_2_, ...), custom_call_target="tpu_custom_call" | custom-call | bytes 128 | tf_op jit(solution)/shard_map/pallas_call | solution.py:366
  49.2 1.4 %shard_map.133.refs_2_.refs_4_ = bf16[128,1024]{1,0:T(8,128)(2,1)S(1)} custom-call(bf16[128,1024]{1,0:T(8,128)(2,1)S(1)} %get-tuple-element.62.refs_0_, bf16[3,1024,2048]{2,1,0:T(8,128)(2,1)S(1)} %get-tuple-element.55.refs_2_.refs_3_.refs_6_.refs_1_, f32[16,128,128]{2,1,0:T(8,128)S(1)} %get-tuple-element.49.refs_3_.refs_1_.refs_7_.refs_2_, ...), custom_call_target="tpu_custom_call" | custom-call | bytes 128 | tf_op jit(solution)/shard_map/pallas_call | solution.py:366
  50.7 1.3 %shard_map.134 = (bf16[64,1024]{1,0:T(8,128)(2,1)S(1)}, f32[64,1024]{1,0:T(8,128)S(1)}) custom-call(s32[4]{0:T(128)S(1)} %pad_add_fusion.place_ref.refs_0_, bf16[128,1024]{1,0:T(8,128)(2,1)S(1)} %get-tuple-element.61.refs_6_.refs_1_, bf16[128,1024]{1,0:T(8,128)(2,1)S(1)} %shard_map.133.refs_2_.refs_4_, ...), custom_call_target="tpu_custom_call" | custom-call | bytes 128 | tf_op jit(solution)/shard_map/pallas_call | solution.py:366
  52.8 1.3 %collective-permute-start.10 = (bf16[64,1024]{1,0:T(8,128)(2,1)S(1)}, bf16[64,1024]{1,0:T(8,128)(2,1)S(1)}, u32[]{:S(2)}, u32[]{:S(2)}) collective-permute-start(bf16[64,1024]{1,0:T(8,128)(2,1)S(1)} %shard_map.132.refs_3_), channel_id=1, source_target_pairs={{4,2},{5,3},{6,0},{7,1},{8,6},{9,7},{10,4},{11,5},{12,10},{13,11},... | collective-permute-start | bytes 393224 | tf_op jit(solution)/shard_map/ppermute | solution.py:391
  56.8 5.1 %collective-permute-done.10.refs_4_ = bf16[64,1024]{1,0:T(8,128)(2,1)S(1)} collective-permute-done((bf16[64,1024]{1,0:T(8,128)(2,1)S(1)}, bf16[64,1024]{1,0:T(8,128)(2,1)S(1)}, u32[]{:S(2)}, u32[]{:S(2)}) %collective-permute-start.10) | collective-permute-done | bytes 131104 | tf_op jit(solution)/shard_map/ppermute | solution.py:391
  61.9 1.4 %collective-permute-done.9.refs_3_ = bf16[64,1024]{1,0:T(8,128)(2,1)S(1)} collective-permute-done((bf16[64,1024]{1,0:T(8,128)(2,1)S(1)}, bf16[64,1024]{1,0:T(8,128)(2,1)S(1)}, u32[]{:S(2)}, u32[]{:S(2)}) %collective-permute-start.9) | collective-permute-done | bytes 131104 | tf_op jit(solution)/shard_map/ppermute | solution.py:391
  64.0 3.5 %collective-permute-start.6 = (bf16[64,1024]{1,0:T(8,128)(2,1)S(1)}, bf16[64,1024]{1,0:T(8,128)(2,1)S(1)}, u32[]{:S(2)}, u32[]{:S(2)}) collective-permute-start(bf16[64,1024]{1,0:T(8,128)(2,1)S(1)} %shard_map.136.refs_5_.refs_1_), channel_id=1, source_target_pairs={{0,4},{1,5},{2,6},{3,7},{4,8},{5,9},{6,10},{7,11},{8,12},{9,13},{1... | collective-permute-start | bytes 393224 | tf_op jit(solution)/shard_map/ppermute | solution.py:391
  67.4 3.7 %collective-permute-start.7 = (bf16[64,1024]{1,0:T(8,128)(2,1)S(1)}, bf16[64,1024]{1,0:T(8,128)(2,1)S(1)}, u32[]{:S(2)}, u32[]{:S(2)}) collective-permute-start(bf16[64,1024]{1,0:T(8,128)(2,1)S(1)} %shard_map.136.refs_5_.refs_1_), channel_id=1, source_target_pairs={{0,6},{1,7},{2,4},{3,5},{4,10},{5,11},{6,8},{7,9},{8,14},{9,15},{1... | collective-permute-start | bytes 393224 | tf_op jit(solution)/shard_map/ppermute | solution.py:391
  71.2 3.3 %shard_map.138 = (bf16[3,128,1024]{2,1,0:T(8,128)(2,1)S(1)}, f32[8,128,128]{2,1,0:T(8,128)S(1)}, bf16[128,1024]{1,0:T(8,128)(2,1)S(1)}, bf16[64,1024]{1,0:T(8,128)(2,1)S(1)}) custom-call(s32[4]{0:T(128)S(1)} %pad_add_fusion.place_ref.refs_0_, bf16[64,1024]{1,0:T(8,128)(2,1)S(1)} %shard_map.137.refs_1_.refs_7_, ...), custom_call_target="tpu_custom_call" | custom-call | bytes 128 | tf_op jit(solution)/shard_map/pallas_call | solution.py:366
  74.5 2.8 %shard_map.139 = (bf16[3,128,1024]{2,1,0:T(8,128)(2,1)S(1)}, f32[8,128,128]{2,1,0:T(8,128)S(1)}) custom-call(bf16[128,1024]{1,0:T(8,128)(2,1)S(1)} %get-tuple-element.70.refs_0_, bf16[3,128,2048]{2,1,0:T(8,128)(2,1)S(1)} %get-tuple-element.68.refs_0_.refs_3_.refs_1_, f32[16,128,128]{2,1,0:T(8,128)S(1)} %shard_map.135.refs_4_.refs_2_, ...), custom_call_target="tpu_custom_call" | custom-call | bytes 128 | tf_op jit(solution)/shard_map/pallas_call | solution.py:366
  77.3 4.0 %shard_map.141 = (bf16[64,1024]{1,0:T(8,128)(2,1)S(1)}, f32[64,1024]{1,0:T(8,128)S(1)}) custom-call(s32[4]{0:T(128)S(1)} %pad_add_fusion.place_ref.refs_0_, bf16[3,128,1024]{2,1,0:T(8,128)(2,1)S(1)} %get-tuple-element.72.refs_5_.refs_1_, bf16[3,128,1024]{2,1,0:T(8,128)(2,1)S(1)} %get-tuple-element.73.refs_2_, ...), custom_call_target="tpu_custom_call" | custom-call | bytes 128 | tf_op jit(solution)/shard_map/pallas_call | solution.py:366
  82.8 2.3 %shard_map.142 = (bf16[128,1024]{1,0:T(8,128)(2,1)S(1)}, bf16[128,1024]{1,0:T(8,128)(2,1)S(1)}, bf16[64,1024]{1,0:T(8,128)(2,1)S(1)}) custom-call(s32[4]{0:T(128)S(1)} %pad_add_fusion.place_ref.refs_0_, s32[6]{0:T(128)S(1)} %copy-done.8, bf16[64,1024]{1,0:T(8,128)(2,1)S(1)} %shard_map.140.refs_4_.refs_2_, ...), custom_call_target="tpu_custom_call" | custom-call | bytes 128 | tf_op jit(solution)/shard_map/pallas_call | solution.py:366
  85.8 1.4 %shard_map.144.refs_2_.refs_4_ = bf16[128,1024]{1,0:T(8,128)(2,1)S(1)} custom-call(bf16[128,1024]{1,0:T(8,128)(2,1)S(1)} %get-tuple-element.76.refs_0_, bf16[3,1024,2048]{2,1,0:T(8,128)(2,1)S(1)} %get-tuple-element.55.refs_2_.refs_3_.refs_6_.refs_1_, f32[16,128,128]{2,1,0:T(8,128)S(1)} %get-tuple-element.49.refs_3_.refs_1_.refs_7_.refs_2_, ...), custom_call_target="tpu_custom_call" | custom-call | bytes 128 | tf_op jit(solution)/shard_map/pallas_call | solution.py:366
  87.3 1.3 %shard_map.145 = (bf16[64,1024]{1,0:T(8,128)(2,1)S(1)}, f32[64,1024]{1,0:T(8,128)S(1)}) custom-call(s32[4]{0:T(128)S(1)} %pad_add_fusion.place_ref.refs_0_, bf16[128,1024]{1,0:T(8,128)(2,1)S(1)} %get-tuple-element.75.refs_6_.refs_1_, bf16[128,1024]{1,0:T(8,128)(2,1)S(1)} %shard_map.144.refs_2_.refs_4_, ...), custom_call_target="tpu_custom_call" | custom-call | bytes 128 | tf_op jit(solution)/shard_map/pallas_call | solution.py:366
  93.5 4.2 %collective-permute-done.17.refs_3_ = bf16[64,1024]{1,0:T(8,128)(2,1)S(1)} collective-permute-done((bf16[64,1024]{1,0:T(8,128)(2,1)S(1)}, bf16[64,1024]{1,0:T(8,128)(2,1)S(1)}, u32[]{:S(2)}, u32[]{:S(2)}) %collective-permute-start.17) | collective-permute-done | bytes 131104 | tf_op jit(solution)/shard_map/ppermute | solution.py:391
  97.7 2.2 %collective-permute-done.18.refs_4_ = bf16[64,1024]{1,0:T(8,128)(2,1)S(1)} collective-permute-done((bf16[64,1024]{1,0:T(8,128)(2,1)S(1)}, bf16[64,1024]{1,0:T(8,128)(2,1)S(1)}, u32[]{:S(2)}, u32[]{:S(2)}) %collective-permute-start.18) | collective-permute-done | bytes 131104 | tf_op jit(solution)/shard_map/ppermute | solution.py:391
  100.6 1.6 %collective-permute-start.15 = (bf16[64,1024]{1,0:T(8,128)(2,1)S(1)}, bf16[64,1024]{1,0:T(8,128)(2,1)S(1)}, u32[]{:S(2)}, u32[]{:S(2)}) collective-permute-start(bf16[64,1024]{1,0:T(8,128)(2,1)S(1)} %shard_map.147.refs_5_.refs_0_), channel_id=1, source_target_pairs={{0,2},{1,3},{2,0},{3,1},{4,6},{5,7},{6,4},{7,5},{8,10},{9,11},{10,... | collective-permute-start | bytes 393224 | tf_op jit(solution)/shard_map/ppermute | solution.py:395
  102.1 3.3 %shard_map.149 = (bf16[3,128,1024]{2,1,0:T(8,128)(2,1)S(1)}, f32[8,128,128]{2,1,0:T(8,128)S(1)}, bf16[128,1024]{1,0:T(8,128)(2,1)S(1)}, bf16[64,1024]{1,0:T(8,128)(2,1)S(1)}) custom-call(s32[4]{0:T(128)S(1)} %pad_add_fusion.place_ref.refs_0_, bf16[64,1024]{1,0:T(8,128)(2,1)S(1)} %shard_map.148.refs_1_.refs_7_, ...), custom_call_target="tpu_custom_call" | custom-call | bytes 128 | tf_op jit(solution)/shard_map/pallas_call | solution.py:366
  105.4 2.8 %shard_map.150 = (bf16[3,128,1024]{2,1,0:T(8,128)(2,1)S(1)}, f32[8,128,128]{2,1,0:T(8,128)S(1)}) custom-call(bf16[128,1024]{1,0:T(8,128)(2,1)S(1)} %get-tuple-element.84.refs_0_, bf16[3,128,2048]{2,1,0:T(8,128)(2,1)S(1)} %get-tuple-element.82.refs_0_.refs_3_.refs_1_, f32[16,128,128]{2,1,0:T(8,128)S(1)} %shard_map.146.refs_4_.refs_2_, ...), custom_call_target="tpu_custom_call" | custom-call | bytes 128 | tf_op jit(solution)/shard_map/pallas_call | solution.py:366
  108.3 4.0 %shard_map.152 = (bf16[64,1024]{1,0:T(8,128)(2,1)S(1)}, f32[64,1024]{1,0:T(8,128)S(1)}) custom-call(s32[4]{0:T(128)S(1)} %pad_add_fusion.place_ref.refs_0_, bf16[3,128,1024]{2,1,0:T(8,128)(2,1)S(1)} %get-tuple-element.86.refs_5_.refs_1_, bf16[3,128,1024]{2,1,0:T(8,128)(2,1)S(1)} %get-tuple-element.87.refs_2_, ...), custom_call_target="tpu_custom_call" | custom-call | bytes 128 | tf_op jit(solution)/shard_map/pallas_call | solution.py:366
  112.9 1.7 %shard_map.153.refs_6_ = f32[16,32]{1,0:T(8,128)} custom-call(f32[8,128,128]{2,1,0:T(8,128)S(1)} %get-tuple-element.91.refs_0_, f32[8,128,128]{2,1,0:T(8,128)S(1)} %get-tuple-element.92.refs_1_, s32[128,128]{1,0:T(8,128)S(1)} %copy-done.6, bf16[64,1024]{1,0:T(8,128)(2,1)S(1)} %get-tuple-element.89.refs_3_), custom_call_target="tpu_custom_call" | custom-call | bytes 128 | tf_op jit(solution)/shard_map/pallas_call | solution.py:366
  116.0 1.3 %collective-permute-start.22 = (bf16[64,1024]{1,0:T(8,128)(2,1)S(1)}, bf16[64,1024]{1,0:T(8,128)(2,1)S(1)}, u32[]{:S(2)}, u32[]{:S(2)}) collective-permute-start(bf16[64,1024]{1,0:T(8,128)(2,1)S(1)} %shard_map.154.refs_3_.refs_0_), channel_id=1, source_target_pairs={{0,2},{1,3},{2,0},{3,1},{4,6},{5,7},{6,4},{7,5},{8,10},{9,11},{10,... | collective-permute-start | bytes 393224 | tf_op jit(solution)/shard_map/ppermute | solution.py:395
  118.6 3.0 %collective-permute-done.22.refs_1_ = bf16[64,1024]{1,0:T(8,128)(2,1)S(1)} collective-permute-done((bf16[64,1024]{1,0:T(8,128)(2,1)S(1)}, bf16[64,1024]{1,0:T(8,128)(2,1)S(1)}, u32[]{:S(2)}, u32[]{:S(2)}) %collective-permute-start.22) | collective-permute-done | bytes 131104 | tf_op jit(solution)/shard_map/ppermute | solution.py:395
  122.7 1.3 %collective-permute-done.23.refs_2_ = bf16[64,1024]{1,0:T(8,128)(2,1)S(1)} collective-permute-done((bf16[64,1024]{1,0:T(8,128)(2,1)S(1)}, bf16[64,1024]{1,0:T(8,128)(2,1)S(1)}, u32[]{:S(2)}, u32[]{:S(2)}) %collective-permute-start.23) | collective-permute-done | bytes 131104 | tf_op jit(solution)/shard_map/ppermute | solution.py:395
  (72 shorter events, 22.1 us)
Async XLA Ops:
  0.7 14.5 %copy-start.3 = (bf16[1,128,1024]{2,1,0:T(8,128)(2,1)S(1)}, bf16[1,128,1024]{2,1,0:T(8,128)(2,1)}, u32[]{:S(2)}) copy-start(bf16[1,128,1024]{2,1,0:T(8,128)(2,1)} %refs_1_.4) | copy-start | bytes 786436
  17.0 1.9 %copy-start = (bf16[1,3,128,1024]{3,2,1,0:T(8,128)(2,1)S(1)}, bf16[1,3,128,1024]{3,2,1,0:T(8,128)(2,1)}, u32[]{:S(2)}) copy-start(bf16[1,3,128,1024]{3,2,1,0:T(8,128)(2,1)} %param.12) | copy-start | bytes 2359300
  17.0 1.8 %copy-start.5 = (f32[1,1024]{1,0:T(1,128)S(1)}, f32[1,1024]{1,0:T(1,128)}, u32[]{:S(2)}) copy-start(f32[1,1024]{1,0:T(1,128)} %refs_2_.7) | copy-start | bytes 12292
  18.3 6.5 %collective-permute-start = (bf16[64,1024]{1,0:T(8,128)(2,1)S(1)}, bf16[64,1024]{1,0:T(8,128)(2,1)S(1)}, u32[]{:S(2)}, u32[]{:S(2)}) collective-permute-start(bf16[64,1024]{1,0:T(8,128)(2,1)S(1)} %get-tuple-element.53.refs_3_), channel_id=1, source_target_pairs={{0,1},{1,0},{2,3},{3,2},{4,5},{5,4},{6,7},{7,6},{8,9},{9,8},{10,11... | collective-permute-start | bytes 393224 | tf_op jit(solution)/shard_map/ppermute | solution.py:395
  25.4 9.9 %copy-start.4 = (bf16[1,128,1024]{2,1,0:T(8,128)(2,1)S(1)}, bf16[1,128,1024]{2,1,0:T(8,128)(2,1)}, u32[]{:S(2)}) copy-start(bf16[1,128,1024]{2,1,0:T(8,128)(2,1)} %param.11) | copy-start | bytes 786436
  25.4 16.0 %collective-permute-start.1 = (bf16[64,1024]{1,0:T(8,128)(2,1)S(1)}, bf16[64,1024]{1,0:T(8,128)(2,1)S(1)}, u32[]{:S(2)}, u32[]{:S(2)}) collective-permute-start(bf16[64,1024]{1,0:T(8,128)(2,1)S(1)} %shard_map.125.refs_2_.refs_1_), channel_id=1, source_target_pairs={{0,4},{1,5},{2,6},{3,7},{4,8},{5,9},{6,10},{7,11},{8,12},{9,13},{1... | collective-permute-start | bytes 393224 | tf_op jit(solution)/shard_map/ppermute | solution.py:391
  30.1 11.4 %collective-permute-start.2 = (bf16[64,1024]{1,0:T(8,128)(2,1)S(1)}, bf16[64,1024]{1,0:T(8,128)(2,1)S(1)}, u32[]{:S(2)}, u32[]{:S(2)}) collective-permute-start(bf16[64,1024]{1,0:T(8,128)(2,1)S(1)} %shard_map.125.refs_2_.refs_1_), channel_id=1, source_target_pairs={{0,6},{1,7},{2,4},{3,5},{4,10},{5,11},{6,8},{7,9},{8,14},{9,15},{1... | collective-permute-start | bytes 393224 | tf_op jit(solution)/shard_map/ppermute | solution.py:391
  41.5 4.7 %copy-start.1 = (bf16[6,128,1024]{2,1,0:T(8,128)(2,1)S(1)}, bf16[6,128,1024]{2,1,0:T(8,128)(2,1)}, u32[]{:S(2)}) copy-start(bf16[6,128,1024]{2,1,0:T(8,128)(2,1)} %refs_4_.3) | copy-start | bytes 4718596
  41.5 4.7 %copy-start.8 = (s32[6]{0:T(128)S(1)}, s32[6]{0:T(128)}, u32[]{:S(2)}) copy-start(s32[6]{0:T(128)} %refs_1_.7) | copy-start | bytes 76
  41.5 4.7 %collective-permute-start.3 = (bf16[64,1024]{1,0:T(8,128)(2,1)S(1)}, bf16[64,1024]{1,0:T(8,128)(2,1)S(1)}, u32[]{:S(2)}, u32[]{:S(2)}) collective-permute-start(bf16[64,1024]{1,0:T(8,128)(2,1)S(1)} %shard_map.129.refs_4_.refs_2_), channel_id=1, source_target_pairs={{0,1},{1,0},{2,3},{3,2},{4,5},{5,4},{6,7},{7,6},{8,9},{9,8},{10,11... | collective-permute-start | bytes 393224 | tf_op jit(solution)/shard_map/ppermute | solution.py:395
  45.6 2.9 %collective-permute-start.4 = (bf16[64,1024]{1,0:T(8,128)(2,1)S(1)}, bf16[64,1024]{1,0:T(8,128)(2,1)S(1)}, u32[]{:S(2)}, u32[]{:S(2)}) collective-permute-start(bf16[64,1024]{1,0:T(8,128)(2,1)S(1)} %get-tuple-element.60.refs_8_), channel_id=1, source_target_pairs={{0,1},{1,0},{2,3},{3,2},{4,5},{5,4},{6,7},{7,6},{8,9},{9,8},{10,11... | collective-permute-start | bytes 393224 | tf_op jit(solution)/shard_map/ppermute | solution.py:395
  52.0 4.2 %collective-permute-start.5 = (bf16[64,1024]{1,0:T(8,128)(2,1)S(1)}, bf16[64,1024]{1,0:T(8,128)(2,1)S(1)}, u32[]{:S(2)}, u32[]{:S(2)}) collective-permute-start(bf16[64,1024]{1,0:T(8,128)(2,1)S(1)} %get-tuple-element.66.refs_2_), channel_id=1, source_target_pairs={{0,1},{1,0},{2,3},{3,2},{4,5},{5,4},{6,7},{7,6},{8,9},{9,8},{10,11... | collective-permute-start | bytes 393224 | tf_op jit(solution)/shard_map/ppermute | solution.py:395
  52.1 4.7 %collective-permute-start.8 = (bf16[64,1024]{1,0:T(8,128)(2,1)S(1)}, bf16[64,1024]{1,0:T(8,128)(2,1)S(1)}, u32[]{:S(2)}, u32[]{:S(2)}) collective-permute-start(bf16[64,1024]{1,0:T(8,128)(2,1)S(1)} %shard_map.125.refs_2_.refs_1_), channel_id=1, source_target_pairs={{12,14},{13,15},{14,12},{15,13},{28,30},{29,31},{30,28},{31,29}} | collective-permute-start | bytes 393224 | tf_op jit(solution)/shard_map/ppermute | solution.py:401
  52.8 9.1 %collective-permute-start.10 = (bf16[64,1024]{1,0:T(8,128)(2,1)S(1)}, bf16[64,1024]{1,0:T(8,128)(2,1)S(1)}, u32[]{:S(2)}, u32[]{:S(2)}) collective-permute-start(bf16[64,1024]{1,0:T(8,128)(2,1)S(1)} %shard_map.132.refs_3_), channel_id=1, source_target_pairs={{4,2},{5,3},{6,0},{7,1},{8,6},{9,7},{10,4},{11,5},{12,10},{13,11},... | collective-permute-start | bytes 393224 | tf_op jit(solution)/shard_map/ppermute | solution.py:391
  54.1 9.2 %collective-permute-start.9 = (bf16[64,1024]{1,0:T(8,128)(2,1)S(1)}, bf16[64,1024]{1,0:T(8,128)(2,1)S(1)}, u32[]{:S(2)}, u32[]{:S(2)}) collective-permute-start(bf16[64,1024]{1,0:T(8,128)(2,1)S(1)} %shard_map.132.refs_3_), channel_id=1, source_target_pairs={{4,0},{5,1},{6,2},{7,3},{8,4},{9,5},{10,6},{11,7},{12,8},{13,9},{1... | collective-permute-start | bytes 393224 | tf_op jit(solution)/shard_map/ppermute | solution.py:391
  63.9 7.3 %collective-permute-start.11 = (bf16[64,1024]{1,0:T(8,128)(2,1)S(1)}, bf16[64,1024]{1,0:T(8,128)(2,1)S(1)}, u32[]{:S(2)}, u32[]{:S(2)}) collective-permute-start(bf16[64,1024]{1,0:T(8,128)(2,1)S(1)} %shard_map.137.refs_1_.refs_7_), channel_id=1, source_target_pairs={{0,1},{1,0},{2,3},{3,2},{4,5},{5,4},{6,7},{7,6},{8,9},{9,8},{10,11... | collective-permute-start | bytes 393224 | tf_op jit(solution)/shard_map/ppermute | solution.py:395
  64.0 13.3 %collective-permute-start.6 = (bf16[64,1024]{1,0:T(8,128)(2,1)S(1)}, bf16[64,1024]{1,0:T(8,128)(2,1)S(1)}, u32[]{:S(2)}, u32[]{:S(2)}) collective-permute-start(bf16[64,1024]{1,0:T(8,128)(2,1)S(1)} %shard_map.136.refs_5_.refs_1_), channel_id=1, source_target_pairs={{0,4},{1,5},{2,6},{3,7},{4,8},{5,9},{6,10},{7,11},{8,12},{9,13},{1... | collective-permute-start | bytes 393224 | tf_op jit(solution)/shard_map/ppermute | solution.py:391
  67.4 9.8 %collective-permute-start.7 = (bf16[64,1024]{1,0:T(8,128)(2,1)S(1)}, bf16[64,1024]{1,0:T(8,128)(2,1)S(1)}, u32[]{:S(2)}, u32[]{:S(2)}) collective-permute-start(bf16[64,1024]{1,0:T(8,128)(2,1)S(1)} %shard_map.136.refs_5_.refs_1_), channel_id=1, source_target_pairs={{0,6},{1,7},{2,4},{3,5},{4,10},{5,11},{6,8},{7,9},{8,14},{9,15},{1... | collective-permute-start | bytes 393224 | tf_op jit(solution)/shard_map/ppermute | solution.py:391
  81.4 1.4 %collective-permute-start.12 = (bf16[64,1024]{1,0:T(8,128)(2,1)S(1)}, bf16[64,1024]{1,0:T(8,128)(2,1)S(1)}, u32[]{:S(2)}, u32[]{:S(2)}) collective-permute-start(bf16[64,1024]{1,0:T(8,128)(2,1)S(1)} %shard_map.140.refs_4_.refs_2_), channel_id=1, source_target_pairs={{0,1},{1,0},{2,3},{3,2},{4,5},{5,4},{6,7},{7,6},{8,9},{9,8},{10,11... | collective-permute-start | bytes 393224 | tf_op jit(solution)/shard_map/ppermute | solution.py:395
  81.4 3.7 %collective-permute-start.13 = (bf16[64,1024]{1,0:T(8,128)(2,1)S(1)}, bf16[64,1024]{1,0:T(8,128)(2,1)S(1)}, u32[]{:S(2)}, u32[]{:S(2)}) collective-permute-start(bf16[64,1024]{1,0:T(8,128)(2,1)S(1)} %get-tuple-element.74.refs_8_), channel_id=1, source_target_pairs={{0,1},{1,0},{2,3},{3,2},{4,5},{5,4},{6,7},{7,6},{8,9},{9,8},{10,11... | collective-permute-start | bytes 393224 | tf_op jit(solution)/shard_map/ppermute | solution.py:395
  88.6 4.3 %collective-permute-start.14 = (bf16[64,1024]{1,0:T(8,128)(2,1)S(1)}, bf16[64,1024]{1,0:T(8,128)(2,1)S(1)}, u32[]{:S(2)}, u32[]{:S(2)}) collective-permute-start(bf16[64,1024]{1,0:T(8,128)(2,1)S(1)} %get-tuple-element.80.refs_2_), channel_id=1, source_target_pairs={{0,1},{1,0},{2,3},{3,2},{4,5},{5,4},{6,7},{7,6},{8,9},{9,8},{10,11... | collective-permute-start | bytes 393224 | tf_op jit(solution)/shard_map/ppermute | solution.py:395
  88.8 4.7 %collective-permute-start.16 = (bf16[64,1024]{1,0:T(8,128)(2,1)S(1)}, bf16[64,1024]{1,0:T(8,128)(2,1)S(1)}, u32[]{:S(2)}, u32[]{:S(2)}) collective-permute-start(bf16[64,1024]{1,0:T(8,128)(2,1)S(1)} %shard_map.136.refs_5_.refs_1_), channel_id=1, source_target_pairs={{12,14},{13,15},{14,12},{15,13},{28,30},{29,31},{30,28},{31,29}} | collective-permute-start | bytes 393224 | tf_op jit(solution)/shard_map/ppermute | solution.py:401
  89.5 8.2 %collective-permute-start.17 = (bf16[64,1024]{1,0:T(8,128)(2,1)S(1)}, bf16[64,1024]{1,0:T(8,128)(2,1)S(1)}, u32[]{:S(2)}, u32[]{:S(2)}) collective-permute-start(bf16[64,1024]{1,0:T(8,128)(2,1)S(1)} %shard_map.143.refs_3_), channel_id=1, source_target_pairs={{4,0},{5,1},{6,2},{7,3},{8,4},{9,5},{10,6},{11,7},{12,8},{13,9},{1... | collective-permute-start | bytes 393224 | tf_op jit(solution)/shard_map/ppermute | solution.py:391
  90.8 9.1 %collective-permute-start.18 = (bf16[64,1024]{1,0:T(8,128)(2,1)S(1)}, bf16[64,1024]{1,0:T(8,128)(2,1)S(1)}, u32[]{:S(2)}, u32[]{:S(2)}) collective-permute-start(bf16[64,1024]{1,0:T(8,128)(2,1)S(1)} %shard_map.143.refs_3_), channel_id=1, source_target_pairs={{4,2},{5,3},{6,0},{7,1},{8,6},{9,7},{10,4},{11,5},{12,10},{13,11},... | collective-permute-start | bytes 393224 | tf_op jit(solution)/shard_map/ppermute | solution.py:391
  100.5 1.6 %collective-permute-start.19 = (bf16[64,1024]{1,0:T(8,128)(2,1)S(1)}, bf16[64,1024]{1,0:T(8,128)(2,1)S(1)}, u32[]{:S(2)}, u32[]{:S(2)}) collective-permute-start(bf16[64,1024]{1,0:T(8,128)(2,1)S(1)} %shard_map.148.refs_1_.refs_7_), channel_id=1, source_target_pairs={{0,1},{1,0},{2,3},{3,2},{4,5},{5,4},{6,7},{7,6},{8,9},{9,8},{10,11... | collective-permute-start | bytes 393224 | tf_op jit(solution)/shard_map/ppermute | solution.py:395
  100.6 7.7 %collective-permute-start.15 = (bf16[64,1024]{1,0:T(8,128)(2,1)S(1)}, bf16[64,1024]{1,0:T(8,128)(2,1)S(1)}, u32[]{:S(2)}, u32[]{:S(2)}) collective-permute-start(bf16[64,1024]{1,0:T(8,128)(2,1)S(1)} %shard_map.147.refs_5_.refs_0_), channel_id=1, source_target_pairs={{0,2},{1,3},{2,0},{3,1},{4,6},{5,7},{6,4},{7,5},{8,10},{9,11},{10,... | collective-permute-start | bytes 393224 | tf_op jit(solution)/shard_map/ppermute | solution.py:395
  108.3 4.6 %copy-start.6 = (s32[128,128]{1,0:T(8,128)S(1)}, s32[128,128]{1,0:T(8,128)}, u32[]{:S(2)}) copy-start(s32[128,128]{1,0:T(8,128)} %refs_2_.6) | copy-start | bytes 196612
  112.3 2.2 %collective-permute-start.21 = (bf16[64,1024]{1,0:T(8,128)(2,1)S(1)}, bf16[64,1024]{1,0:T(8,128)(2,1)S(1)}, u32[]{:S(2)}, u32[]{:S(2)}) collective-permute-start(bf16[64,1024]{1,0:T(8,128)(2,1)S(1)} %get-tuple-element.89.refs_3_), channel_id=1, source_target_pairs={{0,1},{1,0},{2,3},{3,2},{4,5},{5,4},{6,7},{7,6},{8,9},{9,8},{10,11... | collective-permute-start | bytes 393224 | tf_op jit(solution)/shard_map/ppermute | solution.py:395
  112.6 4.7 %collective-permute-start.20 = (bf16[64,1024]{1,0:T(8,128)(2,1)S(1)}, bf16[64,1024]{1,0:T(8,128)(2,1)S(1)}, u32[]{:S(2)}, u32[]{:S(2)}) collective-permute-start(bf16[64,1024]{1,0:T(8,128)(2,1)S(1)} %shard_map.151.refs_4_.refs_1_), channel_id=1, source_target_pairs={{0,1},{1,0},{2,3},{3,2},{4,5},{5,4},{6,7},{7,6},{8,9},{9,8},{10,11... | collective-permute-start | bytes 393224 | tf_op jit(solution)/shard_map/ppermute | solution.py:395
  116.0 5.6 %collective-permute-start.22 = (bf16[64,1024]{1,0:T(8,128)(2,1)S(1)}, bf16[64,1024]{1,0:T(8,128)(2,1)S(1)}, u32[]{:S(2)}, u32[]{:S(2)}) collective-permute-start(bf16[64,1024]{1,0:T(8,128)(2,1)S(1)} %shard_map.154.refs_3_.refs_0_), channel_id=1, source_target_pairs={{0,2},{1,3},{2,0},{3,1},{4,6},{5,7},{6,4},{7,5},{8,10},{9,11},{10,... | collective-permute-start | bytes 393224 | tf_op jit(solution)/shard_map/ppermute | solution.py:395
  121.6 1.0 copy-start.2
  122.6 1.4 %collective-permute-start.23 = (bf16[64,1024]{1,0:T(8,128)(2,1)S(1)}, bf16[64,1024]{1,0:T(8,128)(2,1)S(1)}, u32[]{:S(2)}, u32[]{:S(2)}) collective-permute-start(bf16[64,1024]{1,0:T(8,128)(2,1)S(1)} %shard_map.156.refs_1_.refs_3_), channel_id=1, source_target_pairs={{0,1},{1,0},{2,3},{3,2},{4,5},{5,4},{6,7},{7,6},{8,9},{9,8},{10,11... | collective-permute-start | bytes 393224 | tf_op jit(solution)/shard_map/ppermute | solution.py:395
  (1 other events, 0.7 us)

commit v4 on v3

--- a/solution.py
+++ b/solution.py
@@ -51,8 +51,8 @@
 
 
 def relayout_kernel(
-    place_ref, x_ref, gain_ref, table_ref, bucket_ref, w_ref, back_ref,
-    w_out_ref, qkv_ref, bias_ref, back_out_ref, normed, arrived,
+    place_ref, x_ref, kept_ref, gain_ref, table_ref, bucket_ref, w_ref, back_ref,
+    w_out_ref, qkv_ref, kept_qkv_ref, bias_ref, back_out_ref, normed, arrived,
 ):
     which = pl.program_id(0)
     block = pl.program_id(1)
@@ -61,7 +61,9 @@
     @pl.when((which == 0) & (block == 0))
     def _():
         back_copy.start()
-        normed[...] = rms_normed(x_ref[0], gain_ref[...])
+        tokens = x_ref.shape[1]
+        normed[:tokens] = rms_normed(x_ref[0], gain_ref[...])
+        normed[tokens:] = rms_normed(kept_ref[0, 0], gain_ref[...])
         fill_bias(table_ref, bucket_ref, bias_ref)
 
     depth = w_ref.shape[0]
@@ -84,11 +86,14 @@
             w_out_ref[which, pl.ds(to + ROWS16, ROWS16), lanes] = piece[:, LANES:]
         return carry
 
-    lax.fori_loop(0, depth // (2 * ROWS16), step, 0, unroll=8)
+    lax.fori_loop(0, depth // (2 * ROWS16), step, 0, unroll=16)
 
     @pl.when(block == pl.num_programs(1) - 1)
     def _():
-        qkv_ref[which] = dot(normed[...], w_out_ref[which]).astype(BF16)
+        tokens = x_ref.shape[1]
+        out = dot(normed[...], w_out_ref[which]).astype(BF16)
+        qkv_ref[which] = out[:tokens]
+        kept_qkv_ref[which] = out[tokens:]
 
     @pl.when((which == pl.num_programs(0) - 1) & (block == pl.num_programs(1) - 1))
     def _():
@@ -111,63 +116,39 @@
     return [dot(p, value[:, sl], FIRST).astype(BF16) for p, sl in zip(probs, lanes)]
 
 
-def first_attend_kernel(place_ref, x_ref, qkv_ref, bias_ref, out_ref, x_half_ref):
+def forward_kernel(tick, place_ref, *refs):
+    if tick == 0:
+        x_in_ref, qkv_ref, bias_ref, wo_ref, send_ref, keep_ref, x_half_ref, attended = refs
+    else:
+        (order_ref, mine_ref, other_ref, queue_ref, gain_ref, w_ref, bias_ref, wo_ref,
+         send_ref, keep_ref, x_half_ref, attended, x_ref) = refs
+    core = place_ref[0]
+    half = send_ref.shape[0]
     heads = bias_ref.shape[0]
     group = heads // 2
-    x_half_ref[...] = x_ref[0, rows_at(place_ref[0], x_half_ref.shape[0])]
-
-    def step(g, carry):
-        at = rows_at(g, group * LANES)
-        query, key, value = (qkv_ref[c, :, at] for c in range(3))
-        outs = attend(query, key, value, bias_ref, group, g * group)
-        out_ref[:, at] = jnp.concatenate(outs, axis=1)
-        return carry
-
-    lax.fori_loop(0, 2, step, 0)
-
-
-def project_attend(normed, w_ref, bias_ref, out_ref, part):
-    heads = bias_ref.shape[0] // 2
-    at = slice(part * heads * LANES, (part + 1) * heads * LANES)
-    query, key, value = (dot(normed, w_ref[c, :, at]).astype(BF16) for c in range(3))
-    outs = attend(query, key, value, bias_ref, heads, part * heads)
-    for h, out in enumerate(outs):
-        out_ref[:, h * LANES : (h + 1) * LANES] = out
-
-
-def forward_a_kernel(
-    tick, place_ref, order_ref, mine_ref, other_ref, queue_ref, gain_ref, w_ref, bias_ref,
-    out_ref, normed_ref, x_half_ref, x_ref,
-):
-    core = place_ref[0]
-    half = mine_ref.shape[0]
-    x_ref[rows_at(core, half)] = mine_ref[...]
-    x_ref[rows_at(1 - core, half)] = other_ref[...]
-
-    @pl.when(place_ref[1] == 0)
-    def _():
-        x_ref[...] = queue_ref[order_ref[tick - 1]]
-
-    x_half_ref[...] = x_ref[rows_at(core, half)]
-    normed = rms_normed(x_ref[...], gain_ref[...])
-    normed_ref[...] = normed
-    project_attend(normed, w_ref, bias_ref, out_ref, 0)
-
-
-def forward_b_kernel(normed_ref, w_ref, bias_ref, out_ref):
-    project_attend(normed_ref[...], w_ref, bias_ref, out_ref, 1)
-
-
-def forward_c_kernel(place_ref, *refs):
-    *attended, wo_ref, send_ref, keep_ref, joined = refs
-    core = place_ref[0]
-    half = send_ref.shape[0]
-    width = 0
-    for a in attended:
-        joined[:, width : width + a.shape[1]] = a[...]
-        width += a.shape[1]
-    total = dot(joined[...], wo_ref[...])
-    split_halves(core, total, send_ref, keep_ref)
+    if tick == 0:
+        x_half_ref[...] = x_in_ref[0, rows_at(core, half)]
+    else:
+        x_ref[rows_at(core, half)] = mine_ref[...]
+        x_ref[rows_at(1 - core, half)] = other_ref[...]
+
+        @pl.when(place_ref[1] == 0)
+        def _():
+            x_ref[...] = queue_ref[order_ref[tick - 1]]
+
+        x_half_ref[...] = x_ref[rows_at(core, half)]
+        normed = rms_normed(x_ref[...], gain_ref[...])
+    for part in range(2):
+        at = slice(part * group * LANES, (part + 1) * group * LANES)
+        if tick == 0:
+            query, key, value = (qkv_ref[c, :, at] for c in range(3))
+        else:
+            query, key, value = (dot(normed, w_ref[c, :, at]).astype(BF16) for c in range(3))
+        outs = attend(query, key, value, bias_ref, group, part * group)
+        for h, out in enumerate(outs):
+            first = (part * group + h) * LANES
+            attended[:, first : first + LANES] = out
+    split_halves(core, dot(attended[...], wo_ref[...]), send_ref, keep_ref)
 
 
 def split_halves(core, total, send_ref, keep_ref):
@@ -184,11 +165,11 @@
         keep_ref[...] = total[half:]
 
 
-def stash_kernel(x_ref, gain_ref, w_ref, *refs):
+def stash_kernel(skipped, x_ref, gain_ref, w_ref, *refs):
     *outs, normed = refs
-    ticks, tokens, _ = x_ref.shape
+    ticks, tokens = len(outs), x_ref.shape[1]
     for t in range(ticks):
-        normed[t * tokens : (t + 1) * tokens] = rms_normed(x_ref[t], gain_ref[...])
+        normed[t * tokens : (t + 1) * tokens] = rms_normed(x_ref[skipped + t], gain_ref[...])
     width = min(512, w_ref.shape[2])
 
     def step(i, carry):
@@ -220,17 +201,17 @@
     lax.fori_loop(0, 2, step, 0)
 
 
-def grad_attend(g, qkv_ref, probs_ref, wo_ref, acc_in_ref, stacked_ref, acc_ref, part):
+def grad_attend(g, qkv_ref, probs_ref, wo_ref, acc_in_ref, stacked, acc_ref, part):
     heads = probs_ref.shape[0] // 2
     scale = LANES ** (-0.5)
     at = slice(part * heads * LANES, (part + 1) * heads * LANES)
     grad_attn = dot(g, wo_ref[at], LAST).astype(BF16)
-    for h in range(heads):
-        here = slice((part * heads + h) * LANES, (part * heads + h + 1) * LANES)
+    for local in range(heads):
+        h = part * heads + local
         own = slice(h * LANES, (h + 1) * LANES)
-        q, k, v = (qkv_ref[c, :, here] for c in range(3))
-        ga = grad_attn[:, own]
-        probs = probs_ref[part * heads + h]
+        q, k, v = (qkv_ref[c, :, own] for c in range(3))
+        ga = grad_attn[:, local * LANES : (local + 1) * LANES]
+        probs = probs_ref[h]
         grad_probs = dot(v, ga, LAST)
         total = jnp.sum(probs * grad_probs, axis=0, keepdims=True)
         grad_scores = probs * (grad_probs - total)
@@ -239,42 +220,31 @@
             acc_ref[h] = grad_scores
         else:
             acc_ref[h] = acc_in_ref[h] + grad_scores
-        stacked_ref[0, :, own] = (dot(grad16, k, FIRST) * scale).astype(BF16)
-        stacked_ref[1, :, own] = (dot(grad16, q) * scale).astype(BF16)
-        stacked_ref[2, :, own] = dot(probs.astype(BF16), ga).astype(BF16)
-
-
-def backward_a_kernel(first, place_ref, *refs):
+        stacked[0, :, own] = (dot(grad16, k, FIRST) * scale).astype(BF16)
+        stacked[1, :, own] = (dot(grad16, q) * scale).astype(BF16)
+        stacked[2, :, own] = dot(probs.astype(BF16), ga).astype(BF16)
+
+
+def backward_kernel(first, place_ref, *refs):
     core = place_ref[0]
     if first:
-        full_ref, qkv_ref, probs_ref, wo_ref, stacked_ref, acc_ref, g_ref, g_half_ref = refs
+        full_ref, qkv_ref, probs_ref, w_ref, wo_ref, *refs = refs
+        send_ref, keep_ref, acc_ref, g_half_ref, stacked, g_ref = refs
         acc_in_ref = None
-        half = g_half_ref.shape[0]
         g_ref[...] = full_ref[...]
     else:
-        (mine_ref, other_ref, qkv_ref, probs_ref, wo_ref, acc_in_ref,
-         stacked_ref, acc_ref, g_ref, g_half_ref) = refs
+        mine_ref, other_ref, qkv_ref, probs_ref, w_ref, wo_ref, acc_in_ref, *refs = refs
+        send_ref, keep_ref, acc_ref, g_half_ref, stacked, g_ref = refs
         half = g_half_ref.shape[0]
         g_ref[rows_at(core, half)] = mine_ref[...]
         g_ref[rows_at(1 - core, half)] = other_ref[...]
-    g_half_ref[...] = g_ref[rows_at(core, half)]
-    grad_attend(g_ref[...], qkv_ref, probs_ref, wo_ref, acc_in_ref, stacked_ref, acc_ref, 0)
-
-
-def backward_b_kernel(first, g_ref, qkv_ref, probs_ref, wo_ref, *refs):
-    acc_in_ref = None if first else refs[0]
-    stacked_ref, acc_ref = refs[-2:]
-    grad_attend(g_ref[...], qkv_ref, probs_ref, wo_ref, acc_in_ref, stacked_ref, acc_ref, 1)
-
-
-def backward_c_kernel(place_ref, low_ref, high_ref, w_ref, send_ref, keep_ref):
-    width = low_ref.shape[2]
-    total = None
-    for c in range(3):
-        for part, ref in enumerate((low_ref, high_ref)):
-            term = dot(w_ref[c, :, part * width : (part + 1) * width], ref[c], LAST)
-            total = term if total is None else total + term
-    split_halves(place_ref[0], total.T, send_ref, keep_ref)
+    g_half_ref[...] = g_ref[rows_at(core, g_half_ref.shape[0])]
+    for part in range(2):
+        grad_attend(g_ref[...], qkv_ref, probs_ref, wo_ref, acc_in_ref, stacked, acc_ref, part)
+    total = dot(w_ref[0], stacked[0], LAST)
+    total += dot(w_ref[1], stacked[1], LAST)
+    total += dot(w_ref[2], stacked[2], LAST)
+    split_halves(core, total.T, send_ref, keep_ref)
 
 
 def pair_kernel(first_ref, second_ref, out_ref):
@@ -316,10 +286,10 @@
     out_ref[0, rows_at(1 - core, half)] = other_ref[...]
 
 
-def table_kernel(buckets_here, low_ref, high_ref, bucket_ref, out_ref):
-    heads, tokens, _ = low_ref.shape
+def table_kernel(buckets_here, acc_ref, bucket_ref, out_ref):
+    heads, tokens, _ = acc_ref.shape
     rows = 8
-    cells = 2 * heads * rows
+    cells = heads * rows
     columns = buckets_here * rows
     total = jnp.zeros((cells, columns), F32)
     turned = bucket_ref[...].T
@@ -329,16 +299,14 @@
         hits = jnp.concatenate(
             [(ids == b).astype(F32) for b in range(buckets_here)], axis=0
         ).astype(BF16)
-        part = jnp.concatenate(
-            [r[:, at, :].reshape(heads * rows, tokens) for r in (low_ref, high_ref)], axis=0
-        )
+        part = acc_ref[:, at, :].reshape(cells, tokens)
         high = part.astype(BF16)
         low = (part - high.astype(F32)).astype(BF16)
         total += dot(high, hits, LAST) + dot(low, hits, LAST)
     row = lax.broadcasted_iota(jnp.int32, (cells, columns), 0)
     col = lax.broadcasted_iota(jnp.int32, (cells, columns), 1)
     total = jnp.where((row & (rows - 1)) == (col & (rows - 1)), total, 0.0)
-    summed = jnp.sum(total.reshape(2 * heads, rows, columns), axis=1)
+    summed = jnp.sum(total.reshape(heads, rows, columns), axis=1)
     spread = lax.broadcasted_iota(jnp.int32, (columns, buckets_here), 0) >> 3
     bucket = lax.broadcasted_iota(jnp.int32, (columns, buckets_here), 1)
     fold = (spread == bucket).astype(F32)
@@ -417,7 +385,6 @@
     place = jnp.stack([core, section_index, is_last, head_index < 2]).astype(jnp.int32)
     table = bias_table[0].T
     back = w_out[0].reshape(inner, model_width)
-    per_mac = 2 * tokens * model_width * inner
     run = Chain()
     bits = [1 << b for b in range(1, head_count.bit_length() - 1)]
     cross = bits[-1]
@@ -426,14 +393,15 @@
 
     if heads % ROWS16 == 0:
         rows_first = jnp.transpose(w_qkv[0], (0, 2, 1, 3)).reshape(model_width, 3 * heads, head_dim)
-        blocks = 4
+        blocks = 2
         depth = model_width // blocks
         fixed = lambda rank: lambda c, b: (0,) * rank
-        weights, qkv, bias, wo = pl.pallas_call(
+        weights, qkv, kept_qkv, bias, wo = pl.pallas_call(
             relayout_kernel,
             grid=(3, blocks),
             out_shape=(
                 pltpu.VMEM((3, model_width, inner), BF16),
+                qkv_shape,
                 qkv_shape,
                 scores_shape,
                 pltpu.VMEM((inner, model_width), BF16),
@@ -441,6 +409,7 @@
             in_specs=[
                 SCALARS,
                 pl.BlockSpec((1, tokens, model_width), fixed(3)),
+                pl.BlockSpec((1, 1, tokens, model_width), fixed(4)),
                 pl.BlockSpec((1, model_width), fixed(2)),
                 pl.BlockSpec(table.shape, fixed(2)),
                 pl.BlockSpec((tokens, tokens), fixed(2)),
@@ -450,16 +419,17 @@
             out_specs=(
                 WHOLE,
                 pl.BlockSpec((3, tokens, inner), fixed(3)),
+                pl.BlockSpec((3, tokens, inner), fixed(3)),
                 pl.BlockSpec((heads, tokens, tokens), fixed(3)),
                 WHOLE,
             ),
-            scratch_shapes=[pltpu.VMEM((tokens, model_width), BF16), pltpu.SemaphoreType.DMA],
+            scratch_shapes=[pltpu.VMEM((2 * tokens, model_width), BF16), pltpu.SemaphoreType.DMA],
             compiler_params=pltpu.CompilerParams(vmem_limit_bytes=24 * MIB),
             cost_estimate=pl.CostEstimate(
-                flops=9 * per_mac, bytes_accessed=2 * w_qkv.size, transcendentals=0
+                flops=0, bytes_accessed=2 * w_qkv.size, transcendentals=0
             ),
         )(
-            place, in_hbm(rising), in_hbm(gain), in_hbm(table), in_hbm(buckets),
+            place, in_hbm(rising), in_hbm(stash), in_hbm(gain), in_hbm(table), in_hbm(buckets),
             in_hbm(rows_first), in_hbm(back),
         )
         run.before = qkv
@@ -467,17 +437,17 @@
         wo = back
         weights = jnp.transpose(w_qkv[0], (2, 0, 1, 3)).reshape(3, model_width, inner)
         bias = run(bias_kernel, scores_shape, (table, buckets))
-        qkv = run(
-            stash_kernel,
-            qkv_shape,
-            (rising, gain, weights),
-            scratch=[pltpu.VMEM((tokens, model_width), BF16)],
+        qkv, kept_qkv = (
+            run(
+                functools.partial(stash_kernel, 0),
+                qkv_shape,
+                (rows, gain, weights),
+                scratch=[pltpu.VMEM((tokens, model_width), BF16)],
+            )
+            for rows in (rising, stash[0, :1])
         )
     halves = (shape((half, model_width)), shape((half, model_width), F32))
     half_rows = shape((half, model_width))
-    acc_shape = shape((heads // 2, tokens, tokens), F32)
-    part_shape = shape((tokens, inner // 2))
-    stacked_shape = shape((3, tokens, inner // 2))
     row_scratch = pltpu.VMEM((tokens, model_width), BF16)
 
     def but_last_bit(term):
@@ -494,84 +464,61 @@
         )
         return but_last_bit(term)
 
-    stashed = arrivals = None
+    stashed = [kept_qkv]
     acc = ()
     for t in range(TICKS):
         final = t + 1 == TICKS
+        scratch = [pltpu.VMEM((tokens, inner), BF16)]
         if t == 0:
-            full, x_half = run(
-                first_attend_kernel,
-                (shape((tokens, inner)), half_rows),
-                (place, rising, qkv, bias),
-                scalars=1,
-            )
-            attended = (full,)
+            args = (place, rising, qkv, bias, wo)
         else:
-            low, normed, x_half = run(
-                functools.partial(forward_a_kernel, t),
-                (part_shape, shape((tokens, model_width)), half_rows),
-                (place, order, x_mine, x_other, queue, gain, weights, bias),
-                scratch=[row_scratch],
-                scalars=2,
-            )
+            x_other = swapped(x_mine, 1)
             fallen = down_term(t - 1, keep, received, g_half)
             arrivals = (up, in_last, moved(fallen, -1, 0), moved(fallen, -1, cross))
-            high = run(forward_b_kernel, part_shape, (normed, weights, bias))
-            attended = (low, high)
-        send, keep = run(
-            forward_c_kernel,
-            halves,
-            (place,) + attended + (wo,),
-            scratch=[pltpu.VMEM((tokens, inner), BF16)],
-            scalars=1,
+            args = (place, order, x_mine, x_other, queue, gain, weights, bias, wo)
+            scratch += [row_scratch]
+        up_send, up_keep, x_half = run(
+            functools.partial(forward_kernel, t),
+            halves + (half_rows,),
+            args,
+            scratch=scratch,
+            scalars=1 if t == 0 else 2,
         )
-        received = swapped(send, 1)
+        up_received = swapped(up_send, 1)
+        if t == 1:
+            stashed += run(
+                functools.partial(stash_kernel, 1),
+                (qkv_shape,) * (TICKS - 1),
+                (stash[0], gain, weights),
+                scratch=[pltpu.VMEM(((TICKS - 1) * tokens, model_width), BF16)],
+            )
         if t == 0:
-            stashed = run(
-                stash_kernel,
-                (qkv_shape,) * TICKS,
-                (stash[0], gain, weights),
-                scratch=[pltpu.VMEM((TICKS * tokens, model_width), BF16)],
-            )
+            g_parts = (falling[0],)
         else:
-            probs = run(probs_kernel, scores_shape, (stashed[t], bias))
+            g_mine = run(choose_kernel, half_rows, (place,) + arrivals, scalars=1)
+            g_parts = (g_mine, swapped(g_mine, 1))
+        probs = run(probs_kernel, scores_shape, (stashed[t], bias))
         up = but_last_bit(
-            run(up_term_kernel, half_rows, (place, keep, received, x_half), scalars=1)
+            run(up_term_kernel, half_rows, (place, up_keep, up_received, x_half), scalars=1)
         )
         if final:
             climbed = (up, swapped(up, cross))
         else:
             climbed = (moved(up, 1, 0), moved(up, 1, cross))
             in_last = swapped_in_last(up, cross)
-        if t == 0:
-            probs = run(probs_kernel, scores_shape, (stashed[t], bias))
-            g_parts = (falling[0],)
-        else:
-            g_mine = run(choose_kernel, half_rows, (place,) + arrivals, scalars=1)
-            g_parts = (g_mine, swapped(g_mine, 1))
-
-        stacked_low, acc_low, g_full, g_half = run(
-            functools.partial(backward_a_kernel, t == 0),
-            (stacked_shape, acc_shape, shape((tokens, model_width)), half_rows),
-            (place,) + g_parts + (stashed[t], probs, wo) + acc[:1],
+
+        send, keep, acc_next, g_half = run(
+            functools.partial(backward_kernel, t == 0),
+            halves + (scores_shape, half_rows),
+            (place,) + g_parts + (stashed[t], probs, weights, wo) + acc,
+            scratch=[pltpu.VMEM((3, tokens, inner), BF16), row_scratch],
             scalars=1,
         )
-        stacked_high, acc_high = run(
-            functools.partial(backward_b_kernel, t == 0),
-            (stacked_shape, acc_shape),
-            (g_full, stashed[t], probs, wo) + acc[1:],
-        )
-        acc = (acc_low, acc_high)
+        acc = (acc_next,)
+        received = swapped(send, 1)
         x_mine = run(pair_kernel, half_rows, climbed)
-        x_other = swapped(x_mine, 1)
-        send, keep = run(
-            backward_c_kernel,
-            halves,
-            (place, stacked_low, stacked_high, weights),
-            scalars=1,
-        )
-        received = swapped(send, 1)
-
+
+    x_other = swapped(x_mine, 1)
     rows = shape((1, tokens, model_width))
     table_grad = run(
         functools.partial(table_kernel, bias_table.shape[1]),

time: 126 us -> 111 us (0.88)
  waiting for transfers between devices: 18.2 us -> 8.6 us
  Pallas kernels: 75.7 us -> 67.6 us
  starting transfers between devices: 28.4 us -> 31.3 us
    ppermute x8, waiting for transfers between devices: 12.9 us -> 3.14 us  [moved(): return lax.ppermute(block, ('section', 'head'), route)]
    pallas_call x36 -> x25, Pallas kernels: 61.2 us -> 54.7 us  [__call__(): pl.pallas_call(body, out_shape=outs, in_specs=[SCALARS] * scalars + [WHOL...]
    ppermute x8, starting transfers between devices: 21.4 us -> 24.4 us  [moved(): return lax.ppermute(block, ('section', 'head'), route)]
    pallas_call x1, Pallas kernels: 14.5 us -> 12.9 us  [per_device(): pl.pallas_call(relayout_kernel, grid=(3, blocks), out_shape=(pltpu.VMEM((...]
  transfers between devices with their start and end apart: 24 -> 24, of which waited for: 7 -> 6; matrix products, arithmetic and copies ran while one was open for 0% -> 0% of each run, Pallas kernels for 32% -> 46%
where the time goes in v4:
time: 111 us; the launch traced here: 110 us
  Pallas kernels  67.6 us (61%)
  starting transfers between devices  31.3 us (28%)
  waiting for transfers between devices  8.6 us (8%)
  local copies, waits for them, and re-layouts  1.69 us (2%)
    pallas_call x25, Pallas kernels, __call__(): pl.pallas_call(body, out_shape=outs, in_specs=[SCALARS] * scalars + [WHOL...  54.7 us
    ppermute x8, starting transfers between devices, moved(): return lax.ppermute(block, ('section', 'head'), route)  24.4 us
    pallas_call x1, Pallas kernels, per_device(): pl.pallas_call(relayout_kernel, grid=(3, blocks), out_shape=(pltpu.VMEM((...  12.9 us
    ppermute x14, starting transfers between devices, swapped(): lax.ppermute(block, 'head', [(i, i ^ bit) for i in range(lax.axis_size('h...  5.53 us
    ppermute x14, waiting for transfers between devices, swapped(): lax.ppermute(block, 'head', [(i, i ^ bit) for i in range(lax.axis_size('h...  5.46 us
    ppermute x8, waiting for transfers between devices, moved(): return lax.ppermute(block, ('section', 'head'), route)  3.14 us
  transfers between devices with their start and end apart: 24, of which 6 were waited for; matrix products, arithmetic and copies ran while one was open for 0% of the time, Pallas kernels for 46%

profile of v4, /device:TPU:0, one launch (start us, length us, event | category | flops | bytes accessed | tf_op | source)
XLA Modules:
  0.0 110.3 jit_solution(12054045895913455915)
XLA Ops:
  0.7 12.9 %shard_map.121 = (bf16[3,1024,2048]{2,1,0:T(8,128)(2,1)S(1)}, bf16[3,128,2048]{2,1,0:T(8,128)(2,1)S(1)}, bf16[3,128,2048]{2,1,0:T(8,128)(2,1)S(1)}, f32[16,128,128]{2,1,0:T(8,128)S(1)}, bf16[2048,1024]{1,0:T(8,128)(2,1)S(1)}) custom-call(s32[4]{0:T(128)S(1)} %pad_add_fusion.place_ref.refs_0_, bf16[1,128,1024]{2,1,0:T(8,128)(2,1)} %refs_1_.5, ...), custom_call_target="tpu_custom_call" | custom-call | bytes 12582912 | tf_op jit(solution)/shard_map/pallas_call | solution.py:399
  13.7 2.2 %shard_map.122 = (bf16[64,1024]{1,0:T(8,128)(2,1)S(1)}, f32[64,1024]{1,0:T(8,128)S(1)}, bf16[64,1024]{1,0:T(8,128)(2,1)S(1)}) custom-call(s32[4]{0:T(128)S(1)} %pad_add_fusion.place_ref.refs_0_, bf16[1,128,1024]{2,1,0:T(8,128)(2,1)S(1)} %copy-done.2, bf16[3,128,2048]{2,1,0:T(8,128)(2,1)S(1)} %get-tuple-element.31.refs_2_.refs_5_, ...), custom_call_target="tpu_custom_call" | custom-call | bytes 128 | tf_op jit(solution)/shard_map/pallas_call | solution.py:334
  16.4 0.8 shard_map.123.refs_4_.refs_3_
  17.9 5.8 %collective-permute-start.2 = (bf16[64,1024]{1,0:T(8,128)(2,1)S(1)}, bf16[64,1024]{1,0:T(8,128)(2,1)S(1)}, u32[]{:S(2)}, u32[]{:S(2)}) collective-permute-start(bf16[64,1024]{1,0:T(8,128)(2,1)S(1)} %shard_map.124.refs_6_.refs_1_), channel_id=1, source_target_pairs={{0,6},{1,7},{2,4},{3,5},{4,10},{5,11},{6,8},{7,9},{8,14},{9,15},{1... | collective-permute-start | bytes 393224 | tf_op jit(solution)/shard_map/ppermute | solution.py:359
  23.7 3.5 %collective-permute-start.1 = (bf16[64,1024]{1,0:T(8,128)(2,1)S(1)}, bf16[64,1024]{1,0:T(8,128)(2,1)S(1)}, u32[]{:S(2)}, u32[]{:S(2)}) collective-permute-start(bf16[64,1024]{1,0:T(8,128)(2,1)S(1)} %shard_map.124.refs_6_.refs_1_), channel_id=1, source_target_pairs={{0,4},{1,5},{2,6},{3,7},{4,8},{5,9},{6,10},{7,11},{8,12},{9,13},{1... | collective-permute-start | bytes 393224 | tf_op jit(solution)/shard_map/ppermute | solution.py:359
  27.3 9.3 %shard_map.125 = (bf16[64,1024]{1,0:T(8,128)(2,1)S(1)}, f32[64,1024]{1,0:T(8,128)S(1)}, f32[16,128,128]{2,1,0:T(8,128)S(1)}, bf16[64,1024]{1,0:T(8,128)(2,1)S(1)}) custom-call(s32[4]{0:T(128)S(1)} %pad_add_fusion.place_ref.refs_0_, bf16[128,1024]{1,0:T(8,128)(2,1)S(1)} %bitcast.22, bf16[3,128,2048]{2,1,0:T(8,128)(2,1)S(1)} %get-tuple-element.37.refs_0_.refs_2_, ...), custom_call_target="tpu_custom_call" | custom-call | bytes 128 | tf_op jit(solution)/shard_map/pallas_call | solution.py:334
  38.0 0.7 shard_map.127.refs_9_
  38.7 1.3 %collective-permute-start.8 = (bf16[64,1024]{1,0:T(8,128)(2,1)S(1)}, bf16[64,1024]{1,0:T(8,128)(2,1)S(1)}, u32[]{:S(2)}, u32[]{:S(2)}) collective-permute-start(bf16[64,1024]{1,0:T(8,128)(2,1)S(1)} %shard_map.127.refs_9_), channel_id=1, source_target_pairs={{4,2},{5,3},{6,0},{7,1},{8,6},{9,7},{10,4},{11,5},{12,10},{13,11},... | collective-permute-start | bytes 393224 | tf_op jit(solution)/shard_map/ppermute | solution.py:359
  40.0 1.3 %collective-permute-start.7 = (bf16[64,1024]{1,0:T(8,128)(2,1)S(1)}, bf16[64,1024]{1,0:T(8,128)(2,1)S(1)}, u32[]{:S(2)}, u32[]{:S(2)}) collective-permute-start(bf16[64,1024]{1,0:T(8,128)(2,1)S(1)} %shard_map.127.refs_9_), channel_id=1, source_target_pairs={{4,0},{5,1},{6,2},{7,3},{8,4},{9,5},{10,6},{11,7},{12,8},{13,9},{1... | collective-permute-start | bytes 393224 | tf_op jit(solution)/shard_map/ppermute | solution.py:359
  41.4 4.2 %shard_map.128 = (bf16[64,1024]{1,0:T(8,128)(2,1)S(1)}, f32[64,1024]{1,0:T(8,128)S(1)}, bf16[64,1024]{1,0:T(8,128)(2,1)S(1)}) custom-call(s32[4]{0:T(128)S(1)} %pad_add_fusion.place_ref.refs_0_, s32[6]{0:T(128)S(1)} %copy-done.8, bf16[64,1024]{1,0:T(8,128)(2,1)S(1)} %shard_map.126.refs_6_.refs_2_, bf16[64,1024]{1,0:T(8,128)(2,1)S(1)} %collective-permute-done.3.refs_3_, ...), custom_call_target="tpu_custom_call" | custom-call | bytes 128 | tf_op jit(solution)/shard_map/pallas_call | solution.py:334
  45.8 4.2 %shard_map.129 = (bf16[3,128,2048]{2,1,0:T(8,128)(2,1)S(1)}, bf16[3,128,2048]{2,1,0:T(8,128)(2,1)S(1)}) custom-call(bf16[3,128,1024]{2,1,0:T(8,128)(2,1)S(1)} %bitcast.19, f32[1,1024]{1,0:T(1,128)S(1)} %copy-done.6, bf16[3,1024,2048]{2,1,0:T(8,128)(2,1)S(1)} %get-tuple-element.38.refs_4_.refs_6_.refs_2_.refs_5_, bf16[64,1024]{1,0:T(8,128)(2,1)S(1)} %get-tuple-element.43.refs_3_), custom_call_target="tpu_custom_call" | custom-call | bytes 128 | tf_op jit(solution)/shard_map/pallas_call | solution.py:334
  51.1 0.8 shard_map.131.refs_4_
  52.5 6.1 %collective-permute-start.10 = (bf16[64,1024]{1,0:T(8,128)(2,1)S(1)}, bf16[64,1024]{1,0:T(8,128)(2,1)S(1)}, u32[]{:S(2)}, u32[]{:S(2)}) collective-permute-start(bf16[64,1024]{1,0:T(8,128)(2,1)S(1)} %shard_map.132.refs_8_.refs_1_), channel_id=1, source_target_pairs={{0,6},{1,7},{2,4},{3,5},{4,10},{5,11},{6,8},{7,9},{8,14},{9,15},{1... | collective-permute-start | bytes 393224 | tf_op jit(solution)/shard_map/ppermute | solution.py:359
  58.6 3.9 %collective-permute-start.9 = (bf16[64,1024]{1,0:T(8,128)(2,1)S(1)}, bf16[64,1024]{1,0:T(8,128)(2,1)S(1)}, u32[]{:S(2)}, u32[]{:S(2)}) collective-permute-start(bf16[64,1024]{1,0:T(8,128)(2,1)S(1)} %shard_map.132.refs_8_.refs_1_), channel_id=1, source_target_pairs={{0,4},{1,5},{2,6},{3,7},{4,8},{5,9},{6,10},{7,11},{8,12},{9,13},{1... | collective-permute-start | bytes 393224 | tf_op jit(solution)/shard_map/ppermute | solution.py:359
  62.5 9.3 %shard_map.133 = (bf16[64,1024]{1,0:T(8,128)(2,1)S(1)}, f32[64,1024]{1,0:T(8,128)S(1)}, f32[16,128,128]{2,1,0:T(8,128)S(1)}, bf16[64,1024]{1,0:T(8,128)(2,1)S(1)}) custom-call(s32[4]{0:T(128)S(1)} %pad_add_fusion.place_ref.refs_0_, bf16[64,1024]{1,0:T(8,128)(2,1)S(1)} %shard_map.130.refs_2_.refs_1_, bf16[64,1024]{1,0:T(8,128)(2,1)S(1)} %collective-permute-done.11.refs_2_, ...), custom_call_target="tpu_custom_call" | custom-call | bytes 128 | tf_op jit(solution)/shard_map/pallas_call | solution.py:334
  73.3 0.7 shard_map.135.refs_9_
  74.0 1.3 %collective-permute-start.17 = (bf16[64,1024]{1,0:T(8,128)(2,1)S(1)}, bf16[64,1024]{1,0:T(8,128)(2,1)S(1)}, u32[]{:S(2)}, u32[]{:S(2)}) collective-permute-start(bf16[64,1024]{1,0:T(8,128)(2,1)S(1)} %shard_map.135.refs_9_), channel_id=1, source_target_pairs={{4,2},{5,3},{6,0},{7,1},{8,6},{9,7},{10,4},{11,5},{12,10},{13,11},... | collective-permute-start | bytes 393224 | tf_op jit(solution)/shard_map/ppermute | solution.py:359
  75.3 1.3 %collective-permute-start.16 = (bf16[64,1024]{1,0:T(8,128)(2,1)S(1)}, bf16[64,1024]{1,0:T(8,128)(2,1)S(1)}, u32[]{:S(2)}, u32[]{:S(2)}) collective-permute-start(bf16[64,1024]{1,0:T(8,128)(2,1)S(1)} %shard_map.135.refs_9_), channel_id=1, source_target_pairs={{4,0},{5,1},{6,2},{7,3},{8,4},{9,5},{10,6},{11,7},{12,8},{13,9},{1... | collective-permute-start | bytes 393224 | tf_op jit(solution)/shard_map/ppermute | solution.py:359
  76.6 4.3 %shard_map.136 = (bf16[64,1024]{1,0:T(8,128)(2,1)S(1)}, f32[64,1024]{1,0:T(8,128)S(1)}, bf16[64,1024]{1,0:T(8,128)(2,1)S(1)}) custom-call(s32[4]{0:T(128)S(1)} %pad_add_fusion.place_ref.refs_0_, s32[6]{0:T(128)S(1)} %copy-done.8, bf16[64,1024]{1,0:T(8,128)(2,1)S(1)} %shard_map.134.refs_6_.refs_2_, bf16[64,1024]{1,0:T(8,128)(2,1)S(1)} %collective-permute-done.12.refs_3_, ...), custom_call_target="tpu_custom_call" | custom-call | bytes 128 | tf_op jit(solution)/shard_map/pallas_call | solution.py:334
  81.1 2.0 %collective-permute-done.17.refs_4_ = bf16[64,1024]{1,0:T(8,128)(2,1)S(1)} collective-permute-done((bf16[64,1024]{1,0:T(8,128)(2,1)S(1)}, bf16[64,1024]{1,0:T(8,128)(2,1)S(1)}, u32[]{:S(2)}, u32[]{:S(2)}) %collective-permute-start.17) | collective-permute-done | bytes 131104 | tf_op jit(solution)/shard_map/ppermute | solution.py:359
  83.1 1.1 collective-permute-done.16.refs_3_
  84.9 0.8 shard_map.138.refs_4_
  86.3 1.6 %collective-permute-start.18 = (bf16[64,1024]{1,0:T(8,128)(2,1)S(1)}, bf16[64,1024]{1,0:T(8,128)(2,1)S(1)}, u32[]{:S(2)}, u32[]{:S(2)}) collective-permute-start(bf16[64,1024]{1,0:T(8,128)(2,1)S(1)} %shard_map.139.refs_8_.refs_0_), channel_id=1, source_target_pairs={{0,2},{1,3},{2,0},{3,1},{4,6},{5,7},{6,4},{7,5},{8,10},{9,11},{10,... | collective-permute-start | bytes 393224 | tf_op jit(solution)/shard_map/ppermute | solution.py:363
  87.8 9.3 %shard_map.140 = (bf16[64,1024]{1,0:T(8,128)(2,1)S(1)}, f32[64,1024]{1,0:T(8,128)S(1)}, f32[16,128,128]{2,1,0:T(8,128)S(1)}, bf16[64,1024]{1,0:T(8,128)(2,1)S(1)}) custom-call(s32[4]{0:T(128)S(1)} %pad_add_fusion.place_ref.refs_0_, bf16[64,1024]{1,0:T(8,128)(2,1)S(1)} %shard_map.137.refs_2_.refs_1_, bf16[64,1024]{1,0:T(8,128)(2,1)S(1)} %collective-permute-done.19.refs_2_, ...), custom_call_target="tpu_custom_call" | custom-call | bytes 128 | tf_op jit(solution)/shard_map/pallas_call | solution.py:334
  97.9 1.7 %shard_map.142.refs_6_ = f32[16,32]{1,0:T(8,128)} custom-call(f32[16,128,128]{2,1,0:T(8,128)S(1)} %get-tuple-element.58.refs_0_, s32[128,128]{1,0:T(8,128)S(1)} %copy-done.5, bf16[64,1024]{1,0:T(8,128)(2,1)S(1)} %shard_map.141.refs_2_.refs_1_), custom_call_target="tpu_custom_call" | custom-call | bytes 128 | tf_op jit(solution)/shard_map/pallas_call | solution.py:334
  99.5 0.7 copy-done.7
  100.2 0.7 shard_map.143.refs_3_.refs_0_
  101.5 1.3 %shard_map.144.refs_2_ = bf16[1,128,1024]{2,1,0:T(8,128)(2,1)} custom-call(s32[4]{0:T(128)S(1)} %pad_add_fusion.place_ref.refs_0_, bf16[64,1024]{1,0:T(8,128)(2,1)S(1)} %shard_map.141.refs_2_.refs_1_, bf16[64,1024]{1,0:T(8,128)(2,1)S(1)} %collective-permute-done.20.refs_2_, bf16[64,1024]{1,0:T(8,128)(2,1)S(1)} %shard_map.143.refs_3_.refs_0_), custom_call_target="tpu_custom_call" | custom-call | bytes 128 | tf_op jit(solution)/shard_map/pallas_call | solution.py:334
  102.8 3.8 %collective-permute-done.22.refs_1_ = bf16[64,1024]{1,0:T(8,128)(2,1)S(1)} collective-permute-done((bf16[64,1024]{1,0:T(8,128)(2,1)S(1)}, bf16[64,1024]{1,0:T(8,128)(2,1)S(1)}, u32[]{:S(2)}, u32[]{:S(2)}) %collective-permute-start.22) | collective-permute-done | bytes 131104 | tf_op jit(solution)/shard_map/ppermute | solution.py:363
  106.6 0.9 copy-done.3
  107.7 1.3 %collective-permute-done.23.refs_2_ = bf16[64,1024]{1,0:T(8,128)(2,1)S(1)} collective-permute-done((bf16[64,1024]{1,0:T(8,128)(2,1)S(1)}, bf16[64,1024]{1,0:T(8,128)(2,1)S(1)}, u32[]{:S(2)}, u32[]{:S(2)}) %collective-permute-start.23) | collective-permute-done | bytes 131104 | tf_op jit(solution)/shard_map/ppermute | solution.py:363
  109.0 1.3 %shard_map.146 = bf16[1,128,1024]{2,1,0:T(8,128)(2,1)} custom-call(s32[4]{0:T(128)S(1)} %pad_add_fusion.place_ref.refs_0_, bf16[64,1024]{1,0:T(8,128)(2,1)S(1)} %shard_map.145.refs_1_.refs_3_, bf16[64,1024]{1,0:T(8,128)(2,1)S(1)} %collective-permute-done.23.refs_2_, bf16[64,1024]{1,0:T(8,128)(2,1)S(1)} %shard_map.145.refs_1_.refs_3_), custom_call_target="tpu_custom_call" | custom-call | bytes 128 | tf_op jit(solution)/shard_map/pallas_call | solution.py:334
  (61 shorter events, 8.8 us)
Async XLA Ops:
  0.7 12.9 %copy-start.2 = (bf16[1,128,1024]{2,1,0:T(8,128)(2,1)S(1)}, bf16[1,128,1024]{2,1,0:T(8,128)(2,1)}, u32[]{:S(2)}) copy-start(bf16[1,128,1024]{2,1,0:T(8,128)(2,1)} %refs_1_.5) | copy-start | bytes 786436
  15.9 1.5 %collective-permute-start = (bf16[64,1024]{1,0:T(8,128)(2,1)S(1)}, bf16[64,1024]{1,0:T(8,128)(2,1)S(1)}, u32[]{:S(2)}, u32[]{:S(2)}) collective-permute-start(bf16[64,1024]{1,0:T(8,128)(2,1)S(1)} %get-tuple-element.35.refs_2_), channel_id=1, source_target_pairs={{0,1},{1,0},{2,3},{3,2},{4,5},{5,4},{6,7},{7,6},{8,9},{9,8},{10,11... | collective-permute-start | bytes 393224 | tf_op jit(solution)/shard_map/ppermute | solution.py:363
  17.2 10.1 %copy-start.4 = (bf16[1,128,1024]{2,1,0:T(8,128)(2,1)S(1)}, bf16[1,128,1024]{2,1,0:T(8,128)(2,1)}, u32[]{:S(2)}) copy-start(bf16[1,128,1024]{2,1,0:T(8,128)(2,1)} %param.11) | copy-start | bytes 786436
  17.9 18.7 %collective-permute-start.2 = (bf16[64,1024]{1,0:T(8,128)(2,1)S(1)}, bf16[64,1024]{1,0:T(8,128)(2,1)S(1)}, u32[]{:S(2)}, u32[]{:S(2)}) collective-permute-start(bf16[64,1024]{1,0:T(8,128)(2,1)S(1)} %shard_map.124.refs_6_.refs_1_), channel_id=1, source_target_pairs={{0,6},{1,7},{2,4},{3,5},{4,10},{5,11},{6,8},{7,9},{8,14},{9,15},{1... | collective-permute-start | bytes 393224 | tf_op jit(solution)/shard_map/ppermute | solution.py:359
  23.7 13.0 %collective-permute-start.1 = (bf16[64,1024]{1,0:T(8,128)(2,1)S(1)}, bf16[64,1024]{1,0:T(8,128)(2,1)S(1)}, u32[]{:S(2)}, u32[]{:S(2)}) collective-permute-start(bf16[64,1024]{1,0:T(8,128)(2,1)S(1)} %shard_map.124.refs_6_.refs_1_), channel_id=1, source_target_pairs={{0,4},{1,5},{2,6},{3,7},{4,8},{5,9},{6,10},{7,11},{8,12},{9,13},{1... | collective-permute-start | bytes 393224 | tf_op jit(solution)/shard_map/ppermute | solution.py:359
  27.2 10.8 %copy-start = (bf16[1,3,128,1024]{3,2,1,0:T(8,128)(2,1)S(1)}, bf16[1,3,128,1024]{3,2,1,0:T(8,128)(2,1)}, u32[]{:S(2)}) copy-start(bf16[1,3,128,1024]{3,2,1,0:T(8,128)(2,1)} %kept_ref.1) | copy-start | bytes 2359300
  27.2 10.8 %copy-start.6 = (f32[1,1024]{1,0:T(1,128)S(1)}, f32[1,1024]{1,0:T(1,128)}, u32[]{:S(2)}) copy-start(f32[1,1024]{1,0:T(1,128)} %refs_2_.5) | copy-start | bytes 12292
  36.6 4.8 %copy-start.1 = (bf16[6,128,1024]{2,1,0:T(8,128)(2,1)S(1)}, bf16[6,128,1024]{2,1,0:T(8,128)(2,1)}, u32[]{:S(2)}) copy-start(bf16[6,128,1024]{2,1,0:T(8,128)(2,1)} %refs_4_.3) | copy-start | bytes 4718596
  36.6 4.8 %copy-start.8 = (s32[6]{0:T(128)S(1)}, s32[6]{0:T(128)}, u32[]{:S(2)}) copy-start(s32[6]{0:T(128)} %refs_1_.8) | copy-start | bytes 76
  36.6 1.4 %collective-permute-start.4 = (bf16[64,1024]{1,0:T(8,128)(2,1)S(1)}, bf16[64,1024]{1,0:T(8,128)(2,1)S(1)}, u32[]{:S(2)}, u32[]{:S(2)}) collective-permute-start(bf16[64,1024]{1,0:T(8,128)(2,1)S(1)} %get-tuple-element.39.refs_2_), channel_id=1, source_target_pairs={{0,1},{1,0},{2,3},{3,2},{4,5},{5,4},{6,7},{7,6},{8,9},{9,8},{10,11... | collective-permute-start | bytes 393224 | tf_op jit(solution)/shard_map/ppermute | solution.py:363
  36.7 4.6 %collective-permute-start.3 = (bf16[64,1024]{1,0:T(8,128)(2,1)S(1)}, bf16[64,1024]{1,0:T(8,128)(2,1)S(1)}, u32[]{:S(2)}, u32[]{:S(2)}) collective-permute-start(bf16[64,1024]{1,0:T(8,128)(2,1)S(1)} %shard_map.126.refs_6_.refs_2_), channel_id=1, source_target_pairs={{0,1},{1,0},{2,3},{3,2},{4,5},{5,4},{6,7},{7,6},{8,9},{9,8},{10,11... | collective-permute-start | bytes 393224 | tf_op jit(solution)/shard_map/ppermute | solution.py:363
  37.3 12.7 %collective-permute-start.6 = (bf16[64,1024]{1,0:T(8,128)(2,1)S(1)}, bf16[64,1024]{1,0:T(8,128)(2,1)S(1)}, u32[]{:S(2)}, u32[]{:S(2)}) collective-permute-start(bf16[64,1024]{1,0:T(8,128)(2,1)S(1)} %shard_map.124.refs_6_.refs_1_), channel_id=1, source_target_pairs={{12,14},{13,15},{14,12},{15,13},{28,30},{29,31},{30,28},{31,29}} | collective-permute-start | bytes 393224 | tf_op jit(solution)/shard_map/ppermute | solution.py:369
  38.7 11.3 %collective-permute-start.8 = (bf16[64,1024]{1,0:T(8,128)(2,1)S(1)}, bf16[64,1024]{1,0:T(8,128)(2,1)S(1)}, u32[]{:S(2)}, u32[]{:S(2)}) collective-permute-start(bf16[64,1024]{1,0:T(8,128)(2,1)S(1)} %shard_map.127.refs_9_), channel_id=1, source_target_pairs={{4,2},{5,3},{6,0},{7,1},{8,6},{9,7},{10,4},{11,5},{12,10},{13,11},... | collective-permute-start | bytes 393224 | tf_op jit(solution)/shard_map/ppermute | solution.py:359
  40.0 10.0 %collective-permute-start.7 = (bf16[64,1024]{1,0:T(8,128)(2,1)S(1)}, bf16[64,1024]{1,0:T(8,128)(2,1)S(1)}, u32[]{:S(2)}, u32[]{:S(2)}) collective-permute-start(bf16[64,1024]{1,0:T(8,128)(2,1)S(1)} %shard_map.127.refs_9_), channel_id=1, source_target_pairs={{4,0},{5,1},{6,2},{7,3},{8,4},{9,5},{10,6},{11,7},{12,8},{13,9},{1... | collective-permute-start | bytes 393224 | tf_op jit(solution)/shard_map/ppermute | solution.py:359
  45.6 6.3 %collective-permute-start.5 = (bf16[64,1024]{1,0:T(8,128)(2,1)S(1)}, bf16[64,1024]{1,0:T(8,128)(2,1)S(1)}, u32[]{:S(2)}, u32[]{:S(2)}) collective-permute-start(bf16[64,1024]{1,0:T(8,128)(2,1)S(1)} %get-tuple-element.43.refs_3_), channel_id=1, source_target_pairs={{0,1},{1,0},{2,3},{3,2},{4,5},{5,4},{6,7},{7,6},{8,9},{9,8},{10,11... | collective-permute-start | bytes 393224 | tf_op jit(solution)/shard_map/ppermute | solution.py:363
  50.7 11.9 %collective-permute-start.11 = (bf16[64,1024]{1,0:T(8,128)(2,1)S(1)}, bf16[64,1024]{1,0:T(8,128)(2,1)S(1)}, u32[]{:S(2)}, u32[]{:S(2)}) collective-permute-start(bf16[64,1024]{1,0:T(8,128)(2,1)S(1)} %shard_map.130.refs_2_.refs_1_), channel_id=1, source_target_pairs={{0,1},{1,0},{2,3},{3,2},{4,5},{5,4},{6,7},{7,6},{8,9},{9,8},{10,11... | collective-permute-start | bytes 393224 | tf_op jit(solution)/shard_map/ppermute | solution.py:363
  52.5 20.1 %collective-permute-start.10 = (bf16[64,1024]{1,0:T(8,128)(2,1)S(1)}, bf16[64,1024]{1,0:T(8,128)(2,1)S(1)}, u32[]{:S(2)}, u32[]{:S(2)}) collective-permute-start(bf16[64,1024]{1,0:T(8,128)(2,1)S(1)} %shard_map.132.refs_8_.refs_1_), channel_id=1, source_target_pairs={{0,6},{1,7},{2,4},{3,5},{4,10},{5,11},{6,8},{7,9},{8,14},{9,15},{1... | collective-permute-start | bytes 393224 | tf_op jit(solution)/shard_map/ppermute | solution.py:359
  58.6 14.0 %collective-permute-start.9 = (bf16[64,1024]{1,0:T(8,128)(2,1)S(1)}, bf16[64,1024]{1,0:T(8,128)(2,1)S(1)}, u32[]{:S(2)}, u32[]{:S(2)}) collective-permute-start(bf16[64,1024]{1,0:T(8,128)(2,1)S(1)} %shard_map.132.refs_8_.refs_1_), channel_id=1, source_target_pairs={{0,4},{1,5},{2,6},{3,7},{4,8},{5,9},{6,10},{7,11},{8,12},{9,13},{1... | collective-permute-start | bytes 393224 | tf_op jit(solution)/shard_map/ppermute | solution.py:359
  71.8 1.4 %collective-permute-start.13 = (bf16[64,1024]{1,0:T(8,128)(2,1)S(1)}, bf16[64,1024]{1,0:T(8,128)(2,1)S(1)}, u32[]{:S(2)}, u32[]{:S(2)}) collective-permute-start(bf16[64,1024]{1,0:T(8,128)(2,1)S(1)} %get-tuple-element.47.refs_2_), channel_id=1, source_target_pairs={{0,1},{1,0},{2,3},{3,2},{4,5},{5,4},{6,7},{7,6},{8,9},{9,8},{10,11... | collective-permute-start | bytes 393224 | tf_op jit(solution)/shard_map/ppermute | solution.py:363
  71.9 9.1 %collective-permute-start.15 = (bf16[64,1024]{1,0:T(8,128)(2,1)S(1)}, bf16[64,1024]{1,0:T(8,128)(2,1)S(1)}, u32[]{:S(2)}, u32[]{:S(2)}) collective-permute-start(bf16[64,1024]{1,0:T(8,128)(2,1)S(1)} %shard_map.132.refs_8_.refs_1_), channel_id=1, source_target_pairs={{12,14},{13,15},{14,12},{15,13},{28,30},{29,31},{30,28},{31,29}} | collective-permute-start | bytes 393224 | tf_op jit(solution)/shard_map/ppermute | solution.py:369
  72.7 3.9 %collective-permute-start.12 = (bf16[64,1024]{1,0:T(8,128)(2,1)S(1)}, bf16[64,1024]{1,0:T(8,128)(2,1)S(1)}, u32[]{:S(2)}, u32[]{:S(2)}) collective-permute-start(bf16[64,1024]{1,0:T(8,128)(2,1)S(1)} %shard_map.134.refs_6_.refs_2_), channel_id=1, source_target_pairs={{0,1},{1,0},{2,3},{3,2},{4,5},{5,4},{6,7},{7,6},{8,9},{9,8},{10,11... | collective-permute-start | bytes 393224 | tf_op jit(solution)/shard_map/ppermute | solution.py:363
  74.0 9.1 %collective-permute-start.17 = (bf16[64,1024]{1,0:T(8,128)(2,1)S(1)}, bf16[64,1024]{1,0:T(8,128)(2,1)S(1)}, u32[]{:S(2)}, u32[]{:S(2)}) collective-permute-start(bf16[64,1024]{1,0:T(8,128)(2,1)S(1)} %shard_map.135.refs_9_), channel_id=1, source_target_pairs={{4,2},{5,3},{6,0},{7,1},{8,6},{9,7},{10,4},{11,5},{12,10},{13,11},... | collective-permute-start | bytes 393224 | tf_op jit(solution)/shard_map/ppermute | solution.py:359
  75.3 8.9 %collective-permute-start.16 = (bf16[64,1024]{1,0:T(8,128)(2,1)S(1)}, bf16[64,1024]{1,0:T(8,128)(2,1)S(1)}, u32[]{:S(2)}, u32[]{:S(2)}) collective-permute-start(bf16[64,1024]{1,0:T(8,128)(2,1)S(1)} %shard_map.135.refs_9_), channel_id=1, source_target_pairs={{4,0},{5,1},{6,2},{7,3},{8,4},{9,5},{10,6},{11,7},{12,8},{13,9},{1... | collective-permute-start | bytes 393224 | tf_op jit(solution)/shard_map/ppermute | solution.py:359
  80.8 4.8 %collective-permute-start.14 = (bf16[64,1024]{1,0:T(8,128)(2,1)S(1)}, bf16[64,1024]{1,0:T(8,128)(2,1)S(1)}, u32[]{:S(2)}, u32[]{:S(2)}) collective-permute-start(bf16[64,1024]{1,0:T(8,128)(2,1)S(1)} %get-tuple-element.51.refs_5_), channel_id=1, source_target_pairs={{0,1},{1,0},{2,3},{3,2},{4,5},{5,4},{6,7},{7,6},{8,9},{9,8},{10,11... | collective-permute-start | bytes 393224 | tf_op jit(solution)/shard_map/ppermute | solution.py:363
  84.8 3.1 %collective-permute-start.19 = (bf16[64,1024]{1,0:T(8,128)(2,1)S(1)}, bf16[64,1024]{1,0:T(8,128)(2,1)S(1)}, u32[]{:S(2)}, u32[]{:S(2)}) collective-permute-start(bf16[64,1024]{1,0:T(8,128)(2,1)S(1)} %shard_map.137.refs_2_.refs_1_), channel_id=1, source_target_pairs={{0,1},{1,0},{2,3},{3,2},{4,5},{5,4},{6,7},{7,6},{8,9},{9,8},{10,11... | collective-permute-start | bytes 393224 | tf_op jit(solution)/shard_map/ppermute | solution.py:363
  86.3 11.2 %collective-permute-start.18 = (bf16[64,1024]{1,0:T(8,128)(2,1)S(1)}, bf16[64,1024]{1,0:T(8,128)(2,1)S(1)}, u32[]{:S(2)}, u32[]{:S(2)}) collective-permute-start(bf16[64,1024]{1,0:T(8,128)(2,1)S(1)} %shard_map.139.refs_8_.refs_0_), channel_id=1, source_target_pairs={{0,2},{1,3},{2,0},{3,1},{4,6},{5,7},{6,4},{7,5},{8,10},{9,11},{10,... | collective-permute-start | bytes 393224 | tf_op jit(solution)/shard_map/ppermute | solution.py:363
  87.8 10.0 %copy-start.5 = (s32[128,128]{1,0:T(8,128)S(1)}, s32[128,128]{1,0:T(8,128)}, u32[]{:S(2)}) copy-start(s32[128,128]{1,0:T(8,128)} %refs_1_.9) | copy-start | bytes 196612
  97.2 2.3 %collective-permute-start.21 = (bf16[64,1024]{1,0:T(8,128)(2,1)S(1)}, bf16[64,1024]{1,0:T(8,128)(2,1)S(1)}, u32[]{:S(2)}, u32[]{:S(2)}) collective-permute-start(bf16[64,1024]{1,0:T(8,128)(2,1)S(1)} %get-tuple-element.55.refs_2_), channel_id=1, source_target_pairs={{0,1},{1,0},{2,3},{3,2},{4,5},{5,4},{6,7},{7,6},{8,9},{9,8},{10,11... | collective-permute-start | bytes 393224 | tf_op jit(solution)/shard_map/ppermute | solution.py:363
  97.5 4.0 %collective-permute-start.20 = (bf16[64,1024]{1,0:T(8,128)(2,1)S(1)}, bf16[64,1024]{1,0:T(8,128)(2,1)S(1)}, u32[]{:S(2)}, u32[]{:S(2)}) collective-permute-start(bf16[64,1024]{1,0:T(8,128)(2,1)S(1)} %shard_map.141.refs_2_.refs_1_), channel_id=1, source_target_pairs={{0,1},{1,0},{2,3},{3,2},{4,5},{5,4},{6,7},{7,6},{8,9},{9,8},{10,11... | collective-permute-start | bytes 393224 | tf_op jit(solution)/shard_map/ppermute | solution.py:363
  100.9 5.7 %collective-permute-start.22 = (bf16[64,1024]{1,0:T(8,128)(2,1)S(1)}, bf16[64,1024]{1,0:T(8,128)(2,1)S(1)}, u32[]{:S(2)}, u32[]{:S(2)}) collective-permute-start(bf16[64,1024]{1,0:T(8,128)(2,1)S(1)} %shard_map.143.refs_3_.refs_0_), channel_id=1, source_target_pairs={{0,2},{1,3},{2,0},{3,1},{4,6},{5,7},{6,4},{7,5},{8,10},{9,11},{10,... | collective-permute-start | bytes 393224 | tf_op jit(solution)/shard_map/ppermute | solution.py:363
  106.6 1.0 copy-start.3
  107.6 1.4 %collective-permute-start.23 = (bf16[64,1024]{1,0:T(8,128)(2,1)S(1)}, bf16[64,1024]{1,0:T(8,128)(2,1)S(1)}, u32[]{:S(2)}, u32[]{:S(2)}) collective-permute-start(bf16[64,1024]{1,0:T(8,128)(2,1)S(1)} %shard_map.145.refs_1_.refs_3_), channel_id=1, source_target_pairs={{0,1},{1,0},{2,3},{3,2},{4,5},{5,4},{6,7},{7,6},{8,9},{9,8},{10,11... | collective-permute-start | bytes 393224 | tf_op jit(solution)/shard_map/ppermute | solution.py:363
  (1 other events, 0.7 us)

commit v5 on v4

--- a/solution.py
+++ b/solution.py
@@ -351,9 +351,8 @@
 def moved(block, step, bit):
     sections, heads = lax.axis_size("section"), lax.axis_size("head")
     route = [
-        (s * heads + h, (s + step) * heads + (h ^ bit))
+        (s * heads + h, (s + step) % sections * heads + (h ^ bit))
         for s in range(sections)
-        if s + step in range(sections)
         for h in range(heads)
     ]
     return lax.ppermute(block, ("section", "head"), route)
@@ -361,14 +360,6 @@
 
 def swapped(block, bit):
     return lax.ppermute(block, "head", [(i, i ^ bit) for i in range(lax.axis_size("head"))])
-
-
-def swapped_in_last(block, bit):
-    sections, heads = lax.axis_size("section"), lax.axis_size("head")
-    base = (sections - 1) * heads
-    return lax.ppermute(
-        block, ("section", "head"), [(base + h, base + (h ^ bit)) for h in range(heads)]
-    )
 
 
 def per_device(rising, falling, stash, queue, order, buckets, bias_table, gain, w_qkv, w_out):
@@ -505,7 +496,7 @@
             climbed = (up, swapped(up, cross))
         else:
             climbed = (moved(up, 1, 0), moved(up, 1, cross))
-            in_last = swapped_in_last(up, cross)
+            in_last = swapped(up, cross)
 
         send, keep, acc_next, g_half = run(
             functools.partial(backward_kernel, t == 0),
@@ -520,14 +511,14 @@
 
     x_other = swapped(x_mine, 1)
     rows = shape((1, tokens, model_width))
+    fallen = down_term(TICKS - 1, keep, received, g_half)
+    fallen_other = swapped(fallen, cross)
+    rising_out = run(join_kernel, rows, (place, x_mine, x_other), scalars=1)
     table_grad = run(
         functools.partial(table_kernel, bias_table.shape[1]),
         shape((heads, bias_table.shape[1]), F32),
         acc + (buckets,),
     )
-    fallen = down_term(TICKS - 1, keep, received, g_half)
-    fallen_other = swapped(fallen, cross)
-    rising_out = run(join_kernel, rows, (place, x_mine, x_other), scalars=1)
     lowered = run(pair_kernel, half_rows, (fallen, fallen_other))
     falling_out = run(join_kernel, rows, (place, lowered, swapped(lowered, 1)), scalars=1)
     return (rising_out, falling_out, table_grad.T[None])

time: 111 us -> 97.5 us (0.88)
  starting transfers between devices: 31.3 us -> 22.5 us
  waiting for transfers between devices: 8.6 us -> 4.49 us
    ppermute x8, starting transfers between devices: 24.4 us -> 15.5 us  [moved(): return lax.ppermute(block, ('section', 'head'), route)]
    ppermute x8, waiting for transfers between devices: 3.14 us -> 1.08 us  [moved(): return lax.ppermute(block, ('section', 'head'), route)]
    ppermute x14 -> x16, waiting for transfers between devices: 5.46 us -> 3.41 us  [swapped(): lax.ppermute(block, 'head', [(i, i ^ bit) for i in range(lax.axis_size('h...]
    ppermute x14 -> x16, starting transfers between devices: 5.53 us -> 6.99 us  [swapped(): lax.ppermute(block, 'head', [(i, i ^ bit) for i in range(lax.axis_size('h...]
    ppermute x2 -> x0, starting transfers between devices: 1.33 us -> none  [swapped_in_last(): lax.ppermute(block, ('section', 'head'), [(base + h, base + (h ^ bit)) fo...]
  transfers between devices with their start and end apart: 24 -> 24, of which waited for: 6 -> 6; matrix products, arithmetic and copies ran while one was open for 0% -> 0% of each run, Pallas kernels for 46% -> 52%
where the time goes in v5:
time: 97.5 us; the launch traced here: 97.3 us
  Pallas kernels  67.6 us (69%)
  starting transfers between devices  22.5 us (23%)
  waiting for transfers between devices  4.49 us (5%)
  local copies, waits for them, and re-layouts  1.68 us (2%)
    pallas_call x25, Pallas kernels, __call__(): pl.pallas_call(body, out_shape=outs, in_specs=[SCALARS] * scalars + [WHOL...  54.7 us
    ppermute x8, starting transfers between devices, moved(): return lax.ppermute(block, ('section', 'head'), route)  15.5 us
    pallas_call x1, Pallas kernels, per_device(): pl.pallas_call(relayout_kernel, grid=(3, blocks), out_shape=(pltpu.VMEM((...  12.9 us
    ppermute x16, starting transfers between devices, swapped(): lax.ppermute(block, 'head', [(i, i ^ bit) for i in range(lax.axis_size('h...  6.99 us
    ppermute x16, waiting for transfers between devices, swapped(): lax.ppermute(block, 'head', [(i, i ^ bit) for i in range(lax.axis_size('h...  3.41 us
  transfers between devices with their start and end apart: 24, of which 6 were waited for; matrix products, arithmetic and copies ran while one was open for 0% of the time, Pallas kernels for 52%

profile of v5, /device:TPU:0, one launch (start us, length us, event | category | flops | bytes accessed | tf_op | source)
XLA Modules:
  0.0 97.3 jit_solution(16815058242693505707)
XLA Ops:
  0.7 12.9 %shard_map.121 = (bf16[3,1024,2048]{2,1,0:T(8,128)(2,1)S(1)}, bf16[3,128,2048]{2,1,0:T(8,128)(2,1)S(1)}, bf16[3,128,2048]{2,1,0:T(8,128)(2,1)S(1)}, f32[16,128,128]{2,1,0:T(8,128)S(1)}, bf16[2048,1024]{1,0:T(8,128)(2,1)S(1)}) custom-call(s32[4]{0:T(128)S(1)} %pad_add_fusion.place_ref.refs_0_, bf16[1,128,1024]{2,1,0:T(8,128)(2,1)} %refs_1_.5, ...), custom_call_target="tpu_custom_call" | custom-call | bytes 12582912 | tf_op jit(solution)/shard_map/pallas_call | solution.py:390
  13.7 2.2 %shard_map.122 = (bf16[64,1024]{1,0:T(8,128)(2,1)S(1)}, f32[64,1024]{1,0:T(8,128)S(1)}, bf16[64,1024]{1,0:T(8,128)(2,1)S(1)}) custom-call(s32[4]{0:T(128)S(1)} %pad_add_fusion.place_ref.refs_0_, bf16[1,128,1024]{2,1,0:T(8,128)(2,1)S(1)} %copy-done.2, bf16[3,128,2048]{2,1,0:T(8,128)(2,1)S(1)} %get-tuple-element.31.refs_2_.refs_5_, ...), custom_call_target="tpu_custom_call" | custom-call | bytes 128 | tf_op jit(solution)/shard_map/pallas_call | solution.py:334
  16.4 0.8 shard_map.123.refs_4_.refs_3_
  17.9 3.9 %collective-permute-start.2 = (bf16[64,1024]{1,0:T(8,128)(2,1)S(1)}, bf16[64,1024]{1,0:T(8,128)(2,1)S(1)}, u32[]{:S(2)}, u32[]{:S(2)}) collective-permute-start(bf16[64,1024]{1,0:T(8,128)(2,1)S(1)} %shard_map.124.refs_6_.refs_1_), channel_id=1, source_target_pairs={{0,6},{1,7},{2,4},{3,5},{4,10},{5,11},{6,8},{7,9},{8,14},{9,15},{1... | collective-permute-start | bytes 393224 | tf_op jit(solution)/shard_map/ppermute | solution.py:358
  21.9 1.6 %collective-permute-start.1 = (bf16[64,1024]{1,0:T(8,128)(2,1)S(1)}, bf16[64,1024]{1,0:T(8,128)(2,1)S(1)}, u32[]{:S(2)}, u32[]{:S(2)}) collective-permute-start(bf16[64,1024]{1,0:T(8,128)(2,1)S(1)} %shard_map.124.refs_6_.refs_1_), channel_id=1, source_target_pairs={{0,4},{1,5},{2,6},{3,7},{4,8},{5,9},{6,10},{7,11},{8,12},{9,13},{1... | collective-permute-start | bytes 393224 | tf_op jit(solution)/shard_map/ppermute | solution.py:358
  23.4 9.3 %shard_map.125 = (bf16[64,1024]{1,0:T(8,128)(2,1)S(1)}, f32[64,1024]{1,0:T(8,128)S(1)}, f32[16,128,128]{2,1,0:T(8,128)S(1)}, bf16[64,1024]{1,0:T(8,128)(2,1)S(1)}) custom-call(s32[4]{0:T(128)S(1)} %pad_add_fusion.place_ref.refs_0_, bf16[128,1024]{1,0:T(8,128)(2,1)S(1)} %bitcast.22, bf16[3,128,2048]{2,1,0:T(8,128)(2,1)S(1)} %get-tuple-element.37.refs_0_.refs_2_, ...), custom_call_target="tpu_custom_call" | custom-call | bytes 128 | tf_op jit(solution)/shard_map/pallas_call | solution.py:334
  34.2 0.7 shard_map.127.refs_9_
  34.9 3.1 %collective-permute-start.8 = (bf16[64,1024]{1,0:T(8,128)(2,1)S(1)}, bf16[64,1024]{1,0:T(8,128)(2,1)S(1)}, u32[]{:S(2)}, u32[]{:S(2)}) collective-permute-start(bf16[64,1024]{1,0:T(8,128)(2,1)S(1)} %shard_map.127.refs_9_), channel_id=1, source_target_pairs={{0,14},{1,15},{2,12},{3,13},{4,2},{5,3},{6,0},{7,1},{8,6},{9,7},{1... | collective-permute-start | bytes 393224 | tf_op jit(solution)/shard_map/ppermute | solution.py:358
  38.4 4.2 %shard_map.128 = (bf16[64,1024]{1,0:T(8,128)(2,1)S(1)}, f32[64,1024]{1,0:T(8,128)S(1)}, bf16[64,1024]{1,0:T(8,128)(2,1)S(1)}) custom-call(s32[4]{0:T(128)S(1)} %pad_add_fusion.place_ref.refs_0_, s32[6]{0:T(128)S(1)} %copy-done.8, bf16[64,1024]{1,0:T(8,128)(2,1)S(1)} %shard_map.126.refs_6_.refs_2_, bf16[64,1024]{1,0:T(8,128)(2,1)S(1)} %collective-permute-done.3.refs_3_, ...), custom_call_target="tpu_custom_call" | custom-call | bytes 128 | tf_op jit(solution)/shard_map/pallas_call | solution.py:334
  42.7 4.2 %shard_map.129 = (bf16[3,128,2048]{2,1,0:T(8,128)(2,1)S(1)}, bf16[3,128,2048]{2,1,0:T(8,128)(2,1)S(1)}) custom-call(bf16[3,128,1024]{2,1,0:T(8,128)(2,1)S(1)} %bitcast.19, f32[1,1024]{1,0:T(1,128)S(1)} %copy-done.6, bf16[3,1024,2048]{2,1,0:T(8,128)(2,1)S(1)} %get-tuple-element.38.refs_4_.refs_6_.refs_2_.refs_5_, bf16[64,1024]{1,0:T(8,128)(2,1)S(1)} %get-tuple-element.43.refs_3_), custom_call_target="tpu_custom_call" | custom-call | bytes 128 | tf_op jit(solution)/shard_map/pallas_call | solution.py:334
  48.1 0.8 shard_map.131.refs_4_
  49.0 0.6 shard_map.132.refs_8_.refs_1_
  49.6 1.8 %collective-permute-start.10 = (bf16[64,1024]{1,0:T(8,128)(2,1)S(1)}, bf16[64,1024]{1,0:T(8,128)(2,1)S(1)}, u32[]{:S(2)}, u32[]{:S(2)}) collective-permute-start(bf16[64,1024]{1,0:T(8,128)(2,1)S(1)} %shard_map.132.refs_8_.refs_1_), channel_id=1, source_target_pairs={{0,6},{1,7},{2,4},{3,5},{4,10},{5,11},{6,8},{7,9},{8,14},{9,15},{1... | collective-permute-start | bytes 393224 | tf_op jit(solution)/shard_map/ppermute | solution.py:358
  51.4 9.3 %shard_map.133 = (bf16[64,1024]{1,0:T(8,128)(2,1)S(1)}, f32[64,1024]{1,0:T(8,128)S(1)}, f32[16,128,128]{2,1,0:T(8,128)S(1)}, bf16[64,1024]{1,0:T(8,128)(2,1)S(1)}) custom-call(s32[4]{0:T(128)S(1)} %pad_add_fusion.place_ref.refs_0_, bf16[64,1024]{1,0:T(8,128)(2,1)S(1)} %shard_map.130.refs_2_.refs_1_, bf16[64,1024]{1,0:T(8,128)(2,1)S(1)} %collective-permute-done.11.refs_2_, ...), custom_call_target="tpu_custom_call" | custom-call | bytes 128 | tf_op jit(solution)/shard_map/pallas_call | solution.py:334
  60.8 1.4 %collective-permute-start.15 = (bf16[64,1024]{1,0:T(8,128)(2,1)S(1)}, bf16[64,1024]{1,0:T(8,128)(2,1)S(1)}, u32[]{:S(2)}, u32[]{:S(2)}) collective-permute-start(bf16[64,1024]{1,0:T(8,128)(2,1)S(1)} %shard_map.132.refs_8_.refs_1_), channel_id=1, source_target_pairs={{0,2},{1,3},{2,0},{3,1},{4,6},{5,7},{6,4},{7,5},{8,10},{9,11},{10,... | collective-permute-start | bytes 393224 | tf_op jit(solution)/shard_map/ppermute | solution.py:362
  62.4 0.7 shard_map.135.refs_9_
  63.1 4.3 %collective-permute-start.17 = (bf16[64,1024]{1,0:T(8,128)(2,1)S(1)}, bf16[64,1024]{1,0:T(8,128)(2,1)S(1)}, u32[]{:S(2)}, u32[]{:S(2)}) collective-permute-start(bf16[64,1024]{1,0:T(8,128)(2,1)S(1)} %shard_map.135.refs_9_), channel_id=1, source_target_pairs={{0,14},{1,15},{2,12},{3,13},{4,2},{5,3},{6,0},{7,1},{8,6},{9,7},{1... | collective-permute-start | bytes 393224 | tf_op jit(solution)/shard_map/ppermute | solution.py:358
  67.9 4.3 %shard_map.136 = (bf16[64,1024]{1,0:T(8,128)(2,1)S(1)}, f32[64,1024]{1,0:T(8,128)S(1)}, bf16[64,1024]{1,0:T(8,128)(2,1)S(1)}) custom-call(s32[4]{0:T(128)S(1)} %pad_add_fusion.place_ref.refs_0_, s32[6]{0:T(128)S(1)} %copy-done.8, bf16[64,1024]{1,0:T(8,128)(2,1)S(1)} %shard_map.134.refs_6_.refs_2_, bf16[64,1024]{1,0:T(8,128)(2,1)S(1)} %collective-permute-done.12.refs_3_, ...), custom_call_target="tpu_custom_call" | custom-call | bytes 128 | tf_op jit(solution)/shard_map/pallas_call | solution.py:334
  72.2 1.1 %collective-permute-done.16.refs_3_ = bf16[64,1024]{1,0:T(8,128)(2,1)S(1)} collective-permute-done((bf16[64,1024]{1,0:T(8,128)(2,1)S(1)}, bf16[64,1024]{1,0:T(8,128)(2,1)S(1)}, u32[]{:S(2)}, u32[]{:S(2)}) %collective-permute-start.16) | collective-permute-done | bytes 131104 | tf_op jit(solution)/shard_map/ppermute | solution.py:358
  74.0 0.8 shard_map.138.refs_4_
  75.4 1.3 %collective-permute-start.18 = (bf16[64,1024]{1,0:T(8,128)(2,1)S(1)}, bf16[64,1024]{1,0:T(8,128)(2,1)S(1)}, u32[]{:S(2)}, u32[]{:S(2)}) collective-permute-start(bf16[64,1024]{1,0:T(8,128)(2,1)S(1)} %shard_map.139.refs_8_.refs_0_), channel_id=1, source_target_pairs={{0,2},{1,3},{2,0},{3,1},{4,6},{5,7},{6,4},{7,5},{8,10},{9,11},{10,... | collective-permute-start | bytes 393224 | tf_op jit(solution)/shard_map/ppermute | solution.py:362
  76.7 9.3 %shard_map.140 = (bf16[64,1024]{1,0:T(8,128)(2,1)S(1)}, f32[64,1024]{1,0:T(8,128)S(1)}, f32[16,128,128]{2,1,0:T(8,128)S(1)}, bf16[64,1024]{1,0:T(8,128)(2,1)S(1)}) custom-call(s32[4]{0:T(128)S(1)} %pad_add_fusion.place_ref.refs_0_, bf16[64,1024]{1,0:T(8,128)(2,1)S(1)} %shard_map.137.refs_2_.refs_1_, bf16[64,1024]{1,0:T(8,128)(2,1)S(1)} %collective-permute-done.19.refs_2_, ...), custom_call_target="tpu_custom_call" | custom-call | bytes 128 | tf_op jit(solution)/shard_map/pallas_call | solution.py:334
  86.7 0.7 collective-permute-done.21.refs_4_
  87.5 0.7 shard_map.142.refs_3_.refs_0_
  88.2 0.9 collective-permute-start.22
  89.0 1.3 %shard_map.143.refs_2_ = bf16[1,128,1024]{2,1,0:T(8,128)(2,1)} custom-call(s32[4]{0:T(128)S(1)} %pad_add_fusion.place_ref.refs_0_, bf16[64,1024]{1,0:T(8,128)(2,1)S(1)} %shard_map.141.refs_6_.refs_1_, bf16[64,1024]{1,0:T(8,128)(2,1)S(1)} %collective-permute-done.20.refs_2_, bf16[64,1024]{1,0:T(8,128)(2,1)S(1)} %shard_map.142.refs_3_.refs_0_), custom_call_target="tpu_custom_call" | custom-call | bytes 128 | tf_op jit(solution)/shard_map/pallas_call | solution.py:334
  90.3 0.9 copy-done.3
  91.3 1.7 %shard_map.144.refs_2_ = f32[16,32]{1,0:T(8,128)} custom-call(f32[16,128,128]{2,1,0:T(8,128)S(1)} %get-tuple-element.58.refs_0_, s32[128,128]{1,0:T(8,128)S(1)} %copy-done.5, bf16[1,128,1024]{2,1,0:T(8,128)(2,1)S(1)} %copy-done.3), custom_call_target="tpu_custom_call" | custom-call | bytes 128 | tf_op jit(solution)/shard_map/pallas_call | solution.py:334
  92.9 1.0 collective-permute-done.22.refs_1_
  93.9 0.7 copy-done.7
  94.7 1.3 %collective-permute-done.23.refs_2_ = bf16[64,1024]{1,0:T(8,128)(2,1)S(1)} collective-permute-done((bf16[64,1024]{1,0:T(8,128)(2,1)S(1)}, bf16[64,1024]{1,0:T(8,128)(2,1)S(1)}, u32[]{:S(2)}, u32[]{:S(2)}) %collective-permute-start.23) | collective-permute-done | bytes 131104 | tf_op jit(solution)/shard_map/ppermute | solution.py:362
  96.0 1.3 %shard_map.146 = bf16[1,128,1024]{2,1,0:T(8,128)(2,1)} custom-call(s32[4]{0:T(128)S(1)} %pad_add_fusion.place_ref.refs_0_, bf16[64,1024]{1,0:T(8,128)(2,1)S(1)} %shard_map.145.refs_1_.refs_3_, bf16[64,1024]{1,0:T(8,128)(2,1)S(1)} %collective-permute-done.23.refs_2_, bf16[64,1024]{1,0:T(8,128)(2,1)S(1)} %shard_map.145.refs_1_.refs_3_), custom_call_target="tpu_custom_call" | custom-call | bytes 128 | tf_op jit(solution)/shard_map/pallas_call | solution.py:334
  (61 shorter events, 7.3 us)
Async XLA Ops:
  0.7 12.9 %copy-start.2 = (bf16[1,128,1024]{2,1,0:T(8,128)(2,1)S(1)}, bf16[1,128,1024]{2,1,0:T(8,128)(2,1)}, u32[]{:S(2)}) copy-start(bf16[1,128,1024]{2,1,0:T(8,128)(2,1)} %refs_1_.5) | copy-start | bytes 786436
  15.9 1.5 %collective-permute-start = (bf16[64,1024]{1,0:T(8,128)(2,1)S(1)}, bf16[64,1024]{1,0:T(8,128)(2,1)S(1)}, u32[]{:S(2)}, u32[]{:S(2)}) collective-permute-start(bf16[64,1024]{1,0:T(8,128)(2,1)S(1)} %get-tuple-element.35.refs_2_), channel_id=1, source_target_pairs={{0,1},{1,0},{2,3},{3,2},{4,5},{5,4},{6,7},{7,6},{8,9},{9,8},{10,11... | collective-permute-start | bytes 393224 | tf_op jit(solution)/shard_map/ppermute | solution.py:362
  17.2 6.3 %copy-start.4 = (bf16[1,128,1024]{2,1,0:T(8,128)(2,1)S(1)}, bf16[1,128,1024]{2,1,0:T(8,128)(2,1)}, u32[]{:S(2)}) copy-start(bf16[1,128,1024]{2,1,0:T(8,128)(2,1)} %param.11) | copy-start | bytes 786436
  17.9 14.9 %collective-permute-start.2 = (bf16[64,1024]{1,0:T(8,128)(2,1)S(1)}, bf16[64,1024]{1,0:T(8,128)(2,1)S(1)}, u32[]{:S(2)}, u32[]{:S(2)}) collective-permute-start(bf16[64,1024]{1,0:T(8,128)(2,1)S(1)} %shard_map.124.refs_6_.refs_1_), channel_id=1, source_target_pairs={{0,6},{1,7},{2,4},{3,5},{4,10},{5,11},{6,8},{7,9},{8,14},{9,15},{1... | collective-permute-start | bytes 393224 | tf_op jit(solution)/shard_map/ppermute | solution.py:358
  21.9 11.0 %collective-permute-start.1 = (bf16[64,1024]{1,0:T(8,128)(2,1)S(1)}, bf16[64,1024]{1,0:T(8,128)(2,1)S(1)}, u32[]{:S(2)}, u32[]{:S(2)}) collective-permute-start(bf16[64,1024]{1,0:T(8,128)(2,1)S(1)} %shard_map.124.refs_6_.refs_1_), channel_id=1, source_target_pairs={{0,4},{1,5},{2,6},{3,7},{4,8},{5,9},{6,10},{7,11},{8,12},{9,13},{1... | collective-permute-start | bytes 393224 | tf_op jit(solution)/shard_map/ppermute | solution.py:358
  23.4 10.8 %copy-start = (bf16[1,3,128,1024]{3,2,1,0:T(8,128)(2,1)S(1)}, bf16[1,3,128,1024]{3,2,1,0:T(8,128)(2,1)}, u32[]{:S(2)}) copy-start(bf16[1,3,128,1024]{3,2,1,0:T(8,128)(2,1)} %kept_ref.1) | copy-start | bytes 2359300
  23.4 10.8 %copy-start.6 = (f32[1,1024]{1,0:T(1,128)S(1)}, f32[1,1024]{1,0:T(1,128)}, u32[]{:S(2)}) copy-start(f32[1,1024]{1,0:T(1,128)} %refs_2_.5) | copy-start | bytes 12292
  32.8 5.6 %copy-start.1 = (bf16[6,128,1024]{2,1,0:T(8,128)(2,1)S(1)}, bf16[6,128,1024]{2,1,0:T(8,128)(2,1)}, u32[]{:S(2)}) copy-start(bf16[6,128,1024]{2,1,0:T(8,128)(2,1)} %refs_4_.3) | copy-start | bytes 4718596
  32.8 5.6 %copy-start.8 = (s32[6]{0:T(128)S(1)}, s32[6]{0:T(128)}, u32[]{:S(2)}) copy-start(s32[6]{0:T(128)} %refs_1_.8) | copy-start | bytes 76
  32.8 1.4 %collective-permute-start.4 = (bf16[64,1024]{1,0:T(8,128)(2,1)S(1)}, bf16[64,1024]{1,0:T(8,128)(2,1)S(1)}, u32[]{:S(2)}, u32[]{:S(2)}) collective-permute-start(bf16[64,1024]{1,0:T(8,128)(2,1)S(1)} %get-tuple-element.39.refs_2_), channel_id=1, source_target_pairs={{0,1},{1,0},{2,3},{3,2},{4,5},{5,4},{6,7},{7,6},{8,9},{9,8},{10,11... | collective-permute-start | bytes 393224 | tf_op jit(solution)/shard_map/ppermute | solution.py:362
  32.9 5.5 %collective-permute-start.3 = (bf16[64,1024]{1,0:T(8,128)(2,1)S(1)}, bf16[64,1024]{1,0:T(8,128)(2,1)S(1)}, u32[]{:S(2)}, u32[]{:S(2)}) collective-permute-start(bf16[64,1024]{1,0:T(8,128)(2,1)S(1)} %shard_map.126.refs_6_.refs_2_), channel_id=1, source_target_pairs={{0,1},{1,0},{2,3},{3,2},{4,5},{5,4},{6,7},{7,6},{8,9},{9,8},{10,11... | collective-permute-start | bytes 393224 | tf_op jit(solution)/shard_map/ppermute | solution.py:362
  33.5 13.5 %collective-permute-start.6 = (bf16[64,1024]{1,0:T(8,128)(2,1)S(1)}, bf16[64,1024]{1,0:T(8,128)(2,1)S(1)}, u32[]{:S(2)}, u32[]{:S(2)}) collective-permute-start(bf16[64,1024]{1,0:T(8,128)(2,1)S(1)} %shard_map.124.refs_6_.refs_1_), channel_id=1, source_target_pairs={{0,2},{1,3},{2,0},{3,1},{4,6},{5,7},{6,4},{7,5},{8,10},{9,11},{10,... | collective-permute-start | bytes 393224 | tf_op jit(solution)/shard_map/ppermute | solution.py:362
  34.9 12.0 %collective-permute-start.8 = (bf16[64,1024]{1,0:T(8,128)(2,1)S(1)}, bf16[64,1024]{1,0:T(8,128)(2,1)S(1)}, u32[]{:S(2)}, u32[]{:S(2)}) collective-permute-start(bf16[64,1024]{1,0:T(8,128)(2,1)S(1)} %shard_map.127.refs_9_), channel_id=1, source_target_pairs={{0,14},{1,15},{2,12},{3,13},{4,2},{5,3},{6,0},{7,1},{8,6},{9,7},{1... | collective-permute-start | bytes 393224 | tf_op jit(solution)/shard_map/ppermute | solution.py:358
  38.0 9.0 %collective-permute-start.7 = (bf16[64,1024]{1,0:T(8,128)(2,1)S(1)}, bf16[64,1024]{1,0:T(8,128)(2,1)S(1)}, u32[]{:S(2)}, u32[]{:S(2)}) collective-permute-start(bf16[64,1024]{1,0:T(8,128)(2,1)S(1)} %shard_map.127.refs_9_), channel_id=1, source_target_pairs={{0,12},{1,13},{2,14},{3,15},{4,0},{5,1},{6,2},{7,3},{8,4},{9,5},{1... | collective-permute-start | bytes 393224 | tf_op jit(solution)/shard_map/ppermute | solution.py:358
  42.7 6.3 %collective-permute-start.5 = (bf16[64,1024]{1,0:T(8,128)(2,1)S(1)}, bf16[64,1024]{1,0:T(8,128)(2,1)S(1)}, u32[]{:S(2)}, u32[]{:S(2)}) collective-permute-start(bf16[64,1024]{1,0:T(8,128)(2,1)S(1)} %get-tuple-element.43.refs_3_), channel_id=1, source_target_pairs={{0,1},{1,0},{2,3},{3,2},{4,5},{5,4},{6,7},{7,6},{8,9},{9,8},{10,11... | collective-permute-start | bytes 393224 | tf_op jit(solution)/shard_map/ppermute | solution.py:362
  47.6 3.8 %collective-permute-start.11 = (bf16[64,1024]{1,0:T(8,128)(2,1)S(1)}, bf16[64,1024]{1,0:T(8,128)(2,1)S(1)}, u32[]{:S(2)}, u32[]{:S(2)}) collective-permute-start(bf16[64,1024]{1,0:T(8,128)(2,1)S(1)} %shard_map.130.refs_2_.refs_1_), channel_id=1, source_target_pairs={{0,1},{1,0},{2,3},{3,2},{4,5},{5,4},{6,7},{7,6},{8,9},{9,8},{10,11... | collective-permute-start | bytes 393224 | tf_op jit(solution)/shard_map/ppermute | solution.py:362
  49.6 12.6 %collective-permute-start.10 = (bf16[64,1024]{1,0:T(8,128)(2,1)S(1)}, bf16[64,1024]{1,0:T(8,128)(2,1)S(1)}, u32[]{:S(2)}, u32[]{:S(2)}) collective-permute-start(bf16[64,1024]{1,0:T(8,128)(2,1)S(1)} %shard_map.132.refs_8_.refs_1_), channel_id=1, source_target_pairs={{0,6},{1,7},{2,4},{3,5},{4,10},{5,11},{6,8},{7,9},{8,14},{9,15},{1... | collective-permute-start | bytes 393224 | tf_op jit(solution)/shard_map/ppermute | solution.py:358
  51.4 10.8 %collective-permute-start.9 = (bf16[64,1024]{1,0:T(8,128)(2,1)S(1)}, bf16[64,1024]{1,0:T(8,128)(2,1)S(1)}, u32[]{:S(2)}, u32[]{:S(2)}) collective-permute-start(bf16[64,1024]{1,0:T(8,128)(2,1)S(1)} %shard_map.132.refs_8_.refs_1_), channel_id=1, source_target_pairs={{0,4},{1,5},{2,6},{3,7},{4,8},{5,9},{6,10},{7,11},{8,12},{9,13},{1... | collective-permute-start | bytes 393224 | tf_op jit(solution)/shard_map/ppermute | solution.py:358
  60.7 1.7 %collective-permute-start.13 = (bf16[64,1024]{1,0:T(8,128)(2,1)S(1)}, bf16[64,1024]{1,0:T(8,128)(2,1)S(1)}, u32[]{:S(2)}, u32[]{:S(2)}) collective-permute-start(bf16[64,1024]{1,0:T(8,128)(2,1)S(1)} %get-tuple-element.47.refs_2_), channel_id=1, source_target_pairs={{0,1},{1,0},{2,3},{3,2},{4,5},{5,4},{6,7},{7,6},{8,9},{9,8},{10,11... | collective-permute-start | bytes 393224 | tf_op jit(solution)/shard_map/ppermute | solution.py:362
  60.8 11.5 %collective-permute-start.15 = (bf16[64,1024]{1,0:T(8,128)(2,1)S(1)}, bf16[64,1024]{1,0:T(8,128)(2,1)S(1)}, u32[]{:S(2)}, u32[]{:S(2)}) collective-permute-start(bf16[64,1024]{1,0:T(8,128)(2,1)S(1)} %shard_map.132.refs_8_.refs_1_), channel_id=1, source_target_pairs={{0,2},{1,3},{2,0},{3,1},{4,6},{5,7},{6,4},{7,5},{8,10},{9,11},{10,... | collective-permute-start | bytes 393224 | tf_op jit(solution)/shard_map/ppermute | solution.py:362
  62.2 5.7 %collective-permute-start.12 = (bf16[64,1024]{1,0:T(8,128)(2,1)S(1)}, bf16[64,1024]{1,0:T(8,128)(2,1)S(1)}, u32[]{:S(2)}, u32[]{:S(2)}) collective-permute-start(bf16[64,1024]{1,0:T(8,128)(2,1)S(1)} %shard_map.134.refs_6_.refs_2_), channel_id=1, source_target_pairs={{0,1},{1,0},{2,3},{3,2},{4,5},{5,4},{6,7},{7,6},{8,9},{9,8},{10,11... | collective-permute-start | bytes 393224 | tf_op jit(solution)/shard_map/ppermute | solution.py:362
  63.1 9.1 %collective-permute-start.17 = (bf16[64,1024]{1,0:T(8,128)(2,1)S(1)}, bf16[64,1024]{1,0:T(8,128)(2,1)S(1)}, u32[]{:S(2)}, u32[]{:S(2)}) collective-permute-start(bf16[64,1024]{1,0:T(8,128)(2,1)S(1)} %shard_map.135.refs_9_), channel_id=1, source_target_pairs={{0,14},{1,15},{2,12},{3,13},{4,2},{5,3},{6,0},{7,1},{8,6},{9,7},{1... | collective-permute-start | bytes 393224 | tf_op jit(solution)/shard_map/ppermute | solution.py:358
  67.4 5.9 %collective-permute-start.16 = (bf16[64,1024]{1,0:T(8,128)(2,1)S(1)}, bf16[64,1024]{1,0:T(8,128)(2,1)S(1)}, u32[]{:S(2)}, u32[]{:S(2)}) collective-permute-start(bf16[64,1024]{1,0:T(8,128)(2,1)S(1)} %shard_map.135.refs_9_), channel_id=1, source_target_pairs={{0,12},{1,13},{2,14},{3,15},{4,0},{5,1},{6,2},{7,3},{8,4},{9,5},{1... | collective-permute-start | bytes 393224 | tf_op jit(solution)/shard_map/ppermute | solution.py:358
  72.1 2.6 %collective-permute-start.14 = (bf16[64,1024]{1,0:T(8,128)(2,1)S(1)}, bf16[64,1024]{1,0:T(8,128)(2,1)S(1)}, u32[]{:S(2)}, u32[]{:S(2)}) collective-permute-start(bf16[64,1024]{1,0:T(8,128)(2,1)S(1)} %get-tuple-element.51.refs_5_), channel_id=1, source_target_pairs={{0,1},{1,0},{2,3},{3,2},{4,5},{5,4},{6,7},{7,6},{8,9},{9,8},{10,11... | collective-permute-start | bytes 393224 | tf_op jit(solution)/shard_map/ppermute | solution.py:362
  73.9 2.8 %collective-permute-start.19 = (bf16[64,1024]{1,0:T(8,128)(2,1)S(1)}, bf16[64,1024]{1,0:T(8,128)(2,1)S(1)}, u32[]{:S(2)}, u32[]{:S(2)}) collective-permute-start(bf16[64,1024]{1,0:T(8,128)(2,1)S(1)} %shard_map.137.refs_2_.refs_1_), channel_id=1, source_target_pairs={{0,1},{1,0},{2,3},{3,2},{4,5},{5,4},{6,7},{7,6},{8,9},{9,8},{10,11... | collective-permute-start | bytes 393224 | tf_op jit(solution)/shard_map/ppermute | solution.py:362
  75.4 10.9 %collective-permute-start.18 = (bf16[64,1024]{1,0:T(8,128)(2,1)S(1)}, bf16[64,1024]{1,0:T(8,128)(2,1)S(1)}, u32[]{:S(2)}, u32[]{:S(2)}) collective-permute-start(bf16[64,1024]{1,0:T(8,128)(2,1)S(1)} %shard_map.139.refs_8_.refs_0_), channel_id=1, source_target_pairs={{0,2},{1,3},{2,0},{3,1},{4,6},{5,7},{6,4},{7,5},{8,10},{9,11},{10,... | collective-permute-start | bytes 393224 | tf_op jit(solution)/shard_map/ppermute | solution.py:362
  86.0 4.3 %copy-start.5 = (s32[128,128]{1,0:T(8,128)S(1)}, s32[128,128]{1,0:T(8,128)}, u32[]{:S(2)}) copy-start(s32[128,128]{1,0:T(8,128)} %refs_1_.9) | copy-start | bytes 196612
  86.0 1.4 %collective-permute-start.21 = (bf16[64,1024]{1,0:T(8,128)(2,1)S(1)}, bf16[64,1024]{1,0:T(8,128)(2,1)S(1)}, u32[]{:S(2)}, u32[]{:S(2)}) collective-permute-start(bf16[64,1024]{1,0:T(8,128)(2,1)S(1)} %get-tuple-element.55.refs_2_), channel_id=1, source_target_pairs={{0,1},{1,0},{2,3},{3,2},{4,5},{5,4},{6,7},{7,6},{8,9},{9,8},{10,11... | collective-permute-start | bytes 393224 | tf_op jit(solution)/shard_map/ppermute | solution.py:362
  86.4 2.7 %collective-permute-start.20 = (bf16[64,1024]{1,0:T(8,128)(2,1)S(1)}, bf16[64,1024]{1,0:T(8,128)(2,1)S(1)}, u32[]{:S(2)}, u32[]{:S(2)}) collective-permute-start(bf16[64,1024]{1,0:T(8,128)(2,1)S(1)} %shard_map.141.refs_6_.refs_1_), channel_id=1, source_target_pairs={{0,1},{1,0},{2,3},{3,2},{4,5},{5,4},{6,7},{7,6},{8,9},{9,8},{10,11... | collective-permute-start | bytes 393224 | tf_op jit(solution)/shard_map/ppermute | solution.py:362
  88.2 5.7 %collective-permute-start.22 = (bf16[64,1024]{1,0:T(8,128)(2,1)S(1)}, bf16[64,1024]{1,0:T(8,128)(2,1)S(1)}, u32[]{:S(2)}, u32[]{:S(2)}) collective-permute-start(bf16[64,1024]{1,0:T(8,128)(2,1)S(1)} %shard_map.142.refs_3_.refs_0_), channel_id=1, source_target_pairs={{0,2},{1,3},{2,0},{3,1},{4,6},{5,7},{6,4},{7,5},{8,10},{9,11},{10,... | collective-permute-start | bytes 393224 | tf_op jit(solution)/shard_map/ppermute | solution.py:362
  90.3 1.0 copy-start.3
  94.6 1.4 %collective-permute-start.23 = (bf16[64,1024]{1,0:T(8,128)(2,1)S(1)}, bf16[64,1024]{1,0:T(8,128)(2,1)S(1)}, u32[]{:S(2)}, u32[]{:S(2)}) collective-permute-start(bf16[64,1024]{1,0:T(8,128)(2,1)S(1)} %shard_map.145.refs_1_.refs_3_), channel_id=1, source_target_pairs={{0,1},{1,0},{2,3},{3,2},{4,5},{5,4},{6,7},{7,6},{8,9},{9,8},{10,11... | collective-permute-start | bytes 393224 | tf_op jit(solution)/shard_map/ppermute | solution.py:362
  (1 other events, 0.7 us)

commit v6 on v5

--- a/solution.py
+++ b/solution.py
@@ -37,6 +37,27 @@
     return pl.ds(pl.multiple_of(index * size, size), size)
 
 
+SECOND_CORE, FIRST_SECTION, LAST_SECTION, ADDS_RESIDUAL = range(4)
+
+
+def flag(flags_ref, row):
+    return flags_ref[row : row + 1, :1]
+
+
+def pick(chosen, yes, no):
+    yes, no = yes.astype(F32), no.astype(F32)
+    return jnp.where(jnp.broadcast_to(chosen, yes.shape) > 0.5, yes, no)
+
+
+def joined(second, mine, other):
+    return jnp.concatenate([pick(second, other, mine), pick(second, mine, other)], axis=0)
+
+
+def own_half(second, rows):
+    half = rows.shape[0] // 2
+    return pick(second, rows[half:], rows[:half])
+
+
 def fill_bias(table_ref, bucket_ref, bias_ref):
     ids = bucket_ref[...].T
     rows, count = table_ref.shape
@@ -51,16 +72,21 @@
 
 
 def relayout_kernel(
-    place_ref, x_ref, kept_ref, gain_ref, table_ref, bucket_ref, w_ref, back_ref,
-    w_out_ref, qkv_ref, kept_qkv_ref, bias_ref, back_out_ref, normed, arrived,
+    order_ref, x_ref, kept_ref, gain_ref, table_ref, bucket_ref, w_ref, back_ref, queue_ref, _,
+    w_out_ref, qkv_ref, kept_qkv_ref, bias_ref, back_out_ref, entering_ref, normed, arrived,
 ):
     which = pl.program_id(0)
     block = pl.program_id(1)
-    back_copy = pltpu.make_async_copy(back_ref, back_out_ref, arrived)
+    entering = range(entering_ref.shape[0])
+    copies = [pltpu.make_async_copy(back_ref, back_out_ref, arrived.at[len(entering)])] + [
+        pltpu.make_async_copy(queue_ref.at[order_ref[t]], entering_ref.at[t], arrived.at[t])
+        for t in entering
+    ]
 
     @pl.when((which == 0) & (block == 0))
     def _():
-        back_copy.start()
+        for copy in copies:
+            copy.start()
         tokens = x_ref.shape[1]
         normed[:tokens] = rms_normed(x_ref[0], gain_ref[...])
         normed[tokens:] = rms_normed(kept_ref[0, 0], gain_ref[...])
@@ -97,7 +123,8 @@
 
     @pl.when((which == pl.num_programs(0) - 1) & (block == pl.num_programs(1) - 1))
     def _():
-        back_copy.wait()
+        for copy in copies:
+            copy.wait()
 
 
 def probs_of(query, key, bias, scale):
@@ -116,53 +143,38 @@
     return [dot(p, value[:, sl], FIRST).astype(BF16) for p, sl in zip(probs, lanes)]
 
 
-def forward_kernel(tick, place_ref, *refs):
-    if tick == 0:
-        x_in_ref, qkv_ref, bias_ref, wo_ref, send_ref, keep_ref, x_half_ref, attended = refs
+def forward_kernel(tick, flags_ref, *refs):
+    first = tick == 0
+    if first:
+        x_ref, qkv_ref, bias_ref, wo_ref, send_ref, keep_ref, x_half_ref, attended = refs
     else:
-        (order_ref, mine_ref, other_ref, queue_ref, gain_ref, w_ref, bias_ref, wo_ref,
-         send_ref, keep_ref, x_half_ref, attended, x_ref) = refs
-    core = place_ref[0]
-    half = send_ref.shape[0]
-    heads = bias_ref.shape[0]
-    group = heads // 2
-    if tick == 0:
-        x_half_ref[...] = x_in_ref[0, rows_at(core, half)]
+        (mine_ref, other_ref, entering_ref, gain_ref, w_ref, bias_ref, wo_ref,
+         send_ref, keep_ref, x_half_ref, attended) = refs
+    second = flag(flags_ref, SECOND_CORE)
+    group = bias_ref.shape[0] // 2
+    if first:
+        x = x_ref[0]
     else:
-        x_ref[rows_at(core, half)] = mine_ref[...]
-        x_ref[rows_at(1 - core, half)] = other_ref[...]
-
-        @pl.when(place_ref[1] == 0)
-        def _():
-            x_ref[...] = queue_ref[order_ref[tick - 1]]
-
-        x_half_ref[...] = x_ref[rows_at(core, half)]
-        normed = rms_normed(x_ref[...], gain_ref[...])
+        x = joined(second, mine_ref[...], other_ref[...])
+        x = pick(flag(flags_ref, FIRST_SECTION), entering_ref[tick - 1], x)
+        normed = rms_normed(x, gain_ref[...])
+    x_half_ref[...] = own_half(second, x).astype(BF16)
     for part in range(2):
         at = slice(part * group * LANES, (part + 1) * group * LANES)
-        if tick == 0:
+        if first:
             query, key, value = (qkv_ref[c, :, at] for c in range(3))
         else:
             query, key, value = (dot(normed, w_ref[c, :, at]).astype(BF16) for c in range(3))
         outs = attend(query, key, value, bias_ref, group, part * group)
         for h, out in enumerate(outs):
-            first = (part * group + h) * LANES
-            attended[:, first : first + LANES] = out
-    split_halves(core, dot(attended[...], wo_ref[...]), send_ref, keep_ref)
-
-
-def split_halves(core, total, send_ref, keep_ref):
-    half = send_ref.shape[0]
-
-    @pl.when(core == 0)
-    def _():
-        send_ref[...] = total[half:].astype(BF16)
-        keep_ref[...] = total[:half]
-
-    @pl.when(core != 0)
-    def _():
-        send_ref[...] = total[:half].astype(BF16)
-        keep_ref[...] = total[half:]
+            at = (part * group + h) * LANES
+            attended[:, at : at + LANES] = out
+    split_halves(second, dot(attended[...], wo_ref[...]), send_ref, keep_ref)
+
+
+def split_halves(second, total, send_ref, keep_ref):
+    send_ref[...] = own_half(1.0 - second, total).astype(BF16)
+    keep_ref[...] = own_half(second, total)
 
 
 def stash_kernel(skipped, x_ref, gain_ref, w_ref, *refs):
@@ -225,42 +237,39 @@
         stacked[2, :, own] = dot(probs.astype(BF16), ga).astype(BF16)
 
 
-def backward_kernel(first, place_ref, *refs):
-    core = place_ref[0]
+def backward_kernel(first, flags_ref, *refs):
+    second = flag(flags_ref, SECOND_CORE)
     if first:
         full_ref, qkv_ref, probs_ref, w_ref, wo_ref, *refs = refs
-        send_ref, keep_ref, acc_ref, g_half_ref, stacked, g_ref = refs
+        send_ref, keep_ref, acc_ref, g_half_ref, stacked = refs
         acc_in_ref = None
-        g_ref[...] = full_ref[...]
+        g = full_ref[...]
     else:
         mine_ref, other_ref, qkv_ref, probs_ref, w_ref, wo_ref, acc_in_ref, *refs = refs
-        send_ref, keep_ref, acc_ref, g_half_ref, stacked, g_ref = refs
-        half = g_half_ref.shape[0]
-        g_ref[rows_at(core, half)] = mine_ref[...]
-        g_ref[rows_at(1 - core, half)] = other_ref[...]
-    g_half_ref[...] = g_ref[rows_at(core, g_half_ref.shape[0])]
+        send_ref, keep_ref, acc_ref, g_half_ref, stacked = refs
+        g = joined(second, mine_ref[...], other_ref[...]).astype(BF16)
+    g_half_ref[...] = own_half(second, g).astype(BF16)
     for part in range(2):
-        grad_attend(g_ref[...], qkv_ref, probs_ref, wo_ref, acc_in_ref, stacked, acc_ref, part)
+        grad_attend(g, qkv_ref, probs_ref, wo_ref, acc_in_ref, stacked, acc_ref, part)
     total = dot(w_ref[0], stacked[0], LAST)
     total += dot(w_ref[1], stacked[1], LAST)
     total += dot(w_ref[2], stacked[2], LAST)
-    split_halves(core, total.T, send_ref, keep_ref)
+    split_halves(second, total.T, send_ref, keep_ref)
 
 
 def pair_kernel(first_ref, second_ref, out_ref):
     out_ref[...] = (first_ref[...].astype(F32) + second_ref[...].astype(F32)).astype(BF16)
 
 
-def up_term_kernel(place_ref, keep_ref, received_ref, x_ref, out_ref):
-    residual = place_ref[3].astype(F32)
+def up_term_kernel(flags_ref, keep_ref, received_ref, x_ref, out_ref):
+    residual = flag(flags_ref, ADDS_RESIDUAL)
     total = keep_ref[...] + received_ref[...].astype(F32)
     out_ref[...] = (total + residual * x_ref[...].astype(F32)).astype(BF16)
 
 
-def down_term_kernel(tick, place_ref, stash_ref, gain_ref, keep_ref, received_ref, g_ref, out_ref):
-    half = out_ref.shape[0]
-    residual = place_ref[3].astype(F32)
-    x = stash_ref[tick, rows_at(place_ref[0], half)].astype(F32)
+def down_term_kernel(tick, flags_ref, stash_ref, gain_ref, keep_ref, received_ref, g_ref, out_ref):
+    residual = flag(flags_ref, ADDS_RESIDUAL)
+    x = own_half(flag(flags_ref, SECOND_CORE), stash_ref[tick])
     inverse = lax.rsqrt(jnp.mean(x * x, axis=-1, keepdims=True) + EPSILON)
     weighted = gain_ref[...] * (keep_ref[...] + received_ref[...].astype(F32))
     mean = jnp.mean(x * weighted, axis=-1, keepdims=True)
@@ -269,24 +278,19 @@
     out_ref[...] = (residual * g_ref[...].astype(F32) + back).astype(BF16)
 
 
-def choose_kernel(place_ref, own_ref, own_second_ref, first_ref, second_ref, out_ref):
-    @pl.when(place_ref[2] == 1)
-    def _():
-        pair_kernel(own_ref, own_second_ref, out_ref)
-
-    @pl.when(place_ref[2] == 0)
-    def _():
-        pair_kernel(first_ref, second_ref, out_ref)
-
-
-def join_kernel(place_ref, mine_ref, other_ref, out_ref):
-    core = place_ref[0]
-    half = mine_ref.shape[0]
-    out_ref[0, rows_at(core, half)] = mine_ref[...]
-    out_ref[0, rows_at(1 - core, half)] = other_ref[...]
-
-
-def table_kernel(buckets_here, acc_ref, bucket_ref, out_ref):
+def choose_kernel(flags_ref, own_ref, own_second_ref, first_ref, second_ref, out_ref):
+    own = own_ref[...].astype(F32) + own_second_ref[...].astype(F32)
+    arrived = first_ref[...].astype(F32) + second_ref[...].astype(F32)
+    out_ref[...] = pick(flag(flags_ref, LAST_SECTION), own, arrived).astype(BF16)
+
+
+def join_kernel(flags_ref, mine_ref, other_ref, out_ref, token_ref):
+    second = flag(flags_ref, SECOND_CORE)
+    out_ref[0] = joined(second, mine_ref[...], other_ref[...]).astype(BF16)
+    token_ref[...] = jnp.zeros_like(token_ref)
+
+
+def table_kernel(buckets_here, acc_ref, bucket_ref, out_ref, token_ref):
     heads, tokens, _ = acc_ref.shape
     rows = 8
     cells = heads * rows
@@ -313,6 +317,7 @@
     out_ref[...] = jnp.dot(
         summed, fold, preferred_element_type=F32, precision=lax.Precision.HIGHEST
     )
+    token_ref[...] = jnp.zeros_like(token_ref)
 
 
 def shape(dims, dtype=BF16):
@@ -323,9 +328,9 @@
     def __init__(self):
         self.before = None
 
-    def __call__(self, kernel, out_shape, args, scratch=(), scalars=0, after=(), limit=16):
+    def __call__(self, kernel, out_shape, args, scratch=(), limit=16):
         outs = out_shape if isinstance(out_shape, tuple) else (out_shape,)
-        extra = tuple(after) + (() if self.before is None else (self.before,))
+        extra = () if self.before is None else (self.before,)
         count = len(args)
 
         def body(*refs):
@@ -334,13 +339,13 @@
         results = pl.pallas_call(
             body,
             out_shape=outs,
-            in_specs=[SCALARS] * scalars + [WHOLE] * (count - scalars) + [UNREAD] * len(extra),
+            in_specs=[WHOLE] * count + [UNREAD] * len(extra),
             out_specs=tuple(WHOLE for _ in outs),
             scratch_shapes=list(scratch),
             compiler_params=pltpu.CompilerParams(vmem_limit_bytes=limit * MIB),
             cost_estimate=pl.CostEstimate(flops=0, bytes_accessed=LANES, transcendentals=0),
         )(*args, *extra)
-        self.before = results[0]
+        self.before = results[-1]
         return results if isinstance(out_shape, tuple) else results[0]
 
 
@@ -371,9 +376,13 @@
     tokens = buckets.shape[0]
     half = tokens // 2
     inner = heads * head_dim
-    core = head_index % 2
-    is_last = section_index == section_count - 1
-    place = jnp.stack([core, section_index, is_last, head_index < 2]).astype(jnp.int32)
+    facts = (
+        head_index % 2 == 1,
+        section_index == 0,
+        section_index == section_count - 1,
+        head_index < 2,
+    )
+    flags = jnp.broadcast_to(jnp.stack(facts).astype(F32)[:, None], (len(facts), LANES))
     table = bias_table[0].T
     back = w_out[0].reshape(inner, model_width)
     run = Chain()
@@ -387,7 +396,7 @@
         blocks = 2
         depth = model_width // blocks
         fixed = lambda rank: lambda c, b: (0,) * rank
-        weights, qkv, kept_qkv, bias, wo = pl.pallas_call(
+        weights, qkv, kept_qkv, bias, wo, entering = pl.pallas_call(
             relayout_kernel,
             grid=(3, blocks),
             out_shape=(
@@ -396,6 +405,7 @@
                 qkv_shape,
                 scores_shape,
                 pltpu.VMEM((inner, model_width), BF16),
+                pltpu.VMEM((TICKS - 1, tokens, model_width), BF16),
             ),
             in_specs=[
                 SCALARS,
@@ -406,6 +416,8 @@
                 pl.BlockSpec((tokens, tokens), fixed(2)),
                 pl.BlockSpec((depth, heads, head_dim), lambda c, b: (b, c, 0)),
                 UNREAD,
+                UNREAD,
+                UNREAD,
             ],
             out_specs=(
                 WHOLE,
@@ -413,19 +425,23 @@
                 pl.BlockSpec((3, tokens, inner), fixed(3)),
                 pl.BlockSpec((heads, tokens, tokens), fixed(3)),
                 WHOLE,
+                WHOLE,
             ),
-            scratch_shapes=[pltpu.VMEM((2 * tokens, model_width), BF16), pltpu.SemaphoreType.DMA],
+            scratch_shapes=[pltpu.VMEM((2 * tokens, model_width), BF16), pltpu.SemaphoreType.DMA((TICKS,))],
             compiler_params=pltpu.CompilerParams(vmem_limit_bytes=24 * MIB),
             cost_estimate=pl.CostEstimate(
                 flops=0, bytes_accessed=2 * w_qkv.size, transcendentals=0
             ),
         )(
-            place, in_hbm(rising), in_hbm(stash), in_hbm(gain), in_hbm(table), in_hbm(buckets),
-            in_hbm(rows_first), in_hbm(back),
+            order, in_hbm(rising), in_hbm(stash), in_hbm(gain), in_hbm(table), in_hbm(buckets),
+            in_hbm(rows_first), in_hbm(back), in_hbm(queue), flags,
         )
         run.before = qkv
     else:
         wo = back
+        entering = jnp.stack(
+            [lax.dynamic_index_in_dim(queue, order[t], 0, False) for t in range(TICKS - 1)]
+        )
         weights = jnp.transpose(w_qkv[0], (2, 0, 1, 3)).reshape(3, model_width, inner)
         bias = run(bias_kernel, scores_shape, (table, buckets))
         qkv, kept_qkv = (
@@ -439,7 +455,6 @@
         )
     halves = (shape((half, model_width)), shape((half, model_width), F32))
     half_rows = shape((half, model_width))
-    row_scratch = pltpu.VMEM((tokens, model_width), BF16)
 
     def but_last_bit(term):
         for bit in bits[:-1]:
@@ -450,8 +465,7 @@
         term = run(
             functools.partial(down_term_kernel, tick),
             half_rows,
-            (place, stash[0], gain, keep, received, g_half),
-            scalars=1,
+            (flags, stash[0], gain, keep, received, g_half),
         )
         return but_last_bit(term)
 
@@ -461,36 +475,36 @@
         final = t + 1 == TICKS
         scratch = [pltpu.VMEM((tokens, inner), BF16)]
         if t == 0:
-            args = (place, rising, qkv, bias, wo)
+            args = (flags, rising, qkv, bias, wo)
         else:
             x_other = swapped(x_mine, 1)
             fallen = down_term(t - 1, keep, received, g_half)
             arrivals = (up, in_last, moved(fallen, -1, 0), moved(fallen, -1, cross))
-            args = (place, order, x_mine, x_other, queue, gain, weights, bias, wo)
-            scratch += [row_scratch]
+            args = (flags, x_mine, x_other, entering, gain, weights, bias, wo)
         up_send, up_keep, x_half = run(
             functools.partial(forward_kernel, t),
             halves + (half_rows,),
             args,
             scratch=scratch,
-            scalars=1 if t == 0 else 2,
         )
         up_received = swapped(up_send, 1)
-        if t == 1:
-            stashed += run(
-                functools.partial(stash_kernel, 1),
-                (qkv_shape,) * (TICKS - 1),
-                (stash[0], gain, weights),
-                scratch=[pltpu.VMEM(((TICKS - 1) * tokens, model_width), BF16)],
+        if t > 0:
+            stashed.append(
+                run(
+                    functools.partial(stash_kernel, t),
+                    qkv_shape,
+                    (stash[0], gain, weights),
+                    scratch=[pltpu.VMEM((tokens, model_width), BF16)],
+                )
             )
+        probs = run(probs_kernel, scores_shape, (stashed[t], bias))
         if t == 0:
             g_parts = (falling[0],)
         else:
-            g_mine = run(choose_kernel, half_rows, (place,) + arrivals, scalars=1)
+            g_mine = run(choose_kernel, half_rows, (flags,) + arrivals)
             g_parts = (g_mine, swapped(g_mine, 1))
-        probs = run(probs_kernel, scores_shape, (stashed[t], bias))
         up = but_last_bit(
-            run(up_term_kernel, half_rows, (place, up_keep, up_received, x_half), scalars=1)
+            run(up_term_kernel, half_rows, (flags, up_keep, up_received, x_half))
         )
         if final:
             climbed = (up, swapped(up, cross))
@@ -501,9 +515,8 @@
         send, keep, acc_next, g_half = run(
             functools.partial(backward_kernel, t == 0),
             halves + (scores_shape, half_rows),
-            (place,) + g_parts + (stashed[t], probs, weights, wo) + acc,
-            scratch=[pltpu.VMEM((3, tokens, inner), BF16), row_scratch],
-            scalars=1,
+            (flags,) + g_parts + (stashed[t], probs, weights, wo) + acc,
+            scratch=[pltpu.VMEM((3, tokens, inner), BF16)],
         )
         acc = (acc_next,)
         received = swapped(send, 1)
@@ -513,14 +526,15 @@
     rows = shape((1, tokens, model_width))
     fallen = down_term(TICKS - 1, keep, received, g_half)
     fallen_other = swapped(fallen, cross)
-    rising_out = run(join_kernel, rows, (place, x_mine, x_other), scalars=1)
-    table_grad = run(
+    token = shape((8, LANES), F32)
+    rising_out, _ = run(join_kernel, (rows, token), (flags, x_mine, x_other))
+    table_grad, _ = run(
         functools.partial(table_kernel, bias_table.shape[1]),
-        shape((heads, bias_table.shape[1]), F32),
+        (shape((heads, bias_table.shape[1]), F32), token),
         acc + (buckets,),
     )
     lowered = run(pair_kernel, half_rows, (fallen, fallen_other))
-    falling_out = run(join_kernel, rows, (place, lowered, swapped(lowered, 1)), scalars=1)
+    falling_out, _ = run(join_kernel, (rows, token), (flags, lowered, swapped(lowered, 1)))
     return (rising_out, falling_out, table_grad.T[None])
 
 

time: 97.5 us -> 91 us (0.933)
  Pallas kernels: 67.6 us -> 60.5 us
  waiting for transfers between devices: 4.49 us -> 5.49 us
    pallas_call x25 -> x26, Pallas kernels: 54.7 us -> 47.1 us  [__call__(): pl.pallas_call(body, out_shape=outs, in_specs=[WHOLE] * count + [UNREAD]...]
    ppermute x16, waiting for transfers between devices: 3.41 us -> 5.47 us  [swapped(): lax.ppermute(block, 'head', [(i, i ^ bit) for i in range(lax.axis_size('h...]
    ppermute x8, waiting for transfers between devices: 1.08 us -> 0.02 us  [moved(): return lax.ppermute(block, ('section', 'head'), route)]
    unnamed x18 -> x12, local copies, waits for them, and re-layouts: 1.68 us -> 0.68 us
  transfers between devices with their start and end apart: 24 -> 24, of which waited for: 6 -> 6; matrix products, arithmetic and copies ran while one was open for 0% -> 0% of each run, Pallas kernels for 52% -> 49%
where the time goes in v6:
time: 91 us; the launch traced here: 90.8 us
  Pallas kernels  60.5 us (66%)
  starting transfers between devices  23 us (25%)
  waiting for transfers between devices  5.49 us (6%)
  between operations  0.99 us (1%)
    pallas_call x26, Pallas kernels, __call__(): pl.pallas_call(body, out_shape=outs, in_specs=[WHOLE] * count + [UNREAD]...  47.1 us
    ppermute x8, starting transfers between devices, moved(): return lax.ppermute(block, ('section', 'head'), route)  15.3 us
    pallas_call x1, Pallas kernels, per_device(): pl.pallas_call(relayout_kernel, grid=(3, blocks), out_shape=(pltpu.VMEM((...  13.4 us
    ppermute x16, starting transfers between devices, swapped(): lax.ppermute(block, 'head', [(i, i ^ bit) for i in range(lax.axis_size('h...  7.69 us
    ppermute x16, waiting for transfers between devices, swapped(): lax.ppermute(block, 'head', [(i, i ^ bit) for i in range(lax.axis_size('h...  5.47 us
  transfers between devices with their start and end apart: 24, of which 6 were waited for; matrix products, arithmetic and copies ran while one was open for 0% of the time, Pallas kernels for 49%

profile of v6, /device:TPU:0, one launch (start us, length us, event | category | flops | bytes accessed | tf_op | source)
XLA Modules:
  0.0 90.8 jit_solution(10524047529341768311)
XLA Ops:
  0.8 0.7 copy-done.5
  1.5 13.4 %shard_map.121 = (bf16[3,1024,2048]{2,1,0:T(8,128)(2,1)S(1)}, bf16[3,128,2048]{2,1,0:T(8,128)(2,1)S(1)}, bf16[3,128,2048]{2,1,0:T(8,128)(2,1)S(1)}, f32[16,128,1...) custom-call(s32[6]{0:T(128)S(1)} %copy-done.5, bf16[1,128,1024]{2,1,0:T(8,128)(2,1)} %refs_1_.4, ...), custom_call_target="tpu_custom_call" | custom-call | bytes 12582912 | tf_op jit(solution)/shard_map/pallas_call | solution.py:399
  14.8 1.7 %shard_map.122 = (bf16[64,1024]{1,0:T(8,128)(2,1)S(1)}, f32[64,1024]{1,0:T(8,128)S(1)}, bf16[64,1024]{1,0:T(8,128)(2,1)S(1)}) custom-call(f32[4,128]{1,0:T(4,128)S(1)} %broadcast_in_dim.4._.refs_0_, bf16[1,128,1024]{2,1,0:T(8,128)(2,1)S(1)} %copy-done.1, bf16[3,128,2048]{2,1,0:T(8,128)(2,1)S(1)} %get-tuple-element.35.refs_2_.refs_5_, ...), custom_call_target="tpu_custom_call" | custom-call | bytes 128 | tf_op jit(solution)/shard_map/pallas_call | solution.py:339
  17.1 0.8 shard_map.123.refs_4_.refs_3_
  18.1 3.0 %collective-permute-start.1 = (bf16[64,1024]{1,0:T(8,128)(2,1)S(1)}, bf16[64,1024]{1,0:T(8,128)(2,1)S(1)}, u32[]{:S(2)}, u32[]{:S(2)}) collective-permute-start(bf16[64,1024]{1,0:T(8,128)(2,1)S(1)} %shard_map.124.refs_6_.refs_1_), channel_id=1, source_target_pairs={{0,4},{1,5},{2,6},{3,7},{4,8},{5,9},{6,10},{7,11},{8,12},{9,13},{1... | collective-permute-start | bytes 393224 | tf_op jit(solution)/shard_map/ppermute | solution.py:363
  21.1 2.5 %collective-permute-start.2 = (bf16[64,1024]{1,0:T(8,128)(2,1)S(1)}, bf16[64,1024]{1,0:T(8,128)(2,1)S(1)}, u32[]{:S(2)}, u32[]{:S(2)}) collective-permute-start(bf16[64,1024]{1,0:T(8,128)(2,1)S(1)} %shard_map.124.refs_6_.refs_1_), channel_id=1, source_target_pairs={{0,6},{1,7},{2,4},{3,5},{4,10},{5,11},{6,8},{7,9},{8,14},{9,15},{1... | collective-permute-start | bytes 393224 | tf_op jit(solution)/shard_map/ppermute | solution.py:363
  23.6 8.8 %shard_map.125 = (bf16[64,1024]{1,0:T(8,128)(2,1)S(1)}, f32[64,1024]{1,0:T(8,128)S(1)}, f32[16,128,128]{2,1,0:T(8,128)S(1)}, bf16[64,1024]{1,0:T(8,128)(2,1)S(1)}) custom-call(f32[4,128]{1,0:T(4,128)S(1)} %broadcast_in_dim.4._.refs_0_, bf16[128,1024]{1,0:T(8,128)(2,1)S(1)} %bitcast.23, bf16[3,128,2048]{2,1,0:T(8,128)(2,1)S(1)} %get-tuple-element.41.refs_0_.refs_2_, ...), custom_call_target="tpu_custom_call" | custom-call | bytes 128 | tf_op jit(solution)/shard_map/pallas_call | solution.py:339
  34.0 2.3 %collective-permute-start.7 = (bf16[64,1024]{1,0:T(8,128)(2,1)S(1)}, bf16[64,1024]{1,0:T(8,128)(2,1)S(1)}, u32[]{:S(2)}, u32[]{:S(2)}) collective-permute-start(bf16[64,1024]{1,0:T(8,128)(2,1)S(1)} %shard_map.127.refs_8_), channel_id=1, source_target_pairs={{0,12},{1,13},{2,14},{3,15},{4,0},{5,1},{6,2},{7,3},{8,4},{9,5},{1... | collective-permute-start | bytes 393224 | tf_op jit(solution)/shard_map/ppermute | solution.py:363
  36.3 1.2 %collective-permute-start.8 = (bf16[64,1024]{1,0:T(8,128)(2,1)S(1)}, bf16[64,1024]{1,0:T(8,128)(2,1)S(1)}, u32[]{:S(2)}, u32[]{:S(2)}) collective-permute-start(bf16[64,1024]{1,0:T(8,128)(2,1)S(1)} %shard_map.127.refs_8_), channel_id=1, source_target_pairs={{0,14},{1,15},{2,12},{3,13},{4,2},{5,3},{6,0},{7,1},{8,6},{9,7},{1... | collective-permute-start | bytes 393224 | tf_op jit(solution)/shard_map/ppermute | solution.py:363
  37.5 3.6 %shard_map.128 = (bf16[64,1024]{1,0:T(8,128)(2,1)S(1)}, f32[64,1024]{1,0:T(8,128)S(1)}, bf16[64,1024]{1,0:T(8,128)(2,1)S(1)}) custom-call(f32[4,128]{1,0:T(4,128)S(1)} %broadcast_in_dim.4._.refs_0_, bf16[64,1024]{1,0:T(8,128)(2,1)S(1)} %shard_map.126.refs_6_.refs_1_, bf16[64,1024]{1,0:T(8,128)(2,1)S(1)} %collective-permute-done.3.refs_2_, ...), custom_call_target="tpu_custom_call" | custom-call | bytes 128 | tf_op jit(solution)/shard_map/pallas_call | solution.py:339
  41.2 2.6 %shard_map.129.refs_0_.refs_2_.refs_3_ = bf16[3,128,2048]{2,1,0:T(8,128)(2,1)S(1)} custom-call(bf16[3,128,1024]{2,1,0:T(8,128)(2,1)S(1)} %bitcast.19, f32[1,1024]{1,0:T(1,128)S(1)} %copy-done.4, bf16[3,1024,2048]{2,1,0:T(8,128)(2,1)S(1)} %get-tuple-element.42.refs_4_.refs_5_.refs_2_, bf16[64,1024]{1,0:T(8,128)(2,1)S(1)} %get-tuple-element.49.refs_3_), custom_call_target="tpu_custom_call" | custom-call | bytes 128 | tf_op jit(solution)/shard_map/pallas_call | solution.py:339
  43.8 0.8 shard_map.130.refs_5_.refs_4_
  44.7 0.6 collective-permute-start.11
  45.3 1.8 %collective-permute-start.10 = (bf16[64,1024]{1,0:T(8,128)(2,1)S(1)}, bf16[64,1024]{1,0:T(8,128)(2,1)S(1)}, u32[]{:S(2)}, u32[]{:S(2)}) collective-permute-start(bf16[64,1024]{1,0:T(8,128)(2,1)S(1)} %shard_map.132.refs_8_.refs_1_), channel_id=1, source_target_pairs={{0,6},{1,7},{2,4},{3,5},{4,10},{5,11},{6,8},{7,9},{8,14},{9,15},{1... | collective-permute-start | bytes 393224 | tf_op jit(solution)/shard_map/ppermute | solution.py:363
  47.1 8.8 %shard_map.133 = (bf16[64,1024]{1,0:T(8,128)(2,1)S(1)}, f32[64,1024]{1,0:T(8,128)S(1)}, f32[16,128,128]{2,1,0:T(8,128)S(1)}, bf16[64,1024]{1,0:T(8,128)(2,1)S(1)}) custom-call(f32[4,128]{1,0:T(4,128)S(1)} %broadcast_in_dim.4._.refs_0_, bf16[64,1024]{1,0:T(8,128)(2,1)S(1)} %shard_map.131.refs_4_.refs_1_, ...), custom_call_target="tpu_custom_call" | custom-call | bytes 128 | tf_op jit(solution)/shard_map/pallas_call | solution.py:339
  56.6 1.3 %collective-permute-start.15 = (bf16[64,1024]{1,0:T(8,128)(2,1)S(1)}, bf16[64,1024]{1,0:T(8,128)(2,1)S(1)}, u32[]{:S(2)}, u32[]{:S(2)}) collective-permute-start(bf16[64,1024]{1,0:T(8,128)(2,1)S(1)} %shard_map.132.refs_8_.refs_1_), channel_id=1, source_target_pairs={{0,2},{1,3},{2,0},{3,1},{4,6},{5,7},{6,4},{7,5},{8,10},{9,11},{10,... | collective-permute-start | bytes 393224 | tf_op jit(solution)/shard_map/ppermute | solution.py:367
  58.1 3.9 %collective-permute-start.16 = (bf16[64,1024]{1,0:T(8,128)(2,1)S(1)}, bf16[64,1024]{1,0:T(8,128)(2,1)S(1)}, u32[]{:S(2)}, u32[]{:S(2)}) collective-permute-start(bf16[64,1024]{1,0:T(8,128)(2,1)S(1)} %shard_map.135.refs_8_), channel_id=1, source_target_pairs={{0,12},{1,13},{2,14},{3,15},{4,0},{5,1},{6,2},{7,3},{8,4},{9,5},{1... | collective-permute-start | bytes 393224 | tf_op jit(solution)/shard_map/ppermute | solution.py:363
  62.0 0.6 collective-permute-start.17
  62.6 3.6 %shard_map.136 = (bf16[64,1024]{1,0:T(8,128)(2,1)S(1)}, f32[64,1024]{1,0:T(8,128)S(1)}, bf16[64,1024]{1,0:T(8,128)(2,1)S(1)}) custom-call(f32[4,128]{1,0:T(4,128)S(1)} %broadcast_in_dim.4._.refs_0_, bf16[64,1024]{1,0:T(8,128)(2,1)S(1)} %shard_map.134.refs_6_.refs_1_, bf16[64,1024]{1,0:T(8,128)(2,1)S(1)} %collective-permute-done.12.refs_2_, ...), custom_call_target="tpu_custom_call" | custom-call | bytes 128 | tf_op jit(solution)/shard_map/pallas_call | solution.py:339
  66.2 2.6 %shard_map.137.refs_0_.refs_2_.refs_3_ = bf16[3,128,2048]{2,1,0:T(8,128)(2,1)S(1)} custom-call(bf16[3,128,1024]{2,1,0:T(8,128)(2,1)S(1)} %bitcast.21, f32[1,1024]{1,0:T(1,128)S(1)} %copy-done.4, bf16[3,1024,2048]{2,1,0:T(8,128)(2,1)S(1)} %get-tuple-element.42.refs_4_.refs_5_.refs_2_, bf16[64,1024]{1,0:T(8,128)(2,1)S(1)} %get-tuple-element.56.refs_3_), custom_call_target="tpu_custom_call" | custom-call | bytes 128 | tf_op jit(solution)/shard_map/pallas_call | solution.py:339
  68.8 0.8 shard_map.138.refs_5_.refs_4_
  70.3 0.7 collective-permute-done.14.refs_2_
  71.1 1.4 %collective-permute-start.18 = (bf16[64,1024]{1,0:T(8,128)(2,1)S(1)}, bf16[64,1024]{1,0:T(8,128)(2,1)S(1)}, u32[]{:S(2)}, u32[]{:S(2)}) collective-permute-start(bf16[64,1024]{1,0:T(8,128)(2,1)S(1)} %shard_map.140.refs_8_.refs_0_), channel_id=1, source_target_pairs={{0,2},{1,3},{2,0},{3,1},{4,6},{5,7},{6,4},{7,5},{8,10},{9,11},{10,... | collective-permute-start | bytes 393224 | tf_op jit(solution)/shard_map/ppermute | solution.py:367
  72.4 8.8 %shard_map.141 = (bf16[64,1024]{1,0:T(8,128)(2,1)S(1)}, f32[64,1024]{1,0:T(8,128)S(1)}, f32[16,128,128]{2,1,0:T(8,128)S(1)}, bf16[64,1024]{1,0:T(8,128)(2,1)S(1)}) custom-call(f32[4,128]{1,0:T(4,128)S(1)} %broadcast_in_dim.4._.refs_0_, bf16[64,1024]{1,0:T(8,128)(2,1)S(1)} %shard_map.139.refs_4_.refs_1_, ...), custom_call_target="tpu_custom_call" | custom-call | bytes 128 | tf_op jit(solution)/shard_map/pallas_call | solution.py:339
  81.4 0.5 collective-permute-start.20
  82.0 0.7 collective-permute-done.21.refs_4_
  82.9 0.8 collective-permute-start.22
  83.7 0.8 shard_map.144
  84.5 1.7 %shard_map.145 = (f32[16,32]{1,0:T(8,128)}, f32[8,128]{1,0:T(8,128)S(1)}) custom-call(f32[16,128,128]{2,1,0:T(8,128)S(1)} %get-tuple-element.62.refs_0_, s32[128,128]{1,0:T(8,128)S(1)} %copy-done.3, f32[8,128]{1,0:T(8,128)S(1)} %get-tuple-element.63.refs_2_), custom_call_target="tpu_custom_call" | custom-call | bytes 128 | tf_op jit(solution)/shard_map/pallas_call | solution.py:339
  86.1 2.4 %collective-permute-done.22.refs_1_ = bf16[64,1024]{1,0:T(8,128)(2,1)S(1)} collective-permute-done((bf16[64,1024]{1,0:T(8,128)(2,1)S(1)}, bf16[64,1024]{1,0:T(8,128)(2,1)S(1)}, u32[]{:S(2)}, u32[]{:S(2)}) %collective-permute-start.22) | collective-permute-done | bytes 131104 | tf_op jit(solution)/shard_map/ppermute | solution.py:367
  88.6 1.3 %collective-permute-done.23.refs_2_ = bf16[64,1024]{1,0:T(8,128)(2,1)S(1)} collective-permute-done((bf16[64,1024]{1,0:T(8,128)(2,1)S(1)}, bf16[64,1024]{1,0:T(8,128)(2,1)S(1)}, u32[]{:S(2)}, u32[]{:S(2)}) %collective-permute-start.23) | collective-permute-done | bytes 131104 | tf_op jit(solution)/shard_map/ppermute | solution.py:367
  90.0 0.8 shard_map.147
  (57 shorter events, 4.9 us)
Async XLA Ops:
  0.8 0.7 copy-start.5
  1.5 13.4 %copy-start.1 = (bf16[1,128,1024]{2,1,0:T(8,128)(2,1)S(1)}, bf16[1,128,1024]{2,1,0:T(8,128)(2,1)}, u32[]{:S(2)}) copy-start(bf16[1,128,1024]{2,1,0:T(8,128)(2,1)} %refs_1_.4) | copy-start | bytes 786436
  16.5 1.5 %collective-permute-start = (bf16[64,1024]{1,0:T(8,128)(2,1)S(1)}, bf16[64,1024]{1,0:T(8,128)(2,1)S(1)}, u32[]{:S(2)}, u32[]{:S(2)}) collective-permute-start(bf16[64,1024]{1,0:T(8,128)(2,1)S(1)} %get-tuple-element.39), channel_id=1, source_target_pairs={{0,1},{1,0},{2,3},{3,2},{4,5},{5,4},{6,7},{7,6},{8,9},{9,8},{10,11... | collective-permute-start | bytes 393224 | tf_op jit(solution)/shard_map/ppermute | solution.py:367
  17.9 5.8 %copy-start.2 = (bf16[1,128,1024]{2,1,0:T(8,128)(2,1)S(1)}, bf16[1,128,1024]{2,1,0:T(8,128)(2,1)}, u32[]{:S(2)}) copy-start(bf16[1,128,1024]{2,1,0:T(8,128)(2,1)} %param.11) | copy-start | bytes 786436
  18.1 14.4 %collective-permute-start.1 = (bf16[64,1024]{1,0:T(8,128)(2,1)S(1)}, bf16[64,1024]{1,0:T(8,128)(2,1)S(1)}, u32[]{:S(2)}, u32[]{:S(2)}) collective-permute-start(bf16[64,1024]{1,0:T(8,128)(2,1)S(1)} %shard_map.124.refs_6_.refs_1_), channel_id=1, source_target_pairs={{0,4},{1,5},{2,6},{3,7},{4,8},{5,9},{6,10},{7,11},{8,12},{9,13},{1... | collective-permute-start | bytes 393224 | tf_op jit(solution)/shard_map/ppermute | solution.py:363
  21.1 11.4 %collective-permute-start.2 = (bf16[64,1024]{1,0:T(8,128)(2,1)S(1)}, bf16[64,1024]{1,0:T(8,128)(2,1)S(1)}, u32[]{:S(2)}, u32[]{:S(2)}) collective-permute-start(bf16[64,1024]{1,0:T(8,128)(2,1)S(1)} %shard_map.124.refs_6_.refs_1_), channel_id=1, source_target_pairs={{0,6},{1,7},{2,4},{3,5},{4,10},{5,11},{6,8},{7,9},{8,14},{9,15},{1... | collective-permute-start | bytes 393224 | tf_op jit(solution)/shard_map/ppermute | solution.py:363
  23.6 10.2 %copy-start = (bf16[1,3,128,1024]{3,2,1,0:T(8,128)(2,1)S(1)}, bf16[1,3,128,1024]{3,2,1,0:T(8,128)(2,1)}, u32[]{:S(2)}) copy-start(bf16[1,3,128,1024]{3,2,1,0:T(8,128)(2,1)} %kept_ref.1) | copy-start | bytes 2359300
  23.6 10.2 %copy-start.4 = (f32[1,1024]{1,0:T(1,128)S(1)}, f32[1,1024]{1,0:T(1,128)}, u32[]{:S(2)}) copy-start(f32[1,1024]{1,0:T(1,128)} %refs_2_.5) | copy-start | bytes 12292
  32.4 1.4 %collective-permute-start.4 = (bf16[64,1024]{1,0:T(8,128)(2,1)S(1)}, bf16[64,1024]{1,0:T(8,128)(2,1)S(1)}, u32[]{:S(2)}, u32[]{:S(2)}) collective-permute-start(bf16[64,1024]{1,0:T(8,128)(2,1)S(1)} %get-tuple-element.46), channel_id=1, source_target_pairs={{0,1},{1,0},{2,3},{3,2},{4,5},{5,4},{6,7},{7,6},{8,9},{9,8},{10,11... | collective-permute-start | bytes 393224 | tf_op jit(solution)/shard_map/ppermute | solution.py:367
  32.6 5.0 %collective-permute-start.3 = (bf16[64,1024]{1,0:T(8,128)(2,1)S(1)}, bf16[64,1024]{1,0:T(8,128)(2,1)S(1)}, u32[]{:S(2)}, u32[]{:S(2)}) collective-permute-start(bf16[64,1024]{1,0:T(8,128)(2,1)S(1)} %shard_map.126.refs_6_.refs_1_), channel_id=1, source_target_pairs={{0,1},{1,0},{2,3},{3,2},{4,5},{5,4},{6,7},{7,6},{8,9},{9,8},{10,11... | collective-permute-start | bytes 393224 | tf_op jit(solution)/shard_map/ppermute | solution.py:367
  33.1 11.5 %collective-permute-start.6 = (bf16[64,1024]{1,0:T(8,128)(2,1)S(1)}, bf16[64,1024]{1,0:T(8,128)(2,1)S(1)}, u32[]{:S(2)}, u32[]{:S(2)}) collective-permute-start(bf16[64,1024]{1,0:T(8,128)(2,1)S(1)} %shard_map.124.refs_6_.refs_1_), channel_id=1, source_target_pairs={{0,2},{1,3},{2,0},{3,1},{4,6},{5,7},{6,4},{7,5},{8,10},{9,11},{10,... | collective-permute-start | bytes 393224 | tf_op jit(solution)/shard_map/ppermute | solution.py:367
  34.0 10.5 %collective-permute-start.7 = (bf16[64,1024]{1,0:T(8,128)(2,1)S(1)}, bf16[64,1024]{1,0:T(8,128)(2,1)S(1)}, u32[]{:S(2)}, u32[]{:S(2)}) collective-permute-start(bf16[64,1024]{1,0:T(8,128)(2,1)S(1)} %shard_map.127.refs_8_), channel_id=1, source_target_pairs={{0,12},{1,13},{2,14},{3,15},{4,0},{5,1},{6,2},{7,3},{8,4},{9,5},{1... | collective-permute-start | bytes 393224 | tf_op jit(solution)/shard_map/ppermute | solution.py:363
  36.3 8.3 %collective-permute-start.8 = (bf16[64,1024]{1,0:T(8,128)(2,1)S(1)}, bf16[64,1024]{1,0:T(8,128)(2,1)S(1)}, u32[]{:S(2)}, u32[]{:S(2)}) collective-permute-start(bf16[64,1024]{1,0:T(8,128)(2,1)S(1)} %shard_map.127.refs_8_), channel_id=1, source_target_pairs={{0,14},{1,15},{2,12},{3,13},{4,2},{5,3},{6,0},{7,1},{8,6},{9,7},{1... | collective-permute-start | bytes 393224 | tf_op jit(solution)/shard_map/ppermute | solution.py:363
  41.1 4.2 %collective-permute-start.5 = (bf16[64,1024]{1,0:T(8,128)(2,1)S(1)}, bf16[64,1024]{1,0:T(8,128)(2,1)S(1)}, u32[]{:S(2)}, u32[]{:S(2)}) collective-permute-start(bf16[64,1024]{1,0:T(8,128)(2,1)S(1)} %get-tuple-element.48), channel_id=1, source_target_pairs={{0,1},{1,0},{2,3},{3,2},{4,5},{5,4},{6,7},{7,6},{8,9},{9,8},{10,11... | collective-permute-start | bytes 393224 | tf_op jit(solution)/shard_map/ppermute | solution.py:367
  44.7 2.4 %collective-permute-start.11 = (bf16[64,1024]{1,0:T(8,128)(2,1)S(1)}, bf16[64,1024]{1,0:T(8,128)(2,1)S(1)}, u32[]{:S(2)}, u32[]{:S(2)}) collective-permute-start(bf16[64,1024]{1,0:T(8,128)(2,1)S(1)} %shard_map.131.refs_4_.refs_1_), channel_id=1, source_target_pairs={{0,1},{1,0},{2,3},{3,2},{4,5},{5,4},{6,7},{7,6},{8,9},{9,8},{10,11... | collective-permute-start | bytes 393224 | tf_op jit(solution)/shard_map/ppermute | solution.py:367
  45.3 10.7 %collective-permute-start.10 = (bf16[64,1024]{1,0:T(8,128)(2,1)S(1)}, bf16[64,1024]{1,0:T(8,128)(2,1)S(1)}, u32[]{:S(2)}, u32[]{:S(2)}) collective-permute-start(bf16[64,1024]{1,0:T(8,128)(2,1)S(1)} %shard_map.132.refs_8_.refs_1_), channel_id=1, source_target_pairs={{0,6},{1,7},{2,4},{3,5},{4,10},{5,11},{6,8},{7,9},{8,14},{9,15},{1... | collective-permute-start | bytes 393224 | tf_op jit(solution)/shard_map/ppermute | solution.py:363
  47.1 8.9 %collective-permute-start.9 = (bf16[64,1024]{1,0:T(8,128)(2,1)S(1)}, bf16[64,1024]{1,0:T(8,128)(2,1)S(1)}, u32[]{:S(2)}, u32[]{:S(2)}) collective-permute-start(bf16[64,1024]{1,0:T(8,128)(2,1)S(1)} %shard_map.132.refs_8_.refs_1_), channel_id=1, source_target_pairs={{0,4},{1,5},{2,6},{3,7},{4,8},{5,9},{6,10},{7,11},{8,12},{9,13},{1... | collective-permute-start | bytes 393224 | tf_op jit(solution)/shard_map/ppermute | solution.py:363
  55.9 2.0 %collective-permute-start.13 = (bf16[64,1024]{1,0:T(8,128)(2,1)S(1)}, bf16[64,1024]{1,0:T(8,128)(2,1)S(1)}, u32[]{:S(2)}, u32[]{:S(2)}) collective-permute-start(bf16[64,1024]{1,0:T(8,128)(2,1)S(1)} %get-tuple-element.53), channel_id=1, source_target_pairs={{0,1},{1,0},{2,3},{3,2},{4,5},{5,4},{6,7},{7,6},{8,9},{9,8},{10,11... | collective-permute-start | bytes 393224 | tf_op jit(solution)/shard_map/ppermute | solution.py:367
  56.1 6.6 %collective-permute-start.12 = (bf16[64,1024]{1,0:T(8,128)(2,1)S(1)}, bf16[64,1024]{1,0:T(8,128)(2,1)S(1)}, u32[]{:S(2)}, u32[]{:S(2)}) collective-permute-start(bf16[64,1024]{1,0:T(8,128)(2,1)S(1)} %shard_map.134.refs_6_.refs_1_), channel_id=1, source_target_pairs={{0,1},{1,0},{2,3},{3,2},{4,5},{5,4},{6,7},{7,6},{8,9},{9,8},{10,11... | collective-permute-start | bytes 393224 | tf_op jit(solution)/shard_map/ppermute | solution.py:367
  56.6 13.0 %collective-permute-start.15 = (bf16[64,1024]{1,0:T(8,128)(2,1)S(1)}, bf16[64,1024]{1,0:T(8,128)(2,1)S(1)}, u32[]{:S(2)}, u32[]{:S(2)}) collective-permute-start(bf16[64,1024]{1,0:T(8,128)(2,1)S(1)} %shard_map.132.refs_8_.refs_1_), channel_id=1, source_target_pairs={{0,2},{1,3},{2,0},{3,1},{4,6},{5,7},{6,4},{7,5},{8,10},{9,11},{10,... | collective-permute-start | bytes 393224 | tf_op jit(solution)/shard_map/ppermute | solution.py:367
  58.1 11.5 %collective-permute-start.16 = (bf16[64,1024]{1,0:T(8,128)(2,1)S(1)}, bf16[64,1024]{1,0:T(8,128)(2,1)S(1)}, u32[]{:S(2)}, u32[]{:S(2)}) collective-permute-start(bf16[64,1024]{1,0:T(8,128)(2,1)S(1)} %shard_map.135.refs_8_), channel_id=1, source_target_pairs={{0,12},{1,13},{2,14},{3,15},{4,0},{5,1},{6,2},{7,3},{8,4},{9,5},{1... | collective-permute-start | bytes 393224 | tf_op jit(solution)/shard_map/ppermute | solution.py:363
  62.0 7.7 %collective-permute-start.17 = (bf16[64,1024]{1,0:T(8,128)(2,1)S(1)}, bf16[64,1024]{1,0:T(8,128)(2,1)S(1)}, u32[]{:S(2)}, u32[]{:S(2)}) collective-permute-start(bf16[64,1024]{1,0:T(8,128)(2,1)S(1)} %shard_map.135.refs_8_), channel_id=1, source_target_pairs={{0,14},{1,15},{2,12},{3,13},{4,2},{5,3},{6,0},{7,1},{8,6},{9,7},{1... | collective-permute-start | bytes 393224 | tf_op jit(solution)/shard_map/ppermute | solution.py:363
  69.6 1.4 %collective-permute-start.14 = (bf16[64,1024]{1,0:T(8,128)(2,1)S(1)}, bf16[64,1024]{1,0:T(8,128)(2,1)S(1)}, u32[]{:S(2)}, u32[]{:S(2)}) collective-permute-start(bf16[64,1024]{1,0:T(8,128)(2,1)S(1)} %get-tuple-element.55), channel_id=1, source_target_pairs={{0,1},{1,0},{2,3},{3,2},{4,5},{5,4},{6,7},{7,6},{8,9},{9,8},{10,11... | collective-permute-start | bytes 393224 | tf_op jit(solution)/shard_map/ppermute | solution.py:367
  69.8 2.6 %collective-permute-start.19 = (bf16[64,1024]{1,0:T(8,128)(2,1)S(1)}, bf16[64,1024]{1,0:T(8,128)(2,1)S(1)}, u32[]{:S(2)}, u32[]{:S(2)}) collective-permute-start(bf16[64,1024]{1,0:T(8,128)(2,1)S(1)} %shard_map.139.refs_4_.refs_1_), channel_id=1, source_target_pairs={{0,1},{1,0},{2,3},{3,2},{4,5},{5,4},{6,7},{7,6},{8,9},{9,8},{10,11... | collective-permute-start | bytes 393224 | tf_op jit(solution)/shard_map/ppermute | solution.py:367
  71.1 10.3 %collective-permute-start.18 = (bf16[64,1024]{1,0:T(8,128)(2,1)S(1)}, bf16[64,1024]{1,0:T(8,128)(2,1)S(1)}, u32[]{:S(2)}, u32[]{:S(2)}) collective-permute-start(bf16[64,1024]{1,0:T(8,128)(2,1)S(1)} %shard_map.140.refs_8_.refs_0_), channel_id=1, source_target_pairs={{0,2},{1,3},{2,0},{3,1},{4,6},{5,7},{6,4},{7,5},{8,10},{9,11},{10,... | collective-permute-start | bytes 393224 | tf_op jit(solution)/shard_map/ppermute | solution.py:367
  81.3 3.2 %copy-start.3 = (s32[128,128]{1,0:T(8,128)S(1)}, s32[128,128]{1,0:T(8,128)}, u32[]{:S(2)}) copy-start(s32[128,128]{1,0:T(8,128)} %refs_1_.7) | copy-start | bytes 196612
  81.3 1.4 %collective-permute-start.21 = (bf16[64,1024]{1,0:T(8,128)(2,1)S(1)}, bf16[64,1024]{1,0:T(8,128)(2,1)S(1)}, u32[]{:S(2)}, u32[]{:S(2)}) collective-permute-start(bf16[64,1024]{1,0:T(8,128)(2,1)S(1)} %get-tuple-element.60), channel_id=1, source_target_pairs={{0,1},{1,0},{2,3},{3,2},{4,5},{5,4},{6,7},{7,6},{8,9},{9,8},{10,11... | collective-permute-start | bytes 393224 | tf_op jit(solution)/shard_map/ppermute | solution.py:367
  81.4 2.3 %collective-permute-start.20 = (bf16[64,1024]{1,0:T(8,128)(2,1)S(1)}, bf16[64,1024]{1,0:T(8,128)(2,1)S(1)}, u32[]{:S(2)}, u32[]{:S(2)}) collective-permute-start(bf16[64,1024]{1,0:T(8,128)(2,1)S(1)} %shard_map.142.refs_6_.refs_1_), channel_id=1, source_target_pairs={{0,1},{1,0},{2,3},{3,2},{4,5},{5,4},{6,7},{7,6},{8,9},{9,8},{10,11... | collective-permute-start | bytes 393224 | tf_op jit(solution)/shard_map/ppermute | solution.py:367
  82.9 5.6 %collective-permute-start.22 = (bf16[64,1024]{1,0:T(8,128)(2,1)S(1)}, bf16[64,1024]{1,0:T(8,128)(2,1)S(1)}, u32[]{:S(2)}, u32[]{:S(2)}) collective-permute-start(bf16[64,1024]{1,0:T(8,128)(2,1)S(1)} %shard_map.143.refs_3_.refs_0_), channel_id=1, source_target_pairs={{0,2},{1,3},{2,0},{3,1},{4,6},{5,7},{6,4},{7,5},{8,10},{9,11},{10,... | collective-permute-start | bytes 393224 | tf_op jit(solution)/shard_map/ppermute | solution.py:367
  88.5 1.4 %collective-permute-start.23 = (bf16[64,1024]{1,0:T(8,128)(2,1)S(1)}, bf16[64,1024]{1,0:T(8,128)(2,1)S(1)}, u32[]{:S(2)}, u32[]{:S(2)}) collective-permute-start(bf16[64,1024]{1,0:T(8,128)(2,1)S(1)} %shard_map.146.refs_1_.refs_3_), channel_id=1, source_target_pairs={{0,1},{1,0},{2,3},{3,2},{4,5},{5,4},{6,7},{7,6},{8,9},{9,8},{10,11... | collective-permute-start | bytes 393224 | tf_op jit(solution)/shard_map/ppermute | solution.py:367

commit v7 on v6

--- a/solution.py
+++ b/solution.py
@@ -240,21 +240,23 @@
 def backward_kernel(first, flags_ref, *refs):
     second = flag(flags_ref, SECOND_CORE)
     if first:
-        full_ref, qkv_ref, probs_ref, w_ref, wo_ref, *refs = refs
-        send_ref, keep_ref, acc_ref, g_half_ref, stacked = refs
+        full_ref, qkv_ref, probs_ref, wo_ref, stacked, acc_ref, g_half_ref = refs
         acc_in_ref = None
         g = full_ref[...]
     else:
-        mine_ref, other_ref, qkv_ref, probs_ref, w_ref, wo_ref, acc_in_ref, *refs = refs
-        send_ref, keep_ref, acc_ref, g_half_ref, stacked = refs
+        mine_ref, other_ref, qkv_ref, probs_ref, wo_ref, acc_in_ref, *refs = refs
+        stacked, acc_ref, g_half_ref = refs
         g = joined(second, mine_ref[...], other_ref[...]).astype(BF16)
     g_half_ref[...] = own_half(second, g).astype(BF16)
     for part in range(2):
         grad_attend(g, qkv_ref, probs_ref, wo_ref, acc_in_ref, stacked, acc_ref, part)
+
+
+def input_gradient_kernel(flags_ref, stacked, w_ref, send_ref, keep_ref):
     total = dot(w_ref[0], stacked[0], LAST)
     total += dot(w_ref[1], stacked[1], LAST)
     total += dot(w_ref[2], stacked[2], LAST)
-    split_halves(second, total.T, send_ref, keep_ref)
+    split_halves(flag(flags_ref, SECOND_CORE), total.T, send_ref, keep_ref)
 
 
 def pair_kernel(first_ref, second_ref, out_ref):
@@ -278,10 +280,10 @@
     out_ref[...] = (residual * g_ref[...].astype(F32) + back).astype(BF16)
 
 
-def choose_kernel(flags_ref, own_ref, own_second_ref, first_ref, second_ref, out_ref):
-    own = own_ref[...].astype(F32) + own_second_ref[...].astype(F32)
+def choose_kernel(flags_ref, own_ref, first_ref, second_ref, out_ref):
     arrived = first_ref[...].astype(F32) + second_ref[...].astype(F32)
-    out_ref[...] = pick(flag(flags_ref, LAST_SECTION), own, arrived).astype(BF16)
+    own = flag(flags_ref, LAST_SECTION)
+    out_ref[...] = pick(own, own_ref[...], arrived).astype(BF16)
 
 
 def join_kernel(flags_ref, mine_ref, other_ref, out_ref, token_ref):
@@ -479,7 +481,7 @@
         else:
             x_other = swapped(x_mine, 1)
             fallen = down_term(t - 1, keep, received, g_half)
-            arrivals = (up, in_last, moved(fallen, -1, 0), moved(fallen, -1, cross))
+            arrivals = (lifted, moved(fallen, -1, 0), moved(fallen, -1, cross))
             args = (flags, x_mine, x_other, entering, gain, weights, bias, wo)
         up_send, up_keep, x_half = run(
             functools.partial(forward_kernel, t),
@@ -506,21 +508,18 @@
         up = but_last_bit(
             run(up_term_kernel, half_rows, (flags, up_keep, up_received, x_half))
         )
-        if final:
-            climbed = (up, swapped(up, cross))
-        else:
-            climbed = (moved(up, 1, 0), moved(up, 1, cross))
-            in_last = swapped(up, cross)
-
-        send, keep, acc_next, g_half = run(
+        up_other = swapped(up, cross)
+
+        stacked, acc_next, g_half = run(
             functools.partial(backward_kernel, t == 0),
-            halves + (scores_shape, half_rows),
-            (flags,) + g_parts + (stashed[t], probs, weights, wo) + acc,
-            scratch=[pltpu.VMEM((3, tokens, inner), BF16)],
+            (shape((3, tokens, inner)), scores_shape, half_rows),
+            (flags,) + g_parts + (stashed[t], probs, wo) + acc,
         )
         acc = (acc_next,)
+        lifted = run(pair_kernel, half_rows, (up, up_other))
+        x_mine = lifted if final else moved(lifted, 1, 0)
+        send, keep = run(input_gradient_kernel, halves, (flags, stacked, weights))
         received = swapped(send, 1)
-        x_mine = run(pair_kernel, half_rows, climbed)
 
     x_other = swapped(x_mine, 1)
     rows = shape((1, tokens, model_width))

time: 91 us -> 89.4 us (0.982)
  starting transfers between devices: 23 us -> 16.9 us
  waiting for transfers between devices: 5.49 us -> 9.8 us
    ppermute x8 -> x6, starting transfers between devices: 15.3 us -> 7.87 us  [moved(): return lax.ppermute(block, ('section', 'head'), route)]
    ppermute x8 -> x6, waiting for transfers between devices: 0.02 us -> 5.2 us  [moved(): return lax.ppermute(block, ('section', 'head'), route)]
    ppermute x16, starting transfers between devices: 7.69 us -> 9 us  [swapped(): lax.ppermute(block, 'head', [(i, i ^ bit) for i in range(lax.axis_size('h...]
    pallas_call x26 -> x29, Pallas kernels: 47.1 us -> 47.4 us  [__call__(): pl.pallas_call(body, out_shape=outs, in_specs=[WHOLE] * count + [UNREAD]...]
  transfers between devices with their start and end apart: 24 -> 22, of which waited for: 6 -> 7; matrix products, arithmetic and copies ran while one was open for 0% -> 0% of each run, Pallas kernels for 49% -> 46%
where the time goes in v7:
time: 89.4 us; the launch traced here: 89.3 us
  Pallas kernels  60.8 us (68%)
  starting transfers between devices  16.9 us (19%)
  waiting for transfers between devices  9.8 us (11%)
  between operations  0.98 us (1%)
    pallas_call x29, Pallas kernels, __call__(): pl.pallas_call(body, out_shape=outs, in_specs=[WHOLE] * count + [UNREAD]...  47.4 us
    pallas_call x1, Pallas kernels, per_device(): pl.pallas_call(relayout_kernel, grid=(3, blocks), out_shape=(pltpu.VMEM((...  13.4 us
    ppermute x16, starting transfers between devices, swapped(): lax.ppermute(block, 'head', [(i, i ^ bit) for i in range(lax.axis_size('h...  9 us
    ppermute x6, starting transfers between devices, moved(): return lax.ppermute(block, ('section', 'head'), route)  7.87 us
    ppermute x6, waiting for transfers between devices, moved(): return lax.ppermute(block, ('section', 'head'), route)  5.2 us
    ppermute x16, waiting for transfers between devices, swapped(): lax.ppermute(block, 'head', [(i, i ^ bit) for i in range(lax.axis_size('h...  4.6 us
  transfers between devices with their start and end apart: 22, of which 7 were waited for; matrix products, arithmetic and copies ran while one was open for 0% of the time, Pallas kernels for 46%

profile of v7, /device:TPU:0, one launch (start us, length us, event | category | flops | bytes accessed | tf_op | source)
XLA Modules:
  0.0 89.3 jit_solution(11298301671631237295)
XLA Ops:
  0.8 0.7 copy-done.5
  1.5 13.4 %shard_map.121 = (bf16[3,1024,2048]{2,1,0:T(8,128)(2,1)S(1)}, bf16[3,128,2048]{2,1,0:T(8,128)(2,1)S(1)}, bf16[3,128,2048]{2,1,0:T(8,128)(2,1)S(1)}, f32[16,128,1...) custom-call(s32[6]{0:T(128)S(1)} %copy-done.5, bf16[1,128,1024]{2,1,0:T(8,128)(2,1)} %refs_1_.4, ...), custom_call_target="tpu_custom_call" | custom-call | bytes 12582912 | tf_op jit(solution)/shard_map/pallas_call | solution.py:401
  14.8 1.7 %shard_map.122 = (bf16[64,1024]{1,0:T(8,128)(2,1)S(1)}, f32[64,1024]{1,0:T(8,128)S(1)}, bf16[64,1024]{1,0:T(8,128)(2,1)S(1)}) custom-call(f32[4,128]{1,0:T(4,128)S(1)} %broadcast_in_dim.4._.refs_0_, bf16[1,128,1024]{2,1,0:T(8,128)(2,1)S(1)} %copy-done.1, bf16[3,128,2048]{2,1,0:T(8,128)(2,1)S(1)} %get-tuple-element.38.refs_2_.refs_5_, ...), custom_call_target="tpu_custom_call" | custom-call | bytes 128 | tf_op jit(solution)/shard_map/pallas_call | solution.py:341
  17.1 0.8 shard_map.123.refs_4_.refs_3_
  18.1 2.9 %collective-permute-start.1 = (bf16[64,1024]{1,0:T(8,128)(2,1)S(1)}, bf16[64,1024]{1,0:T(8,128)(2,1)S(1)}, u32[]{:S(2)}, u32[]{:S(2)}) collective-permute-start(bf16[64,1024]{1,0:T(8,128)(2,1)S(1)} %shard_map.124.refs_5_.refs_0_), channel_id=1, source_target_pairs={{0,2},{1,3},{2,0},{3,1},{4,6},{5,7},{6,4},{7,5},{8,10},{9,11},{10,... | collective-permute-start | bytes 393224 | tf_op jit(solution)/shard_map/ppermute | solution.py:369
  21.0 5.4 %shard_map.125 = (bf16[3,128,2048]{2,1,0:T(8,128)(2,1)S(1)}, f32[16,128,128]{2,1,0:T(8,128)S(1)}, bf16[64,1024]{1,0:T(8,128)(2,1)S(1)}) custom-call(f32[4,128]{1,0:T(4,128)S(1)} %broadcast_in_dim.4._.refs_0_, bf16[128,1024]{1,0:T(8,128)(2,1)S(1)} %bitcast.23, bf16[3,128,2048]{2,1,0:T(8,128)(2,1)S(1)} %get-tuple-element.44.refs_0_.refs_2_, ...), custom_call_target="tpu_custom_call" | custom-call | bytes 128 | tf_op jit(solution)/shard_map/pallas_call | solution.py:341
  26.5 1.6 %collective-permute-start.2 = (bf16[64,1024]{1,0:T(8,128)(2,1)S(1)}, bf16[64,1024]{1,0:T(8,128)(2,1)S(1)}, u32[]{:S(2)}, u32[]{:S(2)}) collective-permute-start(bf16[64,1024]{1,0:T(8,128)(2,1)S(1)} %shard_map.126.refs_3_.refs_1_), channel_id=1, source_target_pairs={{0,4},{1,5},{2,6},{3,7},{4,8},{5,9},{6,10},{7,11},{8,12},{9,13},{1... | collective-permute-start | bytes 393224 | tf_op jit(solution)/shard_map/ppermute | solution.py:365
  28.1 3.5 %shard_map.127 = (bf16[64,1024]{1,0:T(8,128)(2,1)S(1)}, f32[64,1024]{1,0:T(8,128)S(1)}) custom-call(f32[4,128]{1,0:T(4,128)S(1)} %broadcast_in_dim.4._.refs_0_, bf16[3,128,2048]{2,1,0:T(8,128)(2,1)S(1)} %get-tuple-element.48.refs_1_, bf16[3,1024,2048]{2,1,0:T(8,128)(2,1)S(1)} %get-tuple-element.47.refs_2_.refs_5_, ...), custom_call_target="tpu_custom_call" | custom-call | bytes 128 | tf_op jit(solution)/shard_map/pallas_call | solution.py:341
  31.7 2.0 %collective-permute-done.2.refs_1_ = bf16[64,1024]{1,0:T(8,128)(2,1)S(1)} collective-permute-done((bf16[64,1024]{1,0:T(8,128)(2,1)S(1)}, bf16[64,1024]{1,0:T(8,128)(2,1)S(1)}, u32[]{:S(2)}, u32[]{:S(2)}) %collective-permute-start.2) | collective-permute-done | bytes 131104 | tf_op jit(solution)/shard_map/ppermute | solution.py:365
  33.9 1.8 %collective-permute-start.6 = (bf16[64,1024]{1,0:T(8,128)(2,1)S(1)}, bf16[64,1024]{1,0:T(8,128)(2,1)S(1)}, u32[]{:S(2)}, u32[]{:S(2)}) collective-permute-start(bf16[64,1024]{1,0:T(8,128)(2,1)S(1)} %shard_map.128.refs_8_), channel_id=1, source_target_pairs={{0,12},{1,13},{2,14},{3,15},{4,0},{5,1},{6,2},{7,3},{8,4},{9,5},{1... | collective-permute-start | bytes 393224 | tf_op jit(solution)/shard_map/ppermute | solution.py:365
  35.7 1.6 %collective-permute-start.7 = (bf16[64,1024]{1,0:T(8,128)(2,1)S(1)}, bf16[64,1024]{1,0:T(8,128)(2,1)S(1)}, u32[]{:S(2)}, u32[]{:S(2)}) collective-permute-start(bf16[64,1024]{1,0:T(8,128)(2,1)S(1)} %shard_map.128.refs_8_), channel_id=1, source_target_pairs={{0,14},{1,15},{2,12},{3,13},{4,2},{5,3},{6,0},{7,1},{8,6},{9,7},{1... | collective-permute-start | bytes 393224 | tf_op jit(solution)/shard_map/ppermute | solution.py:365
  37.3 3.6 %shard_map.129 = (bf16[64,1024]{1,0:T(8,128)(2,1)S(1)}, f32[64,1024]{1,0:T(8,128)S(1)}, bf16[64,1024]{1,0:T(8,128)(2,1)S(1)}) custom-call(f32[4,128]{1,0:T(4,128)S(1)} %broadcast_in_dim.4._.refs_0_, bf16[64,1024]{1,0:T(8,128)(2,1)S(1)} %collective-permute-done.2.refs_1_, bf16[64,1024]{1,0:T(8,128)(2,1)S(1)} %collective-permute-done.3.refs_2_, ...), custom_call_target="tpu_custom_call" | custom-call | bytes 128 | tf_op jit(solution)/shard_map/pallas_call | solution.py:341
  41.0 2.6 %shard_map.130.refs_0_.refs_2_.refs_3_ = bf16[3,128,2048]{2,1,0:T(8,128)(2,1)S(1)} custom-call(bf16[3,128,1024]{2,1,0:T(8,128)(2,1)S(1)} %bitcast.19, f32[1,1024]{1,0:T(1,128)S(1)} %copy-done.4, bf16[3,1024,2048]{2,1,0:T(8,128)(2,1)S(1)} %get-tuple-element.47.refs_2_.refs_5_, bf16[64,1024]{1,0:T(8,128)(2,1)S(1)} %get-tuple-element.53.refs_3_), custom_call_target="tpu_custom_call" | custom-call | bytes 128 | tf_op jit(solution)/shard_map/pallas_call | solution.py:341
  43.5 0.8 shard_map.131.refs_4_
  45.1 1.6 %collective-permute-start.8 = (bf16[64,1024]{1,0:T(8,128)(2,1)S(1)}, bf16[64,1024]{1,0:T(8,128)(2,1)S(1)}, u32[]{:S(2)}, u32[]{:S(2)}) collective-permute-start(bf16[64,1024]{1,0:T(8,128)(2,1)S(1)} %shard_map.133.refs_7_.refs_0_), channel_id=1, source_target_pairs={{0,2},{1,3},{2,0},{3,1},{4,6},{5,7},{6,4},{7,5},{8,10},{9,11},{10,... | collective-permute-start | bytes 393224 | tf_op jit(solution)/shard_map/ppermute | solution.py:369
  46.6 5.4 %shard_map.134 = (bf16[3,128,2048]{2,1,0:T(8,128)(2,1)S(1)}, f32[16,128,128]{2,1,0:T(8,128)S(1)}, bf16[64,1024]{1,0:T(8,128)(2,1)S(1)}) custom-call(f32[4,128]{1,0:T(4,128)S(1)} %broadcast_in_dim.4._.refs_0_, bf16[64,1024]{1,0:T(8,128)(2,1)S(1)} %shard_map.132.refs_4_.refs_1_, bf16[64,1024]{1,0:T(8,128)(2,1)S(1)} %collective-permute-done.9.refs_2_, ...), custom_call_target="tpu_custom_call" | custom-call | bytes 128 | tf_op jit(solution)/shard_map/pallas_call | solution.py:341
  52.5 3.5 %shard_map.136 = (bf16[64,1024]{1,0:T(8,128)(2,1)S(1)}, f32[64,1024]{1,0:T(8,128)S(1)}) custom-call(f32[4,128]{1,0:T(4,128)S(1)} %broadcast_in_dim.4._.refs_0_, bf16[3,128,2048]{2,1,0:T(8,128)(2,1)S(1)} %get-tuple-element.56.refs_1_, bf16[3,1024,2048]{2,1,0:T(8,128)(2,1)S(1)} %get-tuple-element.47.refs_2_.refs_5_, ...), custom_call_target="tpu_custom_call" | custom-call | bytes 128 | tf_op jit(solution)/shard_map/pallas_call | solution.py:341
  56.1 3.0 %collective-permute-done.10.refs_1_ = bf16[64,1024]{1,0:T(8,128)(2,1)S(1)} collective-permute-done((bf16[64,1024]{1,0:T(8,128)(2,1)S(1)}, bf16[64,1024]{1,0:T(8,128)(2,1)S(1)}, u32[]{:S(2)}, u32[]{:S(2)}) %collective-permute-start.10) | collective-permute-done | bytes 131104 | tf_op jit(solution)/shard_map/ppermute | solution.py:365
  59.3 1.8 %collective-permute-start.14 = (bf16[64,1024]{1,0:T(8,128)(2,1)S(1)}, bf16[64,1024]{1,0:T(8,128)(2,1)S(1)}, u32[]{:S(2)}, u32[]{:S(2)}) collective-permute-start(bf16[64,1024]{1,0:T(8,128)(2,1)S(1)} %shard_map.137.refs_8_), channel_id=1, source_target_pairs={{0,12},{1,13},{2,14},{3,15},{4,0},{5,1},{6,2},{7,3},{8,4},{9,5},{1... | collective-permute-start | bytes 393224 | tf_op jit(solution)/shard_map/ppermute | solution.py:365
  61.7 3.6 %shard_map.138 = (bf16[64,1024]{1,0:T(8,128)(2,1)S(1)}, f32[64,1024]{1,0:T(8,128)S(1)}, bf16[64,1024]{1,0:T(8,128)(2,1)S(1)}) custom-call(f32[4,128]{1,0:T(4,128)S(1)} %broadcast_in_dim.4._.refs_0_, bf16[64,1024]{1,0:T(8,128)(2,1)S(1)} %collective-permute-done.10.refs_1_, bf16[64,1024]{1,0:T(8,128)(2,1)S(1)} %collective-permute-done.11.refs_2_, ...), custom_call_target="tpu_custom_call" | custom-call | bytes 128 | tf_op jit(solution)/shard_map/pallas_call | solution.py:341
  65.4 2.5 %shard_map.139.refs_0_.refs_2_.refs_3_ = bf16[3,128,2048]{2,1,0:T(8,128)(2,1)S(1)} custom-call(bf16[3,128,1024]{2,1,0:T(8,128)(2,1)S(1)} %bitcast.21, f32[1,1024]{1,0:T(1,128)S(1)} %copy-done.4, bf16[3,1024,2048]{2,1,0:T(8,128)(2,1)S(1)} %get-tuple-element.47.refs_2_.refs_5_, bf16[64,1024]{1,0:T(8,128)(2,1)S(1)} %get-tuple-element.61.refs_3_), custom_call_target="tpu_custom_call" | custom-call | bytes 128 | tf_op jit(solution)/shard_map/pallas_call | solution.py:341
  67.9 0.8 shard_map.140.refs_4_
  69.5 1.3 %collective-permute-start.16 = (bf16[64,1024]{1,0:T(8,128)(2,1)S(1)}, bf16[64,1024]{1,0:T(8,128)(2,1)S(1)}, u32[]{:S(2)}, u32[]{:S(2)}) collective-permute-start(bf16[64,1024]{1,0:T(8,128)(2,1)S(1)} %shard_map.142.refs_7_.refs_0_), channel_id=1, source_target_pairs={{0,2},{1,3},{2,0},{3,1},{4,6},{5,7},{6,4},{7,5},{8,10},{9,11},{10,... | collective-permute-start | bytes 393224 | tf_op jit(solution)/shard_map/ppermute | solution.py:369
  70.8 5.4 %shard_map.143 = (bf16[3,128,2048]{2,1,0:T(8,128)(2,1)S(1)}, f32[16,128,128]{2,1,0:T(8,128)S(1)}, bf16[64,1024]{1,0:T(8,128)(2,1)S(1)}) custom-call(f32[4,128]{1,0:T(4,128)S(1)} %broadcast_in_dim.4._.refs_0_, bf16[64,1024]{1,0:T(8,128)(2,1)S(1)} %shard_map.141.refs_4_.refs_1_, bf16[64,1024]{1,0:T(8,128)(2,1)S(1)} %collective-permute-done.17.refs_2_, ...), custom_call_target="tpu_custom_call" | custom-call | bytes 128 | tf_op jit(solution)/shard_map/pallas_call | solution.py:341
  76.2 3.5 %shard_map.145 = (bf16[64,1024]{1,0:T(8,128)(2,1)S(1)}, f32[64,1024]{1,0:T(8,128)S(1)}) custom-call(f32[4,128]{1,0:T(4,128)S(1)} %broadcast_in_dim.4._.refs_0_, bf16[3,128,2048]{2,1,0:T(8,128)(2,1)S(1)} %get-tuple-element.64.refs_1_, bf16[3,1024,2048]{2,1,0:T(8,128)(2,1)S(1)} %get-tuple-element.47.refs_2_.refs_5_, ...), custom_call_target="tpu_custom_call" | custom-call | bytes 128 | tf_op jit(solution)/shard_map/pallas_call | solution.py:341
  80.3 0.8 collective-permute-done.19.refs_4_
  81.4 0.9 %collective-permute-start.20 = (bf16[64,1024]{1,0:T(8,128)(2,1)S(1)}, bf16[64,1024]{1,0:T(8,128)(2,1)S(1)}, u32[]{:S(2)}, u32[]{:S(2)}) collective-permute-start(bf16[64,1024]{1,0:T(8,128)(2,1)S(1)} %shard_map.146.refs_3_.refs_0_), channel_id=1, source_target_pairs={{0,2},{1,3},{2,0},{3,1},{4,6},{5,7},{6,4},{7,5},{8,10},{9,11},{10,... | collective-permute-start | bytes 393224 | tf_op jit(solution)/shard_map/ppermute | solution.py:369
  82.3 0.8 shard_map.147
  83.1 1.7 %shard_map.148 = (f32[16,32]{1,0:T(8,128)}, f32[8,128]{1,0:T(8,128)S(1)}) custom-call(f32[16,128,128]{2,1,0:T(8,128)S(1)} %get-tuple-element.68.refs_0_, s32[128,128]{1,0:T(8,128)S(1)} %copy-done.2, f32[8,128]{1,0:T(8,128)S(1)} %get-tuple-element.69.refs_2_), custom_call_target="tpu_custom_call" | custom-call | bytes 128 | tf_op jit(solution)/shard_map/pallas_call | solution.py:341
  84.8 2.2 %collective-permute-done.20.refs_1_ = bf16[64,1024]{1,0:T(8,128)(2,1)S(1)} collective-permute-done((bf16[64,1024]{1,0:T(8,128)(2,1)S(1)}, bf16[64,1024]{1,0:T(8,128)(2,1)S(1)}, u32[]{:S(2)}, u32[]{:S(2)}) %collective-permute-start.20) | collective-permute-done | bytes 131104 | tf_op jit(solution)/shard_map/ppermute | solution.py:369
  87.1 1.3 %collective-permute-done.21.refs_2_ = bf16[64,1024]{1,0:T(8,128)(2,1)S(1)} collective-permute-done((bf16[64,1024]{1,0:T(8,128)(2,1)S(1)}, bf16[64,1024]{1,0:T(8,128)(2,1)S(1)}, u32[]{:S(2)}, u32[]{:S(2)}) %collective-permute-start.21) | collective-permute-done | bytes 131104 | tf_op jit(solution)/shard_map/ppermute | solution.py:369
  88.4 0.8 shard_map.150
  (56 shorter events, 5.1 us)
Async XLA Ops:
  0.8 0.7 copy-start.5
  1.5 13.4 %copy-start.1 = (bf16[1,128,1024]{2,1,0:T(8,128)(2,1)S(1)}, bf16[1,128,1024]{2,1,0:T(8,128)(2,1)}, u32[]{:S(2)}) copy-start(bf16[1,128,1024]{2,1,0:T(8,128)(2,1)} %refs_1_.4) | copy-start | bytes 786436
  16.5 1.5 %collective-permute-start = (bf16[64,1024]{1,0:T(8,128)(2,1)S(1)}, bf16[64,1024]{1,0:T(8,128)(2,1)S(1)}, u32[]{:S(2)}, u32[]{:S(2)}) collective-permute-start(bf16[64,1024]{1,0:T(8,128)(2,1)S(1)} %get-tuple-element.42), channel_id=1, source_target_pairs={{0,1},{1,0},{2,3},{3,2},{4,5},{5,4},{6,7},{7,6},{8,9},{9,8},{10,11... | collective-permute-start | bytes 393224 | tf_op jit(solution)/shard_map/ppermute | solution.py:369
  17.9 3.2 %copy-start.3 = (bf16[1,128,1024]{2,1,0:T(8,128)(2,1)S(1)}, bf16[1,128,1024]{2,1,0:T(8,128)(2,1)}, u32[]{:S(2)}) copy-start(bf16[1,128,1024]{2,1,0:T(8,128)(2,1)} %param.11) | copy-start | bytes 786436
  18.1 8.3 %collective-permute-start.1 = (bf16[64,1024]{1,0:T(8,128)(2,1)S(1)}, bf16[64,1024]{1,0:T(8,128)(2,1)S(1)}, u32[]{:S(2)}, u32[]{:S(2)}) collective-permute-start(bf16[64,1024]{1,0:T(8,128)(2,1)S(1)} %shard_map.124.refs_5_.refs_0_), channel_id=1, source_target_pairs={{0,2},{1,3},{2,0},{3,1},{4,6},{5,7},{6,4},{7,5},{8,10},{9,11},{10,... | collective-permute-start | bytes 393224 | tf_op jit(solution)/shard_map/ppermute | solution.py:369
  26.5 7.2 %collective-permute-start.2 = (bf16[64,1024]{1,0:T(8,128)(2,1)S(1)}, bf16[64,1024]{1,0:T(8,128)(2,1)S(1)}, u32[]{:S(2)}, u32[]{:S(2)}) collective-permute-start(bf16[64,1024]{1,0:T(8,128)(2,1)S(1)} %shard_map.126.refs_3_.refs_1_), channel_id=1, source_target_pairs={{0,4},{1,5},{2,6},{3,7},{4,8},{5,9},{6,10},{7,11},{8,12},{9,13},{1... | collective-permute-start | bytes 393224 | tf_op jit(solution)/shard_map/ppermute | solution.py:365
  28.1 5.6 %copy-start = (bf16[1,3,128,1024]{3,2,1,0:T(8,128)(2,1)S(1)}, bf16[1,3,128,1024]{3,2,1,0:T(8,128)(2,1)}, u32[]{:S(2)}) copy-start(bf16[1,3,128,1024]{3,2,1,0:T(8,128)(2,1)} %kept_ref.1) | copy-start | bytes 2359300
  28.1 5.6 %copy-start.4 = (f32[1,1024]{1,0:T(1,128)S(1)}, f32[1,1024]{1,0:T(1,128)}, u32[]{:S(2)}) copy-start(f32[1,1024]{1,0:T(1,128)} %refs_2_.5) | copy-start | bytes 12292
  31.6 2.1 %collective-permute-start.4 = (bf16[64,1024]{1,0:T(8,128)(2,1)S(1)}, bf16[64,1024]{1,0:T(8,128)(2,1)S(1)}, u32[]{:S(2)}, u32[]{:S(2)}) collective-permute-start(bf16[64,1024]{1,0:T(8,128)(2,1)S(1)} %get-tuple-element.50), channel_id=1, source_target_pairs={{0,1},{1,0},{2,3},{3,2},{4,5},{5,4},{6,7},{7,6},{8,9},{9,8},{10,11... | collective-permute-start | bytes 393224 | tf_op jit(solution)/shard_map/ppermute | solution.py:369
  33.6 3.7 %collective-permute-start.3 = (bf16[64,1024]{1,0:T(8,128)(2,1)S(1)}, bf16[64,1024]{1,0:T(8,128)(2,1)S(1)}, u32[]{:S(2)}, u32[]{:S(2)}) collective-permute-start(bf16[64,1024]{1,0:T(8,128)(2,1)S(1)} %collective-permute-done.2.refs_1_), channel_id=1, source_target_pairs={{0,1},{1,0},{2,3},{3,2},{4,5},{5,4},{6,7},{7,6},{8,9},{9,8},{10,11... | collective-permute-start | bytes 393224 | tf_op jit(solution)/shard_map/ppermute | solution.py:369
  33.9 10.5 %collective-permute-start.6 = (bf16[64,1024]{1,0:T(8,128)(2,1)S(1)}, bf16[64,1024]{1,0:T(8,128)(2,1)S(1)}, u32[]{:S(2)}, u32[]{:S(2)}) collective-permute-start(bf16[64,1024]{1,0:T(8,128)(2,1)S(1)} %shard_map.128.refs_8_), channel_id=1, source_target_pairs={{0,12},{1,13},{2,14},{3,15},{4,0},{5,1},{6,2},{7,3},{8,4},{9,5},{1... | collective-permute-start | bytes 393224 | tf_op jit(solution)/shard_map/ppermute | solution.py:365
  35.7 8.7 %collective-permute-start.7 = (bf16[64,1024]{1,0:T(8,128)(2,1)S(1)}, bf16[64,1024]{1,0:T(8,128)(2,1)S(1)}, u32[]{:S(2)}, u32[]{:S(2)}) collective-permute-start(bf16[64,1024]{1,0:T(8,128)(2,1)S(1)} %shard_map.128.refs_8_), channel_id=1, source_target_pairs={{0,14},{1,15},{2,12},{3,13},{4,2},{5,3},{6,0},{7,1},{8,6},{9,7},{1... | collective-permute-start | bytes 393224 | tf_op jit(solution)/shard_map/ppermute | solution.py:365
  40.9 4.1 %collective-permute-start.5 = (bf16[64,1024]{1,0:T(8,128)(2,1)S(1)}, bf16[64,1024]{1,0:T(8,128)(2,1)S(1)}, u32[]{:S(2)}, u32[]{:S(2)}) collective-permute-start(bf16[64,1024]{1,0:T(8,128)(2,1)S(1)} %get-tuple-element.52), channel_id=1, source_target_pairs={{0,1},{1,0},{2,3},{3,2},{4,5},{5,4},{6,7},{7,6},{8,9},{9,8},{10,11... | collective-permute-start | bytes 393224 | tf_op jit(solution)/shard_map/ppermute | solution.py:369
  44.4 2.2 %collective-permute-start.9 = (bf16[64,1024]{1,0:T(8,128)(2,1)S(1)}, bf16[64,1024]{1,0:T(8,128)(2,1)S(1)}, u32[]{:S(2)}, u32[]{:S(2)}) collective-permute-start(bf16[64,1024]{1,0:T(8,128)(2,1)S(1)} %shard_map.132.refs_4_.refs_1_), channel_id=1, source_target_pairs={{0,1},{1,0},{2,3},{3,2},{4,5},{5,4},{6,7},{7,6},{8,9},{9,8},{10,11... | collective-permute-start | bytes 393224 | tf_op jit(solution)/shard_map/ppermute | solution.py:369
  45.1 7.0 %collective-permute-start.8 = (bf16[64,1024]{1,0:T(8,128)(2,1)S(1)}, bf16[64,1024]{1,0:T(8,128)(2,1)S(1)}, u32[]{:S(2)}, u32[]{:S(2)}) collective-permute-start(bf16[64,1024]{1,0:T(8,128)(2,1)S(1)} %shard_map.133.refs_7_.refs_0_), channel_id=1, source_target_pairs={{0,2},{1,3},{2,0},{3,1},{4,6},{5,7},{6,4},{7,5},{8,10},{9,11},{10,... | collective-permute-start | bytes 393224 | tf_op jit(solution)/shard_map/ppermute | solution.py:369
  52.1 7.0 %collective-permute-start.10 = (bf16[64,1024]{1,0:T(8,128)(2,1)S(1)}, bf16[64,1024]{1,0:T(8,128)(2,1)S(1)}, u32[]{:S(2)}, u32[]{:S(2)}) collective-permute-start(bf16[64,1024]{1,0:T(8,128)(2,1)S(1)} %shard_map.135.refs_3_.refs_1_), channel_id=1, source_target_pairs={{0,4},{1,5},{2,6},{3,7},{4,8},{5,9},{6,10},{7,11},{8,12},{9,13},{1... | collective-permute-start | bytes 393224 | tf_op jit(solution)/shard_map/ppermute | solution.py:365
  56.0 3.1 %collective-permute-start.12 = (bf16[64,1024]{1,0:T(8,128)(2,1)S(1)}, bf16[64,1024]{1,0:T(8,128)(2,1)S(1)}, u32[]{:S(2)}, u32[]{:S(2)}) collective-permute-start(bf16[64,1024]{1,0:T(8,128)(2,1)S(1)} %get-tuple-element.58), channel_id=1, source_target_pairs={{0,1},{1,0},{2,3},{3,2},{4,5},{5,4},{6,7},{7,6},{8,9},{9,8},{10,11... | collective-permute-start | bytes 393224 | tf_op jit(solution)/shard_map/ppermute | solution.py:369
  59.1 2.6 %collective-permute-start.11 = (bf16[64,1024]{1,0:T(8,128)(2,1)S(1)}, bf16[64,1024]{1,0:T(8,128)(2,1)S(1)}, u32[]{:S(2)}, u32[]{:S(2)}) collective-permute-start(bf16[64,1024]{1,0:T(8,128)(2,1)S(1)} %collective-permute-done.10.refs_1_), channel_id=1, source_target_pairs={{0,1},{1,0},{2,3},{3,2},{4,5},{5,4},{6,7},{7,6},{8,9},{9,8},{10,11... | collective-permute-start | bytes 393224 | tf_op jit(solution)/shard_map/ppermute | solution.py:369
  59.3 9.4 %collective-permute-start.14 = (bf16[64,1024]{1,0:T(8,128)(2,1)S(1)}, bf16[64,1024]{1,0:T(8,128)(2,1)S(1)}, u32[]{:S(2)}, u32[]{:S(2)}) collective-permute-start(bf16[64,1024]{1,0:T(8,128)(2,1)S(1)} %shard_map.137.refs_8_), channel_id=1, source_target_pairs={{0,12},{1,13},{2,14},{3,15},{4,0},{5,1},{6,2},{7,3},{8,4},{9,5},{1... | collective-permute-start | bytes 393224 | tf_op jit(solution)/shard_map/ppermute | solution.py:365
  61.2 7.8 %collective-permute-start.15 = (bf16[64,1024]{1,0:T(8,128)(2,1)S(1)}, bf16[64,1024]{1,0:T(8,128)(2,1)S(1)}, u32[]{:S(2)}, u32[]{:S(2)}) collective-permute-start(bf16[64,1024]{1,0:T(8,128)(2,1)S(1)} %shard_map.137.refs_8_), channel_id=1, source_target_pairs={{0,14},{1,15},{2,12},{3,13},{4,2},{5,3},{6,0},{7,1},{8,6},{9,7},{1... | collective-permute-start | bytes 393224 | tf_op jit(solution)/shard_map/ppermute | solution.py:365
  65.3 4.1 %collective-permute-start.13 = (bf16[64,1024]{1,0:T(8,128)(2,1)S(1)}, bf16[64,1024]{1,0:T(8,128)(2,1)S(1)}, u32[]{:S(2)}, u32[]{:S(2)}) collective-permute-start(bf16[64,1024]{1,0:T(8,128)(2,1)S(1)} %get-tuple-element.60), channel_id=1, source_target_pairs={{0,1},{1,0},{2,3},{3,2},{4,5},{5,4},{6,7},{7,6},{8,9},{9,8},{10,11... | collective-permute-start | bytes 393224 | tf_op jit(solution)/shard_map/ppermute | solution.py:369
  69.1 1.7 %collective-permute-start.17 = (bf16[64,1024]{1,0:T(8,128)(2,1)S(1)}, bf16[64,1024]{1,0:T(8,128)(2,1)S(1)}, u32[]{:S(2)}, u32[]{:S(2)}) collective-permute-start(bf16[64,1024]{1,0:T(8,128)(2,1)S(1)} %shard_map.141.refs_4_.refs_1_), channel_id=1, source_target_pairs={{0,1},{1,0},{2,3},{3,2},{4,5},{5,4},{6,7},{7,6},{8,9},{9,8},{10,11... | collective-permute-start | bytes 393224 | tf_op jit(solution)/shard_map/ppermute | solution.py:369
  69.5 6.7 %collective-permute-start.16 = (bf16[64,1024]{1,0:T(8,128)(2,1)S(1)}, bf16[64,1024]{1,0:T(8,128)(2,1)S(1)}, u32[]{:S(2)}, u32[]{:S(2)}) collective-permute-start(bf16[64,1024]{1,0:T(8,128)(2,1)S(1)} %shard_map.142.refs_7_.refs_0_), channel_id=1, source_target_pairs={{0,2},{1,3},{2,0},{3,1},{4,6},{5,7},{6,4},{7,5},{8,10},{9,11},{10,... | collective-permute-start | bytes 393224 | tf_op jit(solution)/shard_map/ppermute | solution.py:369
  79.7 3.4 %copy-start.2 = (s32[128,128]{1,0:T(8,128)S(1)}, s32[128,128]{1,0:T(8,128)}, u32[]{:S(2)}) copy-start(s32[128,128]{1,0:T(8,128)} %refs_1_.7) | copy-start | bytes 196612
  79.8 1.4 %collective-permute-start.19 = (bf16[64,1024]{1,0:T(8,128)(2,1)S(1)}, bf16[64,1024]{1,0:T(8,128)(2,1)S(1)}, u32[]{:S(2)}, u32[]{:S(2)}) collective-permute-start(bf16[64,1024]{1,0:T(8,128)(2,1)S(1)} %get-tuple-element.66), channel_id=1, source_target_pairs={{0,1},{1,0},{2,3},{3,2},{4,5},{5,4},{6,7},{7,6},{8,9},{9,8},{10,11... | collective-permute-start | bytes 393224 | tf_op jit(solution)/shard_map/ppermute | solution.py:369
  79.8 2.5 %collective-permute-start.18 = (bf16[64,1024]{1,0:T(8,128)(2,1)S(1)}, bf16[64,1024]{1,0:T(8,128)(2,1)S(1)}, u32[]{:S(2)}, u32[]{:S(2)}) collective-permute-start(bf16[64,1024]{1,0:T(8,128)(2,1)S(1)} %shard_map.144.refs_3_.refs_1_), channel_id=1, source_target_pairs={{0,1},{1,0},{2,3},{3,2},{4,5},{5,4},{6,7},{7,6},{8,9},{9,8},{10,11... | collective-permute-start | bytes 393224 | tf_op jit(solution)/shard_map/ppermute | solution.py:369
  81.4 5.6 %collective-permute-start.20 = (bf16[64,1024]{1,0:T(8,128)(2,1)S(1)}, bf16[64,1024]{1,0:T(8,128)(2,1)S(1)}, u32[]{:S(2)}, u32[]{:S(2)}) collective-permute-start(bf16[64,1024]{1,0:T(8,128)(2,1)S(1)} %shard_map.146.refs_3_.refs_0_), channel_id=1, source_target_pairs={{0,2},{1,3},{2,0},{3,1},{4,6},{5,7},{6,4},{7,5},{8,10},{9,11},{10,... | collective-permute-start | bytes 393224 | tf_op jit(solution)/shard_map/ppermute | solution.py:369
  87.0 1.4 %collective-permute-start.21 = (bf16[64,1024]{1,0:T(8,128)(2,1)S(1)}, bf16[64,1024]{1,0:T(8,128)(2,1)S(1)}, u32[]{:S(2)}, u32[]{:S(2)}) collective-permute-start(bf16[64,1024]{1,0:T(8,128)(2,1)S(1)} %shard_map.149.refs_1_.refs_3_), channel_id=1, source_target_pairs={{0,1},{1,0},{2,3},{3,2},{4,5},{5,4},{6,7},{7,6},{8,9},{9,8},{10,11... | collective-permute-start | bytes 393224 | tf_op jit(solution)/shard_map/ppermute | solution.py:369

commit v8 on v7

--- a/solution.py
+++ b/solution.py
@@ -112,7 +112,7 @@
             w_out_ref[which, pl.ds(to + ROWS16, ROWS16), lanes] = piece[:, LANES:]
         return carry
 
-    lax.fori_loop(0, depth // (2 * ROWS16), step, 0, unroll=16)
+    lax.fori_loop(0, depth // (2 * ROWS16), step, 0, unroll=32)
 
     @pl.when(block == pl.num_programs(1) - 1)
     def _():
@@ -218,23 +218,23 @@
     scale = LANES ** (-0.5)
     at = slice(part * heads * LANES, (part + 1) * heads * LANES)
     grad_attn = dot(g, wo_ref[at], LAST).astype(BF16)
-    for local in range(heads):
-        h = part * heads + local
-        own = slice(h * LANES, (h + 1) * LANES)
-        q, k, v = (qkv_ref[c, :, own] for c in range(3))
-        ga = grad_attn[:, local * LANES : (local + 1) * LANES]
+    lanes = [slice(h * LANES, (h + 1) * LANES) for h in range(part * heads, (part + 1) * heads)]
+    attn = [grad_attn[:, h * LANES : (h + 1) * LANES] for h in range(heads)]
+    grad_probs = [dot(qkv_ref[2, :, own], ga, LAST) for own, ga in zip(lanes, attn)]
+    halved = []
+    for h, of_probs in enumerate(grad_probs, part * heads):
         probs = probs_ref[h]
-        grad_probs = dot(v, ga, LAST)
-        total = jnp.sum(probs * grad_probs, axis=0, keepdims=True)
-        grad_scores = probs * (grad_probs - total)
-        grad16 = grad_scores.astype(BF16)
+        total = jnp.sum(probs * of_probs, axis=0, keepdims=True)
+        grad_scores = probs * (of_probs - total)
+        halved.append(grad_scores.astype(BF16))
         if acc_in_ref is None:
             acc_ref[h] = grad_scores
         else:
             acc_ref[h] = acc_in_ref[h] + grad_scores
-        stacked[0, :, own] = (dot(grad16, k, FIRST) * scale).astype(BF16)
-        stacked[1, :, own] = (dot(grad16, q) * scale).astype(BF16)
-        stacked[2, :, own] = dot(probs.astype(BF16), ga).astype(BF16)
+    for h, (own, ga, grad16) in enumerate(zip(lanes, attn, halved), part * heads):
+        stacked[0, :, own] = (dot(grad16, qkv_ref[1, :, own], FIRST) * scale).astype(BF16)
+        stacked[1, :, own] = (dot(grad16, qkv_ref[0, :, own]) * scale).astype(BF16)
+        stacked[2, :, own] = dot(probs_ref[h].astype(BF16), ga).astype(BF16)
 
 
 def backward_kernel(first, flags_ref, *refs):
@@ -395,7 +395,7 @@
 
     if heads % ROWS16 == 0:
         rows_first = jnp.transpose(w_qkv[0], (0, 2, 1, 3)).reshape(model_width, 3 * heads, head_dim)
-        blocks = 2
+        blocks = 1
         depth = model_width // blocks
         fixed = lambda rank: lambda c, b: (0,) * rank
         weights, qkv, kept_qkv, bias, wo, entering = pl.pallas_call(
@@ -435,7 +435,7 @@
                 flops=0, bytes_accessed=2 * w_qkv.size, transcendentals=0
             ),
         )(
-            order, in_hbm(rising), in_hbm(stash), in_hbm(gain), in_hbm(table), in_hbm(buckets),
+            in_hbm(order), in_hbm(rising), in_hbm(stash), in_hbm(gain), in_hbm(table), in_hbm(buckets),
             in_hbm(rows_first), in_hbm(back), in_hbm(queue), flags,
         )
         run.before = qkv

time: 89.4 us -> 84.2 us (0.942)
  Pallas kernels: 60.8 us -> 50.9 us
  waiting for transfers between devices: 9.8 us -> 13.5 us
  starting transfers between devices: 16.9 us -> 18.5 us
    pallas_call x29, Pallas kernels: 47.4 us -> 38.8 us  [__call__(): pl.pallas_call(body, out_shape=outs, in_specs=[WHOLE] * count + [UNREAD]...]
    ppermute x16, waiting for transfers between devices: 4.6 us -> 9.05 us  [swapped(): lax.ppermute(block, 'head', [(i, i ^ bit) for i in range(lax.axis_size('h...]
    ppermute x6, starting transfers between devices: 7.87 us -> 9.33 us  [moved(): return lax.ppermute(block, ('section', 'head'), route)]
    pallas_call x1, Pallas kernels: 13.4 us -> 12.2 us  [per_device(): pl.pallas_call(relayout_kernel, grid=(3, blocks), out_shape=(pltpu.VMEM((...]
  transfers between devices with their start and end apart: 22 -> 22, of which waited for: 7 -> 10; matrix products, arithmetic and copies ran while one was open for 0% -> 0% of each run, Pallas kernels for 46% -> 39%
where the time goes in v8:
time: 84.2 us; the launch traced here: 84 us
  Pallas kernels  50.9 us (60%)
  starting transfers between devices  18.5 us (22%)
  waiting for transfers between devices  13.5 us (16%)
  between operations  0.96 us (1%)
    pallas_call x29, Pallas kernels, __call__(): pl.pallas_call(body, out_shape=outs, in_specs=[WHOLE] * count + [UNREAD]...  38.8 us
    pallas_call x1, Pallas kernels, per_device(): pl.pallas_call(relayout_kernel, grid=(3, blocks), out_shape=(pltpu.VMEM((...  12.2 us
    ppermute x6, starting transfers between devices, moved(): return lax.ppermute(block, ('section', 'head'), route)  9.33 us
    ppermute x16, starting transfers between devices, swapped(): lax.ppermute(block, 'head', [(i, i ^ bit) for i in range(lax.axis_size('h...  9.14 us
    ppermute x16, waiting for transfers between devices, swapped(): lax.ppermute(block, 'head', [(i, i ^ bit) for i in range(lax.axis_size('h...  9.05 us
    ppermute x6, waiting for transfers between devices, moved(): return lax.ppermute(block, ('section', 'head'), route)  4.43 us
  transfers between devices with their start and end apart: 22, of which 10 were waited for; matrix products, arithmetic and copies ran while one was open for 0% of the time, Pallas kernels for 39%

profile of v8, /device:TPU:0, one launch (start us, length us, event | category | flops | bytes accessed | tf_op | source)
XLA Modules:
  0.0 84.0 jit_solution(13892603646131009886)
XLA Ops:
  0.8 12.2 %shard_map.121 = (bf16[3,1024,2048]{2,1,0:T(8,128)(2,1)S(1)}, bf16[3,128,2048]{2,1,0:T(8,128)(2,1)S(1)}, bf16[3,128,2048]{2,1,0:T(8,128)(2,1)S(1)}, f32[16,128,1...) custom-call(s32[6]{0:T(128)} %order_ref.1, bf16[1,128,1024]{2,1,0:T(8,128)(2,1)} %refs_1_.4, ...), custom_call_target="tpu_custom_call" | custom-call | bytes 12582912 | tf_op jit(solution)/shard_map/pallas_call | solution.py:401
  13.0 1.7 %shard_map.122 = (bf16[64,1024]{1,0:T(8,128)(2,1)S(1)}, f32[64,1024]{1,0:T(8,128)S(1)}, bf16[64,1024]{1,0:T(8,128)(2,1)S(1)}) custom-call(f32[4,128]{1,0:T(4,128)S(1)} %broadcast_in_dim.4._.refs_0_, bf16[1,128,1024]{2,1,0:T(8,128)(2,1)S(1)} %copy-done.1, bf16[3,128,2048]{2,1,0:T(8,128)(2,1)S(1)} %get-tuple-element.38.refs_2_.refs_5_, ...), custom_call_target="tpu_custom_call" | custom-call | bytes 128 | tf_op jit(solution)/shard_map/pallas_call | solution.py:341
  16.3 2.9 %collective-permute-start.1 = (bf16[64,1024]{1,0:T(8,128)(2,1)S(1)}, bf16[64,1024]{1,0:T(8,128)(2,1)S(1)}, u32[]{:S(2)}, u32[]{:S(2)}) collective-permute-start(bf16[64,1024]{1,0:T(8,128)(2,1)S(1)} %shard_map.124.refs_5_.refs_0_), channel_id=1, source_target_pairs={{0,2},{1,3},{2,0},{3,1},{4,6},{5,7},{6,4},{7,5},{8,10},{9,11},{10,... | collective-permute-start | bytes 393224 | tf_op jit(solution)/shard_map/ppermute | solution.py:369
  19.2 2.4 %shard_map.125 = (bf16[3,128,2048]{2,1,0:T(8,128)(2,1)S(1)}, f32[16,128,128]{2,1,0:T(8,128)S(1)}, bf16[64,1024]{1,0:T(8,128)(2,1)S(1)}) custom-call(f32[4,128]{1,0:T(4,128)S(1)} %broadcast_in_dim.4._.refs_0_, bf16[128,1024]{1,0:T(8,128)(2,1)S(1)} %bitcast.23, bf16[3,128,2048]{2,1,0:T(8,128)(2,1)S(1)} %get-tuple-element.44.refs_0_.refs_2_, ...), custom_call_target="tpu_custom_call" | custom-call | bytes 128 | tf_op jit(solution)/shard_map/pallas_call | solution.py:341
  21.6 1.4 %collective-permute-done.1.refs_1_ = bf16[64,1024]{1,0:T(8,128)(2,1)S(1)} collective-permute-done((bf16[64,1024]{1,0:T(8,128)(2,1)S(1)}, bf16[64,1024]{1,0:T(8,128)(2,1)S(1)}, u32[]{:S(2)}, u32[]{:S(2)}) %collective-permute-start.1) | collective-permute-done | bytes 131104 | tf_op jit(solution)/shard_map/ppermute | solution.py:369
  23.0 1.9 %collective-permute-start.2 = (bf16[64,1024]{1,0:T(8,128)(2,1)S(1)}, bf16[64,1024]{1,0:T(8,128)(2,1)S(1)}, u32[]{:S(2)}, u32[]{:S(2)}) collective-permute-start(bf16[64,1024]{1,0:T(8,128)(2,1)S(1)} %shard_map.126.refs_3_.refs_1_), channel_id=1, source_target_pairs={{0,4},{1,5},{2,6},{3,7},{4,8},{5,9},{6,10},{7,11},{8,12},{9,13},{1... | collective-permute-start | bytes 393224 | tf_op jit(solution)/shard_map/ppermute | solution.py:365
  24.9 3.5 %shard_map.127 = (bf16[64,1024]{1,0:T(8,128)(2,1)S(1)}, f32[64,1024]{1,0:T(8,128)S(1)}) custom-call(f32[4,128]{1,0:T(4,128)S(1)} %broadcast_in_dim.4._.refs_0_, bf16[3,128,2048]{2,1,0:T(8,128)(2,1)S(1)} %get-tuple-element.48.refs_1_, bf16[3,1024,2048]{2,1,0:T(8,128)(2,1)S(1)} %get-tuple-element.47.refs_2_.refs_5_, ...), custom_call_target="tpu_custom_call" | custom-call | bytes 128 | tf_op jit(solution)/shard_map/pallas_call | solution.py:341
  28.5 1.5 %collective-permute-done.2.refs_1_ = bf16[64,1024]{1,0:T(8,128)(2,1)S(1)} collective-permute-done((bf16[64,1024]{1,0:T(8,128)(2,1)S(1)}, bf16[64,1024]{1,0:T(8,128)(2,1)S(1)}, u32[]{:S(2)}, u32[]{:S(2)}) %collective-permute-start.2) | collective-permute-done | bytes 131104 | tf_op jit(solution)/shard_map/ppermute | solution.py:365
  30.1 2.0 %collective-permute-start.6 = (bf16[64,1024]{1,0:T(8,128)(2,1)S(1)}, bf16[64,1024]{1,0:T(8,128)(2,1)S(1)}, u32[]{:S(2)}, u32[]{:S(2)}) collective-permute-start(bf16[64,1024]{1,0:T(8,128)(2,1)S(1)} %shard_map.128.refs_8_), channel_id=1, source_target_pairs={{0,12},{1,13},{2,14},{3,15},{4,0},{5,1},{6,2},{7,3},{8,4},{9,5},{1... | collective-permute-start | bytes 393224 | tf_op jit(solution)/shard_map/ppermute | solution.py:365
  32.2 2.9 %collective-permute-start.7 = (bf16[64,1024]{1,0:T(8,128)(2,1)S(1)}, bf16[64,1024]{1,0:T(8,128)(2,1)S(1)}, u32[]{:S(2)}, u32[]{:S(2)}) collective-permute-start(bf16[64,1024]{1,0:T(8,128)(2,1)S(1)} %shard_map.128.refs_8_), channel_id=1, source_target_pairs={{0,14},{1,15},{2,12},{3,13},{4,2},{5,3},{6,0},{7,1},{8,6},{9,7},{1... | collective-permute-start | bytes 393224 | tf_op jit(solution)/shard_map/ppermute | solution.py:365
  35.0 3.6 %shard_map.129 = (bf16[64,1024]{1,0:T(8,128)(2,1)S(1)}, f32[64,1024]{1,0:T(8,128)S(1)}, bf16[64,1024]{1,0:T(8,128)(2,1)S(1)}) custom-call(f32[4,128]{1,0:T(4,128)S(1)} %broadcast_in_dim.4._.refs_0_, bf16[64,1024]{1,0:T(8,128)(2,1)S(1)} %collective-permute-done.2.refs_1_, bf16[64,1024]{1,0:T(8,128)(2,1)S(1)} %collective-permute-done.3.refs_2_, ...), custom_call_target="tpu_custom_call" | custom-call | bytes 128 | tf_op jit(solution)/shard_map/pallas_call | solution.py:341
  38.7 2.6 %shard_map.130.refs_0_.refs_2_.refs_3_ = bf16[3,128,2048]{2,1,0:T(8,128)(2,1)S(1)} custom-call(bf16[3,128,1024]{2,1,0:T(8,128)(2,1)S(1)} %bitcast.19, f32[1,1024]{1,0:T(1,128)S(1)} %copy-done.4, bf16[3,1024,2048]{2,1,0:T(8,128)(2,1)S(1)} %get-tuple-element.47.refs_2_.refs_5_, bf16[64,1024]{1,0:T(8,128)(2,1)S(1)} %get-tuple-element.53.refs_3_), custom_call_target="tpu_custom_call" | custom-call | bytes 128 | tf_op jit(solution)/shard_map/pallas_call | solution.py:341
  41.3 0.8 shard_map.131.refs_4_
  43.7 2.5 %shard_map.134 = (bf16[3,128,2048]{2,1,0:T(8,128)(2,1)S(1)}, f32[16,128,128]{2,1,0:T(8,128)S(1)}, bf16[64,1024]{1,0:T(8,128)(2,1)S(1)}) custom-call(f32[4,128]{1,0:T(4,128)S(1)} %broadcast_in_dim.4._.refs_0_, bf16[64,1024]{1,0:T(8,128)(2,1)S(1)} %shard_map.132.refs_4_.refs_1_, bf16[64,1024]{1,0:T(8,128)(2,1)S(1)} %collective-permute-done.9.refs_2_, ...), custom_call_target="tpu_custom_call" | custom-call | bytes 128 | tf_op jit(solution)/shard_map/pallas_call | solution.py:341
  46.3 2.0 %collective-permute-done.8.refs_1_ = bf16[64,1024]{1,0:T(8,128)(2,1)S(1)} collective-permute-done((bf16[64,1024]{1,0:T(8,128)(2,1)S(1)}, bf16[64,1024]{1,0:T(8,128)(2,1)S(1)}, u32[]{:S(2)}, u32[]{:S(2)}) %collective-permute-start.8) | collective-permute-done | bytes 131104 | tf_op jit(solution)/shard_map/ppermute | solution.py:369
  48.7 3.5 %shard_map.136 = (bf16[64,1024]{1,0:T(8,128)(2,1)S(1)}, f32[64,1024]{1,0:T(8,128)S(1)}) custom-call(f32[4,128]{1,0:T(4,128)S(1)} %broadcast_in_dim.4._.refs_0_, bf16[3,128,2048]{2,1,0:T(8,128)(2,1)S(1)} %get-tuple-element.56.refs_1_, bf16[3,1024,2048]{2,1,0:T(8,128)(2,1)S(1)} %get-tuple-element.47.refs_2_.refs_5_, ...), custom_call_target="tpu_custom_call" | custom-call | bytes 128 | tf_op jit(solution)/shard_map/pallas_call | solution.py:341
  52.2 3.0 %collective-permute-done.10.refs_1_ = bf16[64,1024]{1,0:T(8,128)(2,1)S(1)} collective-permute-done((bf16[64,1024]{1,0:T(8,128)(2,1)S(1)}, bf16[64,1024]{1,0:T(8,128)(2,1)S(1)}, u32[]{:S(2)}, u32[]{:S(2)}) %collective-permute-start.10) | collective-permute-done | bytes 131104 | tf_op jit(solution)/shard_map/ppermute | solution.py:365
  55.4 2.0 %collective-permute-start.14 = (bf16[64,1024]{1,0:T(8,128)(2,1)S(1)}, bf16[64,1024]{1,0:T(8,128)(2,1)S(1)}, u32[]{:S(2)}, u32[]{:S(2)}) collective-permute-start(bf16[64,1024]{1,0:T(8,128)(2,1)S(1)} %shard_map.137.refs_8_), channel_id=1, source_target_pairs={{0,12},{1,13},{2,14},{3,15},{4,0},{5,1},{6,2},{7,3},{8,4},{9,5},{1... | collective-permute-start | bytes 393224 | tf_op jit(solution)/shard_map/ppermute | solution.py:365
  57.7 3.6 %shard_map.138 = (bf16[64,1024]{1,0:T(8,128)(2,1)S(1)}, f32[64,1024]{1,0:T(8,128)S(1)}, bf16[64,1024]{1,0:T(8,128)(2,1)S(1)}) custom-call(f32[4,128]{1,0:T(4,128)S(1)} %broadcast_in_dim.4._.refs_0_, bf16[64,1024]{1,0:T(8,128)(2,1)S(1)} %collective-permute-done.10.refs_1_, bf16[64,1024]{1,0:T(8,128)(2,1)S(1)} %collective-permute-done.11.refs_2_, ...), custom_call_target="tpu_custom_call" | custom-call | bytes 128 | tf_op jit(solution)/shard_map/pallas_call | solution.py:341
  61.3 2.6 %shard_map.139.refs_0_.refs_2_.refs_3_ = bf16[3,128,2048]{2,1,0:T(8,128)(2,1)S(1)} custom-call(bf16[3,128,1024]{2,1,0:T(8,128)(2,1)S(1)} %bitcast.21, f32[1,1024]{1,0:T(1,128)S(1)} %copy-done.4, bf16[3,1024,2048]{2,1,0:T(8,128)(2,1)S(1)} %get-tuple-element.47.refs_2_.refs_5_, bf16[64,1024]{1,0:T(8,128)(2,1)S(1)} %get-tuple-element.61.refs_3_), custom_call_target="tpu_custom_call" | custom-call | bytes 128 | tf_op jit(solution)/shard_map/pallas_call | solution.py:341
  63.9 0.8 shard_map.140.refs_4_
  65.5 1.5 %collective-permute-start.16 = (bf16[64,1024]{1,0:T(8,128)(2,1)S(1)}, bf16[64,1024]{1,0:T(8,128)(2,1)S(1)}, u32[]{:S(2)}, u32[]{:S(2)}) collective-permute-start(bf16[64,1024]{1,0:T(8,128)(2,1)S(1)} %shard_map.142.refs_7_.refs_0_), channel_id=1, source_target_pairs={{0,2},{1,3},{2,0},{3,1},{4,6},{5,7},{6,4},{7,5},{8,10},{9,11},{10,... | collective-permute-start | bytes 393224 | tf_op jit(solution)/shard_map/ppermute | solution.py:369
  67.0 2.5 %shard_map.143 = (bf16[3,128,2048]{2,1,0:T(8,128)(2,1)S(1)}, f32[16,128,128]{2,1,0:T(8,128)S(1)}, bf16[64,1024]{1,0:T(8,128)(2,1)S(1)}) custom-call(f32[4,128]{1,0:T(4,128)S(1)} %broadcast_in_dim.4._.refs_0_, bf16[64,1024]{1,0:T(8,128)(2,1)S(1)} %shard_map.141.refs_4_.refs_1_, bf16[64,1024]{1,0:T(8,128)(2,1)S(1)} %collective-permute-done.17.refs_2_, ...), custom_call_target="tpu_custom_call" | custom-call | bytes 128 | tf_op jit(solution)/shard_map/pallas_call | solution.py:341
  69.6 1.4 %collective-permute-done.16.refs_1_ = bf16[64,1024]{1,0:T(8,128)(2,1)S(1)} collective-permute-done((bf16[64,1024]{1,0:T(8,128)(2,1)S(1)}, bf16[64,1024]{1,0:T(8,128)(2,1)S(1)}, u32[]{:S(2)}, u32[]{:S(2)}) %collective-permute-start.16) | collective-permute-done | bytes 131104 | tf_op jit(solution)/shard_map/ppermute | solution.py:369
  71.0 3.5 %shard_map.145 = (bf16[64,1024]{1,0:T(8,128)(2,1)S(1)}, f32[64,1024]{1,0:T(8,128)S(1)}) custom-call(f32[4,128]{1,0:T(4,128)S(1)} %broadcast_in_dim.4._.refs_0_, bf16[3,128,2048]{2,1,0:T(8,128)(2,1)S(1)} %get-tuple-element.64.refs_1_, bf16[3,1024,2048]{2,1,0:T(8,128)(2,1)S(1)} %get-tuple-element.47.refs_2_.refs_5_, ...), custom_call_target="tpu_custom_call" | custom-call | bytes 128 | tf_op jit(solution)/shard_map/pallas_call | solution.py:341
  75.1 0.8 collective-permute-done.19.refs_4_
  76.1 1.5 %collective-permute-start.20 = (bf16[64,1024]{1,0:T(8,128)(2,1)S(1)}, bf16[64,1024]{1,0:T(8,128)(2,1)S(1)}, u32[]{:S(2)}, u32[]{:S(2)}) collective-permute-start(bf16[64,1024]{1,0:T(8,128)(2,1)S(1)} %shard_map.146.refs_3_.refs_0_), channel_id=1, source_target_pairs={{0,2},{1,3},{2,0},{3,1},{4,6},{5,7},{6,4},{7,5},{8,10},{9,11},{10,... | collective-permute-start | bytes 393224 | tf_op jit(solution)/shard_map/ppermute | solution.py:369
  77.7 0.8 shard_map.147
  78.5 1.7 %shard_map.148 = (f32[16,32]{1,0:T(8,128)}, f32[8,128]{1,0:T(8,128)S(1)}) custom-call(f32[16,128,128]{2,1,0:T(8,128)S(1)} %get-tuple-element.68.refs_0_, s32[128,128]{1,0:T(8,128)S(1)} %copy-done.2, f32[8,128]{1,0:T(8,128)S(1)} %get-tuple-element.69.refs_2_), custom_call_target="tpu_custom_call" | custom-call | bytes 128 | tf_op jit(solution)/shard_map/pallas_call | solution.py:341
  80.1 1.6 %collective-permute-done.20.refs_1_ = bf16[64,1024]{1,0:T(8,128)(2,1)S(1)} collective-permute-done((bf16[64,1024]{1,0:T(8,128)(2,1)S(1)}, bf16[64,1024]{1,0:T(8,128)(2,1)S(1)}, u32[]{:S(2)}, u32[]{:S(2)}) %collective-permute-start.20) | collective-permute-done | bytes 131104 | tf_op jit(solution)/shard_map/ppermute | solution.py:369
  81.8 1.3 %collective-permute-done.21.refs_2_ = bf16[64,1024]{1,0:T(8,128)(2,1)S(1)} collective-permute-done((bf16[64,1024]{1,0:T(8,128)(2,1)S(1)}, bf16[64,1024]{1,0:T(8,128)(2,1)S(1)}, u32[]{:S(2)}, u32[]{:S(2)}) %collective-permute-start.21) | collective-permute-done | bytes 131104 | tf_op jit(solution)/shard_map/ppermute | solution.py:369
  83.2 0.8 shard_map.150
  (54 shorter events, 6.3 us)
Async XLA Ops:
  0.8 12.2 %copy-start.1 = (bf16[1,128,1024]{2,1,0:T(8,128)(2,1)S(1)}, bf16[1,128,1024]{2,1,0:T(8,128)(2,1)}, u32[]{:S(2)}) copy-start(bf16[1,128,1024]{2,1,0:T(8,128)(2,1)} %refs_1_.4) | copy-start | bytes 786436
  14.7 1.5 %collective-permute-start = (bf16[64,1024]{1,0:T(8,128)(2,1)S(1)}, bf16[64,1024]{1,0:T(8,128)(2,1)S(1)}, u32[]{:S(2)}, u32[]{:S(2)}) collective-permute-start(bf16[64,1024]{1,0:T(8,128)(2,1)S(1)} %get-tuple-element.42), channel_id=1, source_target_pairs={{0,1},{1,0},{2,3},{3,2},{4,5},{5,4},{6,7},{7,6},{8,9},{9,8},{10,11... | collective-permute-start | bytes 393224 | tf_op jit(solution)/shard_map/ppermute | solution.py:369
  16.0 3.2 %copy-start.3 = (bf16[1,128,1024]{2,1,0:T(8,128)(2,1)S(1)}, bf16[1,128,1024]{2,1,0:T(8,128)(2,1)}, u32[]{:S(2)}) copy-start(bf16[1,128,1024]{2,1,0:T(8,128)(2,1)} %param.11) | copy-start | bytes 786436
  16.3 6.7 %collective-permute-start.1 = (bf16[64,1024]{1,0:T(8,128)(2,1)S(1)}, bf16[64,1024]{1,0:T(8,128)(2,1)S(1)}, u32[]{:S(2)}, u32[]{:S(2)}) collective-permute-start(bf16[64,1024]{1,0:T(8,128)(2,1)S(1)} %shard_map.124.refs_5_.refs_0_), channel_id=1, source_target_pairs={{0,2},{1,3},{2,0},{3,1},{4,6},{5,7},{6,4},{7,5},{8,10},{9,11},{10,... | collective-permute-start | bytes 393224 | tf_op jit(solution)/shard_map/ppermute | solution.py:369
  23.0 6.9 %collective-permute-start.2 = (bf16[64,1024]{1,0:T(8,128)(2,1)S(1)}, bf16[64,1024]{1,0:T(8,128)(2,1)S(1)}, u32[]{:S(2)}, u32[]{:S(2)}) collective-permute-start(bf16[64,1024]{1,0:T(8,128)(2,1)S(1)} %shard_map.126.refs_3_.refs_1_), channel_id=1, source_target_pairs={{0,4},{1,5},{2,6},{3,7},{4,8},{5,9},{6,10},{7,11},{8,12},{9,13},{1... | collective-permute-start | bytes 393224 | tf_op jit(solution)/shard_map/ppermute | solution.py:365
  24.9 5.0 %copy-start = (bf16[1,3,128,1024]{3,2,1,0:T(8,128)(2,1)S(1)}, bf16[1,3,128,1024]{3,2,1,0:T(8,128)(2,1)}, u32[]{:S(2)}) copy-start(bf16[1,3,128,1024]{3,2,1,0:T(8,128)(2,1)} %kept_ref.1) | copy-start | bytes 2359300
  24.9 5.0 %copy-start.4 = (f32[1,1024]{1,0:T(1,128)S(1)}, f32[1,1024]{1,0:T(1,128)}, u32[]{:S(2)}) copy-start(f32[1,1024]{1,0:T(1,128)} %refs_2_.5) | copy-start | bytes 12292
  28.4 1.5 %collective-permute-start.4 = (bf16[64,1024]{1,0:T(8,128)(2,1)S(1)}, bf16[64,1024]{1,0:T(8,128)(2,1)S(1)}, u32[]{:S(2)}, u32[]{:S(2)}) collective-permute-start(bf16[64,1024]{1,0:T(8,128)(2,1)S(1)} %get-tuple-element.50), channel_id=1, source_target_pairs={{0,1},{1,0},{2,3},{3,2},{4,5},{5,4},{6,7},{7,6},{8,9},{9,8},{10,11... | collective-permute-start | bytes 393224 | tf_op jit(solution)/shard_map/ppermute | solution.py:369
  29.9 5.1 %collective-permute-start.3 = (bf16[64,1024]{1,0:T(8,128)(2,1)S(1)}, bf16[64,1024]{1,0:T(8,128)(2,1)S(1)}, u32[]{:S(2)}, u32[]{:S(2)}) collective-permute-start(bf16[64,1024]{1,0:T(8,128)(2,1)S(1)} %collective-permute-done.2.refs_1_), channel_id=1, source_target_pairs={{0,1},{1,0},{2,3},{3,2},{4,5},{5,4},{6,7},{7,6},{8,9},{9,8},{10,11... | collective-permute-start | bytes 393224 | tf_op jit(solution)/shard_map/ppermute | solution.py:369
  30.1 12.0 %collective-permute-start.6 = (bf16[64,1024]{1,0:T(8,128)(2,1)S(1)}, bf16[64,1024]{1,0:T(8,128)(2,1)S(1)}, u32[]{:S(2)}, u32[]{:S(2)}) collective-permute-start(bf16[64,1024]{1,0:T(8,128)(2,1)S(1)} %shard_map.128.refs_8_), channel_id=1, source_target_pairs={{0,12},{1,13},{2,14},{3,15},{4,0},{5,1},{6,2},{7,3},{8,4},{9,5},{1... | collective-permute-start | bytes 393224 | tf_op jit(solution)/shard_map/ppermute | solution.py:365
  32.2 9.9 %collective-permute-start.7 = (bf16[64,1024]{1,0:T(8,128)(2,1)S(1)}, bf16[64,1024]{1,0:T(8,128)(2,1)S(1)}, u32[]{:S(2)}, u32[]{:S(2)}) collective-permute-start(bf16[64,1024]{1,0:T(8,128)(2,1)S(1)} %shard_map.128.refs_8_), channel_id=1, source_target_pairs={{0,14},{1,15},{2,12},{3,13},{4,2},{5,3},{6,0},{7,1},{8,6},{9,7},{1... | collective-permute-start | bytes 393224 | tf_op jit(solution)/shard_map/ppermute | solution.py:365
  38.6 4.1 %collective-permute-start.5 = (bf16[64,1024]{1,0:T(8,128)(2,1)S(1)}, bf16[64,1024]{1,0:T(8,128)(2,1)S(1)}, u32[]{:S(2)}, u32[]{:S(2)}) collective-permute-start(bf16[64,1024]{1,0:T(8,128)(2,1)S(1)} %get-tuple-element.52), channel_id=1, source_target_pairs={{0,1},{1,0},{2,3},{3,2},{4,5},{5,4},{6,7},{7,6},{8,9},{9,8},{10,11... | collective-permute-start | bytes 393224 | tf_op jit(solution)/shard_map/ppermute | solution.py:369
  42.2 1.5 %collective-permute-start.9 = (bf16[64,1024]{1,0:T(8,128)(2,1)S(1)}, bf16[64,1024]{1,0:T(8,128)(2,1)S(1)}, u32[]{:S(2)}, u32[]{:S(2)}) collective-permute-start(bf16[64,1024]{1,0:T(8,128)(2,1)S(1)} %shard_map.132.refs_4_.refs_1_), channel_id=1, source_target_pairs={{0,1},{1,0},{2,3},{3,2},{4,5},{5,4},{6,7},{7,6},{8,9},{9,8},{10,11... | collective-permute-start | bytes 393224 | tf_op jit(solution)/shard_map/ppermute | solution.py:369
  42.8 5.5 %collective-permute-start.8 = (bf16[64,1024]{1,0:T(8,128)(2,1)S(1)}, bf16[64,1024]{1,0:T(8,128)(2,1)S(1)}, u32[]{:S(2)}, u32[]{:S(2)}) collective-permute-start(bf16[64,1024]{1,0:T(8,128)(2,1)S(1)} %shard_map.133.refs_7_.refs_0_), channel_id=1, source_target_pairs={{0,2},{1,3},{2,0},{3,1},{4,6},{5,7},{6,4},{7,5},{8,10},{9,11},{10,... | collective-permute-start | bytes 393224 | tf_op jit(solution)/shard_map/ppermute | solution.py:369
  48.4 6.8 %collective-permute-start.10 = (bf16[64,1024]{1,0:T(8,128)(2,1)S(1)}, bf16[64,1024]{1,0:T(8,128)(2,1)S(1)}, u32[]{:S(2)}, u32[]{:S(2)}) collective-permute-start(bf16[64,1024]{1,0:T(8,128)(2,1)S(1)} %shard_map.135.refs_3_.refs_1_), channel_id=1, source_target_pairs={{0,4},{1,5},{2,6},{3,7},{4,8},{5,9},{6,10},{7,11},{8,12},{9,13},{1... | collective-permute-start | bytes 393224 | tf_op jit(solution)/shard_map/ppermute | solution.py:365
  52.1 3.1 %collective-permute-start.12 = (bf16[64,1024]{1,0:T(8,128)(2,1)S(1)}, bf16[64,1024]{1,0:T(8,128)(2,1)S(1)}, u32[]{:S(2)}, u32[]{:S(2)}) collective-permute-start(bf16[64,1024]{1,0:T(8,128)(2,1)S(1)} %get-tuple-element.58), channel_id=1, source_target_pairs={{0,1},{1,0},{2,3},{3,2},{4,5},{5,4},{6,7},{7,6},{8,9},{9,8},{10,11... | collective-permute-start | bytes 393224 | tf_op jit(solution)/shard_map/ppermute | solution.py:369
  55.2 2.5 %collective-permute-start.11 = (bf16[64,1024]{1,0:T(8,128)(2,1)S(1)}, bf16[64,1024]{1,0:T(8,128)(2,1)S(1)}, u32[]{:S(2)}, u32[]{:S(2)}) collective-permute-start(bf16[64,1024]{1,0:T(8,128)(2,1)S(1)} %collective-permute-done.10.refs_1_), channel_id=1, source_target_pairs={{0,1},{1,0},{2,3},{3,2},{4,5},{5,4},{6,7},{7,6},{8,9},{9,8},{10,11... | collective-permute-start | bytes 393224 | tf_op jit(solution)/shard_map/ppermute | solution.py:369
  55.4 9.3 %collective-permute-start.14 = (bf16[64,1024]{1,0:T(8,128)(2,1)S(1)}, bf16[64,1024]{1,0:T(8,128)(2,1)S(1)}, u32[]{:S(2)}, u32[]{:S(2)}) collective-permute-start(bf16[64,1024]{1,0:T(8,128)(2,1)S(1)} %shard_map.137.refs_8_), channel_id=1, source_target_pairs={{0,12},{1,13},{2,14},{3,15},{4,0},{5,1},{6,2},{7,3},{8,4},{9,5},{1... | collective-permute-start | bytes 393224 | tf_op jit(solution)/shard_map/ppermute | solution.py:365
  57.4 7.3 %collective-permute-start.15 = (bf16[64,1024]{1,0:T(8,128)(2,1)S(1)}, bf16[64,1024]{1,0:T(8,128)(2,1)S(1)}, u32[]{:S(2)}, u32[]{:S(2)}) collective-permute-start(bf16[64,1024]{1,0:T(8,128)(2,1)S(1)} %shard_map.137.refs_8_), channel_id=1, source_target_pairs={{0,14},{1,15},{2,12},{3,13},{4,2},{5,3},{6,0},{7,1},{8,6},{9,7},{1... | collective-permute-start | bytes 393224 | tf_op jit(solution)/shard_map/ppermute | solution.py:365
  61.3 4.1 %collective-permute-start.13 = (bf16[64,1024]{1,0:T(8,128)(2,1)S(1)}, bf16[64,1024]{1,0:T(8,128)(2,1)S(1)}, u32[]{:S(2)}, u32[]{:S(2)}) collective-permute-start(bf16[64,1024]{1,0:T(8,128)(2,1)S(1)} %get-tuple-element.60), channel_id=1, source_target_pairs={{0,1},{1,0},{2,3},{3,2},{4,5},{5,4},{6,7},{7,6},{8,9},{9,8},{10,11... | collective-permute-start | bytes 393224 | tf_op jit(solution)/shard_map/ppermute | solution.py:369
  64.8 2.2 %collective-permute-start.17 = (bf16[64,1024]{1,0:T(8,128)(2,1)S(1)}, bf16[64,1024]{1,0:T(8,128)(2,1)S(1)}, u32[]{:S(2)}, u32[]{:S(2)}) collective-permute-start(bf16[64,1024]{1,0:T(8,128)(2,1)S(1)} %shard_map.141.refs_4_.refs_1_), channel_id=1, source_target_pairs={{0,1},{1,0},{2,3},{3,2},{4,5},{5,4},{6,7},{7,6},{8,9},{9,8},{10,11... | collective-permute-start | bytes 393224 | tf_op jit(solution)/shard_map/ppermute | solution.py:369
  65.5 5.5 %collective-permute-start.16 = (bf16[64,1024]{1,0:T(8,128)(2,1)S(1)}, bf16[64,1024]{1,0:T(8,128)(2,1)S(1)}, u32[]{:S(2)}, u32[]{:S(2)}) collective-permute-start(bf16[64,1024]{1,0:T(8,128)(2,1)S(1)} %shard_map.142.refs_7_.refs_0_), channel_id=1, source_target_pairs={{0,2},{1,3},{2,0},{3,1},{4,6},{5,7},{6,4},{7,5},{8,10},{9,11},{10,... | collective-permute-start | bytes 393224 | tf_op jit(solution)/shard_map/ppermute | solution.py:369
  74.5 4.0 %copy-start.2 = (s32[128,128]{1,0:T(8,128)S(1)}, s32[128,128]{1,0:T(8,128)}, u32[]{:S(2)}) copy-start(s32[128,128]{1,0:T(8,128)} %refs_1_.7) | copy-start | bytes 196612
  74.5 1.4 %collective-permute-start.19 = (bf16[64,1024]{1,0:T(8,128)(2,1)S(1)}, bf16[64,1024]{1,0:T(8,128)(2,1)S(1)}, u32[]{:S(2)}, u32[]{:S(2)}) collective-permute-start(bf16[64,1024]{1,0:T(8,128)(2,1)S(1)} %get-tuple-element.66), channel_id=1, source_target_pairs={{0,1},{1,0},{2,3},{3,2},{4,5},{5,4},{6,7},{7,6},{8,9},{9,8},{10,11... | collective-permute-start | bytes 393224 | tf_op jit(solution)/shard_map/ppermute | solution.py:369
  74.6 3.1 %collective-permute-start.18 = (bf16[64,1024]{1,0:T(8,128)(2,1)S(1)}, bf16[64,1024]{1,0:T(8,128)(2,1)S(1)}, u32[]{:S(2)}, u32[]{:S(2)}) collective-permute-start(bf16[64,1024]{1,0:T(8,128)(2,1)S(1)} %shard_map.144.refs_3_.refs_1_), channel_id=1, source_target_pairs={{0,1},{1,0},{2,3},{3,2},{4,5},{5,4},{6,7},{7,6},{8,9},{9,8},{10,11... | collective-permute-start | bytes 393224 | tf_op jit(solution)/shard_map/ppermute | solution.py:369
  76.1 5.6 %collective-permute-start.20 = (bf16[64,1024]{1,0:T(8,128)(2,1)S(1)}, bf16[64,1024]{1,0:T(8,128)(2,1)S(1)}, u32[]{:S(2)}, u32[]{:S(2)}) collective-permute-start(bf16[64,1024]{1,0:T(8,128)(2,1)S(1)} %shard_map.146.refs_3_.refs_0_), channel_id=1, source_target_pairs={{0,2},{1,3},{2,0},{3,1},{4,6},{5,7},{6,4},{7,5},{8,10},{9,11},{10,... | collective-permute-start | bytes 393224 | tf_op jit(solution)/shard_map/ppermute | solution.py:369
  81.8 1.4 %collective-permute-start.21 = (bf16[64,1024]{1,0:T(8,128)(2,1)S(1)}, bf16[64,1024]{1,0:T(8,128)(2,1)S(1)}, u32[]{:S(2)}, u32[]{:S(2)}) collective-permute-start(bf16[64,1024]{1,0:T(8,128)(2,1)S(1)} %shard_map.149.refs_1_.refs_3_), channel_id=1, source_target_pairs={{0,1},{1,0},{2,3},{3,2},{4,5},{5,4},{6,7},{7,6},{8,9},{9,8},{10,11... | collective-permute-start | bytes 393224 | tf_op jit(solution)/shard_map/ppermute | solution.py:369

commit v9 on v8

--- a/solution.py
+++ b/solution.py
@@ -516,10 +516,13 @@
             (flags,) + g_parts + (stashed[t], probs, wo) + acc,
         )
         acc = (acc_next,)
-        lifted = run(pair_kernel, half_rows, (up, up_other))
-        x_mine = lifted if final else moved(lifted, 1, 0)
+        if not final:
+            lifted = run(pair_kernel, half_rows, (up, up_other))
+            x_mine = moved(lifted, 1, 0)
         send, keep = run(input_gradient_kernel, halves, (flags, stacked, weights))
         received = swapped(send, 1)
+        if final:
+            x_mine = run(pair_kernel, half_rows, (up, up_other))
 
     x_other = swapped(x_mine, 1)
     rows = shape((1, tokens, model_width))

time: 84.2 us -> 83.4 us (level)
  starting transfers between devices: 18.5 us -> 17.6 us
    ppermute x16, starting transfers between devices: 9.14 us -> 8.26 us  [swapped(): lax.ppermute(block, 'head', [(i, i ^ bit) for i in range(lax.axis_size('h...]
  transfers between devices with their start and end apart: 22 -> 22, of which waited for: 10 -> 10; matrix products, arithmetic and copies ran while one was open for 0% -> 0% of each run, Pallas kernels for 39% -> 43%
where the time goes in v9:
time: 83.4 us; the launch traced here: 83.2 us
  Pallas kernels  50.9 us (61%)
  starting transfers between devices  17.6 us (21%)
  waiting for transfers between devices  13.6 us (16%)
  between operations  0.97 us (1%)
    pallas_call x29, Pallas kernels, __call__(): pl.pallas_call(body, out_shape=outs, in_specs=[WHOLE] * count + [UNREAD]...  38.8 us
    pallas_call x1, Pallas kernels, per_device(): pl.pallas_call(relayout_kernel, grid=(3, blocks), out_shape=(pltpu.VMEM((...  12.2 us
    ppermute x6, starting transfers between devices, moved(): return lax.ppermute(block, ('section', 'head'), route)  9.33 us
    ppermute x16, waiting for transfers between devices, swapped(): lax.ppermute(block, 'head', [(i, i ^ bit) for i in range(lax.axis_size('h...  9.16 us
    ppermute x16, starting transfers between devices, swapped(): lax.ppermute(block, 'head', [(i, i ^ bit) for i in range(lax.axis_size('h...  8.26 us
    ppermute x6, waiting for transfers between devices, moved(): return lax.ppermute(block, ('section', 'head'), route)  4.43 us
  transfers between devices with their start and end apart: 22, of which 10 were waited for; matrix products, arithmetic and copies ran while one was open for 0% of the time, Pallas kernels for 43%

profile of v9, /device:TPU:0, one launch (start us, length us, event | category | flops | bytes accessed | tf_op | source)
XLA Modules:
  0.0 83.2 jit_solution(11082796593642527267)
XLA Ops:
  0.8 12.2 %shard_map.121 = (bf16[3,1024,2048]{2,1,0:T(8,128)(2,1)S(1)}, bf16[3,128,2048]{2,1,0:T(8,128)(2,1)S(1)}, bf16[3,128,2048]{2,1,0:T(8,128)(2,1)S(1)}, f32[16,128,1...) custom-call(s32[6]{0:T(128)} %order_ref.1, bf16[1,128,1024]{2,1,0:T(8,128)(2,1)} %refs_1_.4, ...), custom_call_target="tpu_custom_call" | custom-call | bytes 12582912 | tf_op jit(solution)/shard_map/pallas_call | solution.py:401
  13.0 1.7 %shard_map.122 = (bf16[64,1024]{1,0:T(8,128)(2,1)S(1)}, f32[64,1024]{1,0:T(8,128)S(1)}, bf16[64,1024]{1,0:T(8,128)(2,1)S(1)}) custom-call(f32[4,128]{1,0:T(4,128)S(1)} %broadcast_in_dim.4._.refs_0_, bf16[1,128,1024]{2,1,0:T(8,128)(2,1)S(1)} %copy-done.1, bf16[3,128,2048]{2,1,0:T(8,128)(2,1)S(1)} %get-tuple-element.38.refs_2_.refs_5_, ...), custom_call_target="tpu_custom_call" | custom-call | bytes 128 | tf_op jit(solution)/shard_map/pallas_call | solution.py:341
  15.2 0.8 shard_map.123.refs_4_.refs_3_
  16.3 2.9 %collective-permute-start.1 = (bf16[64,1024]{1,0:T(8,128)(2,1)S(1)}, bf16[64,1024]{1,0:T(8,128)(2,1)S(1)}, u32[]{:S(2)}, u32[]{:S(2)}) collective-permute-start(bf16[64,1024]{1,0:T(8,128)(2,1)S(1)} %shard_map.124.refs_5_.refs_0_), channel_id=1, source_target_pairs={{0,2},{1,3},{2,0},{3,1},{4,6},{5,7},{6,4},{7,5},{8,10},{9,11},{10,... | collective-permute-start | bytes 393224 | tf_op jit(solution)/shard_map/ppermute | solution.py:369
  19.2 2.4 %shard_map.125 = (bf16[3,128,2048]{2,1,0:T(8,128)(2,1)S(1)}, f32[16,128,128]{2,1,0:T(8,128)S(1)}, bf16[64,1024]{1,0:T(8,128)(2,1)S(1)}) custom-call(f32[4,128]{1,0:T(4,128)S(1)} %broadcast_in_dim.4._.refs_0_, bf16[128,1024]{1,0:T(8,128)(2,1)S(1)} %bitcast.23, bf16[3,128,2048]{2,1,0:T(8,128)(2,1)S(1)} %get-tuple-element.44.refs_0_.refs_2_, ...), custom_call_target="tpu_custom_call" | custom-call | bytes 128 | tf_op jit(solution)/shard_map/pallas_call | solution.py:341
  21.6 1.4 %collective-permute-done.1.refs_1_ = bf16[64,1024]{1,0:T(8,128)(2,1)S(1)} collective-permute-done((bf16[64,1024]{1,0:T(8,128)(2,1)S(1)}, bf16[64,1024]{1,0:T(8,128)(2,1)S(1)}, u32[]{:S(2)}, u32[]{:S(2)}) %collective-permute-start.1) | collective-permute-done | bytes 131104 | tf_op jit(solution)/shard_map/ppermute | solution.py:369
  23.0 1.9 %collective-permute-start.2 = (bf16[64,1024]{1,0:T(8,128)(2,1)S(1)}, bf16[64,1024]{1,0:T(8,128)(2,1)S(1)}, u32[]{:S(2)}, u32[]{:S(2)}) collective-permute-start(bf16[64,1024]{1,0:T(8,128)(2,1)S(1)} %shard_map.126.refs_3_.refs_1_), channel_id=1, source_target_pairs={{0,4},{1,5},{2,6},{3,7},{4,8},{5,9},{6,10},{7,11},{8,12},{9,13},{1... | collective-permute-start | bytes 393224 | tf_op jit(solution)/shard_map/ppermute | solution.py:365
  24.9 3.5 %shard_map.127 = (bf16[64,1024]{1,0:T(8,128)(2,1)S(1)}, f32[64,1024]{1,0:T(8,128)S(1)}) custom-call(f32[4,128]{1,0:T(4,128)S(1)} %broadcast_in_dim.4._.refs_0_, bf16[3,128,2048]{2,1,0:T(8,128)(2,1)S(1)} %get-tuple-element.48.refs_1_, bf16[3,1024,2048]{2,1,0:T(8,128)(2,1)S(1)} %get-tuple-element.47.refs_2_.refs_5_, ...), custom_call_target="tpu_custom_call" | custom-call | bytes 128 | tf_op jit(solution)/shard_map/pallas_call | solution.py:341
  28.5 1.5 %collective-permute-done.2.refs_1_ = bf16[64,1024]{1,0:T(8,128)(2,1)S(1)} collective-permute-done((bf16[64,1024]{1,0:T(8,128)(2,1)S(1)}, bf16[64,1024]{1,0:T(8,128)(2,1)S(1)}, u32[]{:S(2)}, u32[]{:S(2)}) %collective-permute-start.2) | collective-permute-done | bytes 131104 | tf_op jit(solution)/shard_map/ppermute | solution.py:365
  30.1 2.0 %collective-permute-start.6 = (bf16[64,1024]{1,0:T(8,128)(2,1)S(1)}, bf16[64,1024]{1,0:T(8,128)(2,1)S(1)}, u32[]{:S(2)}, u32[]{:S(2)}) collective-permute-start(bf16[64,1024]{1,0:T(8,128)(2,1)S(1)} %shard_map.128.refs_8_), channel_id=1, source_target_pairs={{0,12},{1,13},{2,14},{3,15},{4,0},{5,1},{6,2},{7,3},{8,4},{9,5},{1... | collective-permute-start | bytes 393224 | tf_op jit(solution)/shard_map/ppermute | solution.py:365
  32.2 2.9 %collective-permute-start.7 = (bf16[64,1024]{1,0:T(8,128)(2,1)S(1)}, bf16[64,1024]{1,0:T(8,128)(2,1)S(1)}, u32[]{:S(2)}, u32[]{:S(2)}) collective-permute-start(bf16[64,1024]{1,0:T(8,128)(2,1)S(1)} %shard_map.128.refs_8_), channel_id=1, source_target_pairs={{0,14},{1,15},{2,12},{3,13},{4,2},{5,3},{6,0},{7,1},{8,6},{9,7},{1... | collective-permute-start | bytes 393224 | tf_op jit(solution)/shard_map/ppermute | solution.py:365
  35.0 3.6 %shard_map.129 = (bf16[64,1024]{1,0:T(8,128)(2,1)S(1)}, f32[64,1024]{1,0:T(8,128)S(1)}, bf16[64,1024]{1,0:T(8,128)(2,1)S(1)}) custom-call(f32[4,128]{1,0:T(4,128)S(1)} %broadcast_in_dim.4._.refs_0_, bf16[64,1024]{1,0:T(8,128)(2,1)S(1)} %collective-permute-done.2.refs_1_, bf16[64,1024]{1,0:T(8,128)(2,1)S(1)} %collective-permute-done.3.refs_2_, ...), custom_call_target="tpu_custom_call" | custom-call | bytes 128 | tf_op jit(solution)/shard_map/pallas_call | solution.py:341
  38.7 2.6 %shard_map.130.refs_0_.refs_2_.refs_3_ = bf16[3,128,2048]{2,1,0:T(8,128)(2,1)S(1)} custom-call(bf16[3,128,1024]{2,1,0:T(8,128)(2,1)S(1)} %bitcast.19, f32[1,1024]{1,0:T(1,128)S(1)} %copy-done.4, bf16[3,1024,2048]{2,1,0:T(8,128)(2,1)S(1)} %get-tuple-element.47.refs_2_.refs_5_, bf16[64,1024]{1,0:T(8,128)(2,1)S(1)} %get-tuple-element.53.refs_3_), custom_call_target="tpu_custom_call" | custom-call | bytes 128 | tf_op jit(solution)/shard_map/pallas_call | solution.py:341
  41.3 0.8 shard_map.131.refs_4_
  43.7 2.5 %shard_map.134 = (bf16[3,128,2048]{2,1,0:T(8,128)(2,1)S(1)}, f32[16,128,128]{2,1,0:T(8,128)S(1)}, bf16[64,1024]{1,0:T(8,128)(2,1)S(1)}) custom-call(f32[4,128]{1,0:T(4,128)S(1)} %broadcast_in_dim.4._.refs_0_, bf16[64,1024]{1,0:T(8,128)(2,1)S(1)} %shard_map.132.refs_4_.refs_1_, bf16[64,1024]{1,0:T(8,128)(2,1)S(1)} %collective-permute-done.9.refs_2_, ...), custom_call_target="tpu_custom_call" | custom-call | bytes 128 | tf_op jit(solution)/shard_map/pallas_call | solution.py:341
  46.3 2.0 %collective-permute-done.8.refs_1_ = bf16[64,1024]{1,0:T(8,128)(2,1)S(1)} collective-permute-done((bf16[64,1024]{1,0:T(8,128)(2,1)S(1)}, bf16[64,1024]{1,0:T(8,128)(2,1)S(1)}, u32[]{:S(2)}, u32[]{:S(2)}) %collective-permute-start.8) | collective-permute-done | bytes 131104 | tf_op jit(solution)/shard_map/ppermute | solution.py:369
  48.7 3.5 %shard_map.136 = (bf16[64,1024]{1,0:T(8,128)(2,1)S(1)}, f32[64,1024]{1,0:T(8,128)S(1)}) custom-call(f32[4,128]{1,0:T(4,128)S(1)} %broadcast_in_dim.4._.refs_0_, bf16[3,128,2048]{2,1,0:T(8,128)(2,1)S(1)} %get-tuple-element.56.refs_1_, bf16[3,1024,2048]{2,1,0:T(8,128)(2,1)S(1)} %get-tuple-element.47.refs_2_.refs_5_, ...), custom_call_target="tpu_custom_call" | custom-call | bytes 128 | tf_op jit(solution)/shard_map/pallas_call | solution.py:341
  52.2 3.0 %collective-permute-done.10.refs_1_ = bf16[64,1024]{1,0:T(8,128)(2,1)S(1)} collective-permute-done((bf16[64,1024]{1,0:T(8,128)(2,1)S(1)}, bf16[64,1024]{1,0:T(8,128)(2,1)S(1)}, u32[]{:S(2)}, u32[]{:S(2)}) %collective-permute-start.10) | collective-permute-done | bytes 131104 | tf_op jit(solution)/shard_map/ppermute | solution.py:365
  55.4 2.0 %collective-permute-start.14 = (bf16[64,1024]{1,0:T(8,128)(2,1)S(1)}, bf16[64,1024]{1,0:T(8,128)(2,1)S(1)}, u32[]{:S(2)}, u32[]{:S(2)}) collective-permute-start(bf16[64,1024]{1,0:T(8,128)(2,1)S(1)} %shard_map.137.refs_8_), channel_id=1, source_target_pairs={{0,12},{1,13},{2,14},{3,15},{4,0},{5,1},{6,2},{7,3},{8,4},{9,5},{1... | collective-permute-start | bytes 393224 | tf_op jit(solution)/shard_map/ppermute | solution.py:365
  57.7 3.6 %shard_map.138 = (bf16[64,1024]{1,0:T(8,128)(2,1)S(1)}, f32[64,1024]{1,0:T(8,128)S(1)}, bf16[64,1024]{1,0:T(8,128)(2,1)S(1)}) custom-call(f32[4,128]{1,0:T(4,128)S(1)} %broadcast_in_dim.4._.refs_0_, bf16[64,1024]{1,0:T(8,128)(2,1)S(1)} %collective-permute-done.10.refs_1_, bf16[64,1024]{1,0:T(8,128)(2,1)S(1)} %collective-permute-done.11.refs_2_, ...), custom_call_target="tpu_custom_call" | custom-call | bytes 128 | tf_op jit(solution)/shard_map/pallas_call | solution.py:341
  61.3 2.6 %shard_map.139.refs_0_.refs_2_.refs_3_ = bf16[3,128,2048]{2,1,0:T(8,128)(2,1)S(1)} custom-call(bf16[3,128,1024]{2,1,0:T(8,128)(2,1)S(1)} %bitcast.21, f32[1,1024]{1,0:T(1,128)S(1)} %copy-done.4, bf16[3,1024,2048]{2,1,0:T(8,128)(2,1)S(1)} %get-tuple-element.47.refs_2_.refs_5_, bf16[64,1024]{1,0:T(8,128)(2,1)S(1)} %get-tuple-element.61.refs_3_), custom_call_target="tpu_custom_call" | custom-call | bytes 128 | tf_op jit(solution)/shard_map/pallas_call | solution.py:341
  63.9 0.8 shard_map.140.refs_4_
  65.4 0.7 collective-permute-done.13.refs_2_
  66.1 1.5 %collective-permute-start.16 = (bf16[64,1024]{1,0:T(8,128)(2,1)S(1)}, bf16[64,1024]{1,0:T(8,128)(2,1)S(1)}, u32[]{:S(2)}, u32[]{:S(2)}) collective-permute-start(bf16[64,1024]{1,0:T(8,128)(2,1)S(1)} %shard_map.142.refs_7_.refs_0_), channel_id=1, source_target_pairs={{0,2},{1,3},{2,0},{3,1},{4,6},{5,7},{6,4},{7,5},{8,10},{9,11},{10,... | collective-permute-start | bytes 393224 | tf_op jit(solution)/shard_map/ppermute | solution.py:369
  67.7 2.5 %shard_map.143 = (bf16[3,128,2048]{2,1,0:T(8,128)(2,1)S(1)}, f32[16,128,128]{2,1,0:T(8,128)S(1)}, bf16[64,1024]{1,0:T(8,128)(2,1)S(1)}) custom-call(f32[4,128]{1,0:T(4,128)S(1)} %broadcast_in_dim.4._.refs_0_, bf16[64,1024]{1,0:T(8,128)(2,1)S(1)} %shard_map.141.refs_4_.refs_1_, bf16[64,1024]{1,0:T(8,128)(2,1)S(1)} %collective-permute-done.17.refs_2_, ...), custom_call_target="tpu_custom_call" | custom-call | bytes 128 | tf_op jit(solution)/shard_map/pallas_call | solution.py:341
  70.2 3.5 %shard_map.144 = (bf16[64,1024]{1,0:T(8,128)(2,1)S(1)}, f32[64,1024]{1,0:T(8,128)S(1)}) custom-call(f32[4,128]{1,0:T(4,128)S(1)} %broadcast_in_dim.4._.refs_0_, bf16[3,128,2048]{2,1,0:T(8,128)(2,1)S(1)} %get-tuple-element.63.refs_1_, bf16[3,1024,2048]{2,1,0:T(8,128)(2,1)S(1)} %get-tuple-element.47.refs_2_.refs_5_, ...), custom_call_target="tpu_custom_call" | custom-call | bytes 128 | tf_op jit(solution)/shard_map/pallas_call | solution.py:341
  74.4 0.7 collective-permute-done.19.refs_4_
  76.0 0.8 shard_map.147
  76.8 1.7 %shard_map.148 = (f32[16,32]{1,0:T(8,128)}, f32[8,128]{1,0:T(8,128)S(1)}) custom-call(f32[16,128,128]{2,1,0:T(8,128)S(1)} %get-tuple-element.68.refs_0_, s32[128,128]{1,0:T(8,128)S(1)} %copy-done.2, f32[8,128]{1,0:T(8,128)S(1)} %get-tuple-element.69.refs_2_), custom_call_target="tpu_custom_call" | custom-call | bytes 128 | tf_op jit(solution)/shard_map/pallas_call | solution.py:341
  78.4 2.5 %collective-permute-done.20.refs_1_ = bf16[64,1024]{1,0:T(8,128)(2,1)S(1)} collective-permute-done((bf16[64,1024]{1,0:T(8,128)(2,1)S(1)}, bf16[64,1024]{1,0:T(8,128)(2,1)S(1)}, u32[]{:S(2)}, u32[]{:S(2)}) %collective-permute-start.20) | collective-permute-done | bytes 131104 | tf_op jit(solution)/shard_map/ppermute | solution.py:369
  81.1 1.3 %collective-permute-done.21.refs_2_ = bf16[64,1024]{1,0:T(8,128)(2,1)S(1)} collective-permute-done((bf16[64,1024]{1,0:T(8,128)(2,1)S(1)}, bf16[64,1024]{1,0:T(8,128)(2,1)S(1)}, u32[]{:S(2)}, u32[]{:S(2)}) %collective-permute-start.21) | collective-permute-done | bytes 131104 | tf_op jit(solution)/shard_map/ppermute | solution.py:369
  82.4 0.8 shard_map.150
  (54 shorter events, 6.1 us)
Async XLA Ops:
  0.8 12.2 %copy-start.1 = (bf16[1,128,1024]{2,1,0:T(8,128)(2,1)S(1)}, bf16[1,128,1024]{2,1,0:T(8,128)(2,1)}, u32[]{:S(2)}) copy-start(bf16[1,128,1024]{2,1,0:T(8,128)(2,1)} %refs_1_.4) | copy-start | bytes 786436
  14.7 1.5 %collective-permute-start = (bf16[64,1024]{1,0:T(8,128)(2,1)S(1)}, bf16[64,1024]{1,0:T(8,128)(2,1)S(1)}, u32[]{:S(2)}, u32[]{:S(2)}) collective-permute-start(bf16[64,1024]{1,0:T(8,128)(2,1)S(1)} %get-tuple-element.42), channel_id=1, source_target_pairs={{0,1},{1,0},{2,3},{3,2},{4,5},{5,4},{6,7},{7,6},{8,9},{9,8},{10,11... | collective-permute-start | bytes 393224 | tf_op jit(solution)/shard_map/ppermute | solution.py:369
  16.0 3.2 %copy-start.3 = (bf16[1,128,1024]{2,1,0:T(8,128)(2,1)S(1)}, bf16[1,128,1024]{2,1,0:T(8,128)(2,1)}, u32[]{:S(2)}) copy-start(bf16[1,128,1024]{2,1,0:T(8,128)(2,1)} %param.11) | copy-start | bytes 786436
  16.3 6.7 %collective-permute-start.1 = (bf16[64,1024]{1,0:T(8,128)(2,1)S(1)}, bf16[64,1024]{1,0:T(8,128)(2,1)S(1)}, u32[]{:S(2)}, u32[]{:S(2)}) collective-permute-start(bf16[64,1024]{1,0:T(8,128)(2,1)S(1)} %shard_map.124.refs_5_.refs_0_), channel_id=1, source_target_pairs={{0,2},{1,3},{2,0},{3,1},{4,6},{5,7},{6,4},{7,5},{8,10},{9,11},{10,... | collective-permute-start | bytes 393224 | tf_op jit(solution)/shard_map/ppermute | solution.py:369
  23.0 6.9 %collective-permute-start.2 = (bf16[64,1024]{1,0:T(8,128)(2,1)S(1)}, bf16[64,1024]{1,0:T(8,128)(2,1)S(1)}, u32[]{:S(2)}, u32[]{:S(2)}) collective-permute-start(bf16[64,1024]{1,0:T(8,128)(2,1)S(1)} %shard_map.126.refs_3_.refs_1_), channel_id=1, source_target_pairs={{0,4},{1,5},{2,6},{3,7},{4,8},{5,9},{6,10},{7,11},{8,12},{9,13},{1... | collective-permute-start | bytes 393224 | tf_op jit(solution)/shard_map/ppermute | solution.py:365
  24.9 5.0 %copy-start = (bf16[1,3,128,1024]{3,2,1,0:T(8,128)(2,1)S(1)}, bf16[1,3,128,1024]{3,2,1,0:T(8,128)(2,1)}, u32[]{:S(2)}) copy-start(bf16[1,3,128,1024]{3,2,1,0:T(8,128)(2,1)} %kept_ref.1) | copy-start | bytes 2359300
  24.9 5.0 %copy-start.4 = (f32[1,1024]{1,0:T(1,128)S(1)}, f32[1,1024]{1,0:T(1,128)}, u32[]{:S(2)}) copy-start(f32[1,1024]{1,0:T(1,128)} %refs_2_.5) | copy-start | bytes 12292
  28.4 1.5 %collective-permute-start.4 = (bf16[64,1024]{1,0:T(8,128)(2,1)S(1)}, bf16[64,1024]{1,0:T(8,128)(2,1)S(1)}, u32[]{:S(2)}, u32[]{:S(2)}) collective-permute-start(bf16[64,1024]{1,0:T(8,128)(2,1)S(1)} %get-tuple-element.50), channel_id=1, source_target_pairs={{0,1},{1,0},{2,3},{3,2},{4,5},{5,4},{6,7},{7,6},{8,9},{9,8},{10,11... | collective-permute-start | bytes 393224 | tf_op jit(solution)/shard_map/ppermute | solution.py:369
  29.9 5.1 %collective-permute-start.3 = (bf16[64,1024]{1,0:T(8,128)(2,1)S(1)}, bf16[64,1024]{1,0:T(8,128)(2,1)S(1)}, u32[]{:S(2)}, u32[]{:S(2)}) collective-permute-start(bf16[64,1024]{1,0:T(8,128)(2,1)S(1)} %collective-permute-done.2.refs_1_), channel_id=1, source_target_pairs={{0,1},{1,0},{2,3},{3,2},{4,5},{5,4},{6,7},{7,6},{8,9},{9,8},{10,11... | collective-permute-start | bytes 393224 | tf_op jit(solution)/shard_map/ppermute | solution.py:369
  30.1 12.0 %collective-permute-start.6 = (bf16[64,1024]{1,0:T(8,128)(2,1)S(1)}, bf16[64,1024]{1,0:T(8,128)(2,1)S(1)}, u32[]{:S(2)}, u32[]{:S(2)}) collective-permute-start(bf16[64,1024]{1,0:T(8,128)(2,1)S(1)} %shard_map.128.refs_8_), channel_id=1, source_target_pairs={{0,12},{1,13},{2,14},{3,15},{4,0},{5,1},{6,2},{7,3},{8,4},{9,5},{1... | collective-permute-start | bytes 393224 | tf_op jit(solution)/shard_map/ppermute | solution.py:365
  32.2 9.9 %collective-permute-start.7 = (bf16[64,1024]{1,0:T(8,128)(2,1)S(1)}, bf16[64,1024]{1,0:T(8,128)(2,1)S(1)}, u32[]{:S(2)}, u32[]{:S(2)}) collective-permute-start(bf16[64,1024]{1,0:T(8,128)(2,1)S(1)} %shard_map.128.refs_8_), channel_id=1, source_target_pairs={{0,14},{1,15},{2,12},{3,13},{4,2},{5,3},{6,0},{7,1},{8,6},{9,7},{1... | collective-permute-start | bytes 393224 | tf_op jit(solution)/shard_map/ppermute | solution.py:365
  38.6 4.1 %collective-permute-start.5 = (bf16[64,1024]{1,0:T(8,128)(2,1)S(1)}, bf16[64,1024]{1,0:T(8,128)(2,1)S(1)}, u32[]{:S(2)}, u32[]{:S(2)}) collective-permute-start(bf16[64,1024]{1,0:T(8,128)(2,1)S(1)} %get-tuple-element.52), channel_id=1, source_target_pairs={{0,1},{1,0},{2,3},{3,2},{4,5},{5,4},{6,7},{7,6},{8,9},{9,8},{10,11... | collective-permute-start | bytes 393224 | tf_op jit(solution)/shard_map/ppermute | solution.py:369
  42.2 1.5 %collective-permute-start.9 = (bf16[64,1024]{1,0:T(8,128)(2,1)S(1)}, bf16[64,1024]{1,0:T(8,128)(2,1)S(1)}, u32[]{:S(2)}, u32[]{:S(2)}) collective-permute-start(bf16[64,1024]{1,0:T(8,128)(2,1)S(1)} %shard_map.132.refs_4_.refs_1_), channel_id=1, source_target_pairs={{0,1},{1,0},{2,3},{3,2},{4,5},{5,4},{6,7},{7,6},{8,9},{9,8},{10,11... | collective-permute-start | bytes 393224 | tf_op jit(solution)/shard_map/ppermute | solution.py:369
  42.8 5.5 %collective-permute-start.8 = (bf16[64,1024]{1,0:T(8,128)(2,1)S(1)}, bf16[64,1024]{1,0:T(8,128)(2,1)S(1)}, u32[]{:S(2)}, u32[]{:S(2)}) collective-permute-start(bf16[64,1024]{1,0:T(8,128)(2,1)S(1)} %shard_map.133.refs_7_.refs_0_), channel_id=1, source_target_pairs={{0,2},{1,3},{2,0},{3,1},{4,6},{5,7},{6,4},{7,5},{8,10},{9,11},{10,... | collective-permute-start | bytes 393224 | tf_op jit(solution)/shard_map/ppermute | solution.py:369
  48.4 6.8 %collective-permute-start.10 = (bf16[64,1024]{1,0:T(8,128)(2,1)S(1)}, bf16[64,1024]{1,0:T(8,128)(2,1)S(1)}, u32[]{:S(2)}, u32[]{:S(2)}) collective-permute-start(bf16[64,1024]{1,0:T(8,128)(2,1)S(1)} %shard_map.135.refs_3_.refs_1_), channel_id=1, source_target_pairs={{0,4},{1,5},{2,6},{3,7},{4,8},{5,9},{6,10},{7,11},{8,12},{9,13},{1... | collective-permute-start | bytes 393224 | tf_op jit(solution)/shard_map/ppermute | solution.py:365
  52.1 3.0 %collective-permute-start.12 = (bf16[64,1024]{1,0:T(8,128)(2,1)S(1)}, bf16[64,1024]{1,0:T(8,128)(2,1)S(1)}, u32[]{:S(2)}, u32[]{:S(2)}) collective-permute-start(bf16[64,1024]{1,0:T(8,128)(2,1)S(1)} %get-tuple-element.58), channel_id=1, source_target_pairs={{0,1},{1,0},{2,3},{3,2},{4,5},{5,4},{6,7},{7,6},{8,9},{9,8},{10,11... | collective-permute-start | bytes 393224 | tf_op jit(solution)/shard_map/ppermute | solution.py:369
  55.2 2.5 %collective-permute-start.11 = (bf16[64,1024]{1,0:T(8,128)(2,1)S(1)}, bf16[64,1024]{1,0:T(8,128)(2,1)S(1)}, u32[]{:S(2)}, u32[]{:S(2)}) collective-permute-start(bf16[64,1024]{1,0:T(8,128)(2,1)S(1)} %collective-permute-done.10.refs_1_), channel_id=1, source_target_pairs={{0,1},{1,0},{2,3},{3,2},{4,5},{5,4},{6,7},{7,6},{8,9},{9,8},{10,11... | collective-permute-start | bytes 393224 | tf_op jit(solution)/shard_map/ppermute | solution.py:369
  55.4 9.3 %collective-permute-start.14 = (bf16[64,1024]{1,0:T(8,128)(2,1)S(1)}, bf16[64,1024]{1,0:T(8,128)(2,1)S(1)}, u32[]{:S(2)}, u32[]{:S(2)}) collective-permute-start(bf16[64,1024]{1,0:T(8,128)(2,1)S(1)} %shard_map.137.refs_8_), channel_id=1, source_target_pairs={{0,12},{1,13},{2,14},{3,15},{4,0},{5,1},{6,2},{7,3},{8,4},{9,5},{1... | collective-permute-start | bytes 393224 | tf_op jit(solution)/shard_map/ppermute | solution.py:365
  57.4 7.3 %collective-permute-start.15 = (bf16[64,1024]{1,0:T(8,128)(2,1)S(1)}, bf16[64,1024]{1,0:T(8,128)(2,1)S(1)}, u32[]{:S(2)}, u32[]{:S(2)}) collective-permute-start(bf16[64,1024]{1,0:T(8,128)(2,1)S(1)} %shard_map.137.refs_8_), channel_id=1, source_target_pairs={{0,14},{1,15},{2,12},{3,13},{4,2},{5,3},{6,0},{7,1},{8,6},{9,7},{1... | collective-permute-start | bytes 393224 | tf_op jit(solution)/shard_map/ppermute | solution.py:365
  64.7 1.4 %collective-permute-start.13 = (bf16[64,1024]{1,0:T(8,128)(2,1)S(1)}, bf16[64,1024]{1,0:T(8,128)(2,1)S(1)}, u32[]{:S(2)}, u32[]{:S(2)}) collective-permute-start(bf16[64,1024]{1,0:T(8,128)(2,1)S(1)} %get-tuple-element.60), channel_id=1, source_target_pairs={{0,1},{1,0},{2,3},{3,2},{4,5},{5,4},{6,7},{7,6},{8,9},{9,8},{10,11... | collective-permute-start | bytes 393224 | tf_op jit(solution)/shard_map/ppermute | solution.py:369
  64.8 2.9 %collective-permute-start.17 = (bf16[64,1024]{1,0:T(8,128)(2,1)S(1)}, bf16[64,1024]{1,0:T(8,128)(2,1)S(1)}, u32[]{:S(2)}, u32[]{:S(2)}) collective-permute-start(bf16[64,1024]{1,0:T(8,128)(2,1)S(1)} %shard_map.141.refs_4_.refs_1_), channel_id=1, source_target_pairs={{0,1},{1,0},{2,3},{3,2},{4,5},{5,4},{6,7},{7,6},{8,9},{9,8},{10,11... | collective-permute-start | bytes 393224 | tf_op jit(solution)/shard_map/ppermute | solution.py:369
  66.1 7.7 %collective-permute-start.16 = (bf16[64,1024]{1,0:T(8,128)(2,1)S(1)}, bf16[64,1024]{1,0:T(8,128)(2,1)S(1)}, u32[]{:S(2)}, u32[]{:S(2)}) collective-permute-start(bf16[64,1024]{1,0:T(8,128)(2,1)S(1)} %shard_map.142.refs_7_.refs_0_), channel_id=1, source_target_pairs={{0,2},{1,3},{2,0},{3,1},{4,6},{5,7},{6,4},{7,5},{8,10},{9,11},{10,... | collective-permute-start | bytes 393224 | tf_op jit(solution)/shard_map/ppermute | solution.py:369
  73.7 3.1 %copy-start.2 = (s32[128,128]{1,0:T(8,128)S(1)}, s32[128,128]{1,0:T(8,128)}, u32[]{:S(2)}) copy-start(s32[128,128]{1,0:T(8,128)} %refs_1_.7) | copy-start | bytes 196612
  73.7 1.4 %collective-permute-start.19 = (bf16[64,1024]{1,0:T(8,128)(2,1)S(1)}, bf16[64,1024]{1,0:T(8,128)(2,1)S(1)}, u32[]{:S(2)}, u32[]{:S(2)}) collective-permute-start(bf16[64,1024]{1,0:T(8,128)(2,1)S(1)} %get-tuple-element.66), channel_id=1, source_target_pairs={{0,1},{1,0},{2,3},{3,2},{4,5},{5,4},{6,7},{7,6},{8,9},{9,8},{10,11... | collective-permute-start | bytes 393224 | tf_op jit(solution)/shard_map/ppermute | solution.py:369
  73.9 2.1 %collective-permute-start.18 = (bf16[64,1024]{1,0:T(8,128)(2,1)S(1)}, bf16[64,1024]{1,0:T(8,128)(2,1)S(1)}, u32[]{:S(2)}, u32[]{:S(2)}) collective-permute-start(bf16[64,1024]{1,0:T(8,128)(2,1)S(1)} %shard_map.145.refs_6_.refs_1_), channel_id=1, source_target_pairs={{0,1},{1,0},{2,3},{3,2},{4,5},{5,4},{6,7},{7,6},{8,9},{9,8},{10,11... | collective-permute-start | bytes 393224 | tf_op jit(solution)/shard_map/ppermute | solution.py:369
  75.4 5.6 %collective-permute-start.20 = (bf16[64,1024]{1,0:T(8,128)(2,1)S(1)}, bf16[64,1024]{1,0:T(8,128)(2,1)S(1)}, u32[]{:S(2)}, u32[]{:S(2)}) collective-permute-start(bf16[64,1024]{1,0:T(8,128)(2,1)S(1)} %shard_map.146.refs_3_.refs_0_), channel_id=1, source_target_pairs={{0,2},{1,3},{2,0},{3,1},{4,6},{5,7},{6,4},{7,5},{8,10},{9,11},{10,... | collective-permute-start | bytes 393224 | tf_op jit(solution)/shard_map/ppermute | solution.py:369
  81.0 1.4 %collective-permute-start.21 = (bf16[64,1024]{1,0:T(8,128)(2,1)S(1)}, bf16[64,1024]{1,0:T(8,128)(2,1)S(1)}, u32[]{:S(2)}, u32[]{:S(2)}) collective-permute-start(bf16[64,1024]{1,0:T(8,128)(2,1)S(1)} %shard_map.149.refs_1_.refs_3_), channel_id=1, source_target_pairs={{0,1},{1,0},{2,3},{3,2},{4,5},{5,4},{6,7},{7,6},{8,9},{9,8},{10,11... | collective-permute-start | bytes 393224 | tf_op jit(solution)/shard_map/ppermute | solution.py:369

commit v10 on v9

--- a/solution.py
+++ b/solution.py
@@ -213,8 +213,8 @@
     lax.fori_loop(0, 2, step, 0)
 
 
-def grad_attend(g, qkv_ref, probs_ref, wo_ref, acc_in_ref, stacked, acc_ref, part):
-    heads = probs_ref.shape[0] // 2
+def grad_attend(g, qkv_ref, probs_ref, wo_ref, acc_in_ref, stacked, acc_ref, parts, part):
+    heads = probs_ref.shape[0] // parts
     scale = LANES ** (-0.5)
     at = slice(part * heads * LANES, (part + 1) * heads * LANES)
     grad_attn = dot(g, wo_ref[at], LAST).astype(BF16)
@@ -248,8 +248,7 @@
         stacked, acc_ref, g_half_ref = refs
         g = joined(second, mine_ref[...], other_ref[...]).astype(BF16)
     g_half_ref[...] = own_half(second, g).astype(BF16)
-    for part in range(2):
-        grad_attend(g, qkv_ref, probs_ref, wo_ref, acc_in_ref, stacked, acc_ref, part)
+    grad_attend(g, qkv_ref, probs_ref, wo_ref, acc_in_ref, stacked, acc_ref, 1, 0)
 
 
 def input_gradient_kernel(flags_ref, stacked, w_ref, send_ref, keep_ref):

time: 83.4 us -> 83.4 us (level)
  no operation moved by 1% of the time
where the time goes in v10:
time: 83.4 us; the launch traced here: 83.3 us
  Pallas kernels  50.9 us (61%)
  starting transfers between devices  17.6 us (21%)
  waiting for transfers between devices  13.6 us (16%)
  between operations  0.97 us (1%)
    pallas_call x29, Pallas kernels, __call__(): pl.pallas_call(body, out_shape=outs, in_specs=[WHOLE] * count + [UNREAD]...  38.8 us
    pallas_call x1, Pallas kernels, per_device(): pl.pallas_call(relayout_kernel, grid=(3, blocks), out_shape=(pltpu.VMEM((...  12.2 us
    ppermute x6, starting transfers between devices, moved(): return lax.ppermute(block, ('section', 'head'), route)  9.33 us
    ppermute x16, waiting for transfers between devices, swapped(): lax.ppermute(block, 'head', [(i, i ^ bit) for i in range(lax.axis_size('h...  9.15 us
    ppermute x16, starting transfers between devices, swapped(): lax.ppermute(block, 'head', [(i, i ^ bit) for i in range(lax.axis_size('h...  8.26 us
    ppermute x6, waiting for transfers between devices, moved(): return lax.ppermute(block, ('section', 'head'), route)  4.43 us
  transfers between devices with their start and end apart: 22, of which 10 were waited for; matrix products, arithmetic and copies ran while one was open for 0% of the time, Pallas kernels for 43%

profile of v10, /device:TPU:0, one launch (start us, length us, event | category | flops | bytes accessed | tf_op | source)
XLA Modules:
  0.0 83.3 jit_solution(1267621987008017618)
XLA Ops:
  0.8 12.2 %shard_map.121 = (bf16[3,1024,2048]{2,1,0:T(8,128)(2,1)S(1)}, bf16[3,128,2048]{2,1,0:T(8,128)(2,1)S(1)}, bf16[3,128,2048]{2,1,0:T(8,128)(2,1)S(1)}, f32[16,128,1...) custom-call(s32[6]{0:T(128)} %order_ref.1, bf16[1,128,1024]{2,1,0:T(8,128)(2,1)} %refs_1_.4, ...), custom_call_target="tpu_custom_call" | custom-call | bytes 12582912 | tf_op jit(solution)/shard_map/pallas_call | solution.py:400
  13.0 1.7 %shard_map.122 = (bf16[64,1024]{1,0:T(8,128)(2,1)S(1)}, f32[64,1024]{1,0:T(8,128)S(1)}, bf16[64,1024]{1,0:T(8,128)(2,1)S(1)}) custom-call(f32[4,128]{1,0:T(4,128)S(1)} %broadcast_in_dim.4._.refs_0_, bf16[1,128,1024]{2,1,0:T(8,128)(2,1)S(1)} %copy-done.1, bf16[3,128,2048]{2,1,0:T(8,128)(2,1)S(1)} %get-tuple-element.38.refs_2_.refs_5_, ...), custom_call_target="tpu_custom_call" | custom-call | bytes 128 | tf_op jit(solution)/shard_map/pallas_call | solution.py:340
  15.2 0.8 shard_map.123.refs_4_.refs_3_
  16.3 2.9 %collective-permute-start.1 = (bf16[64,1024]{1,0:T(8,128)(2,1)S(1)}, bf16[64,1024]{1,0:T(8,128)(2,1)S(1)}, u32[]{:S(2)}, u32[]{:S(2)}) collective-permute-start(bf16[64,1024]{1,0:T(8,128)(2,1)S(1)} %shard_map.124.refs_5_.refs_0_), channel_id=1, source_target_pairs={{0,2},{1,3},{2,0},{3,1},{4,6},{5,7},{6,4},{7,5},{8,10},{9,11},{10,... | collective-permute-start | bytes 393224 | tf_op jit(solution)/shard_map/ppermute | solution.py:368
  19.2 2.4 %shard_map.125 = (bf16[3,128,2048]{2,1,0:T(8,128)(2,1)S(1)}, f32[16,128,128]{2,1,0:T(8,128)S(1)}, bf16[64,1024]{1,0:T(8,128)(2,1)S(1)}) custom-call(f32[4,128]{1,0:T(4,128)S(1)} %broadcast_in_dim.4._.refs_0_, bf16[128,1024]{1,0:T(8,128)(2,1)S(1)} %bitcast.23, bf16[3,128,2048]{2,1,0:T(8,128)(2,1)S(1)} %get-tuple-element.44.refs_0_.refs_2_, ...), custom_call_target="tpu_custom_call" | custom-call | bytes 128 | tf_op jit(solution)/shard_map/pallas_call | solution.py:340
  21.6 1.4 %collective-permute-done.1.refs_1_ = bf16[64,1024]{1,0:T(8,128)(2,1)S(1)} collective-permute-done((bf16[64,1024]{1,0:T(8,128)(2,1)S(1)}, bf16[64,1024]{1,0:T(8,128)(2,1)S(1)}, u32[]{:S(2)}, u32[]{:S(2)}) %collective-permute-start.1) | collective-permute-done | bytes 131104 | tf_op jit(solution)/shard_map/ppermute | solution.py:368
  23.0 1.9 %collective-permute-start.2 = (bf16[64,1024]{1,0:T(8,128)(2,1)S(1)}, bf16[64,1024]{1,0:T(8,128)(2,1)S(1)}, u32[]{:S(2)}, u32[]{:S(2)}) collective-permute-start(bf16[64,1024]{1,0:T(8,128)(2,1)S(1)} %shard_map.126.refs_3_.refs_1_), channel_id=1, source_target_pairs={{0,4},{1,5},{2,6},{3,7},{4,8},{5,9},{6,10},{7,11},{8,12},{9,13},{1... | collective-permute-start | bytes 393224 | tf_op jit(solution)/shard_map/ppermute | solution.py:364
  24.9 3.5 %shard_map.127 = (bf16[64,1024]{1,0:T(8,128)(2,1)S(1)}, f32[64,1024]{1,0:T(8,128)S(1)}) custom-call(f32[4,128]{1,0:T(4,128)S(1)} %broadcast_in_dim.4._.refs_0_, bf16[3,128,2048]{2,1,0:T(8,128)(2,1)S(1)} %get-tuple-element.48.refs_1_, bf16[3,1024,2048]{2,1,0:T(8,128)(2,1)S(1)} %get-tuple-element.47.refs_2_.refs_5_, ...), custom_call_target="tpu_custom_call" | custom-call | bytes 128 | tf_op jit(solution)/shard_map/pallas_call | solution.py:340
  28.5 1.5 %collective-permute-done.2.refs_1_ = bf16[64,1024]{1,0:T(8,128)(2,1)S(1)} collective-permute-done((bf16[64,1024]{1,0:T(8,128)(2,1)S(1)}, bf16[64,1024]{1,0:T(8,128)(2,1)S(1)}, u32[]{:S(2)}, u32[]{:S(2)}) %collective-permute-start.2) | collective-permute-done | bytes 131104 | tf_op jit(solution)/shard_map/ppermute | solution.py:364
  30.1 2.0 %collective-permute-start.6 = (bf16[64,1024]{1,0:T(8,128)(2,1)S(1)}, bf16[64,1024]{1,0:T(8,128)(2,1)S(1)}, u32[]{:S(2)}, u32[]{:S(2)}) collective-permute-start(bf16[64,1024]{1,0:T(8,128)(2,1)S(1)} %shard_map.128.refs_8_), channel_id=1, source_target_pairs={{0,12},{1,13},{2,14},{3,15},{4,0},{5,1},{6,2},{7,3},{8,4},{9,5},{1... | collective-permute-start | bytes 393224 | tf_op jit(solution)/shard_map/ppermute | solution.py:364
  32.2 2.9 %collective-permute-start.7 = (bf16[64,1024]{1,0:T(8,128)(2,1)S(1)}, bf16[64,1024]{1,0:T(8,128)(2,1)S(1)}, u32[]{:S(2)}, u32[]{:S(2)}) collective-permute-start(bf16[64,1024]{1,0:T(8,128)(2,1)S(1)} %shard_map.128.refs_8_), channel_id=1, source_target_pairs={{0,14},{1,15},{2,12},{3,13},{4,2},{5,3},{6,0},{7,1},{8,6},{9,7},{1... | collective-permute-start | bytes 393224 | tf_op jit(solution)/shard_map/ppermute | solution.py:364
  35.0 3.6 %shard_map.129 = (bf16[64,1024]{1,0:T(8,128)(2,1)S(1)}, f32[64,1024]{1,0:T(8,128)S(1)}, bf16[64,1024]{1,0:T(8,128)(2,1)S(1)}) custom-call(f32[4,128]{1,0:T(4,128)S(1)} %broadcast_in_dim.4._.refs_0_, bf16[64,1024]{1,0:T(8,128)(2,1)S(1)} %collective-permute-done.2.refs_1_, bf16[64,1024]{1,0:T(8,128)(2,1)S(1)} %collective-permute-done.3.refs_2_, ...), custom_call_target="tpu_custom_call" | custom-call | bytes 128 | tf_op jit(solution)/shard_map/pallas_call | solution.py:340
  38.7 2.6 %shard_map.130.refs_0_.refs_2_.refs_3_ = bf16[3,128,2048]{2,1,0:T(8,128)(2,1)S(1)} custom-call(bf16[3,128,1024]{2,1,0:T(8,128)(2,1)S(1)} %bitcast.19, f32[1,1024]{1,0:T(1,128)S(1)} %copy-done.4, bf16[3,1024,2048]{2,1,0:T(8,128)(2,1)S(1)} %get-tuple-element.47.refs_2_.refs_5_, bf16[64,1024]{1,0:T(8,128)(2,1)S(1)} %get-tuple-element.53.refs_3_), custom_call_target="tpu_custom_call" | custom-call | bytes 128 | tf_op jit(solution)/shard_map/pallas_call | solution.py:340
  41.3 0.8 shard_map.131.refs_4_
  43.7 2.6 %shard_map.134 = (bf16[3,128,2048]{2,1,0:T(8,128)(2,1)S(1)}, f32[16,128,128]{2,1,0:T(8,128)S(1)}, bf16[64,1024]{1,0:T(8,128)(2,1)S(1)}) custom-call(f32[4,128]{1,0:T(4,128)S(1)} %broadcast_in_dim.4._.refs_0_, bf16[64,1024]{1,0:T(8,128)(2,1)S(1)} %shard_map.132.refs_4_.refs_1_, bf16[64,1024]{1,0:T(8,128)(2,1)S(1)} %collective-permute-done.9.refs_2_, ...), custom_call_target="tpu_custom_call" | custom-call | bytes 128 | tf_op jit(solution)/shard_map/pallas_call | solution.py:340
  46.3 2.0 %collective-permute-done.8.refs_1_ = bf16[64,1024]{1,0:T(8,128)(2,1)S(1)} collective-permute-done((bf16[64,1024]{1,0:T(8,128)(2,1)S(1)}, bf16[64,1024]{1,0:T(8,128)(2,1)S(1)}, u32[]{:S(2)}, u32[]{:S(2)}) %collective-permute-start.8) | collective-permute-done | bytes 131104 | tf_op jit(solution)/shard_map/ppermute | solution.py:368
  48.7 3.5 %shard_map.136 = (bf16[64,1024]{1,0:T(8,128)(2,1)S(1)}, f32[64,1024]{1,0:T(8,128)S(1)}) custom-call(f32[4,128]{1,0:T(4,128)S(1)} %broadcast_in_dim.4._.refs_0_, bf16[3,128,2048]{2,1,0:T(8,128)(2,1)S(1)} %get-tuple-element.56.refs_1_, bf16[3,1024,2048]{2,1,0:T(8,128)(2,1)S(1)} %get-tuple-element.47.refs_2_.refs_5_, ...), custom_call_target="tpu_custom_call" | custom-call | bytes 128 | tf_op jit(solution)/shard_map/pallas_call | solution.py:340
  52.2 3.0 %collective-permute-done.10.refs_1_ = bf16[64,1024]{1,0:T(8,128)(2,1)S(1)} collective-permute-done((bf16[64,1024]{1,0:T(8,128)(2,1)S(1)}, bf16[64,1024]{1,0:T(8,128)(2,1)S(1)}, u32[]{:S(2)}, u32[]{:S(2)}) %collective-permute-start.10) | collective-permute-done | bytes 131104 | tf_op jit(solution)/shard_map/ppermute | solution.py:364
  55.4 2.0 %collective-permute-start.14 = (bf16[64,1024]{1,0:T(8,128)(2,1)S(1)}, bf16[64,1024]{1,0:T(8,128)(2,1)S(1)}, u32[]{:S(2)}, u32[]{:S(2)}) collective-permute-start(bf16[64,1024]{1,0:T(8,128)(2,1)S(1)} %shard_map.137.refs_8_), channel_id=1, source_target_pairs={{0,12},{1,13},{2,14},{3,15},{4,0},{5,1},{6,2},{7,3},{8,4},{9,5},{1... | collective-permute-start | bytes 393224 | tf_op jit(solution)/shard_map/ppermute | solution.py:364
  57.7 3.6 %shard_map.138 = (bf16[64,1024]{1,0:T(8,128)(2,1)S(1)}, f32[64,1024]{1,0:T(8,128)S(1)}, bf16[64,1024]{1,0:T(8,128)(2,1)S(1)}) custom-call(f32[4,128]{1,0:T(4,128)S(1)} %broadcast_in_dim.4._.refs_0_, bf16[64,1024]{1,0:T(8,128)(2,1)S(1)} %collective-permute-done.10.refs_1_, bf16[64,1024]{1,0:T(8,128)(2,1)S(1)} %collective-permute-done.11.refs_2_, ...), custom_call_target="tpu_custom_call" | custom-call | bytes 128 | tf_op jit(solution)/shard_map/pallas_call | solution.py:340
  61.3 2.6 %shard_map.139.refs_0_.refs_2_.refs_3_ = bf16[3,128,2048]{2,1,0:T(8,128)(2,1)S(1)} custom-call(bf16[3,128,1024]{2,1,0:T(8,128)(2,1)S(1)} %bitcast.21, f32[1,1024]{1,0:T(1,128)S(1)} %copy-done.4, bf16[3,1024,2048]{2,1,0:T(8,128)(2,1)S(1)} %get-tuple-element.47.refs_2_.refs_5_, bf16[64,1024]{1,0:T(8,128)(2,1)S(1)} %get-tuple-element.61.refs_3_), custom_call_target="tpu_custom_call" | custom-call | bytes 128 | tf_op jit(solution)/shard_map/pallas_call | solution.py:340
  63.9 0.8 shard_map.140.refs_4_
  65.4 0.7 collective-permute-done.13.refs_2_
  66.1 1.5 %collective-permute-start.16 = (bf16[64,1024]{1,0:T(8,128)(2,1)S(1)}, bf16[64,1024]{1,0:T(8,128)(2,1)S(1)}, u32[]{:S(2)}, u32[]{:S(2)}) collective-permute-start(bf16[64,1024]{1,0:T(8,128)(2,1)S(1)} %shard_map.142.refs_7_.refs_0_), channel_id=1, source_target_pairs={{0,2},{1,3},{2,0},{3,1},{4,6},{5,7},{6,4},{7,5},{8,10},{9,11},{10,... | collective-permute-start | bytes 393224 | tf_op jit(solution)/shard_map/ppermute | solution.py:368
  67.7 2.5 %shard_map.143 = (bf16[3,128,2048]{2,1,0:T(8,128)(2,1)S(1)}, f32[16,128,128]{2,1,0:T(8,128)S(1)}, bf16[64,1024]{1,0:T(8,128)(2,1)S(1)}) custom-call(f32[4,128]{1,0:T(4,128)S(1)} %broadcast_in_dim.4._.refs_0_, bf16[64,1024]{1,0:T(8,128)(2,1)S(1)} %shard_map.141.refs_4_.refs_1_, bf16[64,1024]{1,0:T(8,128)(2,1)S(1)} %collective-permute-done.17.refs_2_, ...), custom_call_target="tpu_custom_call" | custom-call | bytes 128 | tf_op jit(solution)/shard_map/pallas_call | solution.py:340
  70.2 3.5 %shard_map.144 = (bf16[64,1024]{1,0:T(8,128)(2,1)S(1)}, f32[64,1024]{1,0:T(8,128)S(1)}) custom-call(f32[4,128]{1,0:T(4,128)S(1)} %broadcast_in_dim.4._.refs_0_, bf16[3,128,2048]{2,1,0:T(8,128)(2,1)S(1)} %get-tuple-element.63.refs_1_, bf16[3,1024,2048]{2,1,0:T(8,128)(2,1)S(1)} %get-tuple-element.47.refs_2_.refs_5_, ...), custom_call_target="tpu_custom_call" | custom-call | bytes 128 | tf_op jit(solution)/shard_map/pallas_call | solution.py:340
  74.4 0.7 collective-permute-done.19.refs_4_
  76.0 0.8 shard_map.147
  76.8 1.7 %shard_map.148 = (f32[16,32]{1,0:T(8,128)}, f32[8,128]{1,0:T(8,128)S(1)}) custom-call(f32[16,128,128]{2,1,0:T(8,128)S(1)} %get-tuple-element.68.refs_0_, s32[128,128]{1,0:T(8,128)S(1)} %copy-done.2, f32[8,128]{1,0:T(8,128)S(1)} %get-tuple-element.69.refs_2_), custom_call_target="tpu_custom_call" | custom-call | bytes 128 | tf_op jit(solution)/shard_map/pallas_call | solution.py:340
  78.5 2.5 %collective-permute-done.20.refs_1_ = bf16[64,1024]{1,0:T(8,128)(2,1)S(1)} collective-permute-done((bf16[64,1024]{1,0:T(8,128)(2,1)S(1)}, bf16[64,1024]{1,0:T(8,128)(2,1)S(1)}, u32[]{:S(2)}, u32[]{:S(2)}) %collective-permute-start.20) | collective-permute-done | bytes 131104 | tf_op jit(solution)/shard_map/ppermute | solution.py:368
  81.1 1.3 %collective-permute-done.21.refs_2_ = bf16[64,1024]{1,0:T(8,128)(2,1)S(1)} collective-permute-done((bf16[64,1024]{1,0:T(8,128)(2,1)S(1)}, bf16[64,1024]{1,0:T(8,128)(2,1)S(1)}, u32[]{:S(2)}, u32[]{:S(2)}) %collective-permute-start.21) | collective-permute-done | bytes 131104 | tf_op jit(solution)/shard_map/ppermute | solution.py:368
  82.4 0.8 shard_map.150
  (54 shorter events, 6.1 us)
Async XLA Ops:
  0.8 12.2 %copy-start.1 = (bf16[1,128,1024]{2,1,0:T(8,128)(2,1)S(1)}, bf16[1,128,1024]{2,1,0:T(8,128)(2,1)}, u32[]{:S(2)}) copy-start(bf16[1,128,1024]{2,1,0:T(8,128)(2,1)} %refs_1_.4) | copy-start | bytes 786436
  14.7 1.5 %collective-permute-start = (bf16[64,1024]{1,0:T(8,128)(2,1)S(1)}, bf16[64,1024]{1,0:T(8,128)(2,1)S(1)}, u32[]{:S(2)}, u32[]{:S(2)}) collective-permute-start(bf16[64,1024]{1,0:T(8,128)(2,1)S(1)} %get-tuple-element.42), channel_id=1, source_target_pairs={{0,1},{1,0},{2,3},{3,2},{4,5},{5,4},{6,7},{7,6},{8,9},{9,8},{10,11... | collective-permute-start | bytes 393224 | tf_op jit(solution)/shard_map/ppermute | solution.py:368
  16.0 3.2 %copy-start.3 = (bf16[1,128,1024]{2,1,0:T(8,128)(2,1)S(1)}, bf16[1,128,1024]{2,1,0:T(8,128)(2,1)}, u32[]{:S(2)}) copy-start(bf16[1,128,1024]{2,1,0:T(8,128)(2,1)} %param.11) | copy-start | bytes 786436
  16.3 6.7 %collective-permute-start.1 = (bf16[64,1024]{1,0:T(8,128)(2,1)S(1)}, bf16[64,1024]{1,0:T(8,128)(2,1)S(1)}, u32[]{:S(2)}, u32[]{:S(2)}) collective-permute-start(bf16[64,1024]{1,0:T(8,128)(2,1)S(1)} %shard_map.124.refs_5_.refs_0_), channel_id=1, source_target_pairs={{0,2},{1,3},{2,0},{3,1},{4,6},{5,7},{6,4},{7,5},{8,10},{9,11},{10,... | collective-permute-start | bytes 393224 | tf_op jit(solution)/shard_map/ppermute | solution.py:368
  23.0 6.9 %collective-permute-start.2 = (bf16[64,1024]{1,0:T(8,128)(2,1)S(1)}, bf16[64,1024]{1,0:T(8,128)(2,1)S(1)}, u32[]{:S(2)}, u32[]{:S(2)}) collective-permute-start(bf16[64,1024]{1,0:T(8,128)(2,1)S(1)} %shard_map.126.refs_3_.refs_1_), channel_id=1, source_target_pairs={{0,4},{1,5},{2,6},{3,7},{4,8},{5,9},{6,10},{7,11},{8,12},{9,13},{1... | collective-permute-start | bytes 393224 | tf_op jit(solution)/shard_map/ppermute | solution.py:364
  24.9 5.0 %copy-start = (bf16[1,3,128,1024]{3,2,1,0:T(8,128)(2,1)S(1)}, bf16[1,3,128,1024]{3,2,1,0:T(8,128)(2,1)}, u32[]{:S(2)}) copy-start(bf16[1,3,128,1024]{3,2,1,0:T(8,128)(2,1)} %kept_ref.1) | copy-start | bytes 2359300
  24.9 5.0 %copy-start.4 = (f32[1,1024]{1,0:T(1,128)S(1)}, f32[1,1024]{1,0:T(1,128)}, u32[]{:S(2)}) copy-start(f32[1,1024]{1,0:T(1,128)} %refs_2_.5) | copy-start | bytes 12292
  28.4 1.5 %collective-permute-start.4 = (bf16[64,1024]{1,0:T(8,128)(2,1)S(1)}, bf16[64,1024]{1,0:T(8,128)(2,1)S(1)}, u32[]{:S(2)}, u32[]{:S(2)}) collective-permute-start(bf16[64,1024]{1,0:T(8,128)(2,1)S(1)} %get-tuple-element.50), channel_id=1, source_target_pairs={{0,1},{1,0},{2,3},{3,2},{4,5},{5,4},{6,7},{7,6},{8,9},{9,8},{10,11... | collective-permute-start | bytes 393224 | tf_op jit(solution)/shard_map/ppermute | solution.py:368
  29.9 5.1 %collective-permute-start.3 = (bf16[64,1024]{1,0:T(8,128)(2,1)S(1)}, bf16[64,1024]{1,0:T(8,128)(2,1)S(1)}, u32[]{:S(2)}, u32[]{:S(2)}) collective-permute-start(bf16[64,1024]{1,0:T(8,128)(2,1)S(1)} %collective-permute-done.2.refs_1_), channel_id=1, source_target_pairs={{0,1},{1,0},{2,3},{3,2},{4,5},{5,4},{6,7},{7,6},{8,9},{9,8},{10,11... | collective-permute-start | bytes 393224 | tf_op jit(solution)/shard_map/ppermute | solution.py:368
  30.1 12.0 %collective-permute-start.6 = (bf16[64,1024]{1,0:T(8,128)(2,1)S(1)}, bf16[64,1024]{1,0:T(8,128)(2,1)S(1)}, u32[]{:S(2)}, u32[]{:S(2)}) collective-permute-start(bf16[64,1024]{1,0:T(8,128)(2,1)S(1)} %shard_map.128.refs_8_), channel_id=1, source_target_pairs={{0,12},{1,13},{2,14},{3,15},{4,0},{5,1},{6,2},{7,3},{8,4},{9,5},{1... | collective-permute-start | bytes 393224 | tf_op jit(solution)/shard_map/ppermute | solution.py:364
  32.2 9.9 %collective-permute-start.7 = (bf16[64,1024]{1,0:T(8,128)(2,1)S(1)}, bf16[64,1024]{1,0:T(8,128)(2,1)S(1)}, u32[]{:S(2)}, u32[]{:S(2)}) collective-permute-start(bf16[64,1024]{1,0:T(8,128)(2,1)S(1)} %shard_map.128.refs_8_), channel_id=1, source_target_pairs={{0,14},{1,15},{2,12},{3,13},{4,2},{5,3},{6,0},{7,1},{8,6},{9,7},{1... | collective-permute-start | bytes 393224 | tf_op jit(solution)/shard_map/ppermute | solution.py:364
  38.6 4.1 %collective-permute-start.5 = (bf16[64,1024]{1,0:T(8,128)(2,1)S(1)}, bf16[64,1024]{1,0:T(8,128)(2,1)S(1)}, u32[]{:S(2)}, u32[]{:S(2)}) collective-permute-start(bf16[64,1024]{1,0:T(8,128)(2,1)S(1)} %get-tuple-element.52), channel_id=1, source_target_pairs={{0,1},{1,0},{2,3},{3,2},{4,5},{5,4},{6,7},{7,6},{8,9},{9,8},{10,11... | collective-permute-start | bytes 393224 | tf_op jit(solution)/shard_map/ppermute | solution.py:368
  42.2 1.5 %collective-permute-start.9 = (bf16[64,1024]{1,0:T(8,128)(2,1)S(1)}, bf16[64,1024]{1,0:T(8,128)(2,1)S(1)}, u32[]{:S(2)}, u32[]{:S(2)}) collective-permute-start(bf16[64,1024]{1,0:T(8,128)(2,1)S(1)} %shard_map.132.refs_4_.refs_1_), channel_id=1, source_target_pairs={{0,1},{1,0},{2,3},{3,2},{4,5},{5,4},{6,7},{7,6},{8,9},{9,8},{10,11... | collective-permute-start | bytes 393224 | tf_op jit(solution)/shard_map/ppermute | solution.py:368
  42.8 5.5 %collective-permute-start.8 = (bf16[64,1024]{1,0:T(8,128)(2,1)S(1)}, bf16[64,1024]{1,0:T(8,128)(2,1)S(1)}, u32[]{:S(2)}, u32[]{:S(2)}) collective-permute-start(bf16[64,1024]{1,0:T(8,128)(2,1)S(1)} %shard_map.133.refs_7_.refs_0_), channel_id=1, source_target_pairs={{0,2},{1,3},{2,0},{3,1},{4,6},{5,7},{6,4},{7,5},{8,10},{9,11},{10,... | collective-permute-start | bytes 393224 | tf_op jit(solution)/shard_map/ppermute | solution.py:368
  48.4 6.8 %collective-permute-start.10 = (bf16[64,1024]{1,0:T(8,128)(2,1)S(1)}, bf16[64,1024]{1,0:T(8,128)(2,1)S(1)}, u32[]{:S(2)}, u32[]{:S(2)}) collective-permute-start(bf16[64,1024]{1,0:T(8,128)(2,1)S(1)} %shard_map.135.refs_3_.refs_1_), channel_id=1, source_target_pairs={{0,4},{1,5},{2,6},{3,7},{4,8},{5,9},{6,10},{7,11},{8,12},{9,13},{1... | collective-permute-start | bytes 393224 | tf_op jit(solution)/shard_map/ppermute | solution.py:364
  52.1 3.0 %collective-permute-start.12 = (bf16[64,1024]{1,0:T(8,128)(2,1)S(1)}, bf16[64,1024]{1,0:T(8,128)(2,1)S(1)}, u32[]{:S(2)}, u32[]{:S(2)}) collective-permute-start(bf16[64,1024]{1,0:T(8,128)(2,1)S(1)} %get-tuple-element.58), channel_id=1, source_target_pairs={{0,1},{1,0},{2,3},{3,2},{4,5},{5,4},{6,7},{7,6},{8,9},{9,8},{10,11... | collective-permute-start | bytes 393224 | tf_op jit(solution)/shard_map/ppermute | solution.py:368
  55.2 2.5 %collective-permute-start.11 = (bf16[64,1024]{1,0:T(8,128)(2,1)S(1)}, bf16[64,1024]{1,0:T(8,128)(2,1)S(1)}, u32[]{:S(2)}, u32[]{:S(2)}) collective-permute-start(bf16[64,1024]{1,0:T(8,128)(2,1)S(1)} %collective-permute-done.10.refs_1_), channel_id=1, source_target_pairs={{0,1},{1,0},{2,3},{3,2},{4,5},{5,4},{6,7},{7,6},{8,9},{9,8},{10,11... | collective-permute-start | bytes 393224 | tf_op jit(solution)/shard_map/ppermute | solution.py:368
  55.4 9.3 %collective-permute-start.14 = (bf16[64,1024]{1,0:T(8,128)(2,1)S(1)}, bf16[64,1024]{1,0:T(8,128)(2,1)S(1)}, u32[]{:S(2)}, u32[]{:S(2)}) collective-permute-start(bf16[64,1024]{1,0:T(8,128)(2,1)S(1)} %shard_map.137.refs_8_), channel_id=1, source_target_pairs={{0,12},{1,13},{2,14},{3,15},{4,0},{5,1},{6,2},{7,3},{8,4},{9,5},{1... | collective-permute-start | bytes 393224 | tf_op jit(solution)/shard_map/ppermute | solution.py:364
  57.4 7.3 %collective-permute-start.15 = (bf16[64,1024]{1,0:T(8,128)(2,1)S(1)}, bf16[64,1024]{1,0:T(8,128)(2,1)S(1)}, u32[]{:S(2)}, u32[]{:S(2)}) collective-permute-start(bf16[64,1024]{1,0:T(8,128)(2,1)S(1)} %shard_map.137.refs_8_), channel_id=1, source_target_pairs={{0,14},{1,15},{2,12},{3,13},{4,2},{5,3},{6,0},{7,1},{8,6},{9,7},{1... | collective-permute-start | bytes 393224 | tf_op jit(solution)/shard_map/ppermute | solution.py:364
  64.7 1.4 %collective-permute-start.13 = (bf16[64,1024]{1,0:T(8,128)(2,1)S(1)}, bf16[64,1024]{1,0:T(8,128)(2,1)S(1)}, u32[]{:S(2)}, u32[]{:S(2)}) collective-permute-start(bf16[64,1024]{1,0:T(8,128)(2,1)S(1)} %get-tuple-element.60), channel_id=1, source_target_pairs={{0,1},{1,0},{2,3},{3,2},{4,5},{5,4},{6,7},{7,6},{8,9},{9,8},{10,11... | collective-permute-start | bytes 393224 | tf_op jit(solution)/shard_map/ppermute | solution.py:368
  64.8 2.9 %collective-permute-start.17 = (bf16[64,1024]{1,0:T(8,128)(2,1)S(1)}, bf16[64,1024]{1,0:T(8,128)(2,1)S(1)}, u32[]{:S(2)}, u32[]{:S(2)}) collective-permute-start(bf16[64,1024]{1,0:T(8,128)(2,1)S(1)} %shard_map.141.refs_4_.refs_1_), channel_id=1, source_target_pairs={{0,1},{1,0},{2,3},{3,2},{4,5},{5,4},{6,7},{7,6},{8,9},{9,8},{10,11... | collective-permute-start | bytes 393224 | tf_op jit(solution)/shard_map/ppermute | solution.py:368
  66.1 7.7 %collective-permute-start.16 = (bf16[64,1024]{1,0:T(8,128)(2,1)S(1)}, bf16[64,1024]{1,0:T(8,128)(2,1)S(1)}, u32[]{:S(2)}, u32[]{:S(2)}) collective-permute-start(bf16[64,1024]{1,0:T(8,128)(2,1)S(1)} %shard_map.142.refs_7_.refs_0_), channel_id=1, source_target_pairs={{0,2},{1,3},{2,0},{3,1},{4,6},{5,7},{6,4},{7,5},{8,10},{9,11},{10,... | collective-permute-start | bytes 393224 | tf_op jit(solution)/shard_map/ppermute | solution.py:368
  73.7 3.1 %copy-start.2 = (s32[128,128]{1,0:T(8,128)S(1)}, s32[128,128]{1,0:T(8,128)}, u32[]{:S(2)}) copy-start(s32[128,128]{1,0:T(8,128)} %refs_1_.7) | copy-start | bytes 196612
  73.7 1.4 %collective-permute-start.19 = (bf16[64,1024]{1,0:T(8,128)(2,1)S(1)}, bf16[64,1024]{1,0:T(8,128)(2,1)S(1)}, u32[]{:S(2)}, u32[]{:S(2)}) collective-permute-start(bf16[64,1024]{1,0:T(8,128)(2,1)S(1)} %get-tuple-element.66), channel_id=1, source_target_pairs={{0,1},{1,0},{2,3},{3,2},{4,5},{5,4},{6,7},{7,6},{8,9},{9,8},{10,11... | collective-permute-start | bytes 393224 | tf_op jit(solution)/shard_map/ppermute | solution.py:368
  73.9 2.1 %collective-permute-start.18 = (bf16[64,1024]{1,0:T(8,128)(2,1)S(1)}, bf16[64,1024]{1,0:T(8,128)(2,1)S(1)}, u32[]{:S(2)}, u32[]{:S(2)}) collective-permute-start(bf16[64,1024]{1,0:T(8,128)(2,1)S(1)} %shard_map.145.refs_6_.refs_1_), channel_id=1, source_target_pairs={{0,1},{1,0},{2,3},{3,2},{4,5},{5,4},{6,7},{7,6},{8,9},{9,8},{10,11... | collective-permute-start | bytes 393224 | tf_op jit(solution)/shard_map/ppermute | solution.py:368
  75.4 5.6 %collective-permute-start.20 = (bf16[64,1024]{1,0:T(8,128)(2,1)S(1)}, bf16[64,1024]{1,0:T(8,128)(2,1)S(1)}, u32[]{:S(2)}, u32[]{:S(2)}) collective-permute-start(bf16[64,1024]{1,0:T(8,128)(2,1)S(1)} %shard_map.146.refs_3_.refs_0_), channel_id=1, source_target_pairs={{0,2},{1,3},{2,0},{3,1},{4,6},{5,7},{6,4},{7,5},{8,10},{9,11},{10,... | collective-permute-start | bytes 393224 | tf_op jit(solution)/shard_map/ppermute | solution.py:368
  81.0 1.4 %collective-permute-start.21 = (bf16[64,1024]{1,0:T(8,128)(2,1)S(1)}, bf16[64,1024]{1,0:T(8,128)(2,1)S(1)}, u32[]{:S(2)}, u32[]{:S(2)}) collective-permute-start(bf16[64,1024]{1,0:T(8,128)(2,1)S(1)} %shard_map.149.refs_1_.refs_3_), channel_id=1, source_target_pairs={{0,1},{1,0},{2,3},{3,2},{4,5},{5,4},{6,7},{7,6},{8,9},{9,8},{10,11... | collective-permute-start | bytes 393224 | tf_op jit(solution)/shard_map/ppermute | solution.py:368
